TPU v7x, 256 devices: a whole 4x4x8 slice. The times are simulated.
256 devices in a mesh: blk: 32 (over z, y_hi, core), cset: 8 (over y_lo, x).
Axes of the slice: x: 4, y: 4 (y_hi: 2, y_lo: 2; y = y_hi * 2 + y_lo), z: 8, core: 2. Of those that a mesh axis runs over, the one named last changes fastest.
Arguments:
- active_table: bfloat16 [65536, 256], P(('blk', 'cset')), may hold values from 0.019897461 to 0.19921875
- passive_table: bfloat16 [65536, 256], P(('blk', 'cset')), may hold values from 0 to 0.15
- adjacency: bfloat16 [32, 8, 9, 8, 128, 128], P('blk', 'cset'), may hold values from 0 to 1, as said below
- tile_dst: int32 [32, 8, 9, 8], P('blk', 'cset'), may hold values from 0 to 1
- tile_src: int32 [32, 8, 9, 8], P('blk', 'cset'), may hold values from 0 to 15
- tile_count: int32 [32, 8, 9], P('blk', 'cset'), may hold values from 1 to 8, as said below
- split_active: int32 [20, 924], replicated, may hold values from 0 to 219, as said below
- split_passive: int32 [20, 924], replicated, may hold values from 0 to 219, as said below
Outputs:
- joined_table: bfloat16 [65536, 1024], P('blk', 'cset')
Inputs may be any that keep to these rules, and one draw needn't show every extreme that they name: For each six-color set s, the 20 pairs (split_active[j, s], split_passive[j, s]) name its 20 divisions into an ordered pair of three-color sets, each once, as columns of the two child tables; a child table's columns hold its 220 color sets in some fixed order, and columns 220 and above are never named. `split_passive`: see split_active; each table is a column order of its own. `tile_count`: the own partition's slot r = 4 is full on every device. `adjacency`: edge weights are 0 or 1.
All inputs are finite; a program needn't handle non-finite values.
Results may differ from a plain program's by a relative error of at most 0.0026.
Values may be sent and summed in bfloat16 or wider, within the bound.
No kernel may reach another device: no remote copies, remote signals or barrier semaphores. Data moves between devices by JAX's collectives and lax.ppermute only.
A program may use at most 64 MiB of HBM per device.

v0:
```python
import jax
import jax.numpy as jnp
from jax import lax
from jax.sharding import PartitionSpec as P

SPLITS = 20
OUTPAD = 1024
TILE = 128


def shifted(block, axis, distance):
    devices = range(lax.axis_size(axis))
    route = [((i - distance) % len(devices), i) for i in devices]
    return lax.ppermute(block, axis, route)


def add_partition(accumulated, incoming, slot, tiles_all, dst_all, src_all, count_all):
    tiles = lax.dynamic_index_in_dim(tiles_all, slot, 0, keepdims=False)
    dst_rows = lax.dynamic_index_in_dim(dst_all, slot, 0, keepdims=False)
    src_rows = lax.dynamic_index_in_dim(src_all, slot, 0, keepdims=False)
    count_now = lax.dynamic_index_in_dim(count_all, slot, 0, keepdims=False)
    blocks = incoming.reshape(incoming.shape[0] // TILE, TILE, incoming.shape[1])
    chosen = jnp.take(blocks, src_rows, axis=0)
    live = (jnp.arange(tiles.shape[0], dtype=jnp.int32) < count_now).astype(jnp.bfloat16)
    masked = tiles * live[:, None, None]
    product = jnp.einsum("tij,tjc->tic", masked, chosen, preferred_element_type=jnp.float32)
    row_tiles = accumulated.shape[0] // TILE
    placing = (dst_rows[:, None] == jnp.arange(row_tiles, dtype=jnp.int32)[None, :]).astype(
        jnp.float32
    )
    summed = jnp.einsum("td,tic->dic", placing, product, precision=lax.Precision.HIGHEST)
    return accumulated + summed.reshape(accumulated.shape)


def combine_sets(left, right, left_cols, right_cols):
    channel = jnp.arange(left.shape[1], dtype=jnp.int32)
    joined = jnp.zeros((left.shape[0], left_cols.shape[1]), jnp.float32)
    for split in range(SPLITS):
        pick_left = (left_cols[split][None, :] == channel[:, None]).astype(jnp.bfloat16)
        pick_right = (right_cols[split][None, :] == channel[:, None]).astype(jnp.bfloat16)
        joined = joined + jnp.dot(left, pick_left, preferred_element_type=jnp.float32) * jnp.dot(
            right, pick_right, preferred_element_type=jnp.float32
        )
    return joined.astype(jnp.bfloat16)


def local(
    active_table,
    passive_table,
    adjacency,
    tile_dst,
    tile_src,
    tile_count,
    split_active,
    split_passive,
):
    tiles_all = adjacency[0, 0]
    dst_all = tile_dst[0, 0]
    src_all = tile_src[0, 0]
    count_all = tile_count[0, 0]
    reach_half = (tiles_all.shape[0] - 1) // 2
    partition_rows = lax.all_gather(passive_table, "cset", axis=0, tiled=True)
    accumulated = jnp.zeros((passive_table.shape[0], passive_table.shape[1]), jnp.float32)
    accumulated = add_partition(
        accumulated, partition_rows, reach_half, tiles_all, dst_all, src_all, count_all
    )

    def upward(step, state):
        moving, summed = state
        moving = shifted(moving, "blk", 1)
        summed = add_partition(
            summed, moving, reach_half - step, tiles_all, dst_all, src_all, count_all
        )
        return (moving, summed)

    def downward(step, state):
        moving, summed = state
        moving = shifted(moving, "blk", -1)
        summed = add_partition(
            summed, moving, reach_half + step, tiles_all, dst_all, src_all, count_all
        )
        return (moving, summed)

    moved, accumulated = lax.fori_loop(1, reach_half + 1, upward, (partition_rows, accumulated))
    moved, accumulated = lax.fori_loop(1, reach_half + 1, downward, (partition_rows, accumulated))
    neighbour = accumulated.astype(jnp.bfloat16)
    extra = OUTPAD - split_active.shape[1]
    left_cols = jnp.pad(split_active, ((0, 0), (0, extra)), constant_values=-1)
    right_cols = jnp.pad(split_passive, ((0, 0), (0, extra)), constant_values=-1)
    wide_active, wide_neighbour = (
        lax.all_gather(active_table, "cset", axis=0, tiled=True),
        lax.all_gather(neighbour, "cset", axis=0, tiled=True),
    )
    width = OUTPAD // lax.axis_size("cset")
    start = lax.axis_index("cset") * width
    own_left = lax.dynamic_slice_in_dim(left_cols, start, width, 1)
    own_right = lax.dynamic_slice_in_dim(right_cols, start, width, 1)
    return combine_sets(wide_active, wide_neighbour, own_left, own_right)


def solution(mesh):
    in_specs = (
        P(("blk", "cset"), None),
        P(("blk", "cset"), None),
        P("blk", "cset", None, None, None, None),
        P("blk", "cset", None, None),
        P("blk", "cset", None, None),
        P("blk", "cset", None),
        P(),
        P(),
    )
    out_specs = P("blk", "cset")
    return jax.shard_map(local, mesh=mesh, in_specs=in_specs, out_specs=out_specs, check_vma=False)
```

profile of v0, /device:TPU:2, one launch (start us, length us, event | category | flops | bytes accessed | tf_op | source)
XLA Modules:
  0.0 336.0 jit_solution(17324726909210273614)
XLA Ops:
  7.3 1.3 dynamic_slice.131
  8.6 0.8 copy.37
  9.4 0.8 copy.38
  10.1 0.9 slice_reduce_fusion
  11.0 0.9 slice_reduce_fusion.1
  12.6 38.7 %all-gather.6.cloned.1.call-done = bf16[2048,256]{1,0:T(8,128)(2,1)} async-done(((bf16[256,256]{1,0:T(8,128)(2,1)}), bf16[2048,256]{1,0:T(8,128)(2,1)}) %all-gather.6.cloned.1.call-update) | async-done | bytes 1048592 | tf_op jit(solution)/shard_map/all_gather | solution.py:62
  51.3 1.9 gather_fusion.2
  53.2 1.3 fusion.74
  54.5 1.2 fusion.72
  55.7 1.0 copy.100
  56.7 88.8 %while.38 = (s32[]{:T(128)}, bf16[2048,256]{1,0:T(8,128)(2,1)}, f32[256,256]{1,0:T(8,128)S(1)}, s32[9,8]{1,0:T(8,128)S(1)}, bf16[9,8,128,128]{3,2,1,0:T(8,128)(2...) while((s32[]{:T(128)}, bf16[2048,256]{1,0:T(8,128)(2,1)}, ...), condition=%wide.region_1.3_spmd, body=%wide.region_0.2_spmd.sunk | while | flops 73860184 | bytes 11801071 | solution.py:84
  58.0 16.7 %collective-permute-done = bf16[2048,256]{1,0:T(8,128)(2,1)S(1)} collective-permute-done((bf16[2048,256]{1,0:T(8,128)(2,1)}, bf16[2048,256]{1,0:T(8,128)(2,1)S(1)}, u32[]{:S(2)}, u32[]{:S(2)}) %collective-permute-start) | collective-permute-done | bytes 1048608 | tf_op jit(solution)/shard_map/while/body/eval_jaxpr/ppermute | solution.py:14
  75.3 1.3 fusion.240
  76.6 1.2 fusion.242
  77.9 1.0 copy.106
  80.2 16.7 %collective-permute-done = bf16[2048,256]{1,0:T(8,128)(2,1)S(1)} collective-permute-done((bf16[2048,256]{1,0:T(8,128)(2,1)}, bf16[2048,256]{1,0:T(8,128)(2,1)S(1)}, u32[]{:S(2)}, u32[]{:S(2)}) %collective-permute-start) | collective-permute-done | bytes 1048608 | tf_op jit(solution)/shard_map/while/body/eval_jaxpr/ppermute | solution.py:14
  97.5 1.3 fusion.240
  98.8 1.2 fusion.242
  100.1 1.0 copy.106
  102.4 16.7 %collective-permute-done = bf16[2048,256]{1,0:T(8,128)(2,1)S(1)} collective-permute-done((bf16[2048,256]{1,0:T(8,128)(2,1)}, bf16[2048,256]{1,0:T(8,128)(2,1)S(1)}, u32[]{:S(2)}, u32[]{:S(2)}) %collective-permute-start) | collective-permute-done | bytes 1048608 | tf_op jit(solution)/shard_map/while/body/eval_jaxpr/ppermute | solution.py:14
  119.7 1.3 fusion.240
  121.0 1.2 fusion.242
  122.3 1.0 copy.106
  124.7 16.7 %collective-permute-done = bf16[2048,256]{1,0:T(8,128)(2,1)S(1)} collective-permute-done((bf16[2048,256]{1,0:T(8,128)(2,1)}, bf16[2048,256]{1,0:T(8,128)(2,1)S(1)}, u32[]{:S(2)}, u32[]{:S(2)}) %collective-permute-start) | collective-permute-done | bytes 1048608 | tf_op jit(solution)/shard_map/while/body/eval_jaxpr/ppermute | solution.py:14
  141.9 1.3 fusion.240
  143.3 1.2 fusion.242
  144.5 1.0 copy.106
  145.5 79.1 %while.39 = (s32[]{:T(128)}, bf16[2048,256]{1,0:T(8,128)(2,1)S(1)}, f32[256,256]{1,0:T(8,128)S(1)}, s32[9,8]{1,0:T(8,128)S(1)}, bf16[9,8,128,128]{3,2,1,0:T(8,12...) while((s32[]{:T(128)}, bf16[2048,256]{1,0:T(8,128)(2,1)S(1)}, ...), condition=%wide.region_3.5_spmd, body=%wide.region_2.4_spmd.sunk | while | flops 73860184 | bytes 11801071 | solution.py:85
  146.8 11.0 %collective-permute-done.1 = bf16[2048,256]{1,0:T(8,128)(2,1)S(1)} collective-permute-done((bf16[2048,256]{1,0:T(8,128)(2,1)S(1)}, bf16[2048,256]{1,0:T(8,128)(2,1)S(1)}, u32[]{:S(2)}, u32[]{:S(2)}) %collective-permute-start.1) | collective-permute-done | bytes 1048608 | tf_op jit(solution)/shard_map/while/body/eval_jaxpr/ppermute | solution.py:14
  158.4 1.3 fusion.246
  159.7 1.2 fusion.248
  161.1 5.6 %collective-permute-start.1 = (bf16[2048,256]{1,0:T(8,128)(2,1)S(1)}, bf16[2048,256]{1,0:T(8,128)(2,1)S(1)}, u32[]{:S(2)}, u32[]{:S(2)}) collective-permute-start(bf16[2048,256]{1,0:T(8,128)(2,1)S(1)} %get-tuple-element.711), channel_id=1, source_target_pairs={{8,0},{16,8},{24,16},{32,24},{40,32},{48,40},{56,48},{64,56},{72,6... | collective-permute-start | bytes 3145736 | tf_op jit(solution)/shard_map/while/body/eval_jaxpr/ppermute | solution.py:14
  168.0 11.0 %collective-permute-done.1 = bf16[2048,256]{1,0:T(8,128)(2,1)S(1)} collective-permute-done((bf16[2048,256]{1,0:T(8,128)(2,1)S(1)}, bf16[2048,256]{1,0:T(8,128)(2,1)S(1)}, u32[]{:S(2)}, u32[]{:S(2)}) %collective-permute-start.1) | collective-permute-done | bytes 1048608 | tf_op jit(solution)/shard_map/while/body/eval_jaxpr/ppermute | solution.py:14
  179.6 1.3 fusion.246
  180.9 1.2 fusion.248
  182.3 5.6 %collective-permute-start.1 = (bf16[2048,256]{1,0:T(8,128)(2,1)S(1)}, bf16[2048,256]{1,0:T(8,128)(2,1)S(1)}, u32[]{:S(2)}, u32[]{:S(2)}) collective-permute-start(bf16[2048,256]{1,0:T(8,128)(2,1)S(1)} %get-tuple-element.711), channel_id=1, source_target_pairs={{8,0},{16,8},{24,16},{32,24},{40,32},{48,40},{56,48},{64,56},{72,6... | collective-permute-start | bytes 3145736 | tf_op jit(solution)/shard_map/while/body/eval_jaxpr/ppermute | solution.py:14
  189.2 11.0 %collective-permute-done.1 = bf16[2048,256]{1,0:T(8,128)(2,1)S(1)} collective-permute-done((bf16[2048,256]{1,0:T(8,128)(2,1)S(1)}, bf16[2048,256]{1,0:T(8,128)(2,1)S(1)}, u32[]{:S(2)}, u32[]{:S(2)}) %collective-permute-start.1) | collective-permute-done | bytes 1048608 | tf_op jit(solution)/shard_map/while/body/eval_jaxpr/ppermute | solution.py:14
  200.8 1.3 fusion.246
  202.1 1.2 fusion.248
  203.5 5.6 %collective-permute-start.1 = (bf16[2048,256]{1,0:T(8,128)(2,1)S(1)}, bf16[2048,256]{1,0:T(8,128)(2,1)S(1)}, u32[]{:S(2)}, u32[]{:S(2)}) collective-permute-start(bf16[2048,256]{1,0:T(8,128)(2,1)S(1)} %get-tuple-element.711), channel_id=1, source_target_pairs={{8,0},{16,8},{24,16},{32,24},{40,32},{48,40},{56,48},{64,56},{72,6... | collective-permute-start | bytes 3145736 | tf_op jit(solution)/shard_map/while/body/eval_jaxpr/ppermute | solution.py:14
  210.4 11.0 %collective-permute-done.1 = bf16[2048,256]{1,0:T(8,128)(2,1)S(1)} collective-permute-done((bf16[2048,256]{1,0:T(8,128)(2,1)S(1)}, bf16[2048,256]{1,0:T(8,128)(2,1)S(1)}, u32[]{:S(2)}, u32[]{:S(2)}) %collective-permute-start.1) | collective-permute-done | bytes 1048608 | tf_op jit(solution)/shard_map/while/body/eval_jaxpr/ppermute | solution.py:14
  222.0 1.3 fusion.246
  223.3 1.2 fusion.248
  226.8 40.4 %all-gather.8.cloned.1.call-done = bf16[2048,256]{1,0:T(8,128)(2,1)} async-done(((bf16[256,256]{1,0:T(8,128)(2,1)}), bf16[2048,256]{1,0:T(8,128)(2,1)}) %all-gather.8.cloned.1.call-update) | async-done | bytes 1048592 | tf_op jit(solution)/shard_map/all_gather | solution.py:92
  267.2 2.8 fusion.95
  270.0 1.5 fusion.85
  271.5 1.6 fusion.87
  273.0 1.5 fusion.89
  274.5 1.5 fusion.91
  276.0 1.5 fusion.93
  277.5 1.5 fusion.83
  278.9 1.5 fusion.81
  280.4 1.5 fusion.99
  281.9 1.5 fusion.101
  283.4 1.4 fusion.103
  284.8 1.5 fusion.105
  286.3 1.5 fusion.107
  288.3 1.5 fusion.97
  289.7 1.5 fusion.113
  291.2 1.5 fusion.115
  292.6 1.5 fusion.117
  295.0 14.5 %all-gather.4.cloned.1.call-done = bf16[2048,256]{1,0:T(8,128)(2,1)} async-done(((bf16[256,256]{1,0:T(8,128)(2,1)}), bf16[2048,256]{1,0:T(8,128)(2,1)}) %all-gather.4.cloned.1.call-update) | async-done | bytes 1048592 | tf_op jit(solution)/shard_map/all_gather | solution.py:91
  309.6 2.2 fusion.46
  328.4 1.0 copy.61
  (150 shorter events, 37.6 us)
Async XLA Ops:
  6.5 44.7 %all-gather.6.cloned.1.call-start = ((), (), s32[]{:S(2)}) async-start(), calls=%async_computation.1 | async-start | bytes 1179648 | tf_op jit(solution)/shard_map/all_gather | solution.py:62
  7.3 259.9 %all-gather.8.cloned.1.call-start = ((), (), s32[]{:S(2)}) async-start(), calls=%async_computation.2 | async-start | bytes 1179648 | tf_op jit(solution)/shard_map/all_gather | solution.py:92
  51.2 4.4 %copy-start.18 = (bf16[2048,256]{1,0:T(8,128)(2,1)S(1)}, bf16[2048,256]{1,0:T(8,128)(2,1)}, u32[]{:S(2)}) copy-start(bf16[2048,256]{1,0:T(8,128)(2,1)} %all-gather.6.cloned.1.call-done) | copy-start | bytes 3145732
  54.5 2.2 copy-start.21
  56.7 18.0 %collective-permute-start = (bf16[2048,256]{1,0:T(8,128)(2,1)}, bf16[2048,256]{1,0:T(8,128)(2,1)S(1)}, u32[]{:S(2)}, u32[]{:S(2)}) collective-permute-start(bf16[2048,256]{1,0:T(8,128)(2,1)} %get-tuple-element.678), channel_id=1, source_target_pairs={{248,0},{0,8},{8,16},{16,24},{24,32},{32,40},{40,48},{48,56},{56,6... | collective-permute-start | bytes 3145736 | tf_op jit(solution)/shard_map/while/body/eval_jaxpr/ppermute | solution.py:14
  78.9 18.0 %collective-permute-start = (bf16[2048,256]{1,0:T(8,128)(2,1)}, bf16[2048,256]{1,0:T(8,128)(2,1)S(1)}, u32[]{:S(2)}, u32[]{:S(2)}) collective-permute-start(bf16[2048,256]{1,0:T(8,128)(2,1)} %get-tuple-element.678), channel_id=1, source_target_pairs={{248,0},{0,8},{8,16},{16,24},{24,32},{32,40},{40,48},{48,56},{56,6... | collective-permute-start | bytes 3145736 | tf_op jit(solution)/shard_map/while/body/eval_jaxpr/ppermute | solution.py:14
  101.1 18.0 %collective-permute-start = (bf16[2048,256]{1,0:T(8,128)(2,1)}, bf16[2048,256]{1,0:T(8,128)(2,1)S(1)}, u32[]{:S(2)}, u32[]{:S(2)}) collective-permute-start(bf16[2048,256]{1,0:T(8,128)(2,1)} %get-tuple-element.678), channel_id=1, source_target_pairs={{248,0},{0,8},{8,16},{16,24},{24,32},{32,40},{40,48},{48,56},{56,6... | collective-permute-start | bytes 3145736 | tf_op jit(solution)/shard_map/while/body/eval_jaxpr/ppermute | solution.py:14
  123.3 18.0 %collective-permute-start = (bf16[2048,256]{1,0:T(8,128)(2,1)}, bf16[2048,256]{1,0:T(8,128)(2,1)S(1)}, u32[]{:S(2)}, u32[]{:S(2)}) collective-permute-start(bf16[2048,256]{1,0:T(8,128)(2,1)} %get-tuple-element.678), channel_id=1, source_target_pairs={{248,0},{0,8},{8,16},{16,24},{24,32},{32,40},{40,48},{48,56},{56,6... | collective-permute-start | bytes 3145736 | tf_op jit(solution)/shard_map/while/body/eval_jaxpr/ppermute | solution.py:14
  145.5 80.6 %copy-start.19 = (s32[20,924]{1,0:T(8,128)S(1)}, s32[20,924]{1,0:T(8,128)}, u32[]{:S(2)}) copy-start(s32[20,924]{1,0:T(8,128)} %param.21) | copy-start | bytes 221764
  145.5 80.7 %copy-start.20 = (s32[20,924]{1,0:T(8,128)S(1)}, s32[20,924]{1,0:T(8,128)}, u32[]{:S(2)}) copy-start(s32[20,924]{1,0:T(8,128)} %param.20) | copy-start | bytes 221764
  145.5 12.3 %collective-permute-start.1 = (bf16[2048,256]{1,0:T(8,128)(2,1)S(1)}, bf16[2048,256]{1,0:T(8,128)(2,1)S(1)}, u32[]{:S(2)}, u32[]{:S(2)}) collective-permute-start(bf16[2048,256]{1,0:T(8,128)(2,1)S(1)} %get-tuple-element.711), channel_id=1, source_target_pairs={{8,0},{16,8},{24,16},{32,24},{40,32},{48,40},{56,48},{64,56},{72,6... | collective-permute-start | bytes 3145736 | tf_op jit(solution)/shard_map/while/body/eval_jaxpr/ppermute | solution.py:14
  161.1 17.9 %collective-permute-start.1 = (bf16[2048,256]{1,0:T(8,128)(2,1)S(1)}, bf16[2048,256]{1,0:T(8,128)(2,1)S(1)}, u32[]{:S(2)}, u32[]{:S(2)}) collective-permute-start(bf16[2048,256]{1,0:T(8,128)(2,1)S(1)} %get-tuple-element.711), channel_id=1, source_target_pairs={{8,0},{16,8},{24,16},{32,24},{40,32},{48,40},{56,48},{64,56},{72,6... | collective-permute-start | bytes 3145736 | tf_op jit(solution)/shard_map/while/body/eval_jaxpr/ppermute | solution.py:14
  182.3 17.9 %collective-permute-start.1 = (bf16[2048,256]{1,0:T(8,128)(2,1)S(1)}, bf16[2048,256]{1,0:T(8,128)(2,1)S(1)}, u32[]{:S(2)}, u32[]{:S(2)}) collective-permute-start(bf16[2048,256]{1,0:T(8,128)(2,1)S(1)} %get-tuple-element.711), channel_id=1, source_target_pairs={{8,0},{16,8},{24,16},{32,24},{40,32},{48,40},{56,48},{64,56},{72,6... | collective-permute-start | bytes 3145736 | tf_op jit(solution)/shard_map/while/body/eval_jaxpr/ppermute | solution.py:14
  203.5 17.9 %collective-permute-start.1 = (bf16[2048,256]{1,0:T(8,128)(2,1)S(1)}, bf16[2048,256]{1,0:T(8,128)(2,1)S(1)}, u32[]{:S(2)}, u32[]{:S(2)}) collective-permute-start(bf16[2048,256]{1,0:T(8,128)(2,1)S(1)} %get-tuple-element.711), channel_id=1, source_target_pairs={{8,0},{16,8},{24,16},{32,24},{40,32},{48,40},{56,48},{64,56},{72,6... | collective-permute-start | bytes 3145736 | tf_op jit(solution)/shard_map/while/body/eval_jaxpr/ppermute | solution.py:14
  225.3 84.2 %all-gather.4.cloned.1.call-start = ((), (), s32[]{:S(2)}) async-start(), calls=%async_computation | async-start | bytes 1179648 | tf_op jit(solution)/shard_map/all_gather | solution.py:91
  267.2 2.8 copy-start
  309.6 2.2 copy-start.1
  309.6 2.2 copy-start.15
  311.7 1.2 copy-start.14
  312.3 1.3 copy-start.13
  313.5 1.3 copy-start.11
  314.1 1.3 copy-start.9
  315.2 1.3 copy-start.7
  315.9 1.3 copy-start.12
  317.0 1.3 copy-start.10
  317.6 1.3 copy-start.8
  318.7 1.3 copy-start.5
  319.4 1.3 copy-start.3
  321.2 1.2 copy-start.6
  321.7 1.3 copy-start.4
  323.0 1.2 copy-start.2
  324.7 1.2 copy-start.16
  325.9 1.2 copy-start.17
Sparse Core Ops, SparseCore 0:
  9.1 42.0 all-gather.5
  225.5 41.7 all-gather.7
  269.0 40.5 all-gather.3
where the time goes:
time: 339 us; the launch traced here: 336 us
  waiting for transfers between devices  206 us (61%)
  matrix products  62 us (18%)
  local copies, waits for them, and re-layouts  30.2 us (9%)
  starting transfers between devices  17.1 us (5%)
  between operations  13.5 us (4%)
  other arithmetic  7.15 us (2%)
    ppermute x8, waiting for transfers between devices, shifted(): return lax.ppermute(block, axis, route)  111 us
    all_gather x1, waiting for transfers between devices, local(): lax.all_gather(neighbour, 'cset', axis=0, tiled=True)  40.4 us
    all_gather x1, waiting for transfers between devices, local(): partition_rows = lax.all_gather(passive_table, 'cset', axis=0, tiled=True)  38.7 us
    dot_general x20, matrix products, combine_sets(): jnp.dot(right, pick_right, preferred_element_type=jnp.float32)  27.8 us
    ppermute x8, starting transfers between devices, shifted(): return lax.ppermute(block, axis, route)  16.8 us
    all_gather x1, waiting for transfers between devices, local(): lax.all_gather(active_table, 'cset', axis=0, tiled=True)  14.5 us
    dot_general x9, matrix products, add_partition(): jnp.einsum('tij,tjc->tic', masked, chosen, preferred_element_type=jnp.flo...  11.9 us
    dot_general x20, matrix products, combine_sets(): jnp.dot(left, pick_left, preferred_element_type=jnp.float32)  11.8 us
  transfers between devices with their start and end apart: 11, of which 11 were waited for; matrix products, arithmetic and copies ran while one was open for 13% of the time, Pallas kernels for 0%

commit v1 on v0

v1 whole, which is shorter than its diff:
```python
import jax
import jax.numpy as jnp
from jax import lax
from jax.experimental import pallas as pl
from jax.experimental.pallas import tpu as pltpu
from jax.sharding import PartitionSpec as P

SPLITS = 20
OUTPAD = 1024
TILE = 128
CHUNK = 256
VMEM_LIMIT = 40 * 1024 * 1024


def routed(block, chips, flip):
    nb, nc = lax.axis_size("blk"), lax.axis_size("cset")
    route = []
    for b in range(nb):
        for c in range(nc):
            target = c ^ (nc // 2) if flip else c
            route.append((b * nc + c, ((b + 2 * chips) % nb) * nc + target))
    return lax.ppermute(block, ("blk", "cset"), route)


def across_cset(block, step):
    nc = lax.axis_size("cset")
    return lax.ppermute(block, "cset", [(c, c ^ step) for c in range(nc)])


def across_cores(block):
    nb = lax.axis_size("blk")
    return lax.ppermute(block, "blk", [(b, b ^ 1) for b in range(nb)])


def pick_kernel(cols_ref, table_ref, out_ref):
    width = cols_ref.shape[2]
    channel = lax.broadcasted_iota(jnp.int32, (table_ref.shape[1], width), 0)
    onehot = (channel == cols_ref[0]).astype(jnp.bfloat16)
    out_ref[0] = jnp.dot(
        table_ref[...], onehot, preferred_element_type=jnp.float32
    ).astype(jnp.bfloat16)


def pick_columns(table, cols):
    rows, channels = table.shape
    splits, _, width = cols.shape
    return pl.pallas_call(
        pick_kernel,
        grid=(splits,),
        in_specs=[
            pl.BlockSpec((1, 1, width), lambda j: (j, 0, 0)),
            pl.BlockSpec((rows, channels), lambda j: (0, 0)),
        ],
        out_specs=pl.BlockSpec((1, rows, width), lambda j: (j, 0, 0)),
        out_shape=jax.ShapeDtypeStruct((splits, rows, width), jnp.bfloat16),
        compiler_params=pltpu.CompilerParams(vmem_limit_bytes=VMEM_LIMIT),
        cost_estimate=pl.CostEstimate(
            flops=2 * splits * rows * channels * width,
            bytes_accessed=2 * splits * rows * width,
            transcendentals=0,
        ),
        name="pick_active",
    )(cols, table)


def sum_kernel(place_ref, tiles_ref, sources_ref, out_ref, wide, gathered, sems):
    slots = tiles_ref.shape[0]
    copies = []
    for t in range(slots):
        copy = pltpu.make_async_copy(
            sources_ref.at[place_ref[0, t]], gathered.at[t], sems.at[t]
        )
        copy.start()
        copies.append(copy)
    wide[0 : 2 * TILE] = jnp.zeros((2 * TILE, slots * TILE), jnp.bfloat16)
    for t in range(slots):
        row = pl.multiple_of(place_ref[1, t] * TILE, TILE)
        wide[pl.ds(row, TILE), t * TILE : (t + 1) * TILE] = tiles_ref[t]
    for copy in copies:
        copy.wait()
    out_ref[...] = jnp.dot(
        wide[0 : 2 * TILE],
        gathered[...].reshape(slots * TILE, gathered.shape[2]),
        preferred_element_type=jnp.float32,
    ).astype(out_ref.dtype)


def sum_tiles(place, tiles, sources, dtype, name):
    slots = tiles.shape[0]
    channels = sources.shape[2]
    return pl.pallas_call(
        sum_kernel,
        in_specs=[
            pl.BlockSpec(memory_space=pltpu.SMEM),
            pl.BlockSpec(memory_space=pltpu.VMEM),
            pl.BlockSpec(memory_space=pl.ANY),
        ],
        out_specs=pl.BlockSpec(memory_space=pltpu.VMEM),
        out_shape=jax.ShapeDtypeStruct((2 * TILE, channels), dtype),
        scratch_shapes=[
            pltpu.VMEM((3 * TILE, slots * TILE), jnp.bfloat16),
            pltpu.VMEM((slots, TILE, channels), jnp.bfloat16),
            pltpu.SemaphoreType.DMA((slots,)),
        ],
        compiler_params=pltpu.CompilerParams(vmem_limit_bytes=VMEM_LIMIT),
        cost_estimate=pl.CostEstimate(
            flops=4 * TILE * TILE * slots * channels,
            bytes_accessed=2 * slots * TILE * (TILE + channels),
            transcendentals=0,
        ),
        name=name,
    )(place, tiles, sources)


def join_kernel(cols_ref, own_ref, n0, n1, n2, n3, picked_ref, out_ref):
    total = own_ref[...]
    for part in (n0, n1, n2, n3):
        total = total + part[...].astype(jnp.float32)
    neighbour = total.astype(jnp.bfloat16)
    width = picked_ref.shape[2]
    channel = lax.broadcasted_iota(jnp.int32, (neighbour.shape[1], width), 0)
    joined = jnp.zeros((neighbour.shape[0], width), jnp.float32)
    for j in range(SPLITS):
        onehot = (channel == cols_ref[j]).astype(jnp.bfloat16)
        joined = joined + picked_ref[j].astype(jnp.float32) * jnp.dot(
            neighbour, onehot, preferred_element_type=jnp.float32
        )
    for piece in range(width // TILE):
        out_ref[piece] = joined[:, piece * TILE : (piece + 1) * TILE].astype(out_ref.dtype)


def join(own, parts, picked, cols):
    rows, channels = own.shape
    splits, _, width = cols.shape
    whole = pl.BlockSpec((rows, channels), lambda q: (0, 0))
    return pl.pallas_call(
        join_kernel,
        grid=(width // CHUNK,),
        in_specs=[pl.BlockSpec((splits, 1, CHUNK), lambda q: (0, 0, q))]
        + [whole] * 5
        + [pl.BlockSpec((splits, rows, CHUNK), lambda q: (0, 0, q))],
        out_specs=pl.BlockSpec((CHUNK // TILE, rows, TILE), lambda q: (q, 0, 0)),
        out_shape=jax.ShapeDtypeStruct((width // TILE, rows, TILE), jnp.bfloat16),
        compiler_params=pltpu.CompilerParams(vmem_limit_bytes=VMEM_LIMIT),
        cost_estimate=pl.CostEstimate(
            flops=2 * splits * rows * channels * width,
            bytes_accessed=2 * splits * rows * width,
            transcendentals=0,
        ),
        name="join_sets",
    )(cols, own, *parts, picked)


def local(
    active_table,
    passive_table,
    adjacency,
    tile_dst,
    tile_src,
    tile_count,
    split_active,
    split_passive,
):
    tiles_all = adjacency[0, 0]
    dst_all, src_all, count_all = tile_dst[0, 0], tile_src[0, 0], tile_count[0, 0]
    reach, slots = dst_all.shape
    nc = lax.axis_size("cset")
    me = lax.axis_index("cset")
    core = lax.axis_index("blk") % 2

    slot_of = jnp.arange(slots, dtype=jnp.int32)[None, :]
    relative = jnp.arange(reach, dtype=jnp.int32) - reach // 2 + core
    parity = relative % 2
    group = relative // 2 + 2
    landing = jnp.where(group % 2 == 1, me ^ (nc // 2), me)
    held = (
        (parity != core).astype(jnp.int32)[:, None] * (2 * nc)
        + ((src_all // 2) ^ landing[:, None]) * 2
        + src_all % 2
    )
    row = jnp.where(slot_of < count_all[:, None], dst_all, 2)

    def pair(which):
        if which == 0:
            start = 0
        elif which == 4:
            start = reach - 2
        else:
            start = 2 * which - core
        rows = lax.dynamic_slice_in_dim(row, start, 2, 0)
        mine = lax.dynamic_slice_in_dim(group, start, 2, 0) == which
        rows = jnp.where(mine[:, None], rows, 2).reshape(-1)
        places = lax.dynamic_slice_in_dim(held, start, 2, 0).reshape(-1)
        tiles = lax.dynamic_slice_in_dim(tiles_all, start, 2, 0)
        return jnp.stack([places, rows]), tiles.reshape(2 * slots, TILE, TILE)

    own_place, own_tiles = pair(2)
    away = []
    for which in (1, 3, 0, 4):
        place, tiles = pair(which)
        chips, flip = which - 2, which % 2 == 1
        away.append((chips, flip, routed(place, chips, flip), routed(tiles, chips, flip)))

    held_rows = jnp.concatenate(
        [passive_table] + [across_cset(passive_table, step) for step in range(1, nc)], axis=0
    )
    both = jnp.concatenate([held_rows, across_cores(held_rows)], axis=0)
    sources = both.reshape(-1, TILE, both.shape[1])

    extra = OUTPAD - split_active.shape[1]
    left_cols = jnp.pad(split_active, ((0, 0), (0, extra)), constant_values=-1)[:, None, :]
    right_cols = jnp.pad(split_passive, ((0, 0), (0, extra)), constant_values=-1)[:, None, :]
    picked = pick_columns(active_table, left_cols)

    parts = []
    for chips, flip, place, tiles in away:
        part = sum_tiles(place, tiles, sources, jnp.bfloat16, "sum_for_others")
        parts.append(routed(part, -chips, flip))
    own = sum_tiles(own_place, own_tiles, sources, jnp.float32, "sum_own")
    joined = join(own, parts, picked, right_cols)
    spread = lax.all_to_all(joined, "cset", split_axis=0, concat_axis=0, tiled=True)
    return spread.reshape(-1, TILE)


def solution(mesh):
    in_specs = (
        P(("blk", "cset"), None),
        P(("blk", "cset"), None),
        P("blk", "cset", None, None, None, None),
        P("blk", "cset", None, None),
        P("blk", "cset", None, None),
        P("blk", "cset", None),
        P(),
        P(),
    )
    out_specs = P("blk", "cset")
    return jax.shard_map(local, mesh=mesh, in_specs=in_specs, out_specs=out_specs, check_vma=False)
```

time: 339 us -> 113 us (0.33)
  waiting for transfers between devices: 206 us -> 3.77 us
  matrix products: 62 us -> 0 us
  Pallas kernels: 0 us -> 29.1 us
  starting transfers between devices: 17.1 us -> 38.4 us
  between operations: 13.5 us -> 0.27 us
  blocking collectives: 0 us -> 11.4 us
  other arithmetic: 7.15 us -> 2.88 us
    ppermute x8 -> x20, waiting for transfers between devices: 111 us -> 3.77 us  [the longest x7 3.29 us: across_cset(): return lax.ppermute(block, 'cset', [(c, c ^ step) for c in range(nc)])]
    all_gather x3 -> x0, waiting for transfers between devices: 93.6 us -> none  [the longest x1 40.4 us: local(): lax.all_gather(neighbour, 'cset', axis=0, tiled=True)]
    dot_general x58 -> x0, matrix products: 62 us -> none  [the longest x20 27.8 us: combine_sets(): jnp.dot(right, pick_right, preferred_element_type=jnp.float32)]
    pallas_call x0 -> x7, Pallas kernels: none -> 29.1 us  [the longest x5 15.2 us: sum_tiles(): pl.pallas_call(sum_kernel, in_specs=[pl.BlockSpec(memory_space=pltpu.SMEM...]
    ppermute x8 -> x20, starting transfers between devices: 16.8 us -> 38.4 us  [the longest x12 27.9 us: routed(): return lax.ppermute(block, ('blk', 'cset'), route)]
    all_to_all x0 -> x1, blocking collectives: none -> 11.4 us  [local(): lax.all_to_all(joined, 'cset', split_axis=0, concat_axis=0, tiled=True)]
    unnamed x45 -> x24, local copies, waits for them, and re-layouts: 7.79 us -> 16 us
    gather x9 -> x0, local copies, waits for them, and re-layouts: 6.52 us -> none  [add_partition(): chosen = jnp.take(blocks, src_rows, axis=0)]
  transfers between devices with their start and end apart: 11 -> 20, of which waited for: 11 -> 3; matrix products, arithmetic and copies ran while one was open for 13% -> 18% of each run, Pallas kernels for 0% -> 20%
where the time goes in v1:
time: 113 us
  starting transfers between devices  38.4 us (34%)
  Pallas kernels  29.1 us (26%)
  local copies, waits for them, and re-layouts  27 us (24%)
  blocking collectives  11.4 us (10%)
  waiting for transfers between devices  3.77 us (3%)
  other arithmetic  2.88 us (3%)
    ppermute x12, starting transfers between devices, routed(): return lax.ppermute(block, ('blk', 'cset'), route)  27.9 us
    unnamed x24, local copies, waits for them, and re-layouts  16 us
    pallas_call x5, Pallas kernels, sum_tiles(): pl.pallas_call(sum_kernel, in_specs=[pl.BlockSpec(memory_space=pltpu.SMEM...  15.2 us
    all_to_all x1, blocking collectives, local(): lax.all_to_all(joined, 'cset', split_axis=0, concat_axis=0, tiled=True)  11.4 us
    ppermute x7, starting transfers between devices, across_cset(): return lax.ppermute(block, 'cset', [(c, c ^ step) for c in range(nc)])  10.5 us
    pallas_call x1, Pallas kernels, pick_columns(): pl.pallas_call(pick_kernel, grid=(splits,), in_specs=[pl.BlockSpec((1, 1,...  7.13 us
    pallas_call x1, Pallas kernels, join(): pl.pallas_call(join_kernel, grid=(width // CHUNK,), in_specs=[pl.BlockSpe...  6.77 us
    ppermute x7, waiting for transfers between devices, across_cset(): return lax.ppermute(block, 'cset', [(c, c ^ step) for c in range(nc)])  3.29 us
  transfers between devices with their start and end apart: 20, of which 3 were waited for; matrix products, arithmetic and copies ran while one was open for 18% of the time, Pallas kernels for 20%

profile of v1, /device:TPU:2, one launch (start us, length us, event | category | flops | bytes accessed | tf_op | source)
XLA Modules:
  0.0 112.9 jit_solution(16713584272321715277)
XLA Ops:
  0.0 3.1 %collective-permute-start.5 = (bf16[256,256]{1,0:T(8,128)(2,1)}, bf16[256,256]{1,0:T(8,128)(2,1)S(1)}, u32[]{:S(2)}, u32[]{:S(2)}) collective-permute-start(bf16[256,256]{1,0:T(8,128)(2,1)} %param.9), channel_id=1, source_target_pairs={{0,6},{1,7},{2,4},{3,5},{4,2},{5,3},{6,0},{7,1},{8,14},{9,15},{10,... | collective-permute-start | bytes 393224 | tf_op jit(solution)/shard_map/ppermute | solution.py:27
  3.1 1.3 %collective-permute-start.4 = (bf16[256,256]{1,0:T(8,128)(2,1)}, bf16[256,256]{1,0:T(8,128)(2,1)}, u32[]{:S(2)}, u32[]{:S(2)}) collective-permute-start(bf16[256,256]{1,0:T(8,128)(2,1)} %param.9), channel_id=1, source_target_pairs={{0,5},{1,4},{2,7},{3,6},{4,1},{5,0},{6,3},{7,2},{8,13},{9,12},{10,... | collective-permute-start | bytes 393224 | tf_op jit(solution)/shard_map/ppermute | solution.py:27
  4.5 1.6 %collective-permute-start.3 = (bf16[256,256]{1,0:T(8,128)(2,1)}, bf16[256,256]{1,0:T(8,128)(2,1)S(1)}, u32[]{:S(2)}, u32[]{:S(2)}) collective-permute-start(bf16[256,256]{1,0:T(8,128)(2,1)} %param.9), channel_id=1, source_target_pairs={{0,4},{1,5},{2,6},{3,7},{4,0},{5,1},{6,2},{7,3},{8,12},{9,13},{10,... | collective-permute-start | bytes 393224 | tf_op jit(solution)/shard_map/ppermute | solution.py:27
  6.1 2.5 %collective-permute-start = (bf16[256,256]{1,0:T(8,128)(2,1)}, bf16[256,256]{1,0:T(8,128)(2,1)S(1)}, u32[]{:S(2)}, u32[]{:S(2)}) collective-permute-start(bf16[256,256]{1,0:T(8,128)(2,1)} %param.9), channel_id=1, source_target_pairs={{0,1},{1,0},{2,3},{3,2},{4,5},{5,4},{6,7},{7,6},{8,9},{9,8},{10,11... | collective-permute-start | bytes 393224 | tf_op jit(solution)/shard_map/ppermute | solution.py:27
  8.7 0.1 slice_compare_fusion
  8.8 3.2 %fusion.11 = (bf16[1,1,2,8,128,128]{5,4,3,2,1,0:T(8,128)(2,1)}, bf16[1,1,2,8,128,128]{5,4,3,2,1,0:T(8,128)(2,1)}, bf16[1,1,2,8,128,128]{5,4,3,2,1,0:T(8,128)(2,1...) fusion(bf16[1,1,9,8,128,128]{5,4,3,2,1,0:T(8,128)(2,1)} %param.10, s32[]{:T(128)S(6)} %select_n.103, ...), kind=kLoop, calls=%fused_computation.69 | loop fusion | bytes 5242892 | tf_op jit(solution)/shard_map/dynamic_slice | solution.py:194
  12.0 0.1 slice_select_fusion
  12.1 0.7 constant_dynamic-update-slice_fusion.7
  12.7 0.1 copy.18
  12.8 0.7 stack_reshape.39
  13.6 0.6 stack_reshape.37
  14.3 0.7 stack_reshape.35
  14.9 0.1 copy.12
  15.0 0.7 stack_reshape.33
  15.7 0.8 collective-permute-done
  16.4 0.7 collective-permute-start.2
  17.2 0.7 constant_dynamic-update-slice_fusion.6
  17.8 1.2 %collective-permute-start.6 = (bf16[256,256]{1,0:T(8,128)(2,1)S(1)}, bf16[256,256]{1,0:T(8,128)(2,1)S(1)}, u32[]{:S(2)}, u32[]{:S(2)}) collective-permute-start(bf16[256,256]{1,0:T(8,128)(2,1)S(1)} %copy-done.3), channel_id=1, source_target_pairs={{0,7},{1,6},{2,5},{3,4},{4,3},{5,2},{6,1},{7,0},{8,15},{9,14},{10,... | collective-permute-start | bytes 393224 | tf_op jit(solution)/shard_map/ppermute | solution.py:27
  19.0 0.7 constant_dynamic-update-slice_fusion.5
  19.7 2.5 %collective-permute-done.2 = bf16[256,256]{1,0:T(8,128)(2,1)S(1)} collective-permute-done((bf16[256,256]{1,0:T(8,128)(2,1)S(1)}, bf16[256,256]{1,0:T(8,128)(2,1)S(1)}, u32[]{:S(2)}, u32[]{:S(2)}) %collective-permute-start.2) | collective-permute-done | bytes 131104 | tf_op jit(solution)/shard_map/ppermute | solution.py:27
  22.2 2.5 %collective-permute-start.12 = (bf16[16,128,128]{2,1,0:T(8,128)(2,1)}, bf16[16,128,128]{2,1,0:T(8,128)(2,1)}, u32[]{:S(2)}, u32[]{:S(2)}) collective-permute-start(bf16[16,128,128]{2,1,0:T(8,128)(2,1)} %bitcast.6), channel_id=1, source_target_pairs={{0,20},{1,21},{2,22},{3,23},{4,16},{5,17},{6,18},{7,19},{8,28},{9,... | collective-permute-start | bytes 1572872 | tf_op jit(solution)/shard_map/ppermute | solution.py:22
  24.7 0.7 constant_dynamic-update-slice_fusion.4
  25.4 0.7 copy-done.4
  26.0 1.9 %collective-permute-start.18 = (bf16[16,128,128]{2,1,0:T(8,128)(2,1)}, bf16[16,128,128]{2,1,0:T(8,128)(2,1)S(1)}, u32[]{:S(2)}, u32[]{:S(2)}) collective-permute-start(bf16[16,128,128]{2,1,0:T(8,128)(2,1)} %bitcast.37), channel_id=1, source_target_pairs={{0,32},{1,33},{2,34},{3,35},{4,36},{5,37},{6,38},{7,39},{8,40},{9,... | collective-permute-start | bytes 1572872 | tf_op jit(solution)/shard_map/ppermute | solution.py:22
  27.9 1.6 %constant_dynamic-update-slice_fusion.3 = (bf16[2048,256]{1,0:T(8,128)(2,1)}, bf16[4096,256]{1,0:T(8,128)(2,1)S(1)}) fusion(bf16[2048,256]{1,0:T(8,128)(2,1)} %get-tuple-element.18, bf16[256,256]{1,0:T(8,128)(2,1)} %copy-done.4, bf16[4096,256]{1,0:T(8,128)(2,1)S(1)} %get-tuple-element.19), kind=kLoop, calls=%fused_computation.3 | loop fusion | bytes 393216
  29.5 3.4 %collective-permute-start.9 = (bf16[16,128,128]{2,1,0:T(8,128)(2,1)}, bf16[16,128,128]{2,1,0:T(8,128)(2,1)}, u32[]{:S(2)}, u32[]{:S(2)}) collective-permute-start(bf16[16,128,128]{2,1,0:T(8,128)(2,1)} %bitcast.39), channel_id=1, source_target_pairs={{0,244},{1,245},{2,246},{3,247},{4,240},{5,241},{6,242},{7,243},{8... | collective-permute-start | bytes 1572872 | tf_op jit(solution)/shard_map/ppermute | solution.py:22
  32.9 1.6 %constant_dynamic-update-slice_fusion.2 = (bf16[2048,256]{1,0:T(8,128)(2,1)}, bf16[4096,256]{1,0:T(8,128)(2,1)S(1)}) fusion(bf16[2048,256]{1,0:T(8,128)(2,1)} %get-tuple-element.16, bf16[256,256]{1,0:T(8,128)(2,1)} %collective-permute-done.4, bf16[4096,256]{1,0:T(8,128)(2,1)S(1)} %get-tuple-element.17), kind=kLoop, calls=%fused_computation.2 | loop fusion | bytes 393216
  34.5 2.2 %collective-permute-start.15 = (bf16[16,128,128]{2,1,0:T(8,128)(2,1)}, bf16[16,128,128]{2,1,0:T(8,128)(2,1)}, u32[]{:S(2)}, u32[]{:S(2)}) collective-permute-start(bf16[16,128,128]{2,1,0:T(8,128)(2,1)} %bitcast.38), channel_id=1, source_target_pairs={{0,224},{1,225},{2,226},{3,227},{4,228},{5,229},{6,230},{7,231},{8... | collective-permute-start | bytes 1572872 | tf_op jit(solution)/shard_map/ppermute | solution.py:22
  36.7 0.7 constant_dynamic-update-slice_fusion.1
  37.4 0.7 constant_dynamic-update-slice_fusion
  38.2 0.1 stack_reshape.38
  38.3 0.1 copy.15
  38.4 0.1 stack_reshape.36
  38.6 0.1 stack_reshape.34
  38.7 0.1 stack_reshape.32
  38.8 0.7 pad_add_fusion.4
  39.5 0.6 pad_add_fusion.3
  40.1 0.7 pad_add_fusion.2
  40.8 0.7 pad_add_fusion.1
  41.5 0.1 stack_reshape.31
  41.7 0.1 stack_reshape.30
  41.8 0.9 pad.8
  42.8 0.9 pad.7
  43.7 7.1 %pick_active.1.picked_ref = bf16[20,256,1024]{2,1,0:T(8,128)(2,1)S(1)} custom-call(s32[20,1,1024]{2,1,0:T(1,128)S(1)} %broadcast_in_dim.69.cols_ref, bf16[256,256]{1,0:T(8,128)(2,1)S(1)} %copy-done.2), custom_call_target="tpu_custom_call" | custom-call | flops 2684354560 | bytes 10485760 | tf_op jit(solution)/shard_map/pick_active/pallas_call | solution.py:47
  50.9 4.0 %copy-done = bf16[20,256,1024]{2,1,0:T(8,128)(2,1)} copy-done((bf16[20,256,1024]{2,1,0:T(8,128)(2,1)}, bf16[20,256,1024]{2,1,0:T(8,128)(2,1)S(1)}, u32[]{:S(2)}) %copy-start) | copy-done | bytes 10485784
  54.9 3.0 %collective-permute-start.8 = (s32[2,16]{1,0:T(2,128)S(1)}, s32[2,16]{1,0:T(2,128)S(1)}, u32[]{:S(2)}, u32[]{:S(2)}) collective-permute-start(s32[2,16]{1,0:T(2,128)S(1)} %pad_add_fusion.1), channel_id=1, source_target_pairs={{0,244},{1,245},{2,246},{3,247},{4,240},{5,241},{6,242},{7,243},{8... | collective-permute-start | bytes 392 | tf_op jit(solution)/shard_map/ppermute | solution.py:22
  57.9 1.3 %constant_dynamic-update-slice_fusion.8 = bf16[4096,256]{1,0:T(8,128)(2,1)S(1)} fusion(bf16[4096,256]{1,0:T(8,128)(2,1)S(1)} %get-tuple-element.11, bf16[2048,256]{1,0:T(8,128)(2,1)} %collective-permute-done.7), kind=kLoop, calls=%fused_computation.8 | loop fusion | bytes 2097152 | tf_op jit(solution)/shard_map/concatenate | solution.py:207
  59.2 0.5 collective-permute-done.8.place_ref
  59.7 2.5 %collective-permute-start.11 = (s32[2,16]{1,0:T(2,128)S(1)}, s32[2,16]{1,0:T(2,128)S(1)}, u32[]{:S(2)}, u32[]{:S(2)}) collective-permute-start(s32[2,16]{1,0:T(2,128)S(1)} %pad_add_fusion.2), channel_id=1, source_target_pairs={{0,20},{1,21},{2,22},{3,23},{4,16},{5,17},{6,18},{7,19},{8,28},{9,... | collective-permute-start | bytes 392 | tf_op jit(solution)/shard_map/ppermute | solution.py:22
  62.1 3.2 %collective-permute-start.14 = (s32[2,16]{1,0:T(2,128)S(1)}, s32[2,16]{1,0:T(2,128)S(1)}, u32[]{:S(2)}, u32[]{:S(2)}) collective-permute-start(s32[2,16]{1,0:T(2,128)S(1)} %pad_add_fusion.3), channel_id=1, source_target_pairs={{0,224},{1,225},{2,226},{3,227},{4,228},{5,229},{6,230},{7,231},{8... | collective-permute-start | bytes 392 | tf_op jit(solution)/shard_map/ppermute | solution.py:22
  65.4 3.2 %sum_for_others.4 = bf16[256,256]{1,0:T(8,128)(2,1)S(1)} custom-call(s32[2,16]{1,0:T(2,128)S(1)} %collective-permute-done.8.place_ref, bf16[16,128,128]{2,1,0:T(8,128)(2,1)} %collective-permute-done.9.tiles_ref, bf16[32,128,256]{2,1,0:T(8,128)(2,1)S(1)} %bitcast.30), custom_call_target="tpu_custom_call" | custom-call | flops 268435456 | bytes 1572864 | tf_op jit(solution)/shard_map/sum_for_others/pallas_call | solution.py:91
  68.6 0.3 collective-permute-start.17
  68.9 0.3 collective-permute-start.10
  69.2 3.2 %sum_for_others.5 = bf16[256,256]{1,0:T(8,128)(2,1)S(1)} custom-call(s32[2,16]{1,0:T(2,128)S(1)} %collective-permute-done.11.place_ref, bf16[16,128,128]{2,1,0:T(8,128)(2,1)} %collective-permute-done.12.tiles_ref, bf16[32,128,256]{2,1,0:T(8,128)(2,1)S(1)} %bitcast.31), custom_call_target="tpu_custom_call" | custom-call | flops 268435456 | bytes 1572864 | tf_op jit(solution)/shard_map/sum_for_others/pallas_call | solution.py:91
  72.5 5.2 %collective-permute-start.13 = (bf16[256,256]{1,0:T(8,128)(2,1)S(1)}, bf16[256,256]{1,0:T(8,128)(2,1)S(1)}, u32[]{:S(2)}, u32[]{:S(2)}) collective-permute-start(bf16[256,256]{1,0:T(8,128)(2,1)S(1)} %sum_for_others.5), channel_id=1, source_target_pairs={{0,244},{1,245},{2,246},{3,247},{4,240},{5,241},{6,242},{7,243},{8... | collective-permute-start | bytes 393224 | tf_op jit(solution)/shard_map/ppermute | solution.py:22
  77.7 3.2 %sum_for_others.6 = bf16[256,256]{1,0:T(8,128)(2,1)S(1)} custom-call(s32[2,16]{1,0:T(2,128)S(1)} %collective-permute-done.14.place_ref, bf16[16,128,128]{2,1,0:T(8,128)(2,1)} %collective-permute-done.15.tiles_ref, bf16[32,128,256]{2,1,0:T(8,128)(2,1)S(1)} %bitcast.32), custom_call_target="tpu_custom_call" | custom-call | flops 268435456 | bytes 1572864 | tf_op jit(solution)/shard_map/sum_for_others/pallas_call | solution.py:91
  81.0 0.1 collective-permute-start.16
  81.1 2.8 %sum_for_others.7 = bf16[256,256]{1,0:T(8,128)(2,1)S(1)} custom-call(s32[2,16]{1,0:T(2,128)S(1)} %collective-permute-done.17.place_ref, bf16[16,128,128]{2,1,0:T(8,128)(2,1)S(1)} %collective-permute-done.18.tiles_ref, bf16[32,128,256]{2,1,0:T(8,128)(2,1)S(1)} %bitcast.33), custom_call_target="tpu_custom_call" | custom-call | flops 268435456 | bytes 1572864 | tf_op jit(solution)/shard_map/sum_for_others/pallas_call | solution.py:91
  83.8 3.3 %collective-permute-start.19 = (bf16[256,256]{1,0:T(8,128)(2,1)S(1)}, bf16[256,256]{1,0:T(8,128)(2,1)S(1)}, u32[]{:S(2)}, u32[]{:S(2)}) collective-permute-start(bf16[256,256]{1,0:T(8,128)(2,1)S(1)} %sum_for_others.7), channel_id=1, source_target_pairs={{0,224},{1,225},{2,226},{3,227},{4,228},{5,229},{6,230},{7,231},{8... | collective-permute-start | bytes 393224 | tf_op jit(solution)/shard_map/ppermute | solution.py:22
  87.1 2.7 %sum_own.1.own_ref = f32[256,256]{1,0:T(8,128)S(1)} custom-call(s32[2,16]{1,0:T(2,128)S(1)} %pad_add_fusion.place_ref, bf16[16,128,128]{2,1,0:T(8,128)(2,1)S(1)} %bitcast.35, bf16[32,128,256]{2,1,0:T(8,128)(2,1)S(1)} %bitcast.34), custom_call_target="tpu_custom_call" | custom-call | flops 268435456 | bytes 1572864 | tf_op jit(solution)/shard_map/sum_own/pallas_call | solution.py:91
  89.9 4.0 %copy-done.1 = bf16[20,256,1024]{2,1,0:T(8,128)(2,1)S(1)} copy-done((bf16[20,256,1024]{2,1,0:T(8,128)(2,1)S(1)}, bf16[20,256,1024]{2,1,0:T(8,128)(2,1)}, u32[]{:S(2)}) %copy-start.1) | copy-done | bytes 10485784
  93.9 6.8 %join_sets.1 = bf16[8,256,128]{2,1,0:T(8,128)(2,1)S(1)} custom-call(s32[20,1,1024]{2,1,0:T(1,128)S(1)} %broadcast_in_dim.60.cols_ref, f32[256,256]{1,0:T(8,128)S(1)} %sum_own.1.own_ref, bf16[256,256]{1,0:T(8,128)(2,1)S(1)} %collective-permute-done.10.n0, bf16[256,256]{1,0:T(8,128)(2,1)S(1)} %collective-permute-done.13.n1, ...), custom_call_target="tpu_custom_call" | custom-call | flops 2684354560 | bytes 10485760 | tf_op jit(solution)/shard_map/join_sets/pallas_call | solution.py:136
  100.7 11.4 %all_to_all.5 = bf16[8,256,128]{2,1,0:T(8,128)(2,1)S(1)} all-to-all(bf16[8,256,128]{2,1,0:T(8,128)(2,1)S(1)} %join_sets.1), channel_id=1, replica_groups=mesh['blk'=32,'cset'=8] {'cset'}, dimensions={0} | all-to-all | bytes 1048576 | tf_op jit(solution)/shard_map/all_to_all | solution.py:221
  112.1 0.8 copy.35
  (47 shorter events, 1.0 us)
Async XLA Ops:
  0.0 34.5 %collective-permute-start.5 = (bf16[256,256]{1,0:T(8,128)(2,1)}, bf16[256,256]{1,0:T(8,128)(2,1)S(1)}, u32[]{:S(2)}, u32[]{:S(2)}) collective-permute-start(bf16[256,256]{1,0:T(8,128)(2,1)} %param.9), channel_id=1, source_target_pairs={{0,6},{1,7},{2,4},{3,5},{4,2},{5,3},{6,0},{7,1},{8,14},{9,15},{10,... | collective-permute-start | bytes 393224 | tf_op jit(solution)/shard_map/ppermute | solution.py:27
  3.1 26.4 %collective-permute-start.4 = (bf16[256,256]{1,0:T(8,128)(2,1)}, bf16[256,256]{1,0:T(8,128)(2,1)}, u32[]{:S(2)}, u32[]{:S(2)}) collective-permute-start(bf16[256,256]{1,0:T(8,128)(2,1)} %param.9), channel_id=1, source_target_pairs={{0,5},{1,4},{2,7},{3,6},{4,1},{5,0},{6,3},{7,2},{8,13},{9,12},{10,... | collective-permute-start | bytes 393224 | tf_op jit(solution)/shard_map/ppermute | solution.py:27
  4.5 20.9 %collective-permute-start.3 = (bf16[256,256]{1,0:T(8,128)(2,1)}, bf16[256,256]{1,0:T(8,128)(2,1)S(1)}, u32[]{:S(2)}, u32[]{:S(2)}) collective-permute-start(bf16[256,256]{1,0:T(8,128)(2,1)} %param.9), channel_id=1, source_target_pairs={{0,4},{1,5},{2,6},{3,7},{4,0},{5,1},{6,2},{7,3},{8,12},{9,13},{10,... | collective-permute-start | bytes 393224 | tf_op jit(solution)/shard_map/ppermute | solution.py:27
  6.0 11.8 %collective-permute-start.1 = (bf16[256,256]{1,0:T(8,128)(2,1)}, bf16[256,256]{1,0:T(8,128)(2,1)S(1)}, u32[]{:S(2)}, u32[]{:S(2)}) collective-permute-start(bf16[256,256]{1,0:T(8,128)(2,1)} %param.9), channel_id=1, source_target_pairs={{0,2},{1,3},{2,0},{3,1},{4,6},{5,7},{6,4},{7,5},{8,10},{9,11},{10,... | collective-permute-start | bytes 393224 | tf_op jit(solution)/shard_map/ppermute | solution.py:27
  6.1 10.3 %collective-permute-start = (bf16[256,256]{1,0:T(8,128)(2,1)}, bf16[256,256]{1,0:T(8,128)(2,1)S(1)}, u32[]{:S(2)}, u32[]{:S(2)}) collective-permute-start(bf16[256,256]{1,0:T(8,128)(2,1)} %param.9), channel_id=1, source_target_pairs={{0,1},{1,0},{2,3},{3,2},{4,5},{5,4},{6,7},{7,6},{8,9},{9,8},{10,11... | collective-permute-start | bytes 393224 | tf_op jit(solution)/shard_map/ppermute | solution.py:27
  8.8 3.2 %copy-start.5 = (s32[1,1,9,8]{2,3,1,0:T(8,128)S(1)}, s32[1,1,9,8]{2,3,1,0:T(8,128)}, u32[]{:S(2)}) copy-start(s32[1,1,9,8]{2,3,1,0:T(8,128)} %param.11) | copy-start | bytes 868
  8.8 3.2 %copy-start.7 = (s32[1,1,9]{2,1,0:T(1,128)S(1)}, s32[1,1,9]{2,1,0:T(1,128)}, u32[]{:S(2)}) copy-start(s32[1,1,9]{2,1,0:T(1,128)} %param.13) | copy-start | bytes 112
  8.8 3.3 %copy-start.3 = (bf16[256,256]{1,0:T(8,128)(2,1)S(1)}, bf16[256,256]{1,0:T(8,128)(2,1)}, u32[]{:S(2)}) copy-start(bf16[256,256]{1,0:T(8,128)(2,1)} %param.9) | copy-start | bytes 393220
  11.9 26.1 %copy-start.6 = (s32[1,1,9,8]{2,3,1,0:T(8,128)S(1)}, s32[1,1,9,8]{2,3,1,0:T(8,128)}, u32[]{:S(2)}) copy-start(s32[1,1,9,8]{2,3,1,0:T(8,128)} %param.12) | copy-start | bytes 868
  11.9 31.8 %copy-start.2 = (bf16[256,256]{1,0:T(8,128)(2,1)S(1)}, bf16[256,256]{1,0:T(8,128)(2,1)}, u32[]{:S(2)}) copy-start(bf16[256,256]{1,0:T(8,128)(2,1)} %table_ref.1) | copy-start | bytes 393220
  16.4 5.8 %collective-permute-start.2 = (bf16[256,256]{1,0:T(8,128)(2,1)S(1)}, bf16[256,256]{1,0:T(8,128)(2,1)S(1)}, u32[]{:S(2)}, u32[]{:S(2)}) collective-permute-start(bf16[256,256]{1,0:T(8,128)(2,1)S(1)} %copy-done.3), channel_id=1, source_target_pairs={{0,3},{1,2},{2,1},{3,0},{4,7},{5,6},{6,5},{7,4},{8,11},{9,10},{10,... | collective-permute-start | bytes 393224 | tf_op jit(solution)/shard_map/ppermute | solution.py:27
  17.8 19.6 %collective-permute-start.6 = (bf16[256,256]{1,0:T(8,128)(2,1)S(1)}, bf16[256,256]{1,0:T(8,128)(2,1)S(1)}, u32[]{:S(2)}, u32[]{:S(2)}) collective-permute-start(bf16[256,256]{1,0:T(8,128)(2,1)S(1)} %copy-done.3), channel_id=1, source_target_pairs={{0,7},{1,6},{2,5},{3,4},{4,3},{5,2},{6,1},{7,0},{8,15},{9,14},{10,... | collective-permute-start | bytes 393224 | tf_op jit(solution)/shard_map/ppermute | solution.py:27
  22.2 46.7 %collective-permute-start.12 = (bf16[16,128,128]{2,1,0:T(8,128)(2,1)}, bf16[16,128,128]{2,1,0:T(8,128)(2,1)}, u32[]{:S(2)}, u32[]{:S(2)}) collective-permute-start(bf16[16,128,128]{2,1,0:T(8,128)(2,1)} %bitcast.6), channel_id=1, source_target_pairs={{0,20},{1,21},{2,22},{3,23},{4,16},{5,17},{6,18},{7,19},{8,28},{9,... | collective-permute-start | bytes 1572872 | tf_op jit(solution)/shard_map/ppermute | solution.py:22
  25.4 0.7 copy-start.4
  26.0 55.0 %collective-permute-start.18 = (bf16[16,128,128]{2,1,0:T(8,128)(2,1)}, bf16[16,128,128]{2,1,0:T(8,128)(2,1)S(1)}, u32[]{:S(2)}, u32[]{:S(2)}) collective-permute-start(bf16[16,128,128]{2,1,0:T(8,128)(2,1)} %bitcast.37), channel_id=1, source_target_pairs={{0,32},{1,33},{2,34},{3,35},{4,36},{5,37},{6,38},{7,39},{8,40},{9,... | collective-permute-start | bytes 1572872 | tf_op jit(solution)/shard_map/ppermute | solution.py:22
  29.5 32.6 %collective-permute-start.9 = (bf16[16,128,128]{2,1,0:T(8,128)(2,1)}, bf16[16,128,128]{2,1,0:T(8,128)(2,1)}, u32[]{:S(2)}, u32[]{:S(2)}) collective-permute-start(bf16[16,128,128]{2,1,0:T(8,128)(2,1)} %bitcast.39), channel_id=1, source_target_pairs={{0,244},{1,245},{2,246},{3,247},{4,240},{5,241},{6,242},{7,243},{8... | collective-permute-start | bytes 1572872 | tf_op jit(solution)/shard_map/ppermute | solution.py:22
  34.5 43.2 %collective-permute-start.15 = (bf16[16,128,128]{2,1,0:T(8,128)(2,1)}, bf16[16,128,128]{2,1,0:T(8,128)(2,1)}, u32[]{:S(2)}, u32[]{:S(2)}) collective-permute-start(bf16[16,128,128]{2,1,0:T(8,128)(2,1)} %bitcast.38), channel_id=1, source_target_pairs={{0,224},{1,225},{2,226},{3,227},{4,228},{5,229},{6,230},{7,231},{8... | collective-permute-start | bytes 1572872 | tf_op jit(solution)/shard_map/ppermute | solution.py:22
  38.0 16.8 %collective-permute-start.7 = (bf16[2048,256]{1,0:T(8,128)(2,1)}, bf16[2048,256]{1,0:T(8,128)(2,1)}, u32[]{:S(2)}, u32[]{:S(2)}) collective-permute-start(bf16[2048,256]{1,0:T(8,128)(2,1)} %get-tuple-element.10), channel_id=1, source_target_pairs={{0,8},{8,0},{16,24},{24,16},{32,40},{40,32},{48,56},{56,48},{64,72... | collective-permute-start | bytes 3145736 | tf_op jit(solution)/shard_map/ppermute | solution.py:32
  50.9 4.0 %copy-start = (bf16[20,256,1024]{2,1,0:T(8,128)(2,1)}, bf16[20,256,1024]{2,1,0:T(8,128)(2,1)S(1)}, u32[]{:S(2)}) copy-start(bf16[20,256,1024]{2,1,0:T(8,128)(2,1)S(1)} %pick_active.1.picked_ref) | copy-start | bytes 31457284
  54.9 4.8 %collective-permute-start.8 = (s32[2,16]{1,0:T(2,128)S(1)}, s32[2,16]{1,0:T(2,128)S(1)}, u32[]{:S(2)}, u32[]{:S(2)}) collective-permute-start(s32[2,16]{1,0:T(2,128)S(1)} %pad_add_fusion.1), channel_id=1, source_target_pairs={{0,244},{1,245},{2,246},{3,247},{4,240},{5,241},{6,242},{7,243},{8... | collective-permute-start | bytes 392 | tf_op jit(solution)/shard_map/ppermute | solution.py:22
  59.7 9.0 %collective-permute-start.11 = (s32[2,16]{1,0:T(2,128)S(1)}, s32[2,16]{1,0:T(2,128)S(1)}, u32[]{:S(2)}, u32[]{:S(2)}) collective-permute-start(s32[2,16]{1,0:T(2,128)S(1)} %pad_add_fusion.2), channel_id=1, source_target_pairs={{0,20},{1,21},{2,22},{3,23},{4,16},{5,17},{6,18},{7,19},{8,28},{9,... | collective-permute-start | bytes 392 | tf_op jit(solution)/shard_map/ppermute | solution.py:22
  62.1 10.3 %collective-permute-start.14 = (s32[2,16]{1,0:T(2,128)S(1)}, s32[2,16]{1,0:T(2,128)S(1)}, u32[]{:S(2)}, u32[]{:S(2)}) collective-permute-start(s32[2,16]{1,0:T(2,128)S(1)} %pad_add_fusion.3), channel_id=1, source_target_pairs={{0,224},{1,225},{2,226},{3,227},{4,228},{5,229},{6,230},{7,231},{8... | collective-permute-start | bytes 392 | tf_op jit(solution)/shard_map/ppermute | solution.py:22
  68.6 12.4 %collective-permute-start.17 = (s32[2,16]{1,0:T(2,128)S(1)}, s32[2,16]{1,0:T(2,128)S(1)}, u32[]{:S(2)}, u32[]{:S(2)}) collective-permute-start(s32[2,16]{1,0:T(2,128)S(1)} %pad_add_fusion.4), channel_id=1, source_target_pairs={{0,32},{1,33},{2,34},{3,35},{4,36},{5,37},{6,38},{7,39},{8,40},{9,... | collective-permute-start | bytes 392 | tf_op jit(solution)/shard_map/ppermute | solution.py:22
  68.9 21.0 %collective-permute-start.10 = (bf16[256,256]{1,0:T(8,128)(2,1)S(1)}, bf16[256,256]{1,0:T(8,128)(2,1)S(1)}, u32[]{:S(2)}, u32[]{:S(2)}) collective-permute-start(bf16[256,256]{1,0:T(8,128)(2,1)S(1)} %sum_for_others.4), channel_id=1, source_target_pairs={{0,20},{1,21},{2,22},{3,23},{4,16},{5,17},{6,18},{7,19},{8,28},{9,... | collective-permute-start | bytes 393224 | tf_op jit(solution)/shard_map/ppermute | solution.py:22
  72.5 17.4 %collective-permute-start.13 = (bf16[256,256]{1,0:T(8,128)(2,1)S(1)}, bf16[256,256]{1,0:T(8,128)(2,1)S(1)}, u32[]{:S(2)}, u32[]{:S(2)}) collective-permute-start(bf16[256,256]{1,0:T(8,128)(2,1)S(1)} %sum_for_others.5), channel_id=1, source_target_pairs={{0,244},{1,245},{2,246},{3,247},{4,240},{5,241},{6,242},{7,243},{8... | collective-permute-start | bytes 393224 | tf_op jit(solution)/shard_map/ppermute | solution.py:22
  81.0 8.9 %collective-permute-start.16 = (bf16[256,256]{1,0:T(8,128)(2,1)S(1)}, bf16[256,256]{1,0:T(8,128)(2,1)S(1)}, u32[]{:S(2)}, u32[]{:S(2)}) collective-permute-start(bf16[256,256]{1,0:T(8,128)(2,1)S(1)} %sum_for_others.6), channel_id=1, source_target_pairs={{0,32},{1,33},{2,34},{3,35},{4,36},{5,37},{6,38},{7,39},{8,40},{9,... | collective-permute-start | bytes 393224 | tf_op jit(solution)/shard_map/ppermute | solution.py:22
  83.8 6.1 %collective-permute-start.19 = (bf16[256,256]{1,0:T(8,128)(2,1)S(1)}, bf16[256,256]{1,0:T(8,128)(2,1)S(1)}, u32[]{:S(2)}, u32[]{:S(2)}) collective-permute-start(bf16[256,256]{1,0:T(8,128)(2,1)S(1)} %sum_for_others.7), channel_id=1, source_target_pairs={{0,224},{1,225},{2,226},{3,227},{4,228},{5,229},{6,230},{7,231},{8... | collective-permute-start | bytes 393224 | tf_op jit(solution)/shard_map/ppermute | solution.py:22
  89.9 4.0 %copy-start.1 = (bf16[20,256,1024]{2,1,0:T(8,128)(2,1)S(1)}, bf16[20,256,1024]{2,1,0:T(8,128)(2,1)}, u32[]{:S(2)}) copy-start(bf16[20,256,1024]{2,1,0:T(8,128)(2,1)} %copy-done) | copy-start | bytes 31457284

commit v2 on v1

v2 whole, which is shorter than its diff:
```python
import jax
import jax.numpy as jnp
from jax import lax
from jax.experimental import pallas as pl
from jax.experimental.pallas import tpu as pltpu
from jax.sharding import PartitionSpec as P

SPLITS = 20
OUTPAD = 1024
TILE = 128
CHUNK = 256
SLOTS = 8
PAIR = 2 * SLOTS
TAIL = 16
AWAY = (1, 3, 0, 4)
VMEM_LIMIT = 16 * 1024 * 1024


def routed(block, chips, flip):
    nb, nc = lax.axis_size("blk"), lax.axis_size("cset")
    route = []
    for b in range(nb):
        for c in range(nc):
            target = c ^ (nc // 2) if flip else c
            route.append((b * nc + c, ((b + 2 * chips) % nb) * nc + target))
    return lax.ppermute(block, ("blk", "cset"), route)


def places(which, at_ref, dst_ref, src_ref, count_ref):
    core = at_ref[0]
    reach = 9
    nc = 8
    first = 2 * which - core
    start = jnp.clip(first, 0, reach - 2)
    held, rows = [], []
    for half in range(2):
        slot = start + half
        parity = slot - first
        for t in range(SLOTS):
            source = src_ref[slot, t]
            inside = jnp.logical_and(parity >= 0, parity < 2)
            held.append(source + jnp.where(parity == 1, 2 * nc, 0))
            live = jnp.logical_and(inside, t < count_ref[slot])
            rows.append(jnp.where(live, dst_ref[slot, t], 2))
    return start, held, rows


def pack_kernel(at_ref, dst_ref, src_ref, count_ref, tiles_ref, *rest):
    outs, tails, sems = rest[: len(AWAY)], rest[-2], rest[-1]
    copies = []
    lane = lax.broadcasted_iota(jnp.int32, (TAIL, TILE), 1)
    line = lax.broadcasted_iota(jnp.int32, (TAIL, TILE), 0)
    for n, which in enumerate(AWAY):
        start, held, rows = places(which, at_ref, dst_ref, src_ref, count_ref)
        begin = pl.multiple_of(start * (SLOTS * TILE), SLOTS * TILE)
        copy = pltpu.make_async_copy(
            tiles_ref.at[pl.ds(begin, PAIR * TILE)], outs[n].at[pl.ds(0, PAIR * TILE)], sems.at[2 * n]
        )
        copy.start()
        copies.append(copy)
        tail = jnp.zeros((TAIL, TILE), jnp.int32)
        for t in range(PAIR):
            tail = jnp.where(lane == t, jnp.where(line == 0, held[t], rows[t]), tail)
        tails[n] = tail.astype(jnp.float32).astype(jnp.bfloat16)
        copy = pltpu.make_async_copy(
            tails.at[n], outs[n].at[pl.ds(PAIR * TILE, TAIL)], sems.at[2 * n + 1]
        )
        copy.start()
        copies.append(copy)
    for copy in copies:
        copy.wait()


SMEM = pl.BlockSpec(memory_space=pltpu.SMEM)
VMEM = pl.BlockSpec(memory_space=pltpu.VMEM)
ANY = pl.BlockSpec(memory_space=pl.ANY)
HBM = pl.BlockSpec(memory_space=pltpu.HBM)


def pack_tiles(at, dst, src, count, tiles):
    return pl.pallas_call(
        pack_kernel,
        in_specs=[SMEM, SMEM, SMEM, SMEM, HBM],
        out_specs=[ANY] * len(AWAY),
        out_shape=[jax.ShapeDtypeStruct((PAIR * TILE + TAIL, TILE), jnp.bfloat16)] * len(AWAY),
        scratch_shapes=[
            pltpu.VMEM((len(AWAY), TAIL, TILE), jnp.bfloat16),
            pltpu.SemaphoreType.DMA((2 * len(AWAY),)),
        ],
        compiler_params=pltpu.CompilerParams(vmem_limit_bytes=VMEM_LIMIT),
        name="pack_tiles",
    )(at, dst, src, count, tiles)


def pick_kernel(cols_ref, table_ref, out_ref):
    width = cols_ref.shape[2]
    channel = lax.broadcasted_iota(jnp.int32, (table_ref.shape[1], width), 0)
    onehot = (channel == cols_ref[0]).astype(jnp.bfloat16)
    out_ref[0] = jnp.dot(
        table_ref[...], onehot, preferred_element_type=jnp.float32
    ).astype(jnp.bfloat16)


def pick_columns(table, cols):
    rows, channels = table.shape
    splits, _, width = cols.shape
    return pl.pallas_call(
        pick_kernel,
        grid=(splits,),
        in_specs=[
            pl.BlockSpec((1, 1, width), lambda j: (j, 0, 0)),
            pl.BlockSpec((rows, channels), lambda j: (0, 0)),
        ],
        out_specs=pl.BlockSpec((1, rows, width), lambda j: (j, 0, 0)),
        out_shape=jax.ShapeDtypeStruct((splits, rows, width), jnp.bfloat16),
        compiler_params=pltpu.CompilerParams(vmem_limit_bytes=VMEM_LIMIT),
        cost_estimate=pl.CostEstimate(
            flops=2 * splits * rows * channels * width,
            bytes_accessed=2 * splits * rows * width,
            transcendentals=0,
        ),
        name="pick_active",
    )(cols, table)


def products(held, rows, tiles, sources, wide):
    wide[0 : 2 * TILE] = jnp.zeros((2 * TILE, PAIR * TILE), jnp.bfloat16)
    for t in range(PAIR):
        row = pl.multiple_of(rows[t] * TILE, TILE)
        wide[pl.ds(row, TILE), t * TILE : (t + 1) * TILE] = tiles[t * TILE : (t + 1) * TILE]
    total = None
    for t in range(0, PAIR, 2):
        chosen = jnp.concatenate(
            [sources[pl.ds(pl.multiple_of(held[n] * TILE, TILE), TILE)] for n in (t, t + 1)], axis=0
        )
        product = jnp.dot(
            wide[0 : 2 * TILE, t * TILE : (t + 2) * TILE], chosen, preferred_element_type=jnp.float32
        )
        total = product if total is None else total + product
    return total


def sum_away_kernel(held_ref, *rest):
    count = len(AWAY)
    tiles_refs, outs = rest[:count], rest[count : 2 * count]
    sources, tiles, wide, tail, tail_s, sems = rest[2 * count :]
    heads = []
    for n in range(count):
        heads.append(pltpu.make_async_copy(tiles_refs[n], tiles.at[n], sems.at[n]))
    heads.append(pltpu.make_async_copy(held_ref, sources, sems.at[count]))
    for copy in heads:
        copy.start()
    for copy in heads:
        copy.wait()
    for n in range(count):
        tail[n] = tiles[n, PAIR * TILE : PAIR * TILE + TAIL].astype(jnp.float32).astype(jnp.int32)
    copy = pltpu.make_async_copy(tail, tail_s, sems.at[count + 1])
    copy.start()
    copy.wait()
    for n in range(count):
        held = [tail_s[n, 0, t] for t in range(PAIR)]
        placed = [tail_s[n, 1, t] for t in range(PAIR)]
        total = products(held, placed, tiles.at[n], sources, wide.at[n % 2])
        outs[n][...] = total.astype(jnp.bfloat16)


def sum_away(sources, messages):
    rows, channels = sources.shape
    count = len(messages)
    return pl.pallas_call(
        sum_away_kernel,
        in_specs=[ANY] * (1 + count),
        out_specs=[VMEM] * count,
        out_shape=[jax.ShapeDtypeStruct((2 * TILE, channels), jnp.bfloat16)] * count,
        scratch_shapes=[
            pltpu.VMEM((rows, channels), jnp.bfloat16),
            pltpu.VMEM((count,) + messages[0].shape, jnp.bfloat16),
            pltpu.VMEM((2, 3 * TILE, PAIR * TILE), jnp.bfloat16),
            pltpu.VMEM((count, TAIL, TILE), jnp.int32),
            pltpu.SMEM((count, TAIL, TILE), jnp.int32),
            pltpu.SemaphoreType.DMA((count + 2,)),
        ],
        compiler_params=pltpu.CompilerParams(vmem_limit_bytes=VMEM_LIMIT),
        cost_estimate=pl.CostEstimate(
            flops=count * 4 * TILE * TILE * PAIR * channels,
            bytes_accessed=2 * (rows * channels + count * PAIR * TILE * TILE),
            transcendentals=0,
        ),
        name="sum_away",
    )(sources, *messages)


def sum_own_kernel(at_ref, dst_ref, src_ref, count_ref, held_ref, tiles_ref, out_ref, *rest):
    sources, tiles, wide, sems = rest
    start, held, placed = places(2, at_ref, dst_ref, src_ref, count_ref)
    begin = pl.multiple_of(start * (SLOTS * TILE), SLOTS * TILE)
    heads = [
        pltpu.make_async_copy(tiles_ref.at[pl.ds(begin, PAIR * TILE)], tiles, sems.at[0]),
        pltpu.make_async_copy(held_ref, sources, sems.at[1]),
    ]
    for copy in heads:
        copy.start()
    for copy in heads:
        copy.wait()
    out_ref[...] = products(held, placed, tiles, sources, wide)


def sum_own(at, dst, src, count, sources, tiles):
    rows, channels = sources.shape
    return pl.pallas_call(
        sum_own_kernel,
        in_specs=[SMEM] * 4 + [ANY] + [HBM],
        out_specs=VMEM,
        out_shape=jax.ShapeDtypeStruct((2 * TILE, channels), jnp.float32),
        scratch_shapes=[
            pltpu.VMEM((rows, channels), jnp.bfloat16),
            pltpu.VMEM((PAIR * TILE, TILE), jnp.bfloat16),
            pltpu.VMEM((3 * TILE, PAIR * TILE), jnp.bfloat16),
            pltpu.SemaphoreType.DMA((2,)),
        ],
        compiler_params=pltpu.CompilerParams(vmem_limit_bytes=VMEM_LIMIT),
        cost_estimate=pl.CostEstimate(
            flops=4 * TILE * TILE * PAIR * channels,
            bytes_accessed=2 * (rows * channels + PAIR * TILE * TILE),
            transcendentals=0,
        ),
        name="sum_own",
    )(at, dst, src, count, sources, tiles)


def join_kernel(cols_ref, own_ref, n0, n1, n2, n3, picked_ref, out_ref):
    total = own_ref[...]
    for part in (n0, n1, n2, n3):
        total = total + part[...].astype(jnp.float32)
    neighbour = total.astype(jnp.bfloat16)
    width = picked_ref.shape[2]
    channel = lax.broadcasted_iota(jnp.int32, (neighbour.shape[1], width), 0)
    joined = jnp.zeros((neighbour.shape[0], width), jnp.float32)
    for j in range(SPLITS):
        onehot = (channel == cols_ref[j]).astype(jnp.bfloat16)
        joined = joined + picked_ref[j].astype(jnp.float32) * jnp.dot(
            neighbour, onehot, preferred_element_type=jnp.float32
        )
    for piece in range(width // TILE):
        out_ref[piece] = joined[:, piece * TILE : (piece + 1) * TILE].astype(out_ref.dtype)


def join(own, parts, picked, cols):
    rows, channels = own.shape
    splits, _, width = cols.shape
    whole = pl.BlockSpec((rows, channels), lambda q: (0, 0))
    return pl.pallas_call(
        join_kernel,
        grid=(width // CHUNK,),
        in_specs=[pl.BlockSpec((splits, 1, CHUNK), lambda q: (0, 0, q))]
        + [whole] * 5
        + [pl.BlockSpec((splits, rows, CHUNK), lambda q: (0, 0, q))],
        out_specs=pl.BlockSpec((CHUNK // TILE, rows, TILE), lambda q: (q, 0, 0)),
        out_shape=jax.ShapeDtypeStruct((width // TILE, rows, TILE), jnp.bfloat16),
        compiler_params=pltpu.CompilerParams(vmem_limit_bytes=VMEM_LIMIT),
        cost_estimate=pl.CostEstimate(
            flops=2 * splits * rows * channels * width,
            bytes_accessed=2 * splits * rows * width,
            transcendentals=0,
        ),
        name="join_sets",
    )(cols, own, *parts, picked)


def local(
    active_table,
    passive_table,
    adjacency,
    tile_dst,
    tile_src,
    tile_count,
    split_active,
    split_passive,
):
    tiles_all = adjacency.reshape(-1, TILE)
    dst, src, count = tile_dst[0, 0], tile_src[0, 0], tile_count[0, 0]
    nc = lax.axis_size("cset")
    at = (lax.axis_index("blk") % 2).astype(jnp.int32)[None]

    messages = pack_tiles(at, dst, src, count, tiles_all)
    *messages, passive_table = lax.optimization_barrier((*messages, passive_table))
    messages = [
        routed(message, which - 2, which % 2 == 1) for which, message in zip(AWAY, messages)
    ]
    copies = jnp.broadcast_to(passive_table[None], (nc,) + passive_table.shape)
    own_rows = lax.all_to_all(copies, "cset", split_axis=0, concat_axis=0, tiled=True)
    own_rows = own_rows.reshape(-1, passive_table.shape[1])
    groups = [[b, b + 1] for b in range(0, lax.axis_size("blk"), 2)]
    twice = jnp.broadcast_to(own_rows[None], (2,) + own_rows.shape)
    sources = lax.all_to_all(
        twice, "blk", split_axis=0, concat_axis=0, tiled=True, axis_index_groups=groups
    ).reshape(-1, own_rows.shape[1])

    parts = sum_away(sources, messages)
    *parts, active_table = lax.optimization_barrier((*parts, active_table))
    parts = [routed(part, 2 - which, which % 2 == 1) for which, part in zip(AWAY, parts)]

    extra = OUTPAD - split_active.shape[1]
    left_cols = jnp.pad(split_active, ((0, 0), (0, extra)), constant_values=-1)[:, None, :]
    right_cols = jnp.pad(split_passive, ((0, 0), (0, extra)), constant_values=-1)[:, None, :]
    picked = pick_columns(active_table, left_cols)
    own = sum_own(at, dst, src, count, sources, tiles_all)
    joined = join(own, parts, picked, right_cols)
    spread = lax.all_to_all(joined, "cset", split_axis=0, concat_axis=0, tiled=True)
    return spread.reshape(-1, TILE)


def solution(mesh):
    in_specs = (
        P(("blk", "cset"), None),
        P(("blk", "cset"), None),
        P("blk", "cset", None, None, None, None),
        P("blk", "cset", None, None),
        P("blk", "cset", None, None),
        P("blk", "cset", None),
        P(),
        P(),
    )
    out_specs = P("blk", "cset")
    return jax.shard_map(local, mesh=mesh, in_specs=in_specs, out_specs=out_specs, check_vma=False)
```

time: 113 us -> 88 us (0.78)
  the two profiles are of different devices: /device:TPU:2 before, /device:TPU:16 now
where the time goes in v2:
time: 88 us; the launch traced here: 87.6 us
  starting transfers between devices  24.1 us (27%)
  Pallas kernels  22.2 us (25%)
  waiting for transfers between devices  17.4 us (20%)
  blocking collectives  16.3 us (19%)
  local copies, waits for them, and re-layouts  7.34 us (8%)
    all_to_all x1, blocking collectives, local(): lax.all_to_all(joined, 'cset', split_axis=0, concat_axis=0, tiled=True)  16.3 us
    ppermute x8, starting transfers between devices, routed(): return lax.ppermute(block, ('blk', 'cset'), route)  15.3 us
    ppermute x8, waiting for transfers between devices, routed(): return lax.ppermute(block, ('blk', 'cset'), route)  11.9 us
    pallas_call x1, Pallas kernels, pick_columns(): pl.pallas_call(pick_kernel, grid=(splits,), in_specs=[pl.BlockSpec((1, 1,...  7.14 us
    pallas_call x1, Pallas kernels, join(): pl.pallas_call(join_kernel, grid=(width // CHUNK,), in_specs=[pl.BlockSpe...  6.77 us
    all_to_all x1, waiting for transfers between devices, local(): lax.all_to_all(copies, 'cset', split_axis=0, concat_axis=0, tiled=True)  5.53 us
    all_to_all x1, starting transfers between devices, local(): lax.all_to_all(copies, 'cset', split_axis=0, concat_axis=0, tiled=True)  5.02 us
    pallas_call x1, Pallas kernels, sum_away(): pl.pallas_call(sum_away_kernel, in_specs=[ANY] * (1 + count), out_specs=[...  4.44 us
  transfers between devices with their start and end apart: 10, of which 4 were waited for; matrix products, arithmetic and copies ran while one was open for 2% of the time, Pallas kernels for 10%

profile of v2, /device:TPU:16, one launch (start us, length us, event | category | flops | bytes accessed | tf_op | source)
XLA Modules:
  0.0 87.6 jit_solution(242670330201913403)
XLA Ops:
  0.0 0.8 copy.11.dst_ref
  0.8 0.8 copy.12.src_ref
  1.5 0.0 copy-start
  1.5 1.7 %copy-done = bf16[1,1,9,8,128,128]{5,4,3,2,1,0:T(8,128)(2,1)S(1)} copy-done((bf16[1,1,9,8,128,128]{5,4,3,2,1,0:T(8,128)(2,1)S(1)}, bf16[1,1,9,8,128,128]{5,4,3,2,1,0:T(8,128)(2,1)}, u32[]{:S(2)}) %copy-start) | copy-done | bytes 2359320
  3.2 0.0 copy-start.3
  3.2 0.7 copy-done.3
  3.9 0.0 copy-start.5
  3.9 0.0 copy-start.6
  3.9 2.2 %pack_tiles.1 = (bf16[2064,128]{1,0:T(8,128)(2,1)}, bf16[2064,128]{1,0:T(8,128)(2,1)}, bf16[2064,128]{1,0:T(8,128)(2,1)}, bf16[2064,128]{1,0:T(8,128)(2,1)}) custom-call(s32[1]{0:T(128)} %bitcast.at_ref, s32[9,8]{1,0:T(8,128)S(1)} %copy.11.dst_ref, s32[9,8]{1,0:T(8,128)S(1)} %copy.12.src_ref, s32[9]{0:T(128)S(1)} %bitcast.12, bf16[9216,128]{1,0:T(8,128)(2,1)S(1)} %bitcast.10), custom_call_target="tpu_custom_call" | custom-call | tf_op jit(solution)/shard_map/pack_tiles/pallas_call | solution.py:81
  6.1 0.0 copy-start.7
  6.1 0.0 copy-done.5
  6.1 1.1 %broadcast_in_dim.24 = bf16[8,256,256]{2,1,0:T(8,128)(2,1)} broadcast(bf16[256,256]{1,0:T(8,128)(2,1)S(1)} %copy-done.5), dimensions={1,2} | broadcast | bytes 1179648 | tf_op jit(solution)/shard_map/broadcast_in_dim | solution.py:290
  7.2 5.0 %all-to-all-start = ((bf16[8,256,256]{2,1,0:T(8,128)(2,1)}), bf16[8,256,256]{2,1,0:T(8,128)(2,1)S(1)}, u32[]{:S(2)}, u32[]{:S(2)}) async-start(bf16[8,256,256]{2,1,0:T(8,128)(2,1)} %broadcast_in_dim.24), calls=%async_computation | async-start | bytes 2097152 | tf_op jit(solution)/shard_map/all_to_all | solution.py:291
  12.2 1.2 %collective-permute-start = (bf16[2064,128]{1,0:T(8,128)(2,1)}, bf16[2064,128]{1,0:T(8,128)(2,1)S(1)}, u32[]{:S(2)}, u32[]{:S(2)}) collective-permute-start(bf16[2064,128]{1,0:T(8,128)(2,1)} %get-tuple-element.28), channel_id=1, source_target_pairs={{0,244},{1,245},{2,246},{3,247},{4,240},{5,241},{6,242},{7,243},{8... | collective-permute-start | bytes 1585160 | tf_op jit(solution)/shard_map/ppermute | solution.py:26
  13.4 1.7 %collective-permute-start.1 = (bf16[2064,128]{1,0:T(8,128)(2,1)}, bf16[2064,128]{1,0:T(8,128)(2,1)S(1)}, u32[]{:S(2)}, u32[]{:S(2)}) collective-permute-start(bf16[2064,128]{1,0:T(8,128)(2,1)} %get-tuple-element.29), channel_id=1, source_target_pairs={{0,20},{1,21},{2,22},{3,23},{4,16},{5,17},{6,18},{7,19},{8,28},{9,... | collective-permute-start | bytes 1585160 | tf_op jit(solution)/shard_map/ppermute | solution.py:26
  15.1 7.1 %collective-permute-start.2 = (bf16[2064,128]{1,0:T(8,128)(2,1)}, bf16[2064,128]{1,0:T(8,128)(2,1)}, u32[]{:S(2)}, u32[]{:S(2)}) collective-permute-start(bf16[2064,128]{1,0:T(8,128)(2,1)} %get-tuple-element.30), channel_id=1, source_target_pairs={{0,224},{1,225},{2,226},{3,227},{4,228},{5,229},{6,230},{7,231},{8... | collective-permute-start | bytes 1585160 | tf_op jit(solution)/shard_map/ppermute | solution.py:26
  22.2 0.0 collective-permute-start.3
  22.2 0.0 copy-done.6
  22.2 0.1 broadcast_in_dim.27.cols_ref
  22.3 0.0 copy-done.7
  22.3 0.1 broadcast_in_dim.22.cols_ref
  22.3 5.5 %all-to-all-done = bf16[8,256,256]{2,1,0:T(8,128)(2,1)S(1)} async-done(((bf16[8,256,256]{2,1,0:T(8,128)(2,1)}), bf16[8,256,256]{2,1,0:T(8,128)(2,1)S(1)}, u32[]{:S(2)}, u32[]{:S(2)}) %all-to-all-start) | async-done | bytes 1048608 | tf_op jit(solution)/shard_map/all_to_all | solution.py:291
  27.9 1.5 %broadcast_in_dim.26 = bf16[2,2048,256]{2,1,0:T(8,128)(2,1)} broadcast(bf16[2048,256]{1,0:T(8,128)(2,1)S(1)} %bitcast.14), dimensions={1,2} | broadcast | bytes 3145728 | tf_op jit(solution)/shard_map/broadcast_in_dim | solution.py:294
  29.3 3.8 %all-to-all-start.1 = ((bf16[2,2048,256]{2,1,0:T(8,128)(2,1)}), bf16[2,2048,256]{2,1,0:T(8,128)(2,1)S(1)}, u32[]{:S(2)}, u32[]{:S(2)}) async-start(bf16[2,2048,256]{2,1,0:T(8,128)(2,1)} %broadcast_in_dim.26), calls=%async_computation.1 | async-start | bytes 4194304 | tf_op jit(solution)/shard_map/all_to_all | solution.py:295
  33.1 0.0 copy-start.2
  33.1 2.6 %collective-permute-done.rest_0_ = bf16[2064,128]{1,0:T(8,128)(2,1)S(1)} collective-permute-done((bf16[2064,128]{1,0:T(8,128)(2,1)}, bf16[2064,128]{1,0:T(8,128)(2,1)S(1)}, u32[]{:S(2)}, u32[]{:S(2)}) %collective-permute-start) | collective-permute-done | bytes 528416 | tf_op jit(solution)/shard_map/ppermute | solution.py:26
  35.7 2.4 %collective-permute-done.1.rest_1_ = bf16[2064,128]{1,0:T(8,128)(2,1)S(1)} collective-permute-done((bf16[2064,128]{1,0:T(8,128)(2,1)}, bf16[2064,128]{1,0:T(8,128)(2,1)S(1)}, u32[]{:S(2)}, u32[]{:S(2)}) %collective-permute-start.1) | collective-permute-done | bytes 528416 | tf_op jit(solution)/shard_map/ppermute | solution.py:26
  38.1 0.0 collective-permute-done.2.rest_2_
  38.1 6.9 %collective-permute-done.3.rest_3_ = bf16[2064,128]{1,0:T(8,128)(2,1)} collective-permute-done((bf16[2064,128]{1,0:T(8,128)(2,1)}, bf16[2064,128]{1,0:T(8,128)(2,1)}, u32[]{:S(2)}, u32[]{:S(2)}) %collective-permute-start.3) | collective-permute-done | bytes 528416 | tf_op jit(solution)/shard_map/ppermute | solution.py:26
  45.0 0.0 all-to-all-done.1
  45.0 4.4 %sum_away.1 = (bf16[256,256]{1,0:T(8,128)(2,1)S(1)}, bf16[256,256]{1,0:T(8,128)(2,1)S(1)}, bf16[256,256]{1,0:T(8,128)(2,1)S(1)}, bf16[256,256]{1,0:T(8,128)(2,1)S(1)}) custom-call(bf16[4096,256]{1,0:T(8,128)(2,1)S(1)} %bitcast.8, bf16[2064,128]{1,0:T(8,128)(2,1)S(1)} %collective-permute-done.rest_0_, bf16[2064,128]{1,0:T(8,128)(2,1)S(1)} %collective-permute-done.1.rest_1_, ...), custom_call_target="tpu_custom_call" | custom-call | flops 1073741824 | bytes 4194304 | tf_op jit(solution)/shard_map/sum_away/pallas_call | solution.py:170
  49.5 0.0 copy-start.1
  49.5 0.0 copy-start.4
  49.5 0.1 collective-permute-start.4
  49.6 2.0 %collective-permute-start.5 = (bf16[256,256]{1,0:T(8,128)(2,1)S(1)}, bf16[256,256]{1,0:T(8,128)(2,1)S(1)}, u32[]{:S(2)}, u32[]{:S(2)}) collective-permute-start(bf16[256,256]{1,0:T(8,128)(2,1)S(1)} %get-tuple-element.37), channel_id=1, source_target_pairs={{0,244},{1,245},{2,246},{3,247},{4,240},{5,241},{6,242},{7,243},{8... | collective-permute-start | bytes 393224 | tf_op jit(solution)/shard_map/ppermute | solution.py:26
  51.6 0.0 collective-permute-start.6
  51.6 3.2 %collective-permute-start.7 = (bf16[256,256]{1,0:T(8,128)(2,1)S(1)}, bf16[256,256]{1,0:T(8,128)(2,1)S(1)}, u32[]{:S(2)}, u32[]{:S(2)}) collective-permute-start(bf16[256,256]{1,0:T(8,128)(2,1)S(1)} %get-tuple-element.39), channel_id=1, source_target_pairs={{0,224},{1,225},{2,226},{3,227},{4,228},{5,229},{6,230},{7,231},{8... | collective-permute-start | bytes 393224 | tf_op jit(solution)/shard_map/ppermute | solution.py:26
  54.8 0.0 copy-done.2
  54.8 7.1 %pick_active.1.picked_ref = bf16[20,256,1024]{2,1,0:T(8,128)(2,1)S(1)} custom-call(s32[20,1,1024]{2,1,0:T(1,128)S(1)} %broadcast_in_dim.27.cols_ref, bf16[256,256]{1,0:T(8,128)(2,1)S(1)} %copy-done.2), custom_call_target="tpu_custom_call" | custom-call | flops 2684354560 | bytes 10485760 | tf_op jit(solution)/shard_map/pick_active/pallas_call | solution.py:107
  62.0 0.0 copy-done.1
  62.0 0.0 copy-done.4
  62.0 1.6 %sum_own.1.own_ref = f32[256,256]{1,0:T(8,128)S(1)} custom-call(s32[1]{0:T(128)} %bitcast.at_ref, s32[9,8]{1,0:T(8,128)S(1)} %copy.11.dst_ref, s32[9,8]{1,0:T(8,128)S(1)} %copy.12.src_ref, s32[9]{0:T(128)S(1)} %bitcast.13, bf16[4096,256]{1,0:T(8,128)(2,1)S(1)} %bitcast.9, bf16[9216,128]{1,0:T(8,128)(2,1)S(1)} %bitcast.11), custom_call_target="tpu_custom_call" | custom-call | flops 268435456 | bytes 2621440 | tf_op jit(solution)/shard_map/sum_own/pallas_call | solution.py:210
  63.7 0.0 collective-permute-done.4.n0
  63.7 0.0 collective-permute-done.5.n1
  63.7 0.0 collective-permute-done.6.n2
  63.7 0.0 collective-permute-done.7.n3
  63.7 6.8 %join_sets.1 = bf16[8,256,128]{2,1,0:T(8,128)(2,1)S(1)} custom-call(s32[20,1,1024]{2,1,0:T(1,128)S(1)} %broadcast_in_dim.22.cols_ref, f32[256,256]{1,0:T(8,128)S(1)} %sum_own.1.own_ref, bf16[256,256]{1,0:T(8,128)(2,1)S(1)} %collective-permute-done.4.n0, bf16[256,256]{1,0:T(8,128)(2,1)S(1)} %collective-permute-done.5.n1, ...), custom_call_target="tpu_custom_call" | custom-call | flops 2684354560 | bytes 10485760 | tf_op jit(solution)/shard_map/join_sets/pallas_call | solution.py:252
  70.5 16.3 %all_to_all.15 = bf16[8,256,128]{2,1,0:T(8,128)(2,1)S(1)} all-to-all(bf16[8,256,128]{2,1,0:T(8,128)(2,1)S(1)} %join_sets.1), channel_id=1, replica_groups=mesh['blk'=32,'cset'=8] {'cset'}, dimensions={0} | all-to-all | bytes 1048576 | tf_op jit(solution)/shard_map/all_to_all | solution.py:309
  86.8 0.8 copy.14
  (2 shorter events, 0.0 us)
Async XLA Ops:
  1.5 1.7 %copy-start = (bf16[1,1,9,8,128,128]{5,4,3,2,1,0:T(8,128)(2,1)S(1)}, bf16[1,1,9,8,128,128]{5,4,3,2,1,0:T(8,128)(2,1)}, u32[]{:S(2)}) copy-start(bf16[1,1,9,8,128,128]{5,4,3,2,1,0:T(8,128)(2,1)} %param.10) | copy-start | bytes 7077892
  3.2 0.7 copy-start.3
  3.9 2.2 %copy-start.5 = (bf16[256,256]{1,0:T(8,128)(2,1)S(1)}, bf16[256,256]{1,0:T(8,128)(2,1)}, u32[]{:S(2)}) copy-start(bf16[256,256]{1,0:T(8,128)(2,1)} %param.9) | copy-start | bytes 393220
  3.9 18.3 %copy-start.6 = (s32[20,924]{1,0:T(8,128)S(1)}, s32[20,924]{1,0:T(8,128)}, u32[]{:S(2)}) copy-start(s32[20,924]{1,0:T(8,128)} %param.14) | copy-start | bytes 221764
  6.1 16.2 %copy-start.7 = (s32[20,924]{1,0:T(8,128)S(1)}, s32[20,924]{1,0:T(8,128)}, u32[]{:S(2)}) copy-start(s32[20,924]{1,0:T(8,128)} %param.15) | copy-start | bytes 221764
  7.2 20.7 %all-to-all-start = ((bf16[8,256,256]{2,1,0:T(8,128)(2,1)}), bf16[8,256,256]{2,1,0:T(8,128)(2,1)S(1)}, u32[]{:S(2)}, u32[]{:S(2)}) async-start(bf16[8,256,256]{2,1,0:T(8,128)(2,1)} %broadcast_in_dim.24), calls=%async_computation | async-start | bytes 2097152 | tf_op jit(solution)/shard_map/all_to_all | solution.py:291
  12.2 23.5 %collective-permute-start = (bf16[2064,128]{1,0:T(8,128)(2,1)}, bf16[2064,128]{1,0:T(8,128)(2,1)S(1)}, u32[]{:S(2)}, u32[]{:S(2)}) collective-permute-start(bf16[2064,128]{1,0:T(8,128)(2,1)} %get-tuple-element.28), channel_id=1, source_target_pairs={{0,244},{1,245},{2,246},{3,247},{4,240},{5,241},{6,242},{7,243},{8... | collective-permute-start | bytes 1585160 | tf_op jit(solution)/shard_map/ppermute | solution.py:26
  13.4 24.7 %collective-permute-start.1 = (bf16[2064,128]{1,0:T(8,128)(2,1)}, bf16[2064,128]{1,0:T(8,128)(2,1)S(1)}, u32[]{:S(2)}, u32[]{:S(2)}) collective-permute-start(bf16[2064,128]{1,0:T(8,128)(2,1)} %get-tuple-element.29), channel_id=1, source_target_pairs={{0,20},{1,21},{2,22},{3,23},{4,16},{5,17},{6,18},{7,19},{8,28},{9,... | collective-permute-start | bytes 1585160 | tf_op jit(solution)/shard_map/ppermute | solution.py:26
  15.1 23.0 %collective-permute-start.2 = (bf16[2064,128]{1,0:T(8,128)(2,1)}, bf16[2064,128]{1,0:T(8,128)(2,1)}, u32[]{:S(2)}, u32[]{:S(2)}) collective-permute-start(bf16[2064,128]{1,0:T(8,128)(2,1)} %get-tuple-element.30), channel_id=1, source_target_pairs={{0,224},{1,225},{2,226},{3,227},{4,228},{5,229},{6,230},{7,231},{8... | collective-permute-start | bytes 1585160 | tf_op jit(solution)/shard_map/ppermute | solution.py:26
  22.2 22.8 %collective-permute-start.3 = (bf16[2064,128]{1,0:T(8,128)(2,1)}, bf16[2064,128]{1,0:T(8,128)(2,1)}, u32[]{:S(2)}, u32[]{:S(2)}) collective-permute-start(bf16[2064,128]{1,0:T(8,128)(2,1)} %get-tuple-element.31), channel_id=1, source_target_pairs={{0,32},{1,33},{2,34},{3,35},{4,36},{5,37},{6,38},{7,39},{8,40},{9,... | collective-permute-start | bytes 1585160 | tf_op jit(solution)/shard_map/ppermute | solution.py:26
  29.3 15.7 %all-to-all-start.1 = ((bf16[2,2048,256]{2,1,0:T(8,128)(2,1)}), bf16[2,2048,256]{2,1,0:T(8,128)(2,1)S(1)}, u32[]{:S(2)}, u32[]{:S(2)}) async-start(bf16[2,2048,256]{2,1,0:T(8,128)(2,1)} %broadcast_in_dim.26), calls=%async_computation.1 | async-start | bytes 4194304 | tf_op jit(solution)/shard_map/all_to_all | solution.py:295
  33.1 21.7 %copy-start.2 = (bf16[256,256]{1,0:T(8,128)(2,1)S(1)}, bf16[256,256]{1,0:T(8,128)(2,1)}, u32[]{:S(2)}) copy-start(bf16[256,256]{1,0:T(8,128)(2,1)} %table_ref) | copy-start | bytes 393220
  49.5 12.5 %copy-start.1 = (bf16[1,1,9,8,128,128]{5,4,3,2,1,0:T(8,128)(2,1)S(1)}, bf16[1,1,9,8,128,128]{5,4,3,2,1,0:T(8,128)(2,1)}, u32[]{:S(2)}) copy-start(bf16[1,1,9,8,128,128]{5,4,3,2,1,0:T(8,128)(2,1)} %param.10) | copy-start | bytes 7077892
  49.5 12.5 %copy-start.4 = (s32[1,1,9]{2,1,0:T(1,128)S(1)}, s32[1,1,9]{2,1,0:T(1,128)}, u32[]{:S(2)}) copy-start(s32[1,1,9]{2,1,0:T(1,128)} %param.13) | copy-start | bytes 112
  49.5 14.2 %collective-permute-start.4 = (bf16[256,256]{1,0:T(8,128)(2,1)S(1)}, bf16[256,256]{1,0:T(8,128)(2,1)S(1)}, u32[]{:S(2)}, u32[]{:S(2)}) collective-permute-start(bf16[256,256]{1,0:T(8,128)(2,1)S(1)} %get-tuple-element.36), channel_id=1, source_target_pairs={{0,20},{1,21},{2,22},{3,23},{4,16},{5,17},{6,18},{7,19},{8,28},{9,... | collective-permute-start | bytes 393224 | tf_op jit(solution)/shard_map/ppermute | solution.py:26
  49.6 14.1 %collective-permute-start.5 = (bf16[256,256]{1,0:T(8,128)(2,1)S(1)}, bf16[256,256]{1,0:T(8,128)(2,1)S(1)}, u32[]{:S(2)}, u32[]{:S(2)}) collective-permute-start(bf16[256,256]{1,0:T(8,128)(2,1)S(1)} %get-tuple-element.37), channel_id=1, source_target_pairs={{0,244},{1,245},{2,246},{3,247},{4,240},{5,241},{6,242},{7,243},{8... | collective-permute-start | bytes 393224 | tf_op jit(solution)/shard_map/ppermute | solution.py:26
  51.6 12.1 %collective-permute-start.6 = (bf16[256,256]{1,0:T(8,128)(2,1)S(1)}, bf16[256,256]{1,0:T(8,128)(2,1)S(1)}, u32[]{:S(2)}, u32[]{:S(2)}) collective-permute-start(bf16[256,256]{1,0:T(8,128)(2,1)S(1)} %get-tuple-element.38), channel_id=1, source_target_pairs={{0,32},{1,33},{2,34},{3,35},{4,36},{5,37},{6,38},{7,39},{8,40},{9,... | collective-permute-start | bytes 393224 | tf_op jit(solution)/shard_map/ppermute | solution.py:26
  51.6 12.1 %collective-permute-start.7 = (bf16[256,256]{1,0:T(8,128)(2,1)S(1)}, bf16[256,256]{1,0:T(8,128)(2,1)S(1)}, u32[]{:S(2)}, u32[]{:S(2)}) collective-permute-start(bf16[256,256]{1,0:T(8,128)(2,1)S(1)} %get-tuple-element.39), channel_id=1, source_target_pairs={{0,224},{1,225},{2,226},{3,227},{4,228},{5,229},{6,230},{7,231},{8... | collective-permute-start | bytes 393224 | tf_op jit(solution)/shard_map/ppermute | solution.py:26

commit v3 on v2

--- a/solution.py
+++ b/solution.py
@@ -14,6 +14,7 @@
 TAIL = 16
 AWAY = (1, 3, 0, 4)
 VMEM_LIMIT = 16 * 1024 * 1024
+PACK_LIMIT = 60 * 1024 * 1024
 
 
 def routed(block, chips, flip):
@@ -37,11 +38,11 @@
         slot = start + half
         parity = slot - first
         for t in range(SLOTS):
-            source = src_ref[slot, t]
+            source = src_ref[0, 0, slot, t]
             inside = jnp.logical_and(parity >= 0, parity < 2)
             held.append(source + jnp.where(parity == 1, 2 * nc, 0))
-            live = jnp.logical_and(inside, t < count_ref[slot])
-            rows.append(jnp.where(live, dst_ref[slot, t], 2))
+            live = jnp.logical_and(inside, t < count_ref[0, 0, slot])
+            rows.append(jnp.where(live, dst_ref[0, 0, slot, t], 2))
     return start, held, rows
 
 
@@ -87,7 +88,7 @@
             pltpu.VMEM((len(AWAY), TAIL, TILE), jnp.bfloat16),
             pltpu.SemaphoreType.DMA((2 * len(AWAY),)),
         ],
-        compiler_params=pltpu.CompilerParams(vmem_limit_bytes=VMEM_LIMIT),
+        compiler_params=pltpu.CompilerParams(vmem_limit_bytes=PACK_LIMIT),
         name="pack_tiles",
     )(at, dst, src, count, tiles)
 
@@ -113,7 +114,7 @@
         ],
         out_specs=pl.BlockSpec((1, rows, width), lambda j: (j, 0, 0)),
         out_shape=jax.ShapeDtypeStruct((splits, rows, width), jnp.bfloat16),
-        compiler_params=pltpu.CompilerParams(vmem_limit_bytes=VMEM_LIMIT),
+        compiler_params=pltpu.CompilerParams(vmem_limit_bytes=PACK_LIMIT),
         cost_estimate=pl.CostEstimate(
             flops=2 * splits * rows * channels * width,
             bytes_accessed=2 * splits * rows * width,
@@ -123,18 +124,23 @@
     )(cols, table)
 
 
-def products(held, rows, tiles, sources, wide):
-    wide[0 : 2 * TILE] = jnp.zeros((2 * TILE, PAIR * TILE), jnp.bfloat16)
-    for t in range(PAIR):
-        row = pl.multiple_of(rows[t] * TILE, TILE)
-        wide[pl.ds(row, TILE), t * TILE : (t + 1) * TILE] = tiles[t * TILE : (t + 1) * TILE]
+def products(held, rows, tiles, sources):
     total = None
     for t in range(0, PAIR, 2):
-        chosen = jnp.concatenate(
-            [sources[pl.ds(pl.multiple_of(held[n] * TILE, TILE), TILE)] for n in (t, t + 1)], axis=0
-        )
+        sides, chosen = [], []
+        for n in (t, t + 1):
+            tile = tiles[n * TILE : (n + 1) * TILE]
+            empty = jnp.zeros_like(tile)
+            sides.append(
+                jnp.concatenate(
+                    [jnp.where(rows[n] == 0, tile, empty), jnp.where(rows[n] == 1, tile, empty)], axis=0
+                )
+            )
+            chosen.append(sources[pl.ds(pl.multiple_of(held[n] * TILE, TILE), TILE)])
         product = jnp.dot(
-            wide[0 : 2 * TILE, t * TILE : (t + 2) * TILE], chosen, preferred_element_type=jnp.float32
+            jnp.concatenate(sides, axis=1),
+            jnp.concatenate(chosen, axis=0),
+            preferred_element_type=jnp.float32,
         )
         total = product if total is None else total + product
     return total
@@ -143,25 +149,32 @@
 def sum_away_kernel(held_ref, *rest):
     count = len(AWAY)
     tiles_refs, outs = rest[:count], rest[count : 2 * count]
-    sources, tiles, wide, tail, tail_s, sems = rest[2 * count :]
-    heads = []
-    for n in range(count):
-        heads.append(pltpu.make_async_copy(tiles_refs[n], tiles.at[n], sems.at[n]))
-    heads.append(pltpu.make_async_copy(held_ref, sources, sems.at[count]))
-    for copy in heads:
+    sources, tiles, tail_b, tail, tail_s, sems = rest[2 * count :]
+    ends = [
+        pltpu.make_async_copy(
+            tiles_refs[n].at[pl.ds(PAIR * TILE, TAIL)], tail_b.at[n], sems.at[count + 2 + n]
+        )
+        for n in range(count)
+    ]
+    whole = pltpu.make_async_copy(held_ref, sources, sems.at[count])
+    heads = [
+        pltpu.make_async_copy(tiles_refs[n].at[pl.ds(0, PAIR * TILE)], tiles.at[n], sems.at[n])
+        for n in range(count)
+    ]
+    for copy in ends + [whole] + heads:
         copy.start()
-    for copy in heads:
+    for copy in ends:
         copy.wait()
-    for n in range(count):
-        tail[n] = tiles[n, PAIR * TILE : PAIR * TILE + TAIL].astype(jnp.float32).astype(jnp.int32)
+    tail[...] = tail_b[...].astype(jnp.float32).astype(jnp.int32)
     copy = pltpu.make_async_copy(tail, tail_s, sems.at[count + 1])
     copy.start()
     copy.wait()
+    whole.wait()
     for n in range(count):
         held = [tail_s[n, 0, t] for t in range(PAIR)]
         placed = [tail_s[n, 1, t] for t in range(PAIR)]
-        total = products(held, placed, tiles.at[n], sources, wide.at[n % 2])
-        outs[n][...] = total.astype(jnp.bfloat16)
+        heads[n].wait()
+        outs[n][...] = products(held, placed, tiles.at[n], sources).astype(jnp.bfloat16)
 
 
 def sum_away(sources, messages):
@@ -174,11 +187,11 @@
         out_shape=[jax.ShapeDtypeStruct((2 * TILE, channels), jnp.bfloat16)] * count,
         scratch_shapes=[
             pltpu.VMEM((rows, channels), jnp.bfloat16),
-            pltpu.VMEM((count,) + messages[0].shape, jnp.bfloat16),
-            pltpu.VMEM((2, 3 * TILE, PAIR * TILE), jnp.bfloat16),
+            pltpu.VMEM((count, PAIR * TILE, TILE), jnp.bfloat16),
+            pltpu.VMEM((count, TAIL, TILE), jnp.bfloat16),
             pltpu.VMEM((count, TAIL, TILE), jnp.int32),
             pltpu.SMEM((count, TAIL, TILE), jnp.int32),
-            pltpu.SemaphoreType.DMA((count + 2,)),
+            pltpu.SemaphoreType.DMA((2 * count + 2,)),
         ],
         compiler_params=pltpu.CompilerParams(vmem_limit_bytes=VMEM_LIMIT),
         cost_estimate=pl.CostEstimate(
@@ -191,7 +204,7 @@
 
 
 def sum_own_kernel(at_ref, dst_ref, src_ref, count_ref, held_ref, tiles_ref, out_ref, *rest):
-    sources, tiles, wide, sems = rest
+    sources, tiles, sems = rest
     start, held, placed = places(2, at_ref, dst_ref, src_ref, count_ref)
     begin = pl.multiple_of(start * (SLOTS * TILE), SLOTS * TILE)
     heads = [
@@ -202,7 +215,7 @@
         copy.start()
     for copy in heads:
         copy.wait()
-    out_ref[...] = products(held, placed, tiles, sources, wide)
+    out_ref[...] = products(held, placed, tiles, sources)
 
 
 def sum_own(at, dst, src, count, sources, tiles):
@@ -215,7 +228,6 @@
         scratch_shapes=[
             pltpu.VMEM((rows, channels), jnp.bfloat16),
             pltpu.VMEM((PAIR * TILE, TILE), jnp.bfloat16),
-            pltpu.VMEM((3 * TILE, PAIR * TILE), jnp.bfloat16),
             pltpu.SemaphoreType.DMA((2,)),
         ],
         compiler_params=pltpu.CompilerParams(vmem_limit_bytes=VMEM_LIMIT),
@@ -278,7 +290,7 @@
     split_passive,
 ):
     tiles_all = adjacency.reshape(-1, TILE)
-    dst, src, count = tile_dst[0, 0], tile_src[0, 0], tile_count[0, 0]
+    dst, src, count = tile_dst, tile_src, tile_count
     nc = lax.axis_size("cset")
     at = (lax.axis_index("blk") % 2).astype(jnp.int32)[None]
 
@@ -296,15 +308,14 @@
         twice, "blk", split_axis=0, concat_axis=0, tiled=True, axis_index_groups=groups
     ).reshape(-1, own_rows.shape[1])
 
-    parts = sum_away(sources, messages)
-    *parts, active_table = lax.optimization_barrier((*parts, active_table))
-    parts = [routed(part, 2 - which, which % 2 == 1) for which, part in zip(AWAY, parts)]
-
     extra = OUTPAD - split_active.shape[1]
     left_cols = jnp.pad(split_active, ((0, 0), (0, extra)), constant_values=-1)[:, None, :]
     right_cols = jnp.pad(split_passive, ((0, 0), (0, extra)), constant_values=-1)[:, None, :]
     picked = pick_columns(active_table, left_cols)
     own = sum_own(at, dst, src, count, sources, tiles_all)
+    sources, picked, own, right_cols = lax.optimization_barrier((sources, picked, own, right_cols))
+    parts = sum_away(sources, messages)
+    parts = [routed(part, 2 - which, which % 2 == 1) for which, part in zip(AWAY, parts)]
     joined = join(own, parts, picked, right_cols)
     spread = lax.all_to_all(joined, "cset", split_axis=0, concat_axis=0, tiled=True)
     return spread.reshape(-1, TILE)

time: 88 us -> 148 us (1.68)
  the two profiles are of different devices: /device:TPU:16 before, /device:TPU:2 now
where the time goes in v3:
time: 148 us; the launch traced here: 146 us
  Pallas kernels  91.8 us (62%)
  starting transfers between devices  26 us (18%)
  blocking collectives  19.7 us (13%)
  local copies, waits for them, and re-layouts  5.51 us (4%)
  waiting for transfers between devices  3.29 us (2%)
    pallas_call x1, Pallas kernels, pack_tiles(): pl.pallas_call(pack_kernel, in_specs=[SMEM, SMEM, SMEM, SMEM, HBM], out_s...  65.8 us
    ppermute x8, starting transfers between devices, routed(): return lax.ppermute(block, ('blk', 'cset'), route)  20.2 us
    all_to_all x1, blocking collectives, local(): lax.all_to_all(joined, 'cset', split_axis=0, concat_axis=0, tiled=True)  13.7 us
    pallas_call x1, Pallas kernels, pick_columns(): pl.pallas_call(pick_kernel, grid=(splits,), in_specs=[pl.BlockSpec((1, 1,...  13.4 us
    pallas_call x1, Pallas kernels, join(): pl.pallas_call(join_kernel, grid=(width // CHUNK,), in_specs=[pl.BlockSpe...  6.77 us
    all_to_all x1, blocking collectives, local(): lax.all_to_all(twice, 'blk', split_axis=0, concat_axis=0, tiled=True, axi...  5.94 us
    all_to_all x1, starting transfers between devices, local(): lax.all_to_all(copies, 'cset', split_axis=0, concat_axis=0, tiled=True)  5.84 us
    pallas_call x1, Pallas kernels, sum_away(): pl.pallas_call(sum_away_kernel, in_specs=[ANY] * (1 + count), out_specs=[...  4.29 us
  transfers between devices with their start and end apart: 9, of which 2 were waited for; matrix products, arithmetic and copies ran while one was open for 1% of the time, Pallas kernels for 10%

profile of v3, /device:TPU:2, one launch (start us, length us, event | category | flops | bytes accessed | tf_op | source)
XLA Modules:
  0.0 146.4 jit_solution(4379949628638477600)
XLA Ops:
  0.0 0.0 copy-start.5
  0.0 1.4 copy.9.dst_ref
  1.4 1.4 copy.10.src_ref
  2.7 0.0 copy-start.6
  2.7 65.8 %pack_tiles.1 = (bf16[2064,128]{1,0:T(8,128)(2,1)}, bf16[2064,128]{1,0:T(8,128)(2,1)}, bf16[2064,128]{1,0:T(8,128)(2,1)}, bf16[2064,128]{1,0:T(8,128)(2,1)}) custom-call(s32[1]{0:T(128)} %bitcast.at_ref, s32[1,1,9,8]{3,2,1,0:T(8,128)} %copy.9.dst_ref, s32[1,1,9,8]{3,2,1,0:T(8,128)} %copy.10.src_ref, s32[1,1,9]{2,1,0:T(1,128)} %count_ref.3, ...), custom_call_target="tpu_custom_call" | custom-call | tf_op jit(solution)/shard_map/pack_tiles/pallas_call | solution.py:82
  68.6 0.0 copy-start.7
  68.6 0.0 copy-done.5
  68.6 1.0 broadcast_in_dim.23
  69.6 5.8 %all-to-all-start = ((bf16[8,256,256]{2,1,0:T(8,128)(2,1)}), bf16[8,256,256]{2,1,0:T(8,128)(2,1)S(1)}, u32[]{:S(2)}, u32[]{:S(2)}) async-start(bf16[8,256,256]{2,1,0:T(8,128)(2,1)} %broadcast_in_dim.23), calls=%async_computation | async-start | bytes 2097152 | tf_op jit(solution)/shard_map/all_to_all | solution.py:303
  75.5 8.2 %collective-permute-start = (bf16[2064,128]{1,0:T(8,128)(2,1)}, bf16[2064,128]{1,0:T(8,128)(2,1)S(1)}, u32[]{:S(2)}, u32[]{:S(2)}) collective-permute-start(bf16[2064,128]{1,0:T(8,128)(2,1)} %get-tuple-element.30), channel_id=1, source_target_pairs={{0,244},{1,245},{2,246},{3,247},{4,240},{5,241},{6,242},{7,243},{8... | collective-permute-start | bytes 1585160 | tf_op jit(solution)/shard_map/ppermute | solution.py:27
  83.7 0.0 collective-permute-start.1
  83.7 1.0 collective-permute-start.2
  84.7 1.0 collective-permute-start.3
  85.7 0.0 copy-done.6
  85.7 0.7 broadcast_in_dim.26.cols_ref
  86.4 0.0 copy-done.7
  86.4 0.1 broadcast_in_dim.27.cols_ref
  86.5 13.4 %pick_active.1.picked_ref = bf16[20,256,1024]{2,1,0:T(8,128)(2,1)} custom-call(s32[20,1,1024]{2,1,0:T(1,128)} %broadcast_in_dim.26.cols_ref, bf16[256,256]{1,0:T(8,128)(2,1)} %table_ref.1), custom_call_target="tpu_custom_call" | custom-call | flops 2684354560 | bytes 10485760 | tf_op jit(solution)/shard_map/pick_active/pallas_call | solution.py:108
  99.9 0.0 all-to-all-done
  99.9 0.0 copy-start.1
  99.9 0.0 copy-start.2
  99.9 0.0 copy-start.3
  99.9 0.0 copy-start.4
  99.9 0.1 broadcast_in_dim.25
  100.1 0.0 copy-start
  100.1 5.9 %all_to_all.15 = bf16[2,2048,256]{2,1,0:T(8,128)(2,1)S(1)} all-to-all(bf16[2,2048,256]{2,1,0:T(8,128)(2,1)S(1)} %broadcast_in_dim.25), channel_id=1, replica_groups={{0,8},{16,24},{32,40},{48,56},{64,72},{80,88},{96,104},{112,120},{128,1..., dimensions={0} | all-to-all | bytes 4194304 | tf_op jit(solution)/shard_map/all_to_all | solution.py:307
  106.0 0.0 copy-done.1
  106.0 0.0 copy-done.2
  106.0 0.0 copy-done.3
  106.0 0.0 copy-done.4
  106.0 1.5 %sum_own.1.own_ref = f32[256,256]{1,0:T(8,128)S(1)} custom-call(s32[1]{0:T(128)} %bitcast.at_ref, s32[1,1,9,8]{3,2,1,0:T(8,128)S(1)} %copy-done.2, s32[1,1,9,8]{3,2,1,0:T(8,128)S(1)} %copy-done.3, s32[1,1,9]{2,1,0:T(1,128)S(1)} %copy-done.4, bf16[4096,256]{1,0:T(8,128)(2,1)S(1)} %bitcast.5, bf16[9216,128]{1,0:T(8,128)(2,1)S(1)} %bitcast.8), custom_call_target="tpu_custom_call" | custom-call | flops 268435456 | bytes 2621440 | tf_op jit(solution)/shard_map/sum_own/pallas_call | solution.py:223
  107.5 0.0 collective-permute-done.rest_0_
  107.6 0.0 collective-permute-done.1.rest_1_
  107.6 0.0 collective-permute-done.2.rest_2_
  107.6 0.0 collective-permute-done.3.rest_3_
  107.6 4.3 %sum_away.1 = (bf16[256,256]{1,0:T(8,128)(2,1)S(1)}, bf16[256,256]{1,0:T(8,128)(2,1)S(1)}, bf16[256,256]{1,0:T(8,128)(2,1)S(1)}, bf16[256,256]{1,0:T(8,128)(2,1)S(1)}) custom-call(bf16[4096,256]{1,0:T(8,128)(2,1)S(1)} %bitcast.6, bf16[2064,128]{1,0:T(8,128)(2,1)S(1)} %collective-permute-done.rest_0_, bf16[2064,128]{1,0:T(8,128)(2,1)S(1)} %collective-permute-done.1.rest_1_, ...), custom_call_target="tpu_custom_call" | custom-call | flops 1073741824 | bytes 4194304 | tf_op jit(solution)/shard_map/sum_away/pallas_call | solution.py:183
  111.9 4.5 %collective-permute-start.4 = (bf16[256,256]{1,0:T(8,128)(2,1)S(1)}, bf16[256,256]{1,0:T(8,128)(2,1)S(1)}, u32[]{:S(2)}, u32[]{:S(2)}) collective-permute-start(bf16[256,256]{1,0:T(8,128)(2,1)S(1)} %get-tuple-element.34), channel_id=1, source_target_pairs={{0,20},{1,21},{2,22},{3,23},{4,16},{5,17},{6,18},{7,19},{8,28},{9,... | collective-permute-start | bytes 393224 | tf_op jit(solution)/shard_map/ppermute | solution.py:27
  116.4 2.2 %collective-permute-start.5 = (bf16[256,256]{1,0:T(8,128)(2,1)S(1)}, bf16[256,256]{1,0:T(8,128)(2,1)S(1)}, u32[]{:S(2)}, u32[]{:S(2)}) collective-permute-start(bf16[256,256]{1,0:T(8,128)(2,1)S(1)} %get-tuple-element.35), channel_id=1, source_target_pairs={{0,244},{1,245},{2,246},{3,247},{4,240},{5,241},{6,242},{7,243},{8... | collective-permute-start | bytes 393224 | tf_op jit(solution)/shard_map/ppermute | solution.py:27
  118.6 0.0 collective-permute-start.6
  118.6 3.2 %collective-permute-start.7 = (bf16[256,256]{1,0:T(8,128)(2,1)S(1)}, bf16[256,256]{1,0:T(8,128)(2,1)S(1)}, u32[]{:S(2)}, u32[]{:S(2)}) collective-permute-start(bf16[256,256]{1,0:T(8,128)(2,1)S(1)} %get-tuple-element.37), channel_id=1, source_target_pairs={{0,224},{1,225},{2,226},{3,227},{4,228},{5,229},{6,230},{7,231},{8... | collective-permute-start | bytes 393224 | tf_op jit(solution)/shard_map/ppermute | solution.py:27
  121.8 0.6 collective-permute-done.4.n0
  122.4 2.7 %collective-permute-done.5.n1 = bf16[256,256]{1,0:T(8,128)(2,1)S(1)} collective-permute-done((bf16[256,256]{1,0:T(8,128)(2,1)S(1)}, bf16[256,256]{1,0:T(8,128)(2,1)S(1)}, u32[]{:S(2)}, u32[]{:S(2)}) %collective-permute-start.5) | collective-permute-done | bytes 131104 | tf_op jit(solution)/shard_map/ppermute | solution.py:27
  125.1 0.0 collective-permute-done.6.n2
  125.1 0.0 collective-permute-done.7.n3
  125.1 0.0 copy-done
  125.1 6.8 %join_sets.1 = bf16[8,256,128]{2,1,0:T(8,128)(2,1)S(1)} custom-call(s32[20,1,1024]{2,1,0:T(1,128)S(1)} %broadcast_in_dim.27.cols_ref, f32[256,256]{1,0:T(8,128)S(1)} %sum_own.1.own_ref, bf16[256,256]{1,0:T(8,128)(2,1)S(1)} %collective-permute-done.4.n0, bf16[256,256]{1,0:T(8,128)(2,1)S(1)} %collective-permute-done.5.n1, ...), custom_call_target="tpu_custom_call" | custom-call | flops 2684354560 | bytes 10485760 | tf_op jit(solution)/shard_map/join_sets/pallas_call | solution.py:264
  131.9 13.7 %all_to_all.16 = bf16[8,256,128]{2,1,0:T(8,128)(2,1)S(1)} all-to-all(bf16[8,256,128]{2,1,0:T(8,128)(2,1)S(1)} %join_sets.1), channel_id=1, replica_groups=mesh['blk'=32,'cset'=8] {'cset'}, dimensions={0} | all-to-all | bytes 1048576 | tf_op jit(solution)/shard_map/all_to_all | solution.py:320
  145.6 0.8 copy.14
  (2 shorter events, 0.0 us)
Async XLA Ops:
  0.0 68.6 %copy-start.5 = (bf16[256,256]{1,0:T(8,128)(2,1)S(1)}, bf16[256,256]{1,0:T(8,128)(2,1)}, u32[]{:S(2)}) copy-start(bf16[256,256]{1,0:T(8,128)(2,1)} %param.9) | copy-start | bytes 393220
  2.7 82.9 %copy-start.6 = (s32[20,924]{1,0:T(8,128)S(1)}, s32[20,924]{1,0:T(8,128)}, u32[]{:S(2)}) copy-start(s32[20,924]{1,0:T(8,128)} %param.14) | copy-start | bytes 221764
  68.6 17.8 %copy-start.7 = (s32[20,924]{1,0:T(8,128)S(1)}, s32[20,924]{1,0:T(8,128)}, u32[]{:S(2)}) copy-start(s32[20,924]{1,0:T(8,128)} %param.15) | copy-start | bytes 221764
  69.6 30.3 %all-to-all-start = ((bf16[8,256,256]{2,1,0:T(8,128)(2,1)}), bf16[8,256,256]{2,1,0:T(8,128)(2,1)S(1)}, u32[]{:S(2)}, u32[]{:S(2)}) async-start(bf16[8,256,256]{2,1,0:T(8,128)(2,1)} %broadcast_in_dim.23), calls=%async_computation | async-start | bytes 2097152 | tf_op jit(solution)/shard_map/all_to_all | solution.py:303
  75.5 32.1 %collective-permute-start = (bf16[2064,128]{1,0:T(8,128)(2,1)}, bf16[2064,128]{1,0:T(8,128)(2,1)S(1)}, u32[]{:S(2)}, u32[]{:S(2)}) collective-permute-start(bf16[2064,128]{1,0:T(8,128)(2,1)} %get-tuple-element.30), channel_id=1, source_target_pairs={{0,244},{1,245},{2,246},{3,247},{4,240},{5,241},{6,242},{7,243},{8... | collective-permute-start | bytes 1585160 | tf_op jit(solution)/shard_map/ppermute | solution.py:27
  83.7 23.9 %collective-permute-start.1 = (bf16[2064,128]{1,0:T(8,128)(2,1)}, bf16[2064,128]{1,0:T(8,128)(2,1)S(1)}, u32[]{:S(2)}, u32[]{:S(2)}) collective-permute-start(bf16[2064,128]{1,0:T(8,128)(2,1)} %get-tuple-element.31), channel_id=1, source_target_pairs={{0,20},{1,21},{2,22},{3,23},{4,16},{5,17},{6,18},{7,19},{8,28},{9,... | collective-permute-start | bytes 1585160 | tf_op jit(solution)/shard_map/ppermute | solution.py:27
  83.7 23.9 %collective-permute-start.2 = (bf16[2064,128]{1,0:T(8,128)(2,1)}, bf16[2064,128]{1,0:T(8,128)(2,1)S(1)}, u32[]{:S(2)}, u32[]{:S(2)}) collective-permute-start(bf16[2064,128]{1,0:T(8,128)(2,1)} %get-tuple-element.32), channel_id=1, source_target_pairs={{0,224},{1,225},{2,226},{3,227},{4,228},{5,229},{6,230},{7,231},{8... | collective-permute-start | bytes 1585160 | tf_op jit(solution)/shard_map/ppermute | solution.py:27
  84.7 22.9 %collective-permute-start.3 = (bf16[2064,128]{1,0:T(8,128)(2,1)}, bf16[2064,128]{1,0:T(8,128)(2,1)S(1)}, u32[]{:S(2)}, u32[]{:S(2)}) collective-permute-start(bf16[2064,128]{1,0:T(8,128)(2,1)} %get-tuple-element.33), channel_id=1, source_target_pairs={{0,32},{1,33},{2,34},{3,35},{4,36},{5,37},{6,38},{7,39},{8,40},{9,... | collective-permute-start | bytes 1585160 | tf_op jit(solution)/shard_map/ppermute | solution.py:27
  99.9 6.1 %copy-start.1 = (bf16[1,1,9,8,128,128]{5,4,3,2,1,0:T(8,128)(2,1)S(1)}, bf16[1,1,9,8,128,128]{5,4,3,2,1,0:T(8,128)(2,1)}, u32[]{:S(2)}) copy-start(bf16[1,1,9,8,128,128]{5,4,3,2,1,0:T(8,128)(2,1)} %param.10) | copy-start | bytes 7077892
  99.9 6.1 %copy-start.2 = (s32[1,1,9,8]{3,2,1,0:T(8,128)S(1)}, s32[1,1,9,8]{3,2,1,0:T(8,128)}, u32[]{:S(2)}) copy-start(s32[1,1,9,8]{3,2,1,0:T(8,128)} %copy.9.dst_ref) | copy-start | bytes 868
  99.9 6.1 %copy-start.3 = (s32[1,1,9,8]{3,2,1,0:T(8,128)S(1)}, s32[1,1,9,8]{3,2,1,0:T(8,128)}, u32[]{:S(2)}) copy-start(s32[1,1,9,8]{3,2,1,0:T(8,128)} %copy.10.src_ref) | copy-start | bytes 868
  99.9 6.1 %copy-start.4 = (s32[1,1,9]{2,1,0:T(1,128)S(1)}, s32[1,1,9]{2,1,0:T(1,128)}, u32[]{:S(2)}) copy-start(s32[1,1,9]{2,1,0:T(1,128)} %count_ref.3) | copy-start | bytes 112
  100.1 25.1 %copy-start = (bf16[20,256,1024]{2,1,0:T(8,128)(2,1)S(1)}, bf16[20,256,1024]{2,1,0:T(8,128)(2,1)}, u32[]{:S(2)}) copy-start(bf16[20,256,1024]{2,1,0:T(8,128)(2,1)} %pick_active.1.picked_ref) | copy-start | bytes 31457284
  111.9 10.5 %collective-permute-start.4 = (bf16[256,256]{1,0:T(8,128)(2,1)S(1)}, bf16[256,256]{1,0:T(8,128)(2,1)S(1)}, u32[]{:S(2)}, u32[]{:S(2)}) collective-permute-start(bf16[256,256]{1,0:T(8,128)(2,1)S(1)} %get-tuple-element.34), channel_id=1, source_target_pairs={{0,20},{1,21},{2,22},{3,23},{4,16},{5,17},{6,18},{7,19},{8,28},{9,... | collective-permute-start | bytes 393224 | tf_op jit(solution)/shard_map/ppermute | solution.py:27
  116.4 8.7 %collective-permute-start.5 = (bf16[256,256]{1,0:T(8,128)(2,1)S(1)}, bf16[256,256]{1,0:T(8,128)(2,1)S(1)}, u32[]{:S(2)}, u32[]{:S(2)}) collective-permute-start(bf16[256,256]{1,0:T(8,128)(2,1)S(1)} %get-tuple-element.35), channel_id=1, source_target_pairs={{0,244},{1,245},{2,246},{3,247},{4,240},{5,241},{6,242},{7,243},{8... | collective-permute-start | bytes 393224 | tf_op jit(solution)/shard_map/ppermute | solution.py:27
  118.6 6.5 %collective-permute-start.6 = (bf16[256,256]{1,0:T(8,128)(2,1)S(1)}, bf16[256,256]{1,0:T(8,128)(2,1)S(1)}, u32[]{:S(2)}, u32[]{:S(2)}) collective-permute-start(bf16[256,256]{1,0:T(8,128)(2,1)S(1)} %get-tuple-element.36), channel_id=1, source_target_pairs={{0,32},{1,33},{2,34},{3,35},{4,36},{5,37},{6,38},{7,39},{8,40},{9,... | collective-permute-start | bytes 393224 | tf_op jit(solution)/shard_map/ppermute | solution.py:27
  118.6 6.5 %collective-permute-start.7 = (bf16[256,256]{1,0:T(8,128)(2,1)S(1)}, bf16[256,256]{1,0:T(8,128)(2,1)S(1)}, u32[]{:S(2)}, u32[]{:S(2)}) collective-permute-start(bf16[256,256]{1,0:T(8,128)(2,1)S(1)} %get-tuple-element.37), channel_id=1, source_target_pairs={{0,224},{1,225},{2,226},{3,227},{4,228},{5,229},{6,230},{7,231},{8... | collective-permute-start | bytes 393224 | tf_op jit(solution)/shard_map/ppermute | solution.py:27

commit v4 on v3

--- a/solution.py
+++ b/solution.py
@@ -8,7 +8,7 @@
 SPLITS = 20
 OUTPAD = 1024
 TILE = 128
-CHUNK = 256
+CHUNK = 512
 SLOTS = 8
 PAIR = 2 * SLOTS
 TAIL = 16
@@ -38,37 +38,41 @@
         slot = start + half
         parity = slot - first
         for t in range(SLOTS):
-            source = src_ref[0, 0, slot, t]
+            source = src_ref[t, slot]
             inside = jnp.logical_and(parity >= 0, parity < 2)
             held.append(source + jnp.where(parity == 1, 2 * nc, 0))
-            live = jnp.logical_and(inside, t < count_ref[0, 0, slot])
-            rows.append(jnp.where(live, dst_ref[0, 0, slot, t], 2))
+            live = jnp.logical_and(inside, t < count_ref[slot])
+            rows.append(jnp.where(live, dst_ref[t, slot], 2))
     return start, held, rows
 
 
 def pack_kernel(at_ref, dst_ref, src_ref, count_ref, tiles_ref, *rest):
-    outs, tails, sems = rest[: len(AWAY)], rest[-2], rest[-1]
-    copies = []
+    outs = rest[: len(AWAY)]
+    held_tiles, sems_in, sems_out = rest[len(AWAY) :]
     lane = lax.broadcasted_iota(jnp.int32, (TAIL, TILE), 1)
     line = lax.broadcasted_iota(jnp.int32, (TAIL, TILE), 0)
-    for n, which in enumerate(AWAY):
-        start, held, rows = places(which, at_ref, dst_ref, src_ref, count_ref)
-        begin = pl.multiple_of(start * (SLOTS * TILE), SLOTS * TILE)
-        copy = pltpu.make_async_copy(
-            tiles_ref.at[pl.ds(begin, PAIR * TILE)], outs[n].at[pl.ds(0, PAIR * TILE)], sems.at[2 * n]
+    found = [places(which, at_ref, dst_ref, src_ref, count_ref) for which in AWAY]
+    arriving, leaving = [], []
+    for n in range(len(AWAY)):
+        begin = pl.multiple_of(found[n][0] * (SLOTS * TILE), SLOTS * TILE)
+        arriving.append(
+            pltpu.make_async_copy(
+                tiles_ref.at[pl.ds(begin, PAIR * TILE)],
+                held_tiles.at[n, pl.ds(0, PAIR * TILE)],
+                sems_in.at[n],
+            )
         )
-        copy.start()
-        copies.append(copy)
+        arriving[n].start()
+    for n in range(len(AWAY)):
+        _, held, rows = found[n]
         tail = jnp.zeros((TAIL, TILE), jnp.int32)
         for t in range(PAIR):
             tail = jnp.where(lane == t, jnp.where(line == 0, held[t], rows[t]), tail)
-        tails[n] = tail.astype(jnp.float32).astype(jnp.bfloat16)
-        copy = pltpu.make_async_copy(
-            tails.at[n], outs[n].at[pl.ds(PAIR * TILE, TAIL)], sems.at[2 * n + 1]
-        )
-        copy.start()
-        copies.append(copy)
-    for copy in copies:
+        held_tiles[n, PAIR * TILE : PAIR * TILE + TAIL] = tail.astype(jnp.float32).astype(jnp.bfloat16)
+        arriving[n].wait()
+        leaving.append(pltpu.make_async_copy(held_tiles.at[n], outs[n], sems_out.at[n]))
+        leaving[n].start()
+    for copy in leaving:
         copy.wait()
 
 
@@ -85,43 +89,13 @@
         out_specs=[ANY] * len(AWAY),
         out_shape=[jax.ShapeDtypeStruct((PAIR * TILE + TAIL, TILE), jnp.bfloat16)] * len(AWAY),
         scratch_shapes=[
-            pltpu.VMEM((len(AWAY), TAIL, TILE), jnp.bfloat16),
-            pltpu.SemaphoreType.DMA((2 * len(AWAY),)),
+            pltpu.VMEM((len(AWAY), PAIR * TILE + TAIL, TILE), jnp.bfloat16),
+            pltpu.SemaphoreType.DMA((len(AWAY),)),
+            pltpu.SemaphoreType.DMA((len(AWAY),)),
         ],
         compiler_params=pltpu.CompilerParams(vmem_limit_bytes=PACK_LIMIT),
         name="pack_tiles",
     )(at, dst, src, count, tiles)
-
-
-def pick_kernel(cols_ref, table_ref, out_ref):
-    width = cols_ref.shape[2]
-    channel = lax.broadcasted_iota(jnp.int32, (table_ref.shape[1], width), 0)
-    onehot = (channel == cols_ref[0]).astype(jnp.bfloat16)
-    out_ref[0] = jnp.dot(
-        table_ref[...], onehot, preferred_element_type=jnp.float32
-    ).astype(jnp.bfloat16)
-
-
-def pick_columns(table, cols):
-    rows, channels = table.shape
-    splits, _, width = cols.shape
-    return pl.pallas_call(
-        pick_kernel,
-        grid=(splits,),
-        in_specs=[
-            pl.BlockSpec((1, 1, width), lambda j: (j, 0, 0)),
-            pl.BlockSpec((rows, channels), lambda j: (0, 0)),
-        ],
-        out_specs=pl.BlockSpec((1, rows, width), lambda j: (j, 0, 0)),
-        out_shape=jax.ShapeDtypeStruct((splits, rows, width), jnp.bfloat16),
-        compiler_params=pltpu.CompilerParams(vmem_limit_bytes=PACK_LIMIT),
-        cost_estimate=pl.CostEstimate(
-            flops=2 * splits * rows * channels * width,
-            bytes_accessed=2 * splits * rows * width,
-            transcendentals=0,
-        ),
-        name="pick_active",
-    )(cols, table)
 
 
 def products(held, rows, tiles, sources):
@@ -240,43 +214,45 @@
     )(at, dst, src, count, sources, tiles)
 
 
-def join_kernel(cols_ref, own_ref, n0, n1, n2, n3, picked_ref, out_ref):
+def join_kernel(left_ref, right_ref, active_ref, own_ref, n0, n1, n2, n3, out_ref):
     total = own_ref[...]
     for part in (n0, n1, n2, n3):
         total = total + part[...].astype(jnp.float32)
     neighbour = total.astype(jnp.bfloat16)
-    width = picked_ref.shape[2]
-    channel = lax.broadcasted_iota(jnp.int32, (neighbour.shape[1], width), 0)
-    joined = jnp.zeros((neighbour.shape[0], width), jnp.float32)
+    active = active_ref[...]
+    shape = (active.shape[1], left_ref.shape[2])
+    channel = lax.broadcasted_iota(jnp.int32, shape, 0).astype(jnp.float32).astype(jnp.bfloat16)
+    one, zero = jnp.ones(shape, jnp.bfloat16), jnp.zeros(shape, jnp.bfloat16)
+    joined = jnp.zeros((active.shape[0], shape[1]), jnp.float32)
     for j in range(SPLITS):
-        onehot = (channel == cols_ref[j]).astype(jnp.bfloat16)
-        joined = joined + picked_ref[j].astype(jnp.float32) * jnp.dot(
-            neighbour, onehot, preferred_element_type=jnp.float32
+        left = jnp.where(channel == left_ref[j], one, zero)
+        right = jnp.where(channel == right_ref[j], one, zero)
+        joined = joined + jnp.dot(active, left, preferred_element_type=jnp.float32) * jnp.dot(
+            neighbour, right, preferred_element_type=jnp.float32
         )
-    for piece in range(width // TILE):
+    for piece in range(shape[1] // TILE):
         out_ref[piece] = joined[:, piece * TILE : (piece + 1) * TILE].astype(out_ref.dtype)
 
 
-def join(own, parts, picked, cols):
+def join(active, own, parts, left, right):
     rows, channels = own.shape
-    splits, _, width = cols.shape
+    splits, _, width = left.shape
     whole = pl.BlockSpec((rows, channels), lambda q: (0, 0))
+    columns = pl.BlockSpec((splits, 1, CHUNK), lambda q: (0, 0, q))
     return pl.pallas_call(
         join_kernel,
         grid=(width // CHUNK,),
-        in_specs=[pl.BlockSpec((splits, 1, CHUNK), lambda q: (0, 0, q))]
-        + [whole] * 5
-        + [pl.BlockSpec((splits, rows, CHUNK), lambda q: (0, 0, q))],
+        in_specs=[columns] * 2 + [whole] * 6,
         out_specs=pl.BlockSpec((CHUNK // TILE, rows, TILE), lambda q: (q, 0, 0)),
         out_shape=jax.ShapeDtypeStruct((width // TILE, rows, TILE), jnp.bfloat16),
         compiler_params=pltpu.CompilerParams(vmem_limit_bytes=VMEM_LIMIT),
         cost_estimate=pl.CostEstimate(
-            flops=2 * splits * rows * channels * width,
-            bytes_accessed=2 * splits * rows * width,
+            flops=4 * splits * rows * channels * width,
+            bytes_accessed=2 * rows * width,
             transcendentals=0,
         ),
         name="join_sets",
-    )(cols, own, *parts, picked)
+    )(left, right, active, own, *parts)
 
 
 def local(
@@ -290,7 +266,7 @@
     split_passive,
 ):
     tiles_all = adjacency.reshape(-1, TILE)
-    dst, src, count = tile_dst, tile_src, tile_count
+    dst, src, count = tile_dst[0, 0].T, tile_src[0, 0].T, tile_count[0, 0]
     nc = lax.axis_size("cset")
     at = (lax.axis_index("blk") % 2).astype(jnp.int32)[None]
 
@@ -309,14 +285,15 @@
     ).reshape(-1, own_rows.shape[1])
 
     extra = OUTPAD - split_active.shape[1]
-    left_cols = jnp.pad(split_active, ((0, 0), (0, extra)), constant_values=-1)[:, None, :]
-    right_cols = jnp.pad(split_passive, ((0, 0), (0, extra)), constant_values=-1)[:, None, :]
-    picked = pick_columns(active_table, left_cols)
+    left, right = (
+        jnp.pad(cols.astype(jnp.bfloat16), ((0, 0), (0, extra)), constant_values=-1)[:, None, :]
+        for cols in (split_active, split_passive)
+    )
     own = sum_own(at, dst, src, count, sources, tiles_all)
-    sources, picked, own, right_cols = lax.optimization_barrier((sources, picked, own, right_cols))
+    sources, own, left, right = lax.optimization_barrier((sources, own, left, right))
     parts = sum_away(sources, messages)
     parts = [routed(part, 2 - which, which % 2 == 1) for which, part in zip(AWAY, parts)]
-    joined = join(own, parts, picked, right_cols)
+    joined = join(active_table, own, parts, left, right)
     spread = lax.all_to_all(joined, "cset", split_axis=0, concat_axis=0, tiled=True)
     return spread.reshape(-1, TILE)
 

time: 148 us -> 78.2 us (0.53)
  Pallas kernels: 91.8 us -> 15 us
  waiting for transfers between devices: 3.29 us -> 16.3 us
  local copies, waits for them, and re-layouts: 5.51 us -> 2.18 us
  blocking collectives: 19.7 us -> 17.7 us
    pallas_call x1, Pallas kernels: 65.8 us -> 3.39 us  [pack_tiles(): pl.pallas_call(pack_kernel, in_specs=[SMEM, SMEM, SMEM, SMEM, HBM], out_s...]
    pallas_call x2 -> x1, Pallas kernels: 20.2 us -> 6.01 us  [join(): pl.pallas_call(join_kernel, grid=(width // CHUNK,), in_specs=[columns] *...]
    ppermute x8, waiting for transfers between devices: 3.29 us -> 12.1 us  [routed(): return lax.ppermute(block, ('blk', 'cset'), route)]
    all_to_all x1, waiting for transfers between devices: 0.01 us -> 4.25 us  [local(): lax.all_to_all(copies, 'cset', split_axis=0, concat_axis=0, tiled=True)]
    unnamed x19 -> x17, local copies, waits for them, and re-layouts: 3.57 us -> 0.84 us
    all_to_all x1, blocking collectives: 13.7 us -> 12.1 us  [local(): lax.all_to_all(joined, 'cset', split_axis=0, concat_axis=0, tiled=True)]
  transfers between devices with their start and end apart: 9 -> 9, of which waited for: 2 -> 7; matrix products, arithmetic and copies ran while one was open for 1% -> 0% of each run, Pallas kernels for 10% -> 2%
where the time goes in v4:
time: 78.2 us; the launch traced here: 76.7 us
  starting transfers between devices  25.4 us (32%)
  blocking collectives  17.7 us (23%)
  waiting for transfers between devices  16.3 us (21%)
  Pallas kernels  15 us (19%)
  local copies, waits for them, and re-layouts  2.18 us (3%)
    ppermute x8, starting transfers between devices, routed(): return lax.ppermute(block, ('blk', 'cset'), route)  19.5 us
    all_to_all x1, blocking collectives, local(): lax.all_to_all(joined, 'cset', split_axis=0, concat_axis=0, tiled=True)  12.1 us
    ppermute x8, waiting for transfers between devices, routed(): return lax.ppermute(block, ('blk', 'cset'), route)  12.1 us
    pallas_call x1, Pallas kernels, join(): pl.pallas_call(join_kernel, grid=(width // CHUNK,), in_specs=[columns] *...  6.01 us
    all_to_all x1, starting transfers between devices, local(): lax.all_to_all(copies, 'cset', split_axis=0, concat_axis=0, tiled=True)  5.84 us
    all_to_all x1, blocking collectives, local(): lax.all_to_all(twice, 'blk', split_axis=0, concat_axis=0, tiled=True, axi...  5.55 us
    pallas_call x1, Pallas kernels, sum_away(): pl.pallas_call(sum_away_kernel, in_specs=[ANY] * (1 + count), out_specs=[...  4.27 us
    all_to_all x1, waiting for transfers between devices, local(): lax.all_to_all(copies, 'cset', split_axis=0, concat_axis=0, tiled=True)  4.25 us
  transfers between devices with their start and end apart: 9, of which 7 were waited for; matrix products, arithmetic and copies ran while one was open for 0% of the time, Pallas kernels for 2%

profile of v4, /device:TPU:2, one launch (start us, length us, event | category | flops | bytes accessed | tf_op | source)
XLA Modules:
  0.0 76.7 jit_solution(3316716608110505318)
XLA Ops:
  0.0 0.0 copy-start.5
  0.0 3.4 %pack_tiles.1 = (bf16[2064,128]{1,0:T(8,128)(2,1)}, bf16[2064,128]{1,0:T(8,128)(2,1)}, bf16[2064,128]{1,0:T(8,128)(2,1)}, bf16[2064,128]{1,0:T(8,128)(2,1)}) custom-call(s32[1]{0:T(128)} %bitcast.at_ref, s32[8,9]{1,0:T(8,128)} %bitcast.20, s32[8,9]{1,0:T(8,128)} %bitcast.22, s32[9]{0:T(128)} %bitcast.24, bf16[9216,128]{1,0:T(8,128)(2,1)} %bitcast.18), custom_call_target="tpu_custom_call" | custom-call | tf_op jit(solution)/shard_map/pack_tiles/pallas_call | solution.py:86
  3.4 0.0 copy-start.6
  3.4 0.0 copy-start.7
  3.4 0.0 copy-done.5
  3.4 1.1 %broadcast_in_dim.23 = bf16[8,256,256]{2,1,0:T(8,128)(2,1)} broadcast(bf16[256,256]{1,0:T(8,128)(2,1)S(1)} %copy-done.5), dimensions={1,2} | broadcast | bytes 1179648 | tf_op jit(solution)/shard_map/broadcast_in_dim | solution.py:278
  4.5 5.8 %all-to-all-start = ((bf16[8,256,256]{2,1,0:T(8,128)(2,1)}), bf16[8,256,256]{2,1,0:T(8,128)(2,1)S(1)}, u32[]{:S(2)}, u32[]{:S(2)}) async-start(bf16[8,256,256]{2,1,0:T(8,128)(2,1)} %broadcast_in_dim.23), calls=%async_computation | async-start | bytes 2097152 | tf_op jit(solution)/shard_map/all_to_all | solution.py:279
  10.3 8.2 %collective-permute-start = (bf16[2064,128]{1,0:T(8,128)(2,1)}, bf16[2064,128]{1,0:T(8,128)(2,1)S(1)}, u32[]{:S(2)}, u32[]{:S(2)}) collective-permute-start(bf16[2064,128]{1,0:T(8,128)(2,1)} %get-tuple-element.31), channel_id=1, source_target_pairs={{0,244},{1,245},{2,246},{3,247},{4,240},{5,241},{6,242},{7,243},{8... | collective-permute-start | bytes 1585160 | tf_op jit(solution)/shard_map/ppermute | solution.py:27
  18.5 0.0 collective-permute-start.1
  18.5 1.0 %collective-permute-start.2 = (bf16[2064,128]{1,0:T(8,128)(2,1)}, bf16[2064,128]{1,0:T(8,128)(2,1)S(1)}, u32[]{:S(2)}, u32[]{:S(2)}) collective-permute-start(bf16[2064,128]{1,0:T(8,128)(2,1)} %get-tuple-element.33), channel_id=1, source_target_pairs={{0,224},{1,225},{2,226},{3,227},{4,228},{5,229},{6,230},{7,231},{8... | collective-permute-start | bytes 1585160 | tf_op jit(solution)/shard_map/ppermute | solution.py:27
  19.5 1.0 %collective-permute-start.3 = (bf16[2064,128]{1,0:T(8,128)(2,1)}, bf16[2064,128]{1,0:T(8,128)(2,1)S(1)}, u32[]{:S(2)}, u32[]{:S(2)}) collective-permute-start(bf16[2064,128]{1,0:T(8,128)(2,1)} %get-tuple-element.34), channel_id=1, source_target_pairs={{0,32},{1,33},{2,34},{3,35},{4,36},{5,37},{6,38},{7,39},{8,40},{9,... | collective-permute-start | bytes 1585160 | tf_op jit(solution)/shard_map/ppermute | solution.py:27
  20.6 0.0 copy-done.6
  20.6 0.0 copy-done.7
  20.6 4.2 %all-to-all-done = bf16[8,256,256]{2,1,0:T(8,128)(2,1)S(1)} async-done(((bf16[8,256,256]{2,1,0:T(8,128)(2,1)}), bf16[8,256,256]{2,1,0:T(8,128)(2,1)S(1)}, u32[]{:S(2)}, u32[]{:S(2)}) %all-to-all-start) | async-done | bytes 1048608 | tf_op jit(solution)/shard_map/all_to_all | solution.py:279
  24.9 0.1 broadcast_in_dim.25
  25.0 0.0 copy-start
  25.0 0.0 copy-start.1
  25.0 0.0 copy-start.2
  25.1 0.0 copy-start.3
  25.1 5.5 %all_to_all.15 = bf16[2,2048,256]{2,1,0:T(8,128)(2,1)S(1)} all-to-all(bf16[2,2048,256]{2,1,0:T(8,128)(2,1)S(1)} %broadcast_in_dim.25), channel_id=1, replica_groups={{0,8},{16,24},{32,40},{48,56},{64,72},{80,88},{96,104},{112,120},{128,1..., dimensions={0} | all-to-all | bytes 4194304 | tf_op jit(solution)/shard_map/all_to_all | solution.py:283
  30.6 0.0 copy-done
  30.6 0.0 copy-done.1
  30.6 0.0 copy-done.2
  30.6 0.0 copy-done.3
  30.6 1.4 %sum_own.1.own_ref = f32[256,256]{1,0:T(8,128)S(1)} custom-call(s32[1]{0:T(128)} %bitcast.at_ref, s32[8,9]{1,0:T(8,128)S(1)} %bitcast.21, s32[8,9]{1,0:T(8,128)S(1)} %bitcast.23, s32[9]{0:T(128)S(1)} %bitcast.25, bf16[4096,256]{1,0:T(8,128)(2,1)S(1)} %bitcast.16, bf16[9216,128]{1,0:T(8,128)(2,1)S(1)} %bitcast.19), custom_call_target="tpu_custom_call" | custom-call | flops 268435456 | bytes 2621440 | tf_op jit(solution)/shard_map/sum_own/pallas_call | solution.py:197
  32.0 0.0 copy-start.4
  32.0 3.5 %collective-permute-done.rest_0_ = bf16[2064,128]{1,0:T(8,128)(2,1)S(1)} collective-permute-done((bf16[2064,128]{1,0:T(8,128)(2,1)}, bf16[2064,128]{1,0:T(8,128)(2,1)S(1)}, u32[]{:S(2)}, u32[]{:S(2)}) %collective-permute-start) | collective-permute-done | bytes 528416 | tf_op jit(solution)/shard_map/ppermute | solution.py:27
  35.5 1.6 %collective-permute-done.1.rest_1_ = bf16[2064,128]{1,0:T(8,128)(2,1)S(1)} collective-permute-done((bf16[2064,128]{1,0:T(8,128)(2,1)}, bf16[2064,128]{1,0:T(8,128)(2,1)S(1)}, u32[]{:S(2)}, u32[]{:S(2)}) %collective-permute-start.1) | collective-permute-done | bytes 528416 | tf_op jit(solution)/shard_map/ppermute | solution.py:27
  37.1 3.9 %collective-permute-done.2.rest_2_ = bf16[2064,128]{1,0:T(8,128)(2,1)S(1)} collective-permute-done((bf16[2064,128]{1,0:T(8,128)(2,1)}, bf16[2064,128]{1,0:T(8,128)(2,1)S(1)}, u32[]{:S(2)}, u32[]{:S(2)}) %collective-permute-start.2) | collective-permute-done | bytes 528416 | tf_op jit(solution)/shard_map/ppermute | solution.py:27
  40.9 0.0 collective-permute-done.3.rest_3_
  40.9 4.3 %sum_away.1 = (bf16[256,256]{1,0:T(8,128)(2,1)S(1)}, bf16[256,256]{1,0:T(8,128)(2,1)S(1)}, bf16[256,256]{1,0:T(8,128)(2,1)S(1)}, bf16[256,256]{1,0:T(8,128)(2,1)S(1)}) custom-call(bf16[4096,256]{1,0:T(8,128)(2,1)S(1)} %bitcast.17, bf16[2064,128]{1,0:T(8,128)(2,1)S(1)} %collective-permute-done.rest_0_, bf16[2064,128]{1,0:T(8,128)(2,1)S(1)} %collective-permute-done.1.rest_1_, ...), custom_call_target="tpu_custom_call" | custom-call | flops 1073741824 | bytes 4194304 | tf_op jit(solution)/shard_map/sum_away/pallas_call | solution.py:157
  45.2 6.1 %collective-permute-start.4 = (bf16[256,256]{1,0:T(8,128)(2,1)S(1)}, bf16[256,256]{1,0:T(8,128)(2,1)S(1)}, u32[]{:S(2)}, u32[]{:S(2)}) collective-permute-start(bf16[256,256]{1,0:T(8,128)(2,1)S(1)} %get-tuple-element.35), channel_id=1, source_target_pairs={{0,20},{1,21},{2,22},{3,23},{4,16},{5,17},{6,18},{7,19},{8,28},{9,... | collective-permute-start | bytes 393224 | tf_op jit(solution)/shard_map/ppermute | solution.py:27
  51.3 0.0 collective-permute-start.5
  51.3 1.6 %collective-permute-start.6 = (bf16[256,256]{1,0:T(8,128)(2,1)S(1)}, bf16[256,256]{1,0:T(8,128)(2,1)S(1)}, u32[]{:S(2)}, u32[]{:S(2)}) collective-permute-start(bf16[256,256]{1,0:T(8,128)(2,1)S(1)} %get-tuple-element.37), channel_id=1, source_target_pairs={{0,32},{1,33},{2,34},{3,35},{4,36},{5,37},{6,38},{7,39},{8,40},{9,... | collective-permute-start | bytes 393224 | tf_op jit(solution)/shard_map/ppermute | solution.py:27
  52.8 1.7 %collective-permute-start.7 = (bf16[256,256]{1,0:T(8,128)(2,1)S(1)}, bf16[256,256]{1,0:T(8,128)(2,1)S(1)}, u32[]{:S(2)}, u32[]{:S(2)}) collective-permute-start(bf16[256,256]{1,0:T(8,128)(2,1)S(1)} %get-tuple-element.38), channel_id=1, source_target_pairs={{0,224},{1,225},{2,226},{3,227},{4,228},{5,229},{6,230},{7,231},{8... | collective-permute-start | bytes 393224 | tf_op jit(solution)/shard_map/ppermute | solution.py:27
  54.5 0.1 copy.10.right_ref
  54.6 0.1 copy.9.left_ref
  54.6 0.5 collective-permute-done.4.n0
  55.2 2.3 %collective-permute-done.5.n1 = bf16[256,256]{1,0:T(8,128)(2,1)S(1)} collective-permute-done((bf16[256,256]{1,0:T(8,128)(2,1)S(1)}, bf16[256,256]{1,0:T(8,128)(2,1)S(1)}, u32[]{:S(2)}, u32[]{:S(2)}) %collective-permute-start.5) | collective-permute-done | bytes 131104 | tf_op jit(solution)/shard_map/ppermute | solution.py:27
  57.4 0.0 collective-permute-done.6.n2
  57.4 0.3 collective-permute-done.7.n3
  57.8 0.0 copy-done.4
  57.8 6.0 %join_sets.1 = bf16[8,256,128]{2,1,0:T(8,128)(2,1)S(1)} custom-call(bf16[20,1,1024]{2,1,0:T(2,128)(2,1)S(1)} %copy.9.left_ref, bf16[20,1,1024]{2,1,0:T(2,128)(2,1)S(1)} %copy.10.right_ref, bf16[256,256]{1,0:T(8,128)(2,1)S(1)} %copy-done.4, f32[256,256]{1,0:T(8,128)S(1)} %sum_own.1.own_ref, bf16[256,256]{1,0:T(8,128)(2,1)S(1)} %collective-permute-done.4.n0, ...), custom_call_target="tpu_custom_call" | custom-call | flops 5368709120 | bytes 524288 | tf_op jit(solution)/shard_map/join_sets/pallas_call | solution.py:242
  63.8 12.1 %all_to_all.16 = bf16[8,256,128]{2,1,0:T(8,128)(2,1)S(1)} all-to-all(bf16[8,256,128]{2,1,0:T(8,128)(2,1)S(1)} %join_sets.1), channel_id=1, replica_groups=mesh['blk'=32,'cset'=8] {'cset'}, dimensions={0} | all-to-all | bytes 1048576 | tf_op jit(solution)/shard_map/all_to_all | solution.py:297
  75.9 0.8 %copy.12 = bf16[2048,128]{1,0:T(8,128)(2,1)} copy(bf16[2048,128]{1,0:T(8,128)(2,1)S(1)} %bitcast.27) | data formatting | bytes 1048576
  (3 shorter events, 0.0 us)
Async XLA Ops:
  0.0 3.4 %copy-start.5 = (bf16[256,256]{1,0:T(8,128)(2,1)S(1)}, bf16[256,256]{1,0:T(8,128)(2,1)}, u32[]{:S(2)}) copy-start(bf16[256,256]{1,0:T(8,128)(2,1)} %param.9) | copy-start | bytes 393220
  3.4 17.2 %copy-start.6 = (s32[20,924]{1,0:T(8,128)S(1)}, s32[20,924]{1,0:T(8,128)}, u32[]{:S(2)}) copy-start(s32[20,924]{1,0:T(8,128)} %param.15) | copy-start | bytes 221764
  3.4 17.2 %copy-start.7 = (s32[20,924]{1,0:T(8,128)S(1)}, s32[20,924]{1,0:T(8,128)}, u32[]{:S(2)}) copy-start(s32[20,924]{1,0:T(8,128)} %param.14) | copy-start | bytes 221764
  4.5 20.4 %all-to-all-start = ((bf16[8,256,256]{2,1,0:T(8,128)(2,1)}), bf16[8,256,256]{2,1,0:T(8,128)(2,1)S(1)}, u32[]{:S(2)}, u32[]{:S(2)}) async-start(bf16[8,256,256]{2,1,0:T(8,128)(2,1)} %broadcast_in_dim.23), calls=%async_computation | async-start | bytes 2097152 | tf_op jit(solution)/shard_map/all_to_all | solution.py:279
  10.3 25.1 %collective-permute-start = (bf16[2064,128]{1,0:T(8,128)(2,1)}, bf16[2064,128]{1,0:T(8,128)(2,1)S(1)}, u32[]{:S(2)}, u32[]{:S(2)}) collective-permute-start(bf16[2064,128]{1,0:T(8,128)(2,1)} %get-tuple-element.31), channel_id=1, source_target_pairs={{0,244},{1,245},{2,246},{3,247},{4,240},{5,241},{6,242},{7,243},{8... | collective-permute-start | bytes 1585160 | tf_op jit(solution)/shard_map/ppermute | solution.py:27
  18.5 18.5 %collective-permute-start.1 = (bf16[2064,128]{1,0:T(8,128)(2,1)}, bf16[2064,128]{1,0:T(8,128)(2,1)S(1)}, u32[]{:S(2)}, u32[]{:S(2)}) collective-permute-start(bf16[2064,128]{1,0:T(8,128)(2,1)} %get-tuple-element.32), channel_id=1, source_target_pairs={{0,20},{1,21},{2,22},{3,23},{4,16},{5,17},{6,18},{7,19},{8,28},{9,... | collective-permute-start | bytes 1585160 | tf_op jit(solution)/shard_map/ppermute | solution.py:27
  18.5 22.4 %collective-permute-start.2 = (bf16[2064,128]{1,0:T(8,128)(2,1)}, bf16[2064,128]{1,0:T(8,128)(2,1)S(1)}, u32[]{:S(2)}, u32[]{:S(2)}) collective-permute-start(bf16[2064,128]{1,0:T(8,128)(2,1)} %get-tuple-element.33), channel_id=1, source_target_pairs={{0,224},{1,225},{2,226},{3,227},{4,228},{5,229},{6,230},{7,231},{8... | collective-permute-start | bytes 1585160 | tf_op jit(solution)/shard_map/ppermute | solution.py:27
  19.5 21.4 %collective-permute-start.3 = (bf16[2064,128]{1,0:T(8,128)(2,1)}, bf16[2064,128]{1,0:T(8,128)(2,1)S(1)}, u32[]{:S(2)}, u32[]{:S(2)}) collective-permute-start(bf16[2064,128]{1,0:T(8,128)(2,1)} %get-tuple-element.34), channel_id=1, source_target_pairs={{0,32},{1,33},{2,34},{3,35},{4,36},{5,37},{6,38},{7,39},{8,40},{9,... | collective-permute-start | bytes 1585160 | tf_op jit(solution)/shard_map/ppermute | solution.py:27
  25.0 5.6 %copy-start = (bf16[1,1,9,8,128,128]{5,4,3,2,1,0:T(8,128)(2,1)S(1)}, bf16[1,1,9,8,128,128]{5,4,3,2,1,0:T(8,128)(2,1)}, u32[]{:S(2)}) copy-start(bf16[1,1,9,8,128,128]{5,4,3,2,1,0:T(8,128)(2,1)} %param.10) | copy-start | bytes 7077892
  25.0 5.6 %copy-start.1 = (s32[1,1,9,8]{2,3,1,0:T(8,128)S(1)}, s32[1,1,9,8]{2,3,1,0:T(8,128)}, u32[]{:S(2)}) copy-start(s32[1,1,9,8]{2,3,1,0:T(8,128)} %param.11) | copy-start | bytes 868
  25.0 5.6 %copy-start.2 = (s32[1,1,9,8]{2,3,1,0:T(8,128)S(1)}, s32[1,1,9,8]{2,3,1,0:T(8,128)}, u32[]{:S(2)}) copy-start(s32[1,1,9,8]{2,3,1,0:T(8,128)} %param.12) | copy-start | bytes 868
  25.1 5.6 %copy-start.3 = (s32[1,1,9]{2,1,0:T(1,128)S(1)}, s32[1,1,9]{2,1,0:T(1,128)}, u32[]{:S(2)}) copy-start(s32[1,1,9]{2,1,0:T(1,128)} %param.13) | copy-start | bytes 112
  32.0 25.8 %copy-start.4 = (bf16[256,256]{1,0:T(8,128)(2,1)S(1)}, bf16[256,256]{1,0:T(8,128)(2,1)}, u32[]{:S(2)}) copy-start(bf16[256,256]{1,0:T(8,128)(2,1)} %active_ref.1) | copy-start | bytes 393220
  45.2 10.0 %collective-permute-start.4 = (bf16[256,256]{1,0:T(8,128)(2,1)S(1)}, bf16[256,256]{1,0:T(8,128)(2,1)S(1)}, u32[]{:S(2)}, u32[]{:S(2)}) collective-permute-start(bf16[256,256]{1,0:T(8,128)(2,1)S(1)} %get-tuple-element.35), channel_id=1, source_target_pairs={{0,20},{1,21},{2,22},{3,23},{4,16},{5,17},{6,18},{7,19},{8,28},{9,... | collective-permute-start | bytes 393224 | tf_op jit(solution)/shard_map/ppermute | solution.py:27
  51.3 6.2 %collective-permute-start.5 = (bf16[256,256]{1,0:T(8,128)(2,1)S(1)}, bf16[256,256]{1,0:T(8,128)(2,1)S(1)}, u32[]{:S(2)}, u32[]{:S(2)}) collective-permute-start(bf16[256,256]{1,0:T(8,128)(2,1)S(1)} %get-tuple-element.36), channel_id=1, source_target_pairs={{0,244},{1,245},{2,246},{3,247},{4,240},{5,241},{6,242},{7,243},{8... | collective-permute-start | bytes 393224 | tf_op jit(solution)/shard_map/ppermute | solution.py:27
  51.3 6.2 %collective-permute-start.6 = (bf16[256,256]{1,0:T(8,128)(2,1)S(1)}, bf16[256,256]{1,0:T(8,128)(2,1)S(1)}, u32[]{:S(2)}, u32[]{:S(2)}) collective-permute-start(bf16[256,256]{1,0:T(8,128)(2,1)S(1)} %get-tuple-element.37), channel_id=1, source_target_pairs={{0,32},{1,33},{2,34},{3,35},{4,36},{5,37},{6,38},{7,39},{8,40},{9,... | collective-permute-start | bytes 393224 | tf_op jit(solution)/shard_map/ppermute | solution.py:27
  52.8 5.0 %collective-permute-start.7 = (bf16[256,256]{1,0:T(8,128)(2,1)S(1)}, bf16[256,256]{1,0:T(8,128)(2,1)S(1)}, u32[]{:S(2)}, u32[]{:S(2)}) collective-permute-start(bf16[256,256]{1,0:T(8,128)(2,1)S(1)} %get-tuple-element.38), channel_id=1, source_target_pairs={{0,224},{1,225},{2,226},{3,227},{4,228},{5,229},{6,230},{7,231},{8... | collective-permute-start | bytes 393224 | tf_op jit(solution)/shard_map/ppermute | solution.py:27

commit v5 on v4

v5 whole, which is shorter than its diff:
```python
import jax
import jax.numpy as jnp
from jax import lax
from jax.experimental import pallas as pl
from jax.experimental.pallas import tpu as pltpu
from jax.sharding import PartitionSpec as P

SPLITS = 20
OUTPAD = 1024
TILE = 128
CHUNK = 512
SLOTS = 8
PAIR = 2 * SLOTS
TAIL = 16
REACH = 9
PART_TILES = 16
VMEM_LIMIT = 16 * 1024 * 1024


def routed(block, hops):
    nb, nc = lax.axis_size("blk"), lax.axis_size("cset")
    route = []
    for b in range(nb):
        chips = hops(b % 2)
        for c in range(nc):
            target = c ^ (nc // 2) if chips % 2 else c
            route.append((b * nc + c, ((b + 2 * chips) % nb) * nc + target))
    return lax.ppermute(block, ("blk", "cset"), route)


def places(slots, dst_ref, src_ref, count_ref):
    held, rows = [], []
    for slot, parity in slots:
        for t in range(SLOTS):
            held.append(src_ref[t, slot] + parity * PART_TILES)
            rows.append(jnp.where(t < count_ref[slot], dst_ref[t, slot], 2))
    return held, rows


def pair_slots(which, core):
    first = 2 * which - core
    return [(first, 0), (first + 1, 1)]


def message_slots(core):
    return [
        [(REACH - 1, core)],
        pair_slots(3, core),
        pair_slots(1, core),
        [(0, core)],
        [(1 + (REACH - 3) * core, 1 - core)],
    ]


HOPS = [
    lambda core: 2,
    lambda core: 1,
    lambda core: -1,
    lambda core: -2,
    lambda core: 4 * core - 2,
]
LENGTHS = [SLOTS, PAIR, PAIR, SLOTS, SLOTS]
BACK = [-2, -1, 1, 2]


def pack_kernel(at_ref, dst_ref, src_ref, count_ref, tiles_ref, *rest):
    outs, sems = rest[: len(HOPS)], rest[len(HOPS)]
    lane = lax.broadcasted_iota(jnp.int32, (TAIL, TILE), 1)
    line = lax.broadcasted_iota(jnp.int32, (TAIL, TILE), 0)
    slots = message_slots(at_ref[0])
    copies = []
    for n, length in enumerate(LENGTHS):
        begin = pl.multiple_of(slots[n][0][0] * (SLOTS * TILE), SLOTS * TILE)
        copies.append(
            pltpu.make_async_copy(
                tiles_ref.at[pl.ds(begin, length * TILE)],
                outs[n].at[pl.ds(0, length * TILE)],
                sems.at[n],
            )
        )
        copies[n].start()
    for n, length in enumerate(LENGTHS):
        held, rows = places(slots[n], dst_ref, src_ref, count_ref)
        tail = jnp.zeros((TAIL, TILE), jnp.int32)
        for t in range(length):
            tail = jnp.where(lane == t, jnp.where(line == 0, held[t], rows[t]), tail)
        outs[n][length * TILE : length * TILE + TAIL] = tail.astype(jnp.float32).astype(jnp.bfloat16)
    for copy in copies:
        copy.wait()


SMEM = pl.BlockSpec(memory_space=pltpu.SMEM)
VMEM = pl.BlockSpec(memory_space=pltpu.VMEM)
ANY = pl.BlockSpec(memory_space=pl.ANY)
HBM = pl.BlockSpec(memory_space=pltpu.HBM)


def in_space(space, *arrays):
    return [pltpu.with_memory_space_constraint(array, space) for array in arrays]


def pack_tiles(at, dst, src, count, tiles):
    return pl.pallas_call(
        pack_kernel,
        in_specs=[SMEM, SMEM, SMEM, SMEM, HBM],
        out_specs=[VMEM] * len(LENGTHS),
        out_shape=[pltpu.VMEM((length * TILE + TAIL, TILE), jnp.bfloat16) for length in LENGTHS],
        scratch_shapes=[pltpu.SemaphoreType.DMA((len(LENGTHS),))],
        compiler_params=pltpu.CompilerParams(vmem_limit_bytes=VMEM_LIMIT),
        name="pack_tiles",
    )(at, *in_space(pltpu.HBM, dst, src, count, tiles))


def products(held, rows, tiles, sources):
    total = None
    for t in range(0, PAIR, 2):
        sides, chosen = [], []
        for n in (t, t + 1):
            tile = tiles(n)
            empty = jnp.zeros_like(tile)
            sides.append(
                jnp.concatenate(
                    [jnp.where(rows[n] == 0, tile, empty), jnp.where(rows[n] == 1, tile, empty)], axis=0
                )
            )
            chosen.append(sources[pl.ds(pl.multiple_of(held[n] * TILE, TILE), TILE)])
        product = jnp.dot(
            jnp.concatenate(sides, axis=1),
            jnp.concatenate(chosen, axis=0),
            preferred_element_type=jnp.float32,
        )
        total = product if total is None else total + product
    return total


def sum_away_kernel(at_ref, sources, *rest):
    count = len(LENGTHS)
    messages, outs = rest[:count], rest[count : count + len(BACK)]
    tail, tail_s, sem = rest[count + len(BACK) :]
    core = at_ref[0]
    for n, length in enumerate(LENGTHS):
        end = messages[n][length * TILE : length * TILE + TAIL]
        tail[n] = end.astype(jnp.float32).astype(jnp.int32)
    copy = pltpu.make_async_copy(tail, tail_s, sem)
    copy.start()
    copy.wait()

    def part(n, keep=None):
        held = [tail_s[n, 0, t] for t in range(LENGTHS[n])]
        rows = [tail_s[n, 1, t] for t in range(LENGTHS[n])]
        if keep is not None:
            rows = [jnp.where(keep, row, 2) for row in rows]
        return [
            (held[t], rows[t], messages[n].at[t * TILE : (t + 1) * TILE]) for t in range(LENGTHS[n])
        ]

    odd_below, odd_above = part(4, core == 1), part(4, core == 0)
    for out, tiles in zip(outs, (part(0) + odd_below, part(1), part(2), part(3) + odd_above)):
        held, rows, refs = zip(*tiles)
        out[...] = products(held, rows, lambda n: refs[n][...], sources).astype(jnp.bfloat16)


def sum_away(at, sources, messages):
    rows, channels = sources.shape
    return pl.pallas_call(
        sum_away_kernel,
        in_specs=[SMEM] + [VMEM] * (1 + len(messages)),
        out_specs=[VMEM] * len(BACK),
        out_shape=[pltpu.VMEM((2 * TILE, channels), jnp.bfloat16)] * len(BACK),
        scratch_shapes=[
            pltpu.VMEM((len(messages), TAIL, TILE), jnp.int32),
            pltpu.SMEM((len(messages), TAIL, TILE), jnp.int32),
            pltpu.SemaphoreType.DMA,
        ],
        compiler_params=pltpu.CompilerParams(vmem_limit_bytes=VMEM_LIMIT),
        cost_estimate=pl.CostEstimate(
            flops=len(BACK) * 4 * TILE * TILE * PAIR * channels,
            bytes_accessed=2 * (rows * channels + len(BACK) * PAIR * TILE * TILE),
            transcendentals=0,
        ),
        name="sum_away",
    )(at, *in_space(pltpu.VMEM, sources, *messages))


def sum_own_kernel(at_ref, dst_ref, src_ref, count_ref, sources_ref, tiles_ref, out_ref, *rest):
    tiles, sem = rest
    slots = pair_slots(2, at_ref[0])
    held, placed = places(slots, dst_ref, src_ref, count_ref)
    begin = pl.multiple_of(slots[0][0] * (SLOTS * TILE), SLOTS * TILE)
    copy = pltpu.make_async_copy(tiles_ref.at[pl.ds(begin, PAIR * TILE)], tiles, sem)
    copy.start()
    copy.wait()
    out_ref[...] = products(held, placed, lambda n: tiles[n * TILE : (n + 1) * TILE], sources_ref)


def sum_own(at, dst, src, count, sources, tiles):
    rows, channels = sources.shape
    return pl.pallas_call(
        sum_own_kernel,
        in_specs=[SMEM] * 4 + [VMEM] + [HBM],
        out_specs=VMEM,
        out_shape=jax.ShapeDtypeStruct((2 * TILE, channels), jnp.float32),
        scratch_shapes=[
            pltpu.VMEM((PAIR * TILE, TILE), jnp.bfloat16),
            pltpu.SemaphoreType.DMA,
        ],
        compiler_params=pltpu.CompilerParams(vmem_limit_bytes=VMEM_LIMIT),
        cost_estimate=pl.CostEstimate(
            flops=4 * TILE * TILE * PAIR * channels,
            bytes_accessed=2 * (rows * channels + PAIR * TILE * TILE),
            transcendentals=0,
        ),
        name="sum_own",
    )(
        at,
        *in_space(pltpu.HBM, dst, src, count),
        *in_space(pltpu.VMEM, sources),
        *in_space(pltpu.HBM, tiles),
    )


def join_kernel(left_ref, right_ref, active_ref, own_ref, n0, n1, n2, n3, out_ref):
    total = own_ref[...]
    for part in (n0, n1, n2, n3):
        total = total + part[...].astype(jnp.float32)
    neighbour = total.astype(jnp.bfloat16)
    active = active_ref[...]
    shape = (active.shape[1], left_ref.shape[2])
    channel = lax.broadcasted_iota(jnp.int32, shape, 0).astype(jnp.float32).astype(jnp.bfloat16)
    one, zero = jnp.ones(shape, jnp.bfloat16), jnp.zeros(shape, jnp.bfloat16)
    joined = jnp.zeros((active.shape[0], shape[1]), jnp.float32)
    for j in range(SPLITS):
        left = jnp.where(channel == left_ref[j], one, zero)
        right = jnp.where(channel == right_ref[j], one, zero)
        joined = joined + jnp.dot(active, left, preferred_element_type=jnp.float32) * jnp.dot(
            neighbour, right, preferred_element_type=jnp.float32
        )
    for piece in range(shape[1] // TILE):
        out_ref[piece] = joined[:, piece * TILE : (piece + 1) * TILE].astype(out_ref.dtype)


def join(active, own, parts, left, right):
    rows, channels = own.shape
    splits, _, width = left.shape
    whole = pl.BlockSpec((rows, channels), lambda q: (0, 0))
    columns = pl.BlockSpec((splits, 1, CHUNK), lambda q: (0, 0, q))
    return pl.pallas_call(
        join_kernel,
        grid=(width // CHUNK,),
        in_specs=[columns] * 2 + [whole] * 6,
        out_specs=pl.BlockSpec((CHUNK // TILE, rows, TILE), lambda q: (q, 0, 0)),
        out_shape=jax.ShapeDtypeStruct((width // TILE, rows, TILE), jnp.bfloat16),
        compiler_params=pltpu.CompilerParams(vmem_limit_bytes=VMEM_LIMIT),
        cost_estimate=pl.CostEstimate(
            flops=4 * splits * rows * channels * width,
            bytes_accessed=2 * rows * width,
            transcendentals=0,
        ),
        name="join_sets",
    )(left, right, active, own, *parts)


def local(
    active_table,
    passive_table,
    adjacency,
    tile_dst,
    tile_src,
    tile_count,
    split_active,
    split_passive,
):
    tiles_all = adjacency.reshape(-1, TILE)
    dst, src, count = tile_dst[0, 0].T, tile_src[0, 0].T, tile_count[0, 0]
    nc = lax.axis_size("cset")
    at = (lax.axis_index("blk") % 2).astype(jnp.int32)[None]

    messages = pack_tiles(at, dst, src, count, tiles_all)
    *messages, passive_table = lax.optimization_barrier((*messages, passive_table))
    messages = [routed(message, hops) for message, hops in zip(messages, HOPS)]
    copies = jnp.broadcast_to(passive_table[None], (nc,) + passive_table.shape)
    own_rows = lax.all_to_all(copies, "cset", split_axis=0, concat_axis=0, tiled=True)
    own_rows = own_rows.reshape(-1, passive_table.shape[1])
    groups = [[b, b + 1] for b in range(0, lax.axis_size("blk"), 2)]
    twice = jnp.broadcast_to(own_rows[None], (2,) + own_rows.shape)
    sources = lax.all_to_all(
        twice, "blk", split_axis=0, concat_axis=0, tiled=True, axis_index_groups=groups
    ).reshape(-1, own_rows.shape[1])

    extra = OUTPAD - split_active.shape[1]
    left, right = (
        jnp.pad(cols.astype(jnp.bfloat16), ((0, 0), (0, extra)), constant_values=-1)[:, None, :]
        for cols in (split_active, split_passive)
    )
    own = sum_own(at, dst, src, count, sources, tiles_all)
    sources, own, left, right = lax.optimization_barrier((sources, own, left, right))
    parts = sum_away(at, sources, messages)
    parts = [routed(part, lambda core, chips=chips: chips) for part, chips in zip(parts, BACK)]
    joined = join(active_table, own, parts, left, right)
    spread = lax.all_to_all(joined, "cset", split_axis=0, concat_axis=0, tiled=True)
    return spread.reshape(-1, TILE)


def solution(mesh):
    in_specs = (
        P(("blk", "cset"), None),
        P(("blk", "cset"), None),
        P("blk", "cset", None, None, None, None),
        P("blk", "cset", None, None),
        P("blk", "cset", None, None),
        P("blk", "cset", None),
        P(),
        P(),
    )
    out_specs = P("blk", "cset")
    return jax.shard_map(local, mesh=mesh, in_specs=in_specs, out_specs=out_specs, check_vma=False)
```

time: 78.2 us -> 75.8 us (0.969)
  waiting for transfers between devices: 16.3 us -> 13.4 us
  local copies, waits for them, and re-layouts: 2.18 us -> 3.37 us
  other arithmetic: 0.02 us -> 0.91 us
  Pallas kernels: 15 us -> 14.2 us
    all_to_all x1, waiting for transfers between devices: 4.25 us -> 1.69 us  [local(): lax.all_to_all(copies, 'cset', split_axis=0, concat_axis=0, tiled=True)]
    broadcast_in_dim x1, local copies, waits for them, and re-layouts: 0.14 us -> 1.36 us  [local(): twice = jnp.broadcast_to(own_rows[None], (2,) + own_rows.shape)]
    pallas_call x1, Pallas kernels: 3.39 us -> 2.4 us  [pack_tiles(): pl.pallas_call(pack_kernel, in_specs=[SMEM, SMEM, SMEM, SMEM, HBM], out_s...]
    convert_element_type x2, other arithmetic: 0.02 us -> 0.91 us  [local(): cols.astype(jnp.bfloat16)]
    ppermute x8 -> x9, starting transfers between devices: 19.5 us -> 19.1 us  [routed(): return lax.ppermute(block, ('blk', 'cset'), route)]
    ppermute x8 -> x9, waiting for transfers between devices: 12.1 us -> 11.7 us  [routed(): return lax.ppermute(block, ('blk', 'cset'), route)]
  transfers between devices with their start and end apart: 9 -> 10, of which waited for: 7 -> 7; matrix products, arithmetic and copies ran while one was open for 0% -> 3% of each run, Pallas kernels for 2% -> 3%
where the time goes in v5:
time: 75.8 us; the launch traced here: 75.1 us
  starting transfers between devices  25.5 us (34%)
  blocking collectives  17.5 us (23%)
  Pallas kernels  14.2 us (19%)
  waiting for transfers between devices  13.4 us (18%)
  local copies, waits for them, and re-layouts  3.37 us (4%)
  other arithmetic  0.91 us (1%)
    ppermute x9, starting transfers between devices, routed(): return lax.ppermute(block, ('blk', 'cset'), route)  19.1 us
    all_to_all x1, blocking collectives, local(): lax.all_to_all(joined, 'cset', split_axis=0, concat_axis=0, tiled=True)  12.1 us
    ppermute x9, waiting for transfers between devices, routed(): return lax.ppermute(block, ('blk', 'cset'), route)  11.7 us
    all_to_all x1, starting transfers between devices, local(): lax.all_to_all(copies, 'cset', split_axis=0, concat_axis=0, tiled=True)  6.39 us
    pallas_call x1, Pallas kernels, join(): pl.pallas_call(join_kernel, grid=(width // CHUNK,), in_specs=[columns] *...  6.02 us
    all_to_all x1, blocking collectives, local(): lax.all_to_all(twice, 'blk', split_axis=0, concat_axis=0, tiled=True, axi...  5.42 us
    pallas_call x1, Pallas kernels, sum_away(): pl.pallas_call(sum_away_kernel, in_specs=[SMEM] + [VMEM] * (1 + len(messa...  3.48 us
    pallas_call x1, Pallas kernels, pack_tiles(): pl.pallas_call(pack_kernel, in_specs=[SMEM, SMEM, SMEM, SMEM, HBM], out_s...  2.4 us
  transfers between devices with their start and end apart: 10, of which 7 were waited for; matrix products, arithmetic and copies ran while one was open for 3% of the time, Pallas kernels for 3%

profile of v5, /device:TPU:2, one launch (start us, length us, event | category | flops | bytes accessed | tf_op | source)
XLA Modules:
  0.0 75.1 jit_solution(7429557678340974527)
XLA Ops:
  0.0 0.0 copy-start.1
  0.0 2.4 %pack_tiles.1 = (bf16[1040,128]{1,0:T(8,128)(2,1)S(1)}, bf16[2064,128]{1,0:T(8,128)(2,1)S(1)}, bf16[2064,128]{1,0:T(8,128)(2,1)S(1)}, bf16[1040,128]{1,0:T(8,128)(2,1)S(1)}, bf16[1040,128]{1,0:T(8,128)(2,1)S(1)}) custom-call(s32[1]{0:T(128)} %bitcast.at_ref, s32[8,9]{1,0:T(8,128)} %bitcast.21, s32[8,9]{1,0:T(8,128)} %bitcast.23, s32[9]{0:T(128)} %bitcast.25, ...), custom_call_target="tpu_custom_call" | custom-call | tf_op jit(solution)/shard_map/pack_tiles/pallas_call | solution.py:103
  2.4 0.0 copy-start.2
  2.4 0.0 copy-done.1
  2.4 1.1 %broadcast_in_dim.23 = bf16[8,256,256]{2,1,0:T(8,128)(2,1)} broadcast(bf16[256,256]{1,0:T(8,128)(2,1)S(1)} %copy-done.1), dimensions={1,2} | broadcast | bytes 1179648 | tf_op jit(solution)/shard_map/broadcast_in_dim | solution.py:281
  3.5 6.4 %all-to-all-start = ((bf16[8,256,256]{2,1,0:T(8,128)(2,1)}), bf16[8,256,256]{2,1,0:T(8,128)(2,1)}, u32[]{:S(2)}, u32[]{:S(2)}) async-start(bf16[8,256,256]{2,1,0:T(8,128)(2,1)} %broadcast_in_dim.23), calls=%async_computation | async-start | bytes 2097152 | tf_op jit(solution)/shard_map/all_to_all | solution.py:282
  9.9 2.4 %collective-permute-start.1 = (bf16[2064,128]{1,0:T(8,128)(2,1)S(1)}, bf16[2064,128]{1,0:T(8,128)(2,1)S(1)}, u32[]{:S(2)}, u32[]{:S(2)}) collective-permute-start(bf16[2064,128]{1,0:T(8,128)(2,1)S(1)} %get-tuple-element.35), channel_id=1, source_target_pairs={{0,20},{1,21},{2,22},{3,23},{4,16},{5,17},{6,18},{7,19},{8,28},{9,... | collective-permute-start | bytes 1585160 | tf_op jit(solution)/shard_map/ppermute | solution.py:28
  12.2 5.3 %collective-permute-start.2 = (bf16[2064,128]{1,0:T(8,128)(2,1)S(1)}, bf16[2064,128]{1,0:T(8,128)(2,1)S(1)}, u32[]{:S(2)}, u32[]{:S(2)}) collective-permute-start(bf16[2064,128]{1,0:T(8,128)(2,1)S(1)} %get-tuple-element.36), channel_id=1, source_target_pairs={{0,244},{1,245},{2,246},{3,247},{4,240},{5,241},{6,242},{7,243},{8... | collective-permute-start | bytes 1585160 | tf_op jit(solution)/shard_map/ppermute | solution.py:28
  17.5 0.0 collective-permute-start
  17.5 3.2 %collective-permute-start.3 = (bf16[1040,128]{1,0:T(8,128)(2,1)S(1)}, bf16[1040,128]{1,0:T(8,128)(2,1)S(1)}, u32[]{:S(2)}, u32[]{:S(2)}) collective-permute-start(bf16[1040,128]{1,0:T(8,128)(2,1)S(1)} %get-tuple-element.37), channel_id=1, source_target_pairs={{0,224},{1,225},{2,226},{3,227},{4,228},{5,229},{6,230},{7,231},{8... | collective-permute-start | bytes 798728 | tf_op jit(solution)/shard_map/ppermute | solution.py:28
  20.8 0.6 collective-permute-start.4
  21.4 0.0 copy-done.2
  21.4 0.9 %convert_element_type.9 = bf16[20,924]{1,0:T(8,128)(2,1)S(1)} convert(s32[20,924]{1,0:T(8,128)} %param.14) | non-fusion elementwise | flops 18480 | bytes 110880 | tf_op jit(solution)/shard_map/convert_element_type | solution.py:292
  22.3 1.7 %all-to-all-done = bf16[8,256,256]{2,1,0:T(8,128)(2,1)} async-done(((bf16[8,256,256]{2,1,0:T(8,128)(2,1)}), bf16[8,256,256]{2,1,0:T(8,128)(2,1)}, u32[]{:S(2)}, u32[]{:S(2)}) %all-to-all-start) | async-done | bytes 1048608 | tf_op jit(solution)/shard_map/all_to_all | solution.py:282
  24.0 1.4 %broadcast_in_dim.25 = bf16[2,2048,256]{2,1,0:T(8,128)(2,1)S(1)} broadcast(bf16[2048,256]{1,0:T(8,128)(2,1)} %bitcast.7), dimensions={1,2} | broadcast | bytes 3145728 | tf_op jit(solution)/shard_map/broadcast_in_dim | solution.py:285
  25.3 5.4 %all_to_all.15 = bf16[2,2048,256]{2,1,0:T(8,128)(2,1)S(1)} all-to-all(bf16[2,2048,256]{2,1,0:T(8,128)(2,1)S(1)} %broadcast_in_dim.25), channel_id=1, replica_groups={{0,8},{16,24},{32,40},{48,56},{64,72},{80,88},{96,104},{112,120},{128,1..., dimensions={0} | all-to-all | bytes 4194304 | tf_op jit(solution)/shard_map/all_to_all | solution.py:286
  30.8 2.3 %sum_own.1.own_ref = f32[256,256]{1,0:T(8,128)S(1)} custom-call(s32[1]{0:T(128)} %bitcast.at_ref, s32[8,9]{1,0:T(8,128)} %bitcast.22, s32[8,9]{1,0:T(8,128)} %bitcast.24, s32[9]{0:T(128)} %bitcast.26, bf16[4096,256]{1,0:T(8,128)(2,1)S(1)} %bitcast.16, bf16[9216,128]{1,0:T(8,128)(2,1)} %bitcast.19), custom_call_target="tpu_custom_call" | custom-call | flops 268435456 | bytes 2621440 | tf_op jit(solution)/shard_map/sum_own/pallas_call | solution.py:198
  33.1 0.0 copy-start
  33.1 0.0 collective-permute-done.rest_0_
  33.1 0.9 %collective-permute-done.3.rest_3_ = bf16[1040,128]{1,0:T(8,128)(2,1)S(1)} collective-permute-done((bf16[1040,128]{1,0:T(8,128)(2,1)S(1)}, bf16[1040,128]{1,0:T(8,128)(2,1)S(1)}, u32[]{:S(2)}, u32[]{:S(2)}) %collective-permute-start.3) | collective-permute-done | bytes 266272 | tf_op jit(solution)/shard_map/ppermute | solution.py:28
  34.0 2.9 %collective-permute-done.4.rest_4_ = bf16[1040,128]{1,0:T(8,128)(2,1)} collective-permute-done((bf16[1040,128]{1,0:T(8,128)(2,1)S(1)}, bf16[1040,128]{1,0:T(8,128)(2,1)}, u32[]{:S(2)}, u32[]{:S(2)}) %collective-permute-start.4) | collective-permute-done | bytes 266272 | tf_op jit(solution)/shard_map/ppermute | solution.py:28
  36.8 0.0 collective-permute-done.1.rest_1_
  36.9 0.8 %collective-permute-done.2.rest_2_ = bf16[2064,128]{1,0:T(8,128)(2,1)S(1)} collective-permute-done((bf16[2064,128]{1,0:T(8,128)(2,1)S(1)}, bf16[2064,128]{1,0:T(8,128)(2,1)S(1)}, u32[]{:S(2)}, u32[]{:S(2)}) %collective-permute-start.2) | collective-permute-done | bytes 528416 | tf_op jit(solution)/shard_map/ppermute | solution.py:28
  37.7 3.5 %sum_away.1 = (bf16[256,256]{1,0:T(8,128)(2,1)S(1)}, bf16[256,256]{1,0:T(8,128)(2,1)S(1)}, bf16[256,256]{1,0:T(8,128)(2,1)S(1)}, bf16[256,256]{1,0:T(8,128)(2,1)S(1)}) custom-call(s32[1]{0:T(128)} %bitcast.at_ref, bf16[4096,256]{1,0:T(8,128)(2,1)S(1)} %bitcast.17, bf16[1040,128]{1,0:T(8,128)(2,1)S(1)} %collective-permute-done.rest_0_, ...), custom_call_target="tpu_custom_call" | custom-call | flops 1073741824 | bytes 4194304 | tf_op jit(solution)/shard_map/sum_away/pallas_call | solution.py:165
  41.2 4.2 %collective-permute-start.5 = (bf16[256,256]{1,0:T(8,128)(2,1)S(1)}, bf16[256,256]{1,0:T(8,128)(2,1)S(1)}, u32[]{:S(2)}, u32[]{:S(2)}) collective-permute-start(bf16[256,256]{1,0:T(8,128)(2,1)S(1)} %get-tuple-element.39), channel_id=1, source_target_pairs={{0,224},{1,225},{2,226},{3,227},{4,228},{5,229},{6,230},{7,231},{8... | collective-permute-start | bytes 393224 | tf_op jit(solution)/shard_map/ppermute | solution.py:28
  45.4 2.5 %collective-permute-start.6 = (bf16[256,256]{1,0:T(8,128)(2,1)S(1)}, bf16[256,256]{1,0:T(8,128)(2,1)S(1)}, u32[]{:S(2)}, u32[]{:S(2)}) collective-permute-start(bf16[256,256]{1,0:T(8,128)(2,1)S(1)} %get-tuple-element.40), channel_id=1, source_target_pairs={{0,244},{1,245},{2,246},{3,247},{4,240},{5,241},{6,242},{7,243},{8... | collective-permute-start | bytes 393224 | tf_op jit(solution)/shard_map/ppermute | solution.py:28
  47.8 0.8 %collective-permute-start.7 = (bf16[256,256]{1,0:T(8,128)(2,1)S(1)}, bf16[256,256]{1,0:T(8,128)(2,1)S(1)}, u32[]{:S(2)}, u32[]{:S(2)}) collective-permute-start(bf16[256,256]{1,0:T(8,128)(2,1)S(1)} %get-tuple-element.41), channel_id=1, source_target_pairs={{0,20},{1,21},{2,22},{3,23},{4,16},{5,17},{6,18},{7,19},{8,28},{9,... | collective-permute-start | bytes 393224 | tf_op jit(solution)/shard_map/ppermute | solution.py:28
  48.6 0.2 collective-permute-start.8
  48.9 0.1 copy.10.right_ref
  48.9 0.1 copy.9.left_ref
  49.0 0.3 collective-permute-done.5.n0
  49.3 2.5 %collective-permute-done.6.n1 = bf16[256,256]{1,0:T(8,128)(2,1)S(1)} collective-permute-done((bf16[256,256]{1,0:T(8,128)(2,1)S(1)}, bf16[256,256]{1,0:T(8,128)(2,1)S(1)}, u32[]{:S(2)}, u32[]{:S(2)}) %collective-permute-start.6) | collective-permute-done | bytes 131104 | tf_op jit(solution)/shard_map/ppermute | solution.py:28
  51.7 4.4 %collective-permute-done.7.n2 = bf16[256,256]{1,0:T(8,128)(2,1)S(1)} collective-permute-done((bf16[256,256]{1,0:T(8,128)(2,1)S(1)}, bf16[256,256]{1,0:T(8,128)(2,1)S(1)}, u32[]{:S(2)}, u32[]{:S(2)}) %collective-permute-start.7) | collective-permute-done | bytes 131104 | tf_op jit(solution)/shard_map/ppermute | solution.py:28
  56.1 0.0 collective-permute-done.8.n3
  56.1 0.0 copy-done
  56.1 6.0 %join_sets.1 = bf16[8,256,128]{2,1,0:T(8,128)(2,1)S(1)} custom-call(bf16[20,1,1024]{2,1,0:T(2,128)(2,1)S(1)} %copy.9.left_ref, bf16[20,1,1024]{2,1,0:T(2,128)(2,1)S(1)} %copy.10.right_ref, bf16[256,256]{1,0:T(8,128)(2,1)S(1)} %copy-done, f32[256,256]{1,0:T(8,128)S(1)} %sum_own.1.own_ref, bf16[256,256]{1,0:T(8,128)(2,1)S(1)} %collective-permute-done.5.n0, ...), custom_call_target="tpu_custom_call" | custom-call | flops 5368709120 | bytes 524288 | tf_op jit(solution)/shard_map/join_sets/pallas_call | solution.py:247
  62.2 12.1 %all_to_all.16 = bf16[8,256,128]{2,1,0:T(8,128)(2,1)S(1)} all-to-all(bf16[8,256,128]{2,1,0:T(8,128)(2,1)S(1)} %join_sets.1), channel_id=1, replica_groups=mesh['blk'=32,'cset'=8] {'cset'}, dimensions={0} | all-to-all | bytes 1048576 | tf_op jit(solution)/shard_map/all_to_all | solution.py:300
  74.3 0.8 %copy.12 = bf16[2048,128]{1,0:T(8,128)(2,1)} copy(bf16[2048,128]{1,0:T(8,128)(2,1)S(1)} %bitcast.20) | data formatting | bytes 1048576
  (2 shorter events, 0.0 us)
Async XLA Ops:
  0.0 2.4 %copy-start.1 = (bf16[256,256]{1,0:T(8,128)(2,1)S(1)}, bf16[256,256]{1,0:T(8,128)(2,1)}, u32[]{:S(2)}) copy-start(bf16[256,256]{1,0:T(8,128)(2,1)} %param.9) | copy-start | bytes 393220
  2.4 18.9 %copy-start.2 = (s32[20,924]{1,0:T(8,128)S(1)}, s32[20,924]{1,0:T(8,128)}, u32[]{:S(2)}) copy-start(s32[20,924]{1,0:T(8,128)} %param.15) | copy-start | bytes 221764
  3.5 20.5 %all-to-all-start = ((bf16[8,256,256]{2,1,0:T(8,128)(2,1)}), bf16[8,256,256]{2,1,0:T(8,128)(2,1)}, u32[]{:S(2)}, u32[]{:S(2)}) async-start(bf16[8,256,256]{2,1,0:T(8,128)(2,1)} %broadcast_in_dim.23), calls=%async_computation | async-start | bytes 2097152 | tf_op jit(solution)/shard_map/all_to_all | solution.py:282
  9.9 27.0 %collective-permute-start.1 = (bf16[2064,128]{1,0:T(8,128)(2,1)S(1)}, bf16[2064,128]{1,0:T(8,128)(2,1)S(1)}, u32[]{:S(2)}, u32[]{:S(2)}) collective-permute-start(bf16[2064,128]{1,0:T(8,128)(2,1)S(1)} %get-tuple-element.35), channel_id=1, source_target_pairs={{0,20},{1,21},{2,22},{3,23},{4,16},{5,17},{6,18},{7,19},{8,28},{9,... | collective-permute-start | bytes 1585160 | tf_op jit(solution)/shard_map/ppermute | solution.py:28
  12.2 25.4 %collective-permute-start.2 = (bf16[2064,128]{1,0:T(8,128)(2,1)S(1)}, bf16[2064,128]{1,0:T(8,128)(2,1)S(1)}, u32[]{:S(2)}, u32[]{:S(2)}) collective-permute-start(bf16[2064,128]{1,0:T(8,128)(2,1)S(1)} %get-tuple-element.36), channel_id=1, source_target_pairs={{0,244},{1,245},{2,246},{3,247},{4,240},{5,241},{6,242},{7,243},{8... | collective-permute-start | bytes 1585160 | tf_op jit(solution)/shard_map/ppermute | solution.py:28
  17.5 15.6 %collective-permute-start = (bf16[1040,128]{1,0:T(8,128)(2,1)S(1)}, bf16[1040,128]{1,0:T(8,128)(2,1)S(1)}, u32[]{:S(2)}, u32[]{:S(2)}) collective-permute-start(bf16[1040,128]{1,0:T(8,128)(2,1)S(1)} %get-tuple-element.34), channel_id=1, source_target_pairs={{0,32},{1,33},{2,34},{3,35},{4,36},{5,37},{6,38},{7,39},{8,40},{9,... | collective-permute-start | bytes 798728 | tf_op jit(solution)/shard_map/ppermute | solution.py:28
  17.5 16.5 %collective-permute-start.3 = (bf16[1040,128]{1,0:T(8,128)(2,1)S(1)}, bf16[1040,128]{1,0:T(8,128)(2,1)S(1)}, u32[]{:S(2)}, u32[]{:S(2)}) collective-permute-start(bf16[1040,128]{1,0:T(8,128)(2,1)S(1)} %get-tuple-element.37), channel_id=1, source_target_pairs={{0,224},{1,225},{2,226},{3,227},{4,228},{5,229},{6,230},{7,231},{8... | collective-permute-start | bytes 798728 | tf_op jit(solution)/shard_map/ppermute | solution.py:28
  20.8 16.1 %collective-permute-start.4 = (bf16[1040,128]{1,0:T(8,128)(2,1)S(1)}, bf16[1040,128]{1,0:T(8,128)(2,1)}, u32[]{:S(2)}, u32[]{:S(2)}) collective-permute-start(bf16[1040,128]{1,0:T(8,128)(2,1)S(1)} %get-tuple-element.38), channel_id=1, source_target_pairs={{0,224},{1,225},{2,226},{3,227},{4,228},{5,229},{6,230},{7,231},{8... | collective-permute-start | bytes 798728 | tf_op jit(solution)/shard_map/ppermute | solution.py:28
  33.1 23.0 %copy-start = (bf16[256,256]{1,0:T(8,128)(2,1)S(1)}, bf16[256,256]{1,0:T(8,128)(2,1)}, u32[]{:S(2)}) copy-start(bf16[256,256]{1,0:T(8,128)(2,1)} %active_ref.1) | copy-start | bytes 393220
  41.2 8.1 %collective-permute-start.5 = (bf16[256,256]{1,0:T(8,128)(2,1)S(1)}, bf16[256,256]{1,0:T(8,128)(2,1)S(1)}, u32[]{:S(2)}, u32[]{:S(2)}) collective-permute-start(bf16[256,256]{1,0:T(8,128)(2,1)S(1)} %get-tuple-element.39), channel_id=1, source_target_pairs={{0,224},{1,225},{2,226},{3,227},{4,228},{5,229},{6,230},{7,231},{8... | collective-permute-start | bytes 393224 | tf_op jit(solution)/shard_map/ppermute | solution.py:28
  45.4 6.3 %collective-permute-start.6 = (bf16[256,256]{1,0:T(8,128)(2,1)S(1)}, bf16[256,256]{1,0:T(8,128)(2,1)S(1)}, u32[]{:S(2)}, u32[]{:S(2)}) collective-permute-start(bf16[256,256]{1,0:T(8,128)(2,1)S(1)} %get-tuple-element.40), channel_id=1, source_target_pairs={{0,244},{1,245},{2,246},{3,247},{4,240},{5,241},{6,242},{7,243},{8... | collective-permute-start | bytes 393224 | tf_op jit(solution)/shard_map/ppermute | solution.py:28
  47.8 8.3 %collective-permute-start.7 = (bf16[256,256]{1,0:T(8,128)(2,1)S(1)}, bf16[256,256]{1,0:T(8,128)(2,1)S(1)}, u32[]{:S(2)}, u32[]{:S(2)}) collective-permute-start(bf16[256,256]{1,0:T(8,128)(2,1)S(1)} %get-tuple-element.41), channel_id=1, source_target_pairs={{0,20},{1,21},{2,22},{3,23},{4,16},{5,17},{6,18},{7,19},{8,28},{9,... | collective-permute-start | bytes 393224 | tf_op jit(solution)/shard_map/ppermute | solution.py:28
  48.6 7.5 %collective-permute-start.8 = (bf16[256,256]{1,0:T(8,128)(2,1)S(1)}, bf16[256,256]{1,0:T(8,128)(2,1)S(1)}, u32[]{:S(2)}, u32[]{:S(2)}) collective-permute-start(bf16[256,256]{1,0:T(8,128)(2,1)S(1)} %get-tuple-element.42), channel_id=1, source_target_pairs={{0,32},{1,33},{2,34},{3,35},{4,36},{5,37},{6,38},{7,39},{8,40},{9,... | collective-permute-start | bytes 393224 | tf_op jit(solution)/shard_map/ppermute | solution.py:28

commit v6 on v5

--- a/solution.py
+++ b/solution.py
@@ -60,11 +60,10 @@
     lambda core: 4 * core - 2,
 ]
 LENGTHS = [SLOTS, PAIR, PAIR, SLOTS, SLOTS]
-BACK = [-2, -1, 1, 2]
-
-
-def pack_kernel(at_ref, dst_ref, src_ref, count_ref, tiles_ref, *rest):
-    outs, sems = rest[: len(HOPS)], rest[len(HOPS)]
+
+
+def pack_kernel(at_ref, dst_ref, src_ref, count_ref, tiles_ref, rows_ref, *rest):
+    outs, (repeated, sems) = rest[: len(HOPS)], rest[len(HOPS) :]
     lane = lax.broadcasted_iota(jnp.int32, (TAIL, TILE), 1)
     line = lax.broadcasted_iota(jnp.int32, (TAIL, TILE), 0)
     slots = message_slots(at_ref[0])
@@ -78,7 +77,10 @@
                 sems.at[n],
             )
         )
-        copies[n].start()
+    for n in range(repeated.shape[0]):
+        copies.append(pltpu.make_async_copy(rows_ref, repeated.at[n], sems.at[len(HOPS) + n]))
+    for copy in copies:
+        copy.start()
     for n, length in enumerate(LENGTHS):
         held, rows = places(slots[n], dst_ref, src_ref, count_ref)
         tail = jnp.zeros((TAIL, TILE), jnp.int32)
@@ -99,16 +101,17 @@
     return [pltpu.with_memory_space_constraint(array, space) for array in arrays]
 
 
-def pack_tiles(at, dst, src, count, tiles):
+def pack_tiles(at, dst, src, count, tiles, rows, times):
     return pl.pallas_call(
         pack_kernel,
-        in_specs=[SMEM, SMEM, SMEM, SMEM, HBM],
-        out_specs=[VMEM] * len(LENGTHS),
-        out_shape=[pltpu.VMEM((length * TILE + TAIL, TILE), jnp.bfloat16) for length in LENGTHS],
-        scratch_shapes=[pltpu.SemaphoreType.DMA((len(LENGTHS),))],
+        in_specs=[SMEM, SMEM, SMEM, SMEM, HBM, HBM],
+        out_specs=[VMEM] * (len(LENGTHS) + 1),
+        out_shape=[pltpu.VMEM((length * TILE + TAIL, TILE), jnp.bfloat16) for length in LENGTHS]
+        + [pltpu.VMEM((times,) + rows.shape, rows.dtype)],
+        scratch_shapes=[pltpu.SemaphoreType.DMA((len(LENGTHS) + times,))],
         compiler_params=pltpu.CompilerParams(vmem_limit_bytes=VMEM_LIMIT),
         name="pack_tiles",
-    )(at, *in_space(pltpu.HBM, dst, src, count, tiles))
+    )(at, *in_space(pltpu.HBM, dst, src, count, tiles, rows))
 
 
 def products(held, rows, tiles, sources):
@@ -133,40 +136,51 @@
     return total
 
 
-def sum_away_kernel(at_ref, sources, *rest):
-    count = len(LENGTHS)
-    messages, outs = rest[:count], rest[count : count + len(BACK)]
-    tail, tail_s, sem = rest[count + len(BACK) :]
-    core = at_ref[0]
-    for n, length in enumerate(LENGTHS):
-        end = messages[n][length * TILE : length * TILE + TAIL]
+def read_places(messages, tail, tail_s, sem):
+    lengths = [message.shape[0] // TILE for message in messages]
+    for n, message in enumerate(messages):
+        end = message[lengths[n] * TILE : lengths[n] * TILE + TAIL]
         tail[n] = end.astype(jnp.float32).astype(jnp.int32)
     copy = pltpu.make_async_copy(tail, tail_s, sem)
     copy.start()
     copy.wait()
-
-    def part(n, keep=None):
-        held = [tail_s[n, 0, t] for t in range(LENGTHS[n])]
-        rows = [tail_s[n, 1, t] for t in range(LENGTHS[n])]
-        if keep is not None:
-            rows = [jnp.where(keep, row, 2) for row in rows]
-        return [
-            (held[t], rows[t], messages[n].at[t * TILE : (t + 1) * TILE]) for t in range(LENGTHS[n])
+    return [
+        [
+            (tail_s[n, 0, t], tail_s[n, 1, t], message.at[t * TILE : (t + 1) * TILE])
+            for t in range(lengths[n])
         ]
-
-    odd_below, odd_above = part(4, core == 1), part(4, core == 0)
-    for out, tiles in zip(outs, (part(0) + odd_below, part(1), part(2), part(3) + odd_above)):
-        held, rows, refs = zip(*tiles)
-        out[...] = products(held, rows, lambda n: refs[n][...], sources).astype(jnp.bfloat16)
-
-
-def sum_away(at, sources, messages):
+        for n, message in enumerate(messages)
+    ]
+
+
+def write_products(out, tiles, sources):
+    held, rows, refs = zip(*tiles)
+    out[...] = products(held, rows, lambda n: refs[n][...], sources).astype(jnp.bfloat16)
+
+
+def sum_near_kernel(at_ref, sources, from_below, from_above, to_below, to_above, *scratch):
+    below, above = read_places((from_below, from_above), *scratch)
+    write_products(to_below, below, sources)
+    write_products(to_above, above, sources)
+
+
+def sum_far_kernel(at_ref, sources, from_below, from_above, odd, to_below, to_above, *scratch):
+    below, above, extra = read_places((from_below, from_above, odd), *scratch)
+
+    def kept(core):
+        return [(held, jnp.where(at_ref[0] == core, row, 2), tile) for held, row, tile in extra]
+
+    write_products(to_below, below + kept(1), sources)
+    write_products(to_above, above + kept(0), sources)
+
+
+def sum_away(kernel, at, sources, messages, name):
     rows, channels = sources.shape
     return pl.pallas_call(
-        sum_away_kernel,
+        kernel,
         in_specs=[SMEM] + [VMEM] * (1 + len(messages)),
-        out_specs=[VMEM] * len(BACK),
-        out_shape=[pltpu.VMEM((2 * TILE, channels), jnp.bfloat16)] * len(BACK),
+        out_specs=[VMEM] * 2,
+        out_shape=[pltpu.VMEM((2 * TILE, channels), jnp.bfloat16)] * 2,
         scratch_shapes=[
             pltpu.VMEM((len(messages), TAIL, TILE), jnp.int32),
             pltpu.SMEM((len(messages), TAIL, TILE), jnp.int32),
@@ -174,11 +188,11 @@
         ],
         compiler_params=pltpu.CompilerParams(vmem_limit_bytes=VMEM_LIMIT),
         cost_estimate=pl.CostEstimate(
-            flops=len(BACK) * 4 * TILE * TILE * PAIR * channels,
-            bytes_accessed=2 * (rows * channels + len(BACK) * PAIR * TILE * TILE),
+            flops=2 * 4 * TILE * TILE * PAIR * channels,
+            bytes_accessed=2 * (rows * channels + 2 * PAIR * TILE * TILE),
             transcendentals=0,
         ),
-        name="sum_away",
+        name=name,
     )(at, *in_space(pltpu.VMEM, sources, *messages))
 
 
@@ -275,10 +289,8 @@
     nc = lax.axis_size("cset")
     at = (lax.axis_index("blk") % 2).astype(jnp.int32)[None]
 
-    messages = pack_tiles(at, dst, src, count, tiles_all)
-    *messages, passive_table = lax.optimization_barrier((*messages, passive_table))
+    *messages, copies = pack_tiles(at, dst, src, count, tiles_all, passive_table, nc)
     messages = [routed(message, hops) for message, hops in zip(messages, HOPS)]
-    copies = jnp.broadcast_to(passive_table[None], (nc,) + passive_table.shape)
     own_rows = lax.all_to_all(copies, "cset", split_axis=0, concat_axis=0, tiled=True)
     own_rows = own_rows.reshape(-1, passive_table.shape[1])
     groups = [[b, b + 1] for b in range(0, lax.axis_size("blk"), 2)]
@@ -293,9 +305,21 @@
         for cols in (split_active, split_passive)
     )
     own = sum_own(at, dst, src, count, sources, tiles_all)
-    sources, own, left, right = lax.optimization_barrier((sources, own, left, right))
-    parts = sum_away(at, sources, messages)
-    parts = [routed(part, lambda core, chips=chips: chips) for part, chips in zip(parts, BACK)]
+    sources, left, right = lax.optimization_barrier((sources, left, right))
+    far_up, near_up, near_down, far_down, odd = messages
+    far_below, far_above = sum_away(
+        sum_far_kernel, at, sources, (far_up, far_down, odd), "sum_far"
+    )
+    far_below, far_above, sources = lax.optimization_barrier((far_below, far_above, sources))
+    near_below, near_above = sum_away(
+        sum_near_kernel, at, sources, (near_up, near_down), "sum_near"
+    )
+    parts = [
+        routed(far_above, lambda core: 2),
+        routed(far_below, lambda core: -2),
+        routed(near_above, lambda core: 1),
+        routed(near_below, lambda core: -1),
+    ]
     joined = join(active_table, own, parts, left, right)
     spread = lax.all_to_all(joined, "cset", split_axis=0, concat_axis=0, tiled=True)
     return spread.reshape(-1, TILE)

time: 75.8 us -> 74.3 us (0.980)
  the two profiles are of different devices: /device:TPU:2 before, /device:TPU:96 now
where the time goes in v6:
time: 74.3 us; the launch traced here: 73.9 us
  starting transfers between devices  20.5 us (28%)
  blocking collectives  18.4 us (25%)
  Pallas kernels  16.1 us (22%)
  waiting for transfers between devices  15.6 us (21%)
  local copies, waits for them, and re-layouts  2.31 us (3%)
  other arithmetic  0.91 us (1%)
    ppermute x9, starting transfers between devices, routed(): return lax.ppermute(block, ('blk', 'cset'), route)  15.2 us
    all_to_all x1, blocking collectives, local(): lax.all_to_all(joined, 'cset', split_axis=0, concat_axis=0, tiled=True)  13 us
    ppermute x9, waiting for transfers between devices, routed(): return lax.ppermute(block, ('blk', 'cset'), route)  9.2 us
    all_to_all x1, waiting for transfers between devices, local(): lax.all_to_all(copies, 'cset', split_axis=0, concat_axis=0, tiled=True)  6.35 us
    pallas_call x1, Pallas kernels, join(): pl.pallas_call(join_kernel, grid=(width // CHUNK,), in_specs=[columns] *...  6.02 us
    all_to_all x1, blocking collectives, local(): lax.all_to_all(twice, 'blk', split_axis=0, concat_axis=0, tiled=True, axi...  5.42 us
    all_to_all x1, starting transfers between devices, local(): lax.all_to_all(copies, 'cset', split_axis=0, concat_axis=0, tiled=True)  5.32 us
    pallas_call x1, Pallas kernels, pack_tiles(): pl.pallas_call(pack_kernel, in_specs=[SMEM, SMEM, SMEM, SMEM, HBM, HBM],...  4.32 us
  transfers between devices with their start and end apart: 10, of which 4 were waited for; matrix products, arithmetic and copies ran while one was open for 3% of the time, Pallas kernels for 6%

profile of v6, /device:TPU:96, one launch (start us, length us, event | category | flops | bytes accessed | tf_op | source)
XLA Modules:
  0.0 73.9 jit_solution(585094302532085077)
XLA Ops:
  0.0 0.0 copy-start.1
  0.0 4.3 %pack_tiles.1 = (bf16[1040,128]{1,0:T(8,128)(2,1)}, bf16[2064,128]{1,0:T(8,128)(2,1)S(1)}, bf16[2064,128]{1,0:T(8,128)(2,1)S(1)}, bf16[1040,128]{1,0:T(8,128)(2,...) custom-call(s32[1]{0:T(128)} %bitcast.at_ref, s32[8,9]{1,0:T(8,128)} %bitcast.22, s32[8,9]{1,0:T(8,128)} %bitcast.24, ...), custom_call_target="tpu_custom_call" | custom-call | tf_op jit(solution)/shard_map/pack_tiles/pallas_call | solution.py:105
  4.3 5.3 %all-to-all-start = ((bf16[8,256,256]{2,1,0:T(8,128)(2,1)}), bf16[8,256,256]{2,1,0:T(8,128)(2,1)}, u32[]{:S(2)}, u32[]{:S(2)}) async-start(bf16[8,256,256]{2,1,0:T(8,128)(2,1)} %get-tuple-element.21), calls=%async_computation | async-start | bytes 2097152 | tf_op jit(solution)/shard_map/all_to_all | solution.py:294
  9.7 3.5 %collective-permute-start.5 = (bf16[2064,128]{1,0:T(8,128)(2,1)S(1)}, bf16[2064,128]{1,0:T(8,128)(2,1)S(1)}, u32[]{:S(2)}, u32[]{:S(2)}) collective-permute-start(bf16[2064,128]{1,0:T(8,128)(2,1)S(1)} %get-tuple-element.33), channel_id=1, source_target_pairs={{0,20},{1,21},{2,22},{3,23},{4,16},{5,17},{6,18},{7,19},{8,28},{9,... | collective-permute-start | bytes 1585160 | tf_op jit(solution)/shard_map/ppermute | solution.py:28
  13.1 0.7 collective-permute-start.6
  13.8 4.3 %collective-permute-start = (bf16[1040,128]{1,0:T(8,128)(2,1)}, bf16[1040,128]{1,0:T(8,128)(2,1)S(1)}, u32[]{:S(2)}, u32[]{:S(2)}) collective-permute-start(bf16[1040,128]{1,0:T(8,128)(2,1)} %get-tuple-element.25), channel_id=1, source_target_pairs={{0,32},{1,33},{2,34},{3,35},{4,36},{5,37},{6,38},{7,39},{8,40},{9,... | collective-permute-start | bytes 798728 | tf_op jit(solution)/shard_map/ppermute | solution.py:28
  18.1 0.0 collective-permute-start.1
  18.1 0.0 collective-permute-start.2
  18.1 0.0 copy-done.1
  18.2 0.9 %convert_element_type.9 = bf16[20,924]{1,0:T(8,128)(2,1)S(1)} convert(s32[20,924]{1,0:T(8,128)} %param.14) | non-fusion elementwise | flops 18480 | bytes 110880 | tf_op jit(solution)/shard_map/convert_element_type | solution.py:304
  19.1 6.4 %all-to-all-done = bf16[8,256,256]{2,1,0:T(8,128)(2,1)} async-done(((bf16[8,256,256]{2,1,0:T(8,128)(2,1)}), bf16[8,256,256]{2,1,0:T(8,128)(2,1)}, u32[]{:S(2)}, u32[]{:S(2)}) %all-to-all-start) | async-done | bytes 1048608 | tf_op jit(solution)/shard_map/all_to_all | solution.py:294
  25.4 1.4 %broadcast_in_dim.18 = bf16[2,2048,256]{2,1,0:T(8,128)(2,1)S(1)} broadcast(bf16[2048,256]{1,0:T(8,128)(2,1)} %bitcast.7), dimensions={1,2} | broadcast | bytes 3145728 | tf_op jit(solution)/shard_map/broadcast_in_dim | solution.py:297
  26.8 5.4 %all_to_all.15 = bf16[2,2048,256]{2,1,0:T(8,128)(2,1)S(1)} all-to-all(bf16[2,2048,256]{2,1,0:T(8,128)(2,1)S(1)} %broadcast_in_dim.18), channel_id=1, replica_groups={{0,8},{16,24},{32,40},{48,56},{64,72},{80,88},{96,104},{112,120},{128,1..., dimensions={0} | all-to-all | bytes 4194304 | tf_op jit(solution)/shard_map/all_to_all | solution.py:298
  32.2 0.0 collective-permute-done.from_below
  32.2 2.8 %collective-permute-done.1.from_above = bf16[1040,128]{1,0:T(8,128)(2,1)S(1)} collective-permute-done((bf16[1040,128]{1,0:T(8,128)(2,1)S(1)}, bf16[1040,128]{1,0:T(8,128)(2,1)S(1)}, u32[]{:S(2)}, u32[]{:S(2)}) %collective-permute-start.1) | collective-permute-done | bytes 266272 | tf_op jit(solution)/shard_map/ppermute | solution.py:28
  35.0 2.9 %collective-permute-done.2.odd = bf16[1040,128]{1,0:T(8,128)(2,1)S(1)} collective-permute-done((bf16[1040,128]{1,0:T(8,128)(2,1)S(1)}, bf16[1040,128]{1,0:T(8,128)(2,1)S(1)}, u32[]{:S(2)}, u32[]{:S(2)}) %collective-permute-start.2) | collective-permute-done | bytes 266272 | tf_op jit(solution)/shard_map/ppermute | solution.py:28
  37.9 1.7 %sum_far.1 = (bf16[256,256]{1,0:T(8,128)(2,1)S(1)}, bf16[256,256]{1,0:T(8,128)(2,1)S(1)}) custom-call(s32[1]{0:T(128)} %bitcast.at_ref, bf16[4096,256]{1,0:T(8,128)(2,1)S(1)} %bitcast.16, bf16[1040,128]{1,0:T(8,128)(2,1)S(1)} %collective-permute-done.from_below, bf16[1040,128]{1,0:T(8,128)(2,1)S(1)} %collective-permute-done.1.from_above, ...), custom_call_target="tpu_custom_call" | custom-call | flops 536870912 | bytes 3145728 | tf_op jit(solution)/shard_map/sum_far/pallas_call | solution.py:179
  39.6 0.0 collective-permute-done.5.from_below
  39.6 0.0 collective-permute-done.6.from_above
  39.6 1.6 %sum_near.1 = (bf16[256,256]{1,0:T(8,128)(2,1)S(1)}, bf16[256,256]{1,0:T(8,128)(2,1)S(1)}) custom-call(s32[1]{0:T(128)} %bitcast.at_ref, bf16[4096,256]{1,0:T(8,128)(2,1)S(1)} %bitcast.17, bf16[2064,128]{1,0:T(8,128)(2,1)S(1)} %collective-permute-done.5.from_below, bf16[2064,128]{1,0:T(8,128)(2,1)S(1)} %collective-permute-done.6.from_above), custom_call_target="tpu_custom_call" | custom-call | flops 536870912 | bytes 3145728 | tf_op jit(solution)/shard_map/sum_near/pallas_call | solution.py:179
  41.2 0.1 collective-permute-start.7
  41.3 4.1 %collective-permute-start.8 = (bf16[256,256]{1,0:T(8,128)(2,1)S(1)}, bf16[256,256]{1,0:T(8,128)(2,1)S(1)}, u32[]{:S(2)}, u32[]{:S(2)}) collective-permute-start(bf16[256,256]{1,0:T(8,128)(2,1)S(1)} %get-tuple-element.36), channel_id=1, source_target_pairs={{0,244},{1,245},{2,246},{3,247},{4,240},{5,241},{6,242},{7,243},{8... | collective-permute-start | bytes 393224 | tf_op jit(solution)/shard_map/ppermute | solution.py:28
  45.4 2.5 %collective-permute-start.3 = (bf16[256,256]{1,0:T(8,128)(2,1)S(1)}, bf16[256,256]{1,0:T(8,128)(2,1)S(1)}, u32[]{:S(2)}, u32[]{:S(2)}) collective-permute-start(bf16[256,256]{1,0:T(8,128)(2,1)S(1)} %get-tuple-element.30), channel_id=1, source_target_pairs={{0,32},{1,33},{2,34},{3,35},{4,36},{5,37},{6,38},{7,39},{8,40},{9,... | collective-permute-start | bytes 393224 | tf_op jit(solution)/shard_map/ppermute | solution.py:28
  47.9 0.0 collective-permute-start.4
  47.9 0.1 copy.10.right_ref
  48.0 0.1 copy.9.left_ref
  48.0 0.0 copy-start
  48.0 2.5 %sum_own.1.own_ref = f32[256,256]{1,0:T(8,128)S(1)} custom-call(s32[1]{0:T(128)} %bitcast.at_ref, s32[8,9]{1,0:T(8,128)} %bitcast.23, s32[8,9]{1,0:T(8,128)} %bitcast.25, s32[9]{0:T(128)} %bitcast.27, bf16[4096,256]{1,0:T(8,128)(2,1)S(1)} %bitcast.18, bf16[9216,128]{1,0:T(8,128)(2,1)} %bitcast.20), custom_call_target="tpu_custom_call" | custom-call | flops 268435456 | bytes 2621440 | tf_op jit(solution)/shard_map/sum_own/pallas_call | solution.py:212
  50.5 0.0 collective-permute-done.7.n2
  50.5 0.0 collective-permute-done.8.n3
  50.5 0.0 collective-permute-done.3.n0
  50.5 3.5 %collective-permute-done.4.n1 = bf16[256,256]{1,0:T(8,128)(2,1)S(1)} collective-permute-done((bf16[256,256]{1,0:T(8,128)(2,1)S(1)}, bf16[256,256]{1,0:T(8,128)(2,1)S(1)}, u32[]{:S(2)}, u32[]{:S(2)}) %collective-permute-start.4) | collective-permute-done | bytes 131104 | tf_op jit(solution)/shard_map/ppermute | solution.py:28
  54.1 0.0 copy-done
  54.1 6.0 %join_sets.1 = bf16[8,256,128]{2,1,0:T(8,128)(2,1)S(1)} custom-call(bf16[20,1,1024]{2,1,0:T(2,128)(2,1)S(1)} %copy.9.left_ref, bf16[20,1,1024]{2,1,0:T(2,128)(2,1)S(1)} %copy.10.right_ref, bf16[256,256]{1,0:T(8,128)(2,1)S(1)} %copy-done, f32[256,256]{1,0:T(8,128)S(1)} %sum_own.1.own_ref, bf16[256,256]{1,0:T(8,128)(2,1)S(1)} %collective-permute-done.3.n0, ...), custom_call_target="tpu_custom_call" | custom-call | flops 5368709120 | bytes 524288 | tf_op jit(solution)/shard_map/join_sets/pallas_call | solution.py:261
  60.1 13.0 %all_to_all.16 = bf16[8,256,128]{2,1,0:T(8,128)(2,1)S(1)} all-to-all(bf16[8,256,128]{2,1,0:T(8,128)(2,1)S(1)} %join_sets.1), channel_id=1, replica_groups=mesh['blk'=32,'cset'=8] {'cset'}, dimensions={0} | all-to-all | bytes 1048576 | tf_op jit(solution)/shard_map/all_to_all | solution.py:324
  73.1 0.8 %copy.12 = bf16[2048,128]{1,0:T(8,128)(2,1)} copy(bf16[2048,128]{1,0:T(8,128)(2,1)S(1)} %bitcast.21) | data formatting | bytes 1048576
  (2 shorter events, 0.0 us)
Async XLA Ops:
  0.0 18.1 %copy-start.1 = (s32[20,924]{1,0:T(8,128)S(1)}, s32[20,924]{1,0:T(8,128)}, u32[]{:S(2)}) copy-start(s32[20,924]{1,0:T(8,128)} %param.15) | copy-start | bytes 221764
  4.3 21.1 %all-to-all-start = ((bf16[8,256,256]{2,1,0:T(8,128)(2,1)}), bf16[8,256,256]{2,1,0:T(8,128)(2,1)}, u32[]{:S(2)}, u32[]{:S(2)}) async-start(bf16[8,256,256]{2,1,0:T(8,128)(2,1)} %get-tuple-element.21), calls=%async_computation | async-start | bytes 2097152 | tf_op jit(solution)/shard_map/all_to_all | solution.py:294
  9.7 29.9 %collective-permute-start.5 = (bf16[2064,128]{1,0:T(8,128)(2,1)S(1)}, bf16[2064,128]{1,0:T(8,128)(2,1)S(1)}, u32[]{:S(2)}, u32[]{:S(2)}) collective-permute-start(bf16[2064,128]{1,0:T(8,128)(2,1)S(1)} %get-tuple-element.33), channel_id=1, source_target_pairs={{0,20},{1,21},{2,22},{3,23},{4,16},{5,17},{6,18},{7,19},{8,28},{9,... | collective-permute-start | bytes 1585160 | tf_op jit(solution)/shard_map/ppermute | solution.py:28
  13.1 26.5 %collective-permute-start.6 = (bf16[2064,128]{1,0:T(8,128)(2,1)S(1)}, bf16[2064,128]{1,0:T(8,128)(2,1)S(1)}, u32[]{:S(2)}, u32[]{:S(2)}) collective-permute-start(bf16[2064,128]{1,0:T(8,128)(2,1)S(1)} %get-tuple-element.34), channel_id=1, source_target_pairs={{0,244},{1,245},{2,246},{3,247},{4,240},{5,241},{6,242},{7,243},{8... | collective-permute-start | bytes 1585160 | tf_op jit(solution)/shard_map/ppermute | solution.py:28
  13.8 18.4 %collective-permute-start = (bf16[1040,128]{1,0:T(8,128)(2,1)}, bf16[1040,128]{1,0:T(8,128)(2,1)S(1)}, u32[]{:S(2)}, u32[]{:S(2)}) collective-permute-start(bf16[1040,128]{1,0:T(8,128)(2,1)} %get-tuple-element.25), channel_id=1, source_target_pairs={{0,32},{1,33},{2,34},{3,35},{4,36},{5,37},{6,38},{7,39},{8,40},{9,... | collective-permute-start | bytes 798728 | tf_op jit(solution)/shard_map/ppermute | solution.py:28
  18.1 16.9 %collective-permute-start.1 = (bf16[1040,128]{1,0:T(8,128)(2,1)S(1)}, bf16[1040,128]{1,0:T(8,128)(2,1)S(1)}, u32[]{:S(2)}, u32[]{:S(2)}) collective-permute-start(bf16[1040,128]{1,0:T(8,128)(2,1)S(1)} %get-tuple-element.26), channel_id=1, source_target_pairs={{0,224},{1,225},{2,226},{3,227},{4,228},{5,229},{6,230},{7,231},{8... | collective-permute-start | bytes 798728 | tf_op jit(solution)/shard_map/ppermute | solution.py:28
  18.1 19.7 %collective-permute-start.2 = (bf16[1040,128]{1,0:T(8,128)(2,1)S(1)}, bf16[1040,128]{1,0:T(8,128)(2,1)S(1)}, u32[]{:S(2)}, u32[]{:S(2)}) collective-permute-start(bf16[1040,128]{1,0:T(8,128)(2,1)S(1)} %get-tuple-element.27), channel_id=1, source_target_pairs={{0,224},{1,225},{2,226},{3,227},{4,228},{5,229},{6,230},{7,231},{8... | collective-permute-start | bytes 798728 | tf_op jit(solution)/shard_map/ppermute | solution.py:28
  41.2 9.3 %collective-permute-start.7 = (bf16[256,256]{1,0:T(8,128)(2,1)S(1)}, bf16[256,256]{1,0:T(8,128)(2,1)S(1)}, u32[]{:S(2)}, u32[]{:S(2)}) collective-permute-start(bf16[256,256]{1,0:T(8,128)(2,1)S(1)} %get-tuple-element.35), channel_id=1, source_target_pairs={{0,20},{1,21},{2,22},{3,23},{4,16},{5,17},{6,18},{7,19},{8,28},{9,... | collective-permute-start | bytes 393224 | tf_op jit(solution)/shard_map/ppermute | solution.py:28
  41.3 9.2 %collective-permute-start.8 = (bf16[256,256]{1,0:T(8,128)(2,1)S(1)}, bf16[256,256]{1,0:T(8,128)(2,1)S(1)}, u32[]{:S(2)}, u32[]{:S(2)}) collective-permute-start(bf16[256,256]{1,0:T(8,128)(2,1)S(1)} %get-tuple-element.36), channel_id=1, source_target_pairs={{0,244},{1,245},{2,246},{3,247},{4,240},{5,241},{6,242},{7,243},{8... | collective-permute-start | bytes 393224 | tf_op jit(solution)/shard_map/ppermute | solution.py:28
  45.4 5.1 %collective-permute-start.3 = (bf16[256,256]{1,0:T(8,128)(2,1)S(1)}, bf16[256,256]{1,0:T(8,128)(2,1)S(1)}, u32[]{:S(2)}, u32[]{:S(2)}) collective-permute-start(bf16[256,256]{1,0:T(8,128)(2,1)S(1)} %get-tuple-element.30), channel_id=1, source_target_pairs={{0,32},{1,33},{2,34},{3,35},{4,36},{5,37},{6,38},{7,39},{8,40},{9,... | collective-permute-start | bytes 393224 | tf_op jit(solution)/shard_map/ppermute | solution.py:28
  47.9 6.2 %collective-permute-start.4 = (bf16[256,256]{1,0:T(8,128)(2,1)S(1)}, bf16[256,256]{1,0:T(8,128)(2,1)S(1)}, u32[]{:S(2)}, u32[]{:S(2)}) collective-permute-start(bf16[256,256]{1,0:T(8,128)(2,1)S(1)} %get-tuple-element.31), channel_id=1, source_target_pairs={{0,224},{1,225},{2,226},{3,227},{4,228},{5,229},{6,230},{7,231},{8... | collective-permute-start | bytes 393224 | tf_op jit(solution)/shard_map/ppermute | solution.py:28
  48.0 6.0 %copy-start = (bf16[256,256]{1,0:T(8,128)(2,1)S(1)}, bf16[256,256]{1,0:T(8,128)(2,1)}, u32[]{:S(2)}) copy-start(bf16[256,256]{1,0:T(8,128)(2,1)} %active_ref.1) | copy-start | bytes 393220

commit v7 on v6

--- a/solution.py
+++ b/solution.py
@@ -77,10 +77,10 @@
                 sems.at[n],
             )
         )
-    for n in range(repeated.shape[0]):
-        copies.append(pltpu.make_async_copy(rows_ref, repeated.at[n], sems.at[len(HOPS) + n]))
     for copy in copies:
         copy.start()
+    for n in range(repeated.shape[0]):
+        repeated[n] = rows_ref[...]
     for n, length in enumerate(LENGTHS):
         held, rows = places(slots[n], dst_ref, src_ref, count_ref)
         tail = jnp.zeros((TAIL, TILE), jnp.int32)
@@ -104,14 +104,14 @@
 def pack_tiles(at, dst, src, count, tiles, rows, times):
     return pl.pallas_call(
         pack_kernel,
-        in_specs=[SMEM, SMEM, SMEM, SMEM, HBM, HBM],
+        in_specs=[SMEM, SMEM, SMEM, SMEM, HBM, VMEM],
         out_specs=[VMEM] * (len(LENGTHS) + 1),
         out_shape=[pltpu.VMEM((length * TILE + TAIL, TILE), jnp.bfloat16) for length in LENGTHS]
         + [pltpu.VMEM((times,) + rows.shape, rows.dtype)],
-        scratch_shapes=[pltpu.SemaphoreType.DMA((len(LENGTHS) + times,))],
+        scratch_shapes=[pltpu.SemaphoreType.DMA((len(LENGTHS),))],
         compiler_params=pltpu.CompilerParams(vmem_limit_bytes=VMEM_LIMIT),
         name="pack_tiles",
-    )(at, *in_space(pltpu.HBM, dst, src, count, tiles, rows))
+    )(at, *in_space(pltpu.HBM, dst, src, count, tiles), rows)
 
 
 def products(held, rows, tiles, sources):
@@ -227,51 +227,108 @@
         name="sum_own",
     )(
         at,
-        *in_space(pltpu.HBM, dst, src, count),
+        dst,
+        src,
+        count,
         *in_space(pltpu.VMEM, sources),
-        *in_space(pltpu.HBM, tiles),
+        tiles,
     )
 
 
-def join_kernel(left_ref, right_ref, active_ref, own_ref, n0, n1, n2, n3, out_ref):
+def onehot(columns, channels):
+    shape = (channels, columns.shape[1])
+    channel = lax.broadcasted_iota(jnp.int32, shape, 0).astype(jnp.float32).astype(jnp.bfloat16)
+    one, zero = jnp.ones(shape, jnp.bfloat16), jnp.zeros(shape, jnp.bfloat16)
+    return jnp.where(channel == columns, one, zero)
+
+
+def columns_kernel(left_ref, right_ref, left_out, right_out):
+    for ref, out in ((left_ref, left_out), (right_ref, right_out)):
+        out[...] = jnp.full(out.shape, -1, jnp.bfloat16)
+        for j in range(SPLITS):
+            row = ref[j : j + 1].astype(jnp.float32).astype(jnp.bfloat16)
+            out[j, :, : ref.shape[1]] = row
+
+
+def as_columns(left, right):
+    return pl.pallas_call(
+        columns_kernel,
+        in_specs=[VMEM] * 2,
+        out_specs=[VMEM] * 2,
+        out_shape=[pltpu.VMEM((SPLITS, 1, OUTPAD), jnp.bfloat16)] * 2,
+        compiler_params=pltpu.CompilerParams(vmem_limit_bytes=VMEM_LIMIT),
+        name="as_columns",
+    )(left, right)
+
+
+def pick_kernel(columns_ref, table_ref, out_ref):
+    table = table_ref[...]
+    for j in range(SPLITS):
+        for begin in range(0, out_ref.shape[2], CHUNK):
+            part = slice(begin, begin + CHUNK)
+            picked = jnp.dot(
+                table,
+                onehot(columns_ref[j, :, part], table.shape[1]),
+                preferred_element_type=jnp.float32,
+            )
+            out_ref[j, :, part] = picked.astype(jnp.bfloat16)
+
+
+def pick_columns(table, columns):
+    rows, channels = table.shape
+    splits, _, width = columns.shape
+    return pl.pallas_call(
+        pick_kernel,
+        in_specs=[VMEM] * 2,
+        out_specs=VMEM,
+        out_shape=pltpu.VMEM((splits, rows, width), jnp.bfloat16),
+        compiler_params=pltpu.CompilerParams(vmem_limit_bytes=VMEM_LIMIT),
+        cost_estimate=pl.CostEstimate(
+            flops=2 * splits * rows * channels * width,
+            bytes_accessed=2 * splits * rows * width,
+            transcendentals=0,
+        ),
+        name="pick_active",
+    )(columns, table)
+
+
+def join_kernel(columns_ref, picked_ref, own_ref, n0, n1, n2, n3, out_ref):
     total = own_ref[...]
     for part in (n0, n1, n2, n3):
         total = total + part[...].astype(jnp.float32)
     neighbour = total.astype(jnp.bfloat16)
-    active = active_ref[...]
-    shape = (active.shape[1], left_ref.shape[2])
-    channel = lax.broadcasted_iota(jnp.int32, shape, 0).astype(jnp.float32).astype(jnp.bfloat16)
-    one, zero = jnp.ones(shape, jnp.bfloat16), jnp.zeros(shape, jnp.bfloat16)
-    joined = jnp.zeros((active.shape[0], shape[1]), jnp.float32)
-    for j in range(SPLITS):
-        left = jnp.where(channel == left_ref[j], one, zero)
-        right = jnp.where(channel == right_ref[j], one, zero)
-        joined = joined + jnp.dot(active, left, preferred_element_type=jnp.float32) * jnp.dot(
-            neighbour, right, preferred_element_type=jnp.float32
-        )
-    for piece in range(shape[1] // TILE):
-        out_ref[piece] = joined[:, piece * TILE : (piece + 1) * TILE].astype(out_ref.dtype)
-
-
-def join(active, own, parts, left, right):
-    rows, channels = own.shape
-    splits, _, width = left.shape
-    whole = pl.BlockSpec((rows, channels), lambda q: (0, 0))
-    columns = pl.BlockSpec((splits, 1, CHUNK), lambda q: (0, 0, q))
+    rows, channels = neighbour.shape
+    for begin in range(0, picked_ref.shape[2], CHUNK):
+        part = slice(begin, begin + CHUNK)
+        joined = jnp.zeros((rows, CHUNK), jnp.float32)
+        for j in range(SPLITS):
+            joined = joined + picked_ref[j, :, part].astype(jnp.float32) * jnp.dot(
+                neighbour,
+                onehot(columns_ref[j, :, part], channels),
+                preferred_element_type=jnp.float32,
+            )
+        for piece in range(CHUNK // TILE):
+            out_ref[begin // TILE + piece] = joined[:, piece * TILE : (piece + 1) * TILE].astype(
+                out_ref.dtype
+            )
+
+
+def join(picked, own, parts, columns):
+    splits, rows, width = picked.shape
+    channels = own.shape[1]
     return pl.pallas_call(
         join_kernel,
-        grid=(width // CHUNK,),
-        in_specs=[columns] * 2 + [whole] * 6,
-        out_specs=pl.BlockSpec((CHUNK // TILE, rows, TILE), lambda q: (q, 0, 0)),
-        out_shape=jax.ShapeDtypeStruct((width // TILE, rows, TILE), jnp.bfloat16),
+        in_specs=[VMEM] * 7,
+        out_specs=VMEM,
+        out_shape=pltpu.VMEM((width // TILE, rows, TILE), jnp.bfloat16),
         compiler_params=pltpu.CompilerParams(vmem_limit_bytes=VMEM_LIMIT),
         cost_estimate=pl.CostEstimate(
-            flops=4 * splits * rows * channels * width,
+            flops=2 * splits * rows * channels * width,
             bytes_accessed=2 * rows * width,
             transcendentals=0,
         ),
         name="join_sets",
-    )(left, right, active, own, *parts)
+    )(columns, *in_space(pltpu.VMEM, picked, own, *parts))
 
 
 def local(
@@ -299,13 +356,9 @@
         twice, "blk", split_axis=0, concat_axis=0, tiled=True, axis_index_groups=groups
     ).reshape(-1, own_rows.shape[1])
 
-    extra = OUTPAD - split_active.shape[1]
-    left, right = (
-        jnp.pad(cols.astype(jnp.bfloat16), ((0, 0), (0, extra)), constant_values=-1)[:, None, :]
-        for cols in (split_active, split_passive)
-    )
+    left, right = as_columns(split_active, split_passive)
     own = sum_own(at, dst, src, count, sources, tiles_all)
-    sources, left, right = lax.optimization_barrier((sources, left, right))
+    sources, own, left, right = lax.optimization_barrier((sources, own, left, right))
     far_up, near_up, near_down, far_down, odd = messages
     far_below, far_above = sum_away(
         sum_far_kernel, at, sources, (far_up, far_down, odd), "sum_far"
@@ -314,13 +367,15 @@
     near_below, near_above = sum_away(
         sum_near_kernel, at, sources, (near_up, near_down), "sum_near"
     )
+    near_below, near_above, left = lax.optimization_barrier((near_below, near_above, left))
+    picked = pick_columns(active_table, left)
     parts = [
         routed(far_above, lambda core: 2),
         routed(far_below, lambda core: -2),
         routed(near_above, lambda core: 1),
         routed(near_below, lambda core: -1),
     ]
-    joined = join(active_table, own, parts, left, right)
+    joined = join(picked, own, parts, right)
     spread = lax.all_to_all(joined, "cset", split_axis=0, concat_axis=0, tiled=True)
     return spread.reshape(-1, TILE)
 

time: 74.3 us -> 71.8 us (0.966)
  Pallas kernels: 16.1 us -> 14.5 us
  waiting for transfers between devices: 15.6 us -> 14.6 us
  other arithmetic: 0.91 us -> 0 us
  local copies, waits for them, and re-layouts: 2.31 us -> 3.1 us
    ppermute x9, waiting for transfers between devices: 9.2 us -> 7.48 us  [routed(): return lax.ppermute(block, ('blk', 'cset'), route)]
    pallas_call x1, Pallas kernels: 2.45 us -> 1.19 us  [sum_own(): pl.pallas_call(sum_own_kernel, in_specs=[SMEM] * 4 + [VMEM] + [HBM], out_...]
    unnamed x5 -> x17, local copies, waits for them, and re-layouts: 0.8 us -> 1.74 us
    convert_element_type x2 -> x0, other arithmetic: 0.91 us -> none  [local(): cols.astype(jnp.bfloat16)]
    all_to_all x1, waiting for transfers between devices: 6.35 us -> 7.15 us  [local(): lax.all_to_all(copies, 'cset', split_axis=0, concat_axis=0, tiled=True)]
    pallas_call x2 -> x4, Pallas kernels: 10.3 us -> 10 us  [the longest x1 3.58 us: pack_tiles(): pl.pallas_call(pack_kernel, in_specs=[SMEM, SMEM, SMEM, SMEM, HBM, VMEM],...]
  transfers between devices with their start and end apart: 10 -> 10, of which waited for: 4 -> 4; matrix products, arithmetic and copies ran while one was open for 3% -> 2% of each run, Pallas kernels for 6% -> 8%
where the time goes in v7:
time: 71.8 us; the launch traced here: 71.4 us
  starting transfers between devices  20.5 us (29%)
  blocking collectives  18.6 us (26%)
  waiting for transfers between devices  14.6 us (20%)
  Pallas kernels  14.5 us (20%)
  local copies, waits for them, and re-layouts  3.1 us (4%)
    ppermute x9, starting transfers between devices, routed(): return lax.ppermute(block, ('blk', 'cset'), route)  15.2 us
    all_to_all x1, blocking collectives, local(): lax.all_to_all(joined, 'cset', split_axis=0, concat_axis=0, tiled=True)  13 us
    ppermute x9, waiting for transfers between devices, routed(): return lax.ppermute(block, ('blk', 'cset'), route)  7.48 us
    all_to_all x1, waiting for transfers between devices, local(): lax.all_to_all(copies, 'cset', split_axis=0, concat_axis=0, tiled=True)  7.15 us
    all_to_all x1, blocking collectives, local(): lax.all_to_all(twice, 'blk', split_axis=0, concat_axis=0, tiled=True, axi...  5.55 us
    all_to_all x1, starting transfers between devices, local(): lax.all_to_all(copies, 'cset', split_axis=0, concat_axis=0, tiled=True)  5.32 us
    pallas_call x1, Pallas kernels, pack_tiles(): pl.pallas_call(pack_kernel, in_specs=[SMEM, SMEM, SMEM, SMEM, HBM, VMEM],...  3.58 us
    pallas_call x1, Pallas kernels, join(): pl.pallas_call(join_kernel, in_specs=[VMEM] * 7, out_specs=VMEM, out_shap...  3.39 us
  transfers between devices with their start and end apart: 10, of which 4 were waited for; matrix products, arithmetic and copies ran while one was open for 2% of the time, Pallas kernels for 8%

profile of v7, /device:TPU:96, one launch (start us, length us, event | category | flops | bytes accessed | tf_op | source)
XLA Modules:
  0.0 71.4 jit_solution(15550403072883203692)
XLA Ops:
  0.0 0.0 copy-start.1
  0.0 0.9 %copy-done.1 = bf16[256,256]{1,0:T(8,128)(2,1)S(1)} copy-done((bf16[256,256]{1,0:T(8,128)(2,1)S(1)}, bf16[256,256]{1,0:T(8,128)(2,1)}, u32[]{:S(2)}) %copy-start.1) | copy-done | bytes 131096
  0.9 0.0 copy-start.3
  0.9 0.0 copy-start.4
  0.9 3.6 %pack_tiles.1 = (bf16[1040,128]{1,0:T(8,128)(2,1)}, bf16[2064,128]{1,0:T(8,128)(2,1)S(1)}, bf16[2064,128]{1,0:T(8,128)(2,1)S(1)}, bf16[1040,128]{1,0:T(8,128)(2,...) custom-call(s32[1]{0:T(128)} %bitcast.at_ref, s32[8,9]{1,0:T(8,128)} %bitcast.17, s32[8,9]{1,0:T(8,128)} %bitcast.19, ...), custom_call_target="tpu_custom_call" | custom-call | tf_op jit(solution)/shard_map/pack_tiles/pallas_call | solution.py:105
  4.5 5.3 %all-to-all-start = ((bf16[8,256,256]{2,1,0:T(8,128)(2,1)}), bf16[8,256,256]{2,1,0:T(8,128)(2,1)}, u32[]{:S(2)}, u32[]{:S(2)}) async-start(bf16[8,256,256]{2,1,0:T(8,128)(2,1)} %get-tuple-element.27), calls=%async_computation | async-start | bytes 2097152 | tf_op jit(solution)/shard_map/all_to_all | solution.py:351
  9.8 3.5 %collective-permute-start.3 = (bf16[2064,128]{1,0:T(8,128)(2,1)S(1)}, bf16[2064,128]{1,0:T(8,128)(2,1)S(1)}, u32[]{:S(2)}, u32[]{:S(2)}) collective-permute-start(bf16[2064,128]{1,0:T(8,128)(2,1)S(1)} %get-tuple-element.38), channel_id=1, source_target_pairs={{0,20},{1,21},{2,22},{3,23},{4,16},{5,17},{6,18},{7,19},{8,28},{9,... | collective-permute-start | bytes 1585160 | tf_op jit(solution)/shard_map/ppermute | solution.py:28
  13.3 0.7 collective-permute-start.4
  14.0 4.3 %collective-permute-start = (bf16[1040,128]{1,0:T(8,128)(2,1)}, bf16[1040,128]{1,0:T(8,128)(2,1)S(1)}, u32[]{:S(2)}, u32[]{:S(2)}) collective-permute-start(bf16[1040,128]{1,0:T(8,128)(2,1)} %get-tuple-element.32), channel_id=1, source_target_pairs={{0,32},{1,33},{2,34},{3,35},{4,36},{5,37},{6,38},{7,39},{8,40},{9,... | collective-permute-start | bytes 798728 | tf_op jit(solution)/shard_map/ppermute | solution.py:28
  18.3 0.0 collective-permute-start.1
  18.3 0.0 collective-permute-start.2
  18.3 0.0 copy-done.3
  18.3 0.0 copy-done.4
  18.3 0.1 as_columns.1
  18.5 7.2 %all-to-all-done = bf16[8,256,256]{2,1,0:T(8,128)(2,1)} async-done(((bf16[8,256,256]{2,1,0:T(8,128)(2,1)}), bf16[8,256,256]{2,1,0:T(8,128)(2,1)}, u32[]{:S(2)}, u32[]{:S(2)}) %all-to-all-start) | async-done | bytes 1048608 | tf_op jit(solution)/shard_map/all_to_all | solution.py:351
  25.6 1.4 %broadcast_in_dim.12 = bf16[2,2048,256]{2,1,0:T(8,128)(2,1)S(1)} broadcast(bf16[2048,256]{1,0:T(8,128)(2,1)} %bitcast.7), dimensions={1,2} | broadcast | bytes 3145728 | tf_op jit(solution)/shard_map/broadcast_in_dim | solution.py:354
  27.0 0.0 copy-start
  27.0 0.0 copy-start.5
  27.0 0.0 copy-start.6
  27.0 0.0 copy-start.7
  27.0 5.5 %all_to_all.15 = bf16[2,2048,256]{2,1,0:T(8,128)(2,1)S(1)} all-to-all(bf16[2,2048,256]{2,1,0:T(8,128)(2,1)S(1)} %broadcast_in_dim.12), channel_id=1, replica_groups={{0,8},{16,24},{32,40},{48,56},{64,72},{80,88},{96,104},{112,120},{128,1..., dimensions={0} | all-to-all | bytes 4194304 | tf_op jit(solution)/shard_map/all_to_all | solution.py:355
  32.6 0.0 copy-done
  32.6 0.0 copy-done.5
  32.6 0.0 copy-done.6
  32.6 0.0 copy-done.7
  32.6 1.2 %sum_own.1.own_ref = f32[256,256]{1,0:T(8,128)S(1)} custom-call(s32[1]{0:T(128)} %bitcast.at_ref, s32[8,9]{1,0:T(8,128)S(1)} %bitcast.18, s32[8,9]{1,0:T(8,128)S(1)} %bitcast.20, s32[9]{0:T(128)S(1)} %bitcast.22, bf16[4096,256]{1,0:T(8,128)(2,1)S(1)} %bitcast.12, bf16[9216,128]{1,0:T(8,128)(2,1)S(1)} %bitcast.16), custom_call_target="tpu_custom_call" | custom-call | flops 268435456 | bytes 2621440 | tf_op jit(solution)/shard_map/sum_own/pallas_call | solution.py:212
  33.8 0.0 copy-start.2
  33.8 0.0 collective-permute-done.from_below
  33.8 1.4 %collective-permute-done.1.from_above = bf16[1040,128]{1,0:T(8,128)(2,1)S(1)} collective-permute-done((bf16[1040,128]{1,0:T(8,128)(2,1)}, bf16[1040,128]{1,0:T(8,128)(2,1)S(1)}, u32[]{:S(2)}, u32[]{:S(2)}) %collective-permute-start.1) | collective-permute-done | bytes 266272 | tf_op jit(solution)/shard_map/ppermute | solution.py:28
  35.2 2.9 %collective-permute-done.2.odd = bf16[1040,128]{1,0:T(8,128)(2,1)S(1)} collective-permute-done((bf16[1040,128]{1,0:T(8,128)(2,1)S(1)}, bf16[1040,128]{1,0:T(8,128)(2,1)S(1)}, u32[]{:S(2)}, u32[]{:S(2)}) %collective-permute-start.2) | collective-permute-done | bytes 266272 | tf_op jit(solution)/shard_map/ppermute | solution.py:28
  38.1 1.7 %sum_far.1 = (bf16[256,256]{1,0:T(8,128)(2,1)S(1)}, bf16[256,256]{1,0:T(8,128)(2,1)S(1)}) custom-call(s32[1]{0:T(128)} %bitcast.at_ref, bf16[4096,256]{1,0:T(8,128)(2,1)S(1)} %bitcast.13, bf16[1040,128]{1,0:T(8,128)(2,1)S(1)} %collective-permute-done.from_below, bf16[1040,128]{1,0:T(8,128)(2,1)S(1)} %collective-permute-done.1.from_above, ...), custom_call_target="tpu_custom_call" | custom-call | flops 536870912 | bytes 3145728 | tf_op jit(solution)/shard_map/sum_far/pallas_call | solution.py:179
  39.8 0.0 collective-permute-done.3.from_below
  39.8 0.0 collective-permute-done.4.from_above
  39.8 1.6 %sum_near.1 = (bf16[256,256]{1,0:T(8,128)(2,1)S(1)}, bf16[256,256]{1,0:T(8,128)(2,1)S(1)}) custom-call(s32[1]{0:T(128)} %bitcast.at_ref, bf16[4096,256]{1,0:T(8,128)(2,1)S(1)} %bitcast.14, bf16[2064,128]{1,0:T(8,128)(2,1)S(1)} %collective-permute-done.3.from_below, bf16[2064,128]{1,0:T(8,128)(2,1)S(1)} %collective-permute-done.4.from_above), custom_call_target="tpu_custom_call" | custom-call | flops 536870912 | bytes 3145728 | tf_op jit(solution)/shard_map/sum_near/pallas_call | solution.py:179
  41.4 0.1 collective-permute-start.7
  41.4 4.1 %collective-permute-start.8 = (bf16[256,256]{1,0:T(8,128)(2,1)S(1)}, bf16[256,256]{1,0:T(8,128)(2,1)S(1)}, u32[]{:S(2)}, u32[]{:S(2)}) collective-permute-start(bf16[256,256]{1,0:T(8,128)(2,1)S(1)} %get-tuple-element.48), channel_id=1, source_target_pairs={{0,244},{1,245},{2,246},{3,247},{4,240},{5,241},{6,242},{7,243},{8... | collective-permute-start | bytes 393224 | tf_op jit(solution)/shard_map/ppermute | solution.py:28
  45.6 2.5 %collective-permute-start.5 = (bf16[256,256]{1,0:T(8,128)(2,1)S(1)}, bf16[256,256]{1,0:T(8,128)(2,1)S(1)}, u32[]{:S(2)}, u32[]{:S(2)}) collective-permute-start(bf16[256,256]{1,0:T(8,128)(2,1)S(1)} %get-tuple-element.45), channel_id=1, source_target_pairs={{0,32},{1,33},{2,34},{3,35},{4,36},{5,37},{6,38},{7,39},{8,40},{9,... | collective-permute-start | bytes 393224 | tf_op jit(solution)/shard_map/ppermute | solution.py:28
  48.1 0.0 collective-permute-start.6
  48.1 0.0 copy-done.2
  48.1 2.9 %pick_active.1.picked_ref = bf16[20,256,1024]{2,1,0:T(8,128)(2,1)S(1)} custom-call(bf16[20,1,1024]{2,1,0:T(2,128)(2,1)S(1)} %get-tuple-element.43.columns_ref, bf16[256,256]{1,0:T(8,128)(2,1)S(1)} %copy-done.2), custom_call_target="tpu_custom_call" | custom-call | flops 2684354560 | bytes 10485760 | tf_op jit(solution)/shard_map/pick_active/pallas_call | solution.py:280
  51.0 0.0 collective-permute-done.7.n2
  51.0 0.0 collective-permute-done.8.n3
  51.0 0.0 collective-permute-done.5.n0
  51.0 3.2 %collective-permute-done.6.n1 = bf16[256,256]{1,0:T(8,128)(2,1)S(1)} collective-permute-done((bf16[256,256]{1,0:T(8,128)(2,1)S(1)}, bf16[256,256]{1,0:T(8,128)(2,1)S(1)}, u32[]{:S(2)}, u32[]{:S(2)}) %collective-permute-start.6) | collective-permute-done | bytes 131104 | tf_op jit(solution)/shard_map/ppermute | solution.py:28
  54.2 3.4 %join_sets.1 = bf16[8,256,128]{2,1,0:T(8,128)(2,1)S(1)} custom-call(bf16[20,1,1024]{2,1,0:T(2,128)(2,1)S(1)} %get-tuple-element.30.columns_ref, bf16[20,256,1024]{2,1,0:T(8,128)(2,1)S(1)} %pick_active.1.picked_ref, f32[256,256]{1,0:T(8,128)S(1)} %sum_own.1.own_ref, bf16[256,256]{1,0:T(8,128)(2,1)S(1)} %collective-permute-done.5.n0, ...), custom_call_target="tpu_custom_call" | custom-call | flops 2684354560 | bytes 524288 | tf_op jit(solution)/shard_map/join_sets/pallas_call | solution.py:319
  57.6 13.0 %all_to_all.16 = bf16[8,256,128]{2,1,0:T(8,128)(2,1)S(1)} all-to-all(bf16[8,256,128]{2,1,0:T(8,128)(2,1)S(1)} %join_sets.1), channel_id=1, replica_groups=mesh['blk'=32,'cset'=8] {'cset'}, dimensions={0} | all-to-all | bytes 1048576 | tf_op jit(solution)/shard_map/all_to_all | solution.py:379
  70.6 0.8 %copy.10 = bf16[2048,128]{1,0:T(8,128)(2,1)} copy(bf16[2048,128]{1,0:T(8,128)(2,1)S(1)} %bitcast.23) | data formatting | bytes 1048576
Async XLA Ops:
  0.0 0.9 %copy-start.1 = (bf16[256,256]{1,0:T(8,128)(2,1)S(1)}, bf16[256,256]{1,0:T(8,128)(2,1)}, u32[]{:S(2)}) copy-start(bf16[256,256]{1,0:T(8,128)(2,1)} %rows_ref.1) | copy-start | bytes 393220
  0.9 17.4 %copy-start.3 = (s32[20,924]{1,0:T(8,128)S(1)}, s32[20,924]{1,0:T(8,128)}, u32[]{:S(2)}) copy-start(s32[20,924]{1,0:T(8,128)} %left_ref.1) | copy-start | bytes 221764
  0.9 17.4 %copy-start.4 = (s32[20,924]{1,0:T(8,128)S(1)}, s32[20,924]{1,0:T(8,128)}, u32[]{:S(2)}) copy-start(s32[20,924]{1,0:T(8,128)} %right_ref.1) | copy-start | bytes 221764
  4.5 21.1 %all-to-all-start = ((bf16[8,256,256]{2,1,0:T(8,128)(2,1)}), bf16[8,256,256]{2,1,0:T(8,128)(2,1)}, u32[]{:S(2)}, u32[]{:S(2)}) async-start(bf16[8,256,256]{2,1,0:T(8,128)(2,1)} %get-tuple-element.27), calls=%async_computation | async-start | bytes 2097152 | tf_op jit(solution)/shard_map/all_to_all | solution.py:351
  9.8 29.9 %collective-permute-start.3 = (bf16[2064,128]{1,0:T(8,128)(2,1)S(1)}, bf16[2064,128]{1,0:T(8,128)(2,1)S(1)}, u32[]{:S(2)}, u32[]{:S(2)}) collective-permute-start(bf16[2064,128]{1,0:T(8,128)(2,1)S(1)} %get-tuple-element.38), channel_id=1, source_target_pairs={{0,20},{1,21},{2,22},{3,23},{4,16},{5,17},{6,18},{7,19},{8,28},{9,... | collective-permute-start | bytes 1585160 | tf_op jit(solution)/shard_map/ppermute | solution.py:28
  13.3 26.5 %collective-permute-start.4 = (bf16[2064,128]{1,0:T(8,128)(2,1)S(1)}, bf16[2064,128]{1,0:T(8,128)(2,1)S(1)}, u32[]{:S(2)}, u32[]{:S(2)}) collective-permute-start(bf16[2064,128]{1,0:T(8,128)(2,1)S(1)} %get-tuple-element.39), channel_id=1, source_target_pairs={{0,244},{1,245},{2,246},{3,247},{4,240},{5,241},{6,242},{7,243},{8... | collective-permute-start | bytes 1585160 | tf_op jit(solution)/shard_map/ppermute | solution.py:28
  14.0 19.9 %collective-permute-start = (bf16[1040,128]{1,0:T(8,128)(2,1)}, bf16[1040,128]{1,0:T(8,128)(2,1)S(1)}, u32[]{:S(2)}, u32[]{:S(2)}) collective-permute-start(bf16[1040,128]{1,0:T(8,128)(2,1)} %get-tuple-element.32), channel_id=1, source_target_pairs={{0,32},{1,33},{2,34},{3,35},{4,36},{5,37},{6,38},{7,39},{8,40},{9,... | collective-permute-start | bytes 798728 | tf_op jit(solution)/shard_map/ppermute | solution.py:28
  18.3 16.9 %collective-permute-start.1 = (bf16[1040,128]{1,0:T(8,128)(2,1)}, bf16[1040,128]{1,0:T(8,128)(2,1)S(1)}, u32[]{:S(2)}, u32[]{:S(2)}) collective-permute-start(bf16[1040,128]{1,0:T(8,128)(2,1)} %get-tuple-element.33), channel_id=1, source_target_pairs={{0,224},{1,225},{2,226},{3,227},{4,228},{5,229},{6,230},{7,231},{8... | collective-permute-start | bytes 798728 | tf_op jit(solution)/shard_map/ppermute | solution.py:28
  18.3 19.8 %collective-permute-start.2 = (bf16[1040,128]{1,0:T(8,128)(2,1)S(1)}, bf16[1040,128]{1,0:T(8,128)(2,1)S(1)}, u32[]{:S(2)}, u32[]{:S(2)}) collective-permute-start(bf16[1040,128]{1,0:T(8,128)(2,1)S(1)} %get-tuple-element.34), channel_id=1, source_target_pairs={{0,224},{1,225},{2,226},{3,227},{4,228},{5,229},{6,230},{7,231},{8... | collective-permute-start | bytes 798728 | tf_op jit(solution)/shard_map/ppermute | solution.py:28
  27.0 5.6 %copy-start = (bf16[1,1,9,8,128,128]{5,4,3,2,1,0:T(8,128)(2,1)S(1)}, bf16[1,1,9,8,128,128]{5,4,3,2,1,0:T(8,128)(2,1)}, u32[]{:S(2)}) copy-start(bf16[1,1,9,8,128,128]{5,4,3,2,1,0:T(8,128)(2,1)} %param.10) | copy-start | bytes 7077892
  27.0 5.6 %copy-start.5 = (s32[1,1,9,8]{2,3,1,0:T(8,128)S(1)}, s32[1,1,9,8]{2,3,1,0:T(8,128)}, u32[]{:S(2)}) copy-start(s32[1,1,9,8]{2,3,1,0:T(8,128)} %param.11) | copy-start | bytes 868
  27.0 5.6 %copy-start.6 = (s32[1,1,9,8]{2,3,1,0:T(8,128)S(1)}, s32[1,1,9,8]{2,3,1,0:T(8,128)}, u32[]{:S(2)}) copy-start(s32[1,1,9,8]{2,3,1,0:T(8,128)} %param.12) | copy-start | bytes 868
  27.0 5.6 %copy-start.7 = (s32[1,1,9]{2,1,0:T(1,128)S(1)}, s32[1,1,9]{2,1,0:T(1,128)}, u32[]{:S(2)}) copy-start(s32[1,1,9]{2,1,0:T(1,128)} %param.13) | copy-start | bytes 112
  33.8 14.3 %copy-start.2 = (bf16[256,256]{1,0:T(8,128)(2,1)S(1)}, bf16[256,256]{1,0:T(8,128)(2,1)}, u32[]{:S(2)}) copy-start(bf16[256,256]{1,0:T(8,128)(2,1)} %table_ref.1) | copy-start | bytes 393220
  41.4 9.6 %collective-permute-start.7 = (bf16[256,256]{1,0:T(8,128)(2,1)S(1)}, bf16[256,256]{1,0:T(8,128)(2,1)S(1)}, u32[]{:S(2)}, u32[]{:S(2)}) collective-permute-start(bf16[256,256]{1,0:T(8,128)(2,1)S(1)} %get-tuple-element.47), channel_id=1, source_target_pairs={{0,20},{1,21},{2,22},{3,23},{4,16},{5,17},{6,18},{7,19},{8,28},{9,... | collective-permute-start | bytes 393224 | tf_op jit(solution)/shard_map/ppermute | solution.py:28
  41.4 9.5 %collective-permute-start.8 = (bf16[256,256]{1,0:T(8,128)(2,1)S(1)}, bf16[256,256]{1,0:T(8,128)(2,1)S(1)}, u32[]{:S(2)}, u32[]{:S(2)}) collective-permute-start(bf16[256,256]{1,0:T(8,128)(2,1)S(1)} %get-tuple-element.48), channel_id=1, source_target_pairs={{0,244},{1,245},{2,246},{3,247},{4,240},{5,241},{6,242},{7,243},{8... | collective-permute-start | bytes 393224 | tf_op jit(solution)/shard_map/ppermute | solution.py:28
  45.6 5.4 %collective-permute-start.5 = (bf16[256,256]{1,0:T(8,128)(2,1)S(1)}, bf16[256,256]{1,0:T(8,128)(2,1)S(1)}, u32[]{:S(2)}, u32[]{:S(2)}) collective-permute-start(bf16[256,256]{1,0:T(8,128)(2,1)S(1)} %get-tuple-element.45), channel_id=1, source_target_pairs={{0,32},{1,33},{2,34},{3,35},{4,36},{5,37},{6,38},{7,39},{8,40},{9,... | collective-permute-start | bytes 393224 | tf_op jit(solution)/shard_map/ppermute | solution.py:28
  48.1 6.2 %collective-permute-start.6 = (bf16[256,256]{1,0:T(8,128)(2,1)S(1)}, bf16[256,256]{1,0:T(8,128)(2,1)S(1)}, u32[]{:S(2)}, u32[]{:S(2)}) collective-permute-start(bf16[256,256]{1,0:T(8,128)(2,1)S(1)} %get-tuple-element.46), channel_id=1, source_target_pairs={{0,224},{1,225},{2,226},{3,227},{4,228},{5,229},{6,230},{7,231},{8... | collective-permute-start | bytes 393224 | tf_op jit(solution)/shard_map/ppermute | solution.py:28

commit v8 on v7

--- a/solution.py
+++ b/solution.py
@@ -44,26 +44,26 @@
 
 def message_slots(core):
     return [
-        [(REACH - 1, core)],
         pair_slots(3, core),
         pair_slots(1, core),
+        [(REACH - 1, core)],
         [(0, core)],
         [(1 + (REACH - 3) * core, 1 - core)],
     ]
 
 
 HOPS = [
-    lambda core: 2,
     lambda core: 1,
     lambda core: -1,
+    lambda core: 2,
     lambda core: -2,
     lambda core: 4 * core - 2,
 ]
-LENGTHS = [SLOTS, PAIR, PAIR, SLOTS, SLOTS]
-
-
-def pack_kernel(at_ref, dst_ref, src_ref, count_ref, tiles_ref, rows_ref, *rest):
-    outs, (repeated, sems) = rest[: len(HOPS)], rest[len(HOPS) :]
+LENGTHS = [PAIR, PAIR, SLOTS, SLOTS, SLOTS]
+
+
+def pack_kernel(at_ref, dst_ref, src_ref, count_ref, tiles_ref, *rest):
+    outs, sems = rest[: len(HOPS)], rest[len(HOPS)]
     lane = lax.broadcasted_iota(jnp.int32, (TAIL, TILE), 1)
     line = lax.broadcasted_iota(jnp.int32, (TAIL, TILE), 0)
     slots = message_slots(at_ref[0])
@@ -79,8 +79,6 @@
         )
     for copy in copies:
         copy.start()
-    for n in range(repeated.shape[0]):
-        repeated[n] = rows_ref[...]
     for n, length in enumerate(LENGTHS):
         held, rows = places(slots[n], dst_ref, src_ref, count_ref)
         tail = jnp.zeros((TAIL, TILE), jnp.int32)
@@ -101,17 +99,16 @@
     return [pltpu.with_memory_space_constraint(array, space) for array in arrays]
 
 
-def pack_tiles(at, dst, src, count, tiles, rows, times):
+def pack_tiles(at, dst, src, count, tiles):
     return pl.pallas_call(
         pack_kernel,
-        in_specs=[SMEM, SMEM, SMEM, SMEM, HBM, VMEM],
-        out_specs=[VMEM] * (len(LENGTHS) + 1),
-        out_shape=[pltpu.VMEM((length * TILE + TAIL, TILE), jnp.bfloat16) for length in LENGTHS]
-        + [pltpu.VMEM((times,) + rows.shape, rows.dtype)],
+        in_specs=[SMEM, SMEM, SMEM, SMEM, HBM],
+        out_specs=[VMEM] * len(LENGTHS),
+        out_shape=[pltpu.VMEM((length * TILE + TAIL, TILE), jnp.bfloat16) for length in LENGTHS],
         scratch_shapes=[pltpu.SemaphoreType.DMA((len(LENGTHS),))],
         compiler_params=pltpu.CompilerParams(vmem_limit_bytes=VMEM_LIMIT),
         name="pack_tiles",
-    )(at, *in_space(pltpu.HBM, dst, src, count, tiles), rows)
+    )(at, *in_space(pltpu.HBM, dst, src, count, tiles))
 
 
 def products(held, rows, tiles, sources):
@@ -257,6 +254,7 @@
         out_specs=[VMEM] * 2,
         out_shape=[pltpu.VMEM((SPLITS, 1, OUTPAD), jnp.bfloat16)] * 2,
         compiler_params=pltpu.CompilerParams(vmem_limit_bytes=VMEM_LIMIT),
+        cost_estimate=pl.CostEstimate(flops=10000000000, bytes_accessed=1, transcendentals=0),
         name="as_columns",
     )(left, right)
 
@@ -346,8 +344,10 @@
     nc = lax.axis_size("cset")
     at = (lax.axis_index("blk") % 2).astype(jnp.int32)[None]
 
-    *messages, copies = pack_tiles(at, dst, src, count, tiles_all, passive_table, nc)
+    messages = pack_tiles(at, dst, src, count, tiles_all)
+    *messages, passive_table = lax.optimization_barrier((*messages, passive_table))
     messages = [routed(message, hops) for message, hops in zip(messages, HOPS)]
+    copies = jnp.broadcast_to(passive_table[None], (nc,) + passive_table.shape)
     own_rows = lax.all_to_all(copies, "cset", split_axis=0, concat_axis=0, tiled=True)
     own_rows = own_rows.reshape(-1, passive_table.shape[1])
     groups = [[b, b + 1] for b in range(0, lax.axis_size("blk"), 2)]
@@ -359,7 +359,7 @@
     left, right = as_columns(split_active, split_passive)
     own = sum_own(at, dst, src, count, sources, tiles_all)
     sources, own, left, right = lax.optimization_barrier((sources, own, left, right))
-    far_up, near_up, near_down, far_down, odd = messages
+    near_up, near_down, far_up, far_down, odd = messages
     far_below, far_above = sum_away(
         sum_far_kernel, at, sources, (far_up, far_down, odd), "sum_far"
     )

time: 71.8 us -> 74.4 us (1.036)
  the two profiles are of different devices: /device:TPU:96 before, /device:TPU:2 now
where the time goes in v8:
time: 74.4 us; the launch traced here: 74 us
  starting transfers between devices  26.8 us (36%)
  blocking collectives  17.4 us (23%)
  Pallas kernels  14.1 us (19%)
  waiting for transfers between devices  12.3 us (17%)
  local copies, waits for them, and re-layouts  3.23 us (4%)
    ppermute x9, starting transfers between devices, routed(): return lax.ppermute(block, ('blk', 'cset'), route)  22 us
    all_to_all x1, waiting for transfers between devices, local(): lax.all_to_all(copies, 'cset', split_axis=0, concat_axis=0, tiled=True)  12.3 us
    all_to_all x1, blocking collectives, local(): lax.all_to_all(joined, 'cset', split_axis=0, concat_axis=0, tiled=True)  11.8 us
    all_to_all x1, blocking collectives, local(): lax.all_to_all(twice, 'blk', split_axis=0, concat_axis=0, tiled=True, axi...  5.55 us
    all_to_all x1, starting transfers between devices, local(): lax.all_to_all(copies, 'cset', split_axis=0, concat_axis=0, tiled=True)  4.83 us
    pallas_call x1, Pallas kernels, join(): pl.pallas_call(join_kernel, in_specs=[VMEM] * 7, out_specs=VMEM, out_shap...  3.4 us
    pallas_call x2, Pallas kernels, sum_away(): pl.pallas_call(kernel, in_specs=[SMEM] + [VMEM] * (1 + len(messages)), ou...  3.26 us
    pallas_call x1, Pallas kernels, pack_tiles(): pl.pallas_call(pack_kernel, in_specs=[SMEM, SMEM, SMEM, SMEM, HBM], out_s...  3.2 us
  transfers between devices with their start and end apart: 10, of which 1 were waited for; matrix products, arithmetic and copies ran while one was open for 3% of the time, Pallas kernels for 8%

profile of v8, /device:TPU:2, one launch (start us, length us, event | category | flops | bytes accessed | tf_op | source)
XLA Modules:
  0.0 74.0 jit_solution(5638906917410486687)
XLA Ops:
  0.0 0.0 copy-start.7
  0.0 0.0 copy-start.5
  0.0 0.0 copy-start.6
  0.0 3.2 %pack_tiles.1 = (bf16[2064,128]{1,0:T(8,128)(2,1)S(1)}, bf16[2064,128]{1,0:T(8,128)(2,1)S(1)}, bf16[1040,128]{1,0:T(8,128)(2,1)}, bf16[1040,128]{1,0:T(8,128)(2,1)}, bf16[1040,128]{1,0:T(8,128)(2,1)S(1)}) custom-call(s32[1]{0:T(128)} %bitcast.at_ref, s32[8,9]{1,0:T(8,128)} %bitcast.17, s32[8,9]{1,0:T(8,128)} %bitcast.19, s32[9]{0:T(128)} %bitcast.21, ...), custom_call_target="tpu_custom_call" | custom-call | tf_op jit(solution)/shard_map/pack_tiles/pallas_call | solution.py:103
  3.2 2.0 %collective-permute-start = (bf16[1040,128]{1,0:T(8,128)(2,1)}, bf16[1040,128]{1,0:T(8,128)(2,1)S(1)}, u32[]{:S(2)}, u32[]{:S(2)}) collective-permute-start(bf16[1040,128]{1,0:T(8,128)(2,1)} %get-tuple-element.42), channel_id=1, source_target_pairs={{0,32},{1,33},{2,34},{3,35},{4,36},{5,37},{6,38},{7,39},{8,40},{9,... | collective-permute-start | bytes 798728 | tf_op jit(solution)/shard_map/ppermute | solution.py:28
  5.2 4.0 %collective-permute-start.1 = (bf16[1040,128]{1,0:T(8,128)(2,1)}, bf16[1040,128]{1,0:T(8,128)(2,1)S(1)}, u32[]{:S(2)}, u32[]{:S(2)}) collective-permute-start(bf16[1040,128]{1,0:T(8,128)(2,1)} %get-tuple-element.43), channel_id=1, source_target_pairs={{0,224},{1,225},{2,226},{3,227},{4,228},{5,229},{6,230},{7,231},{8... | collective-permute-start | bytes 798728 | tf_op jit(solution)/shard_map/ppermute | solution.py:28
  9.2 1.9 %collective-permute-start.2 = (bf16[1040,128]{1,0:T(8,128)(2,1)S(1)}, bf16[1040,128]{1,0:T(8,128)(2,1)S(1)}, u32[]{:S(2)}, u32[]{:S(2)}) collective-permute-start(bf16[1040,128]{1,0:T(8,128)(2,1)S(1)} %get-tuple-element.44), channel_id=1, source_target_pairs={{0,224},{1,225},{2,226},{3,227},{4,228},{5,229},{6,230},{7,231},{8... | collective-permute-start | bytes 798728 | tf_op jit(solution)/shard_map/ppermute | solution.py:28
  11.2 3.0 %collective-permute-start.3 = (bf16[2064,128]{1,0:T(8,128)(2,1)S(1)}, bf16[2064,128]{1,0:T(8,128)(2,1)S(1)}, u32[]{:S(2)}, u32[]{:S(2)}) collective-permute-start(bf16[2064,128]{1,0:T(8,128)(2,1)S(1)} %get-tuple-element.48), channel_id=1, source_target_pairs={{0,20},{1,21},{2,22},{3,23},{4,16},{5,17},{6,18},{7,19},{8,28},{9,... | collective-permute-start | bytes 1585160 | tf_op jit(solution)/shard_map/ppermute | solution.py:28
  14.2 2.3 %collective-permute-start.4 = (bf16[2064,128]{1,0:T(8,128)(2,1)S(1)}, bf16[2064,128]{1,0:T(8,128)(2,1)S(1)}, u32[]{:S(2)}, u32[]{:S(2)}) collective-permute-start(bf16[2064,128]{1,0:T(8,128)(2,1)S(1)} %get-tuple-element.49), channel_id=1, source_target_pairs={{0,244},{1,245},{2,246},{3,247},{4,240},{5,241},{6,242},{7,243},{8... | collective-permute-start | bytes 1585160 | tf_op jit(solution)/shard_map/ppermute | solution.py:28
  16.5 0.0 copy-done.7
  16.5 1.0 %broadcast_in_dim.17 = bf16[8,256,256]{2,1,0:T(8,128)(2,1)} broadcast(bf16[256,256]{1,0:T(8,128)(2,1)S(1)} %copy-done.7), dimensions={1,2} | broadcast | bytes 1179648 | tf_op jit(solution)/shard_map/broadcast_in_dim | solution.py:350
  17.6 4.8 %all-to-all-start = ((bf16[8,256,256]{2,1,0:T(8,128)(2,1)}), bf16[8,256,256]{2,1,0:T(8,128)(2,1)}, u32[]{:S(2)}, u32[]{:S(2)}) async-start(bf16[8,256,256]{2,1,0:T(8,128)(2,1)} %broadcast_in_dim.17), calls=%async_computation | async-start | bytes 2097152 | tf_op jit(solution)/shard_map/all_to_all | solution.py:351
  22.4 0.0 copy-done.5
  22.4 0.0 copy-done.6
  22.4 0.1 as_columns.1
  22.6 12.3 %all-to-all-done = bf16[8,256,256]{2,1,0:T(8,128)(2,1)} async-done(((bf16[8,256,256]{2,1,0:T(8,128)(2,1)}), bf16[8,256,256]{2,1,0:T(8,128)(2,1)}, u32[]{:S(2)}, u32[]{:S(2)}) %all-to-all-start) | async-done | bytes 1048608 | tf_op jit(solution)/shard_map/all_to_all | solution.py:351
  34.9 1.4 %broadcast_in_dim.19 = bf16[2,2048,256]{2,1,0:T(8,128)(2,1)S(1)} broadcast(bf16[2048,256]{1,0:T(8,128)(2,1)} %bitcast.7), dimensions={1,2} | broadcast | bytes 3145728 | tf_op jit(solution)/shard_map/broadcast_in_dim | solution.py:354
  36.2 0.0 copy-start
  36.2 0.0 copy-start.2
  36.3 0.0 copy-start.3
  36.3 0.0 copy-start.4
  36.3 5.5 %all_to_all.15 = bf16[2,2048,256]{2,1,0:T(8,128)(2,1)S(1)} all-to-all(bf16[2,2048,256]{2,1,0:T(8,128)(2,1)S(1)} %broadcast_in_dim.19), channel_id=1, replica_groups={{0,8},{16,24},{32,40},{48,56},{64,72},{80,88},{96,104},{112,120},{128,1..., dimensions={0} | all-to-all | bytes 4194304 | tf_op jit(solution)/shard_map/all_to_all | solution.py:355
  41.8 0.0 copy-done
  41.8 0.0 copy-done.2
  41.8 0.0 copy-done.3
  41.8 0.0 copy-done.4
  41.9 1.2 %sum_own.1.own_ref = f32[256,256]{1,0:T(8,128)S(1)} custom-call(s32[1]{0:T(128)} %bitcast.at_ref, s32[8,9]{1,0:T(8,128)S(1)} %bitcast.18, s32[8,9]{1,0:T(8,128)S(1)} %bitcast.20, s32[9]{0:T(128)S(1)} %bitcast.22, bf16[4096,256]{1,0:T(8,128)(2,1)S(1)} %bitcast.12, bf16[9216,128]{1,0:T(8,128)(2,1)S(1)} %bitcast.16), custom_call_target="tpu_custom_call" | custom-call | flops 268435456 | bytes 2621440 | tf_op jit(solution)/shard_map/sum_own/pallas_call | solution.py:209
  43.0 0.0 copy-start.1
  43.1 0.0 collective-permute-done.from_below
  43.1 0.0 collective-permute-done.1.from_above
  43.1 0.0 collective-permute-done.2.odd
  43.1 1.7 %sum_far.1 = (bf16[256,256]{1,0:T(8,128)(2,1)S(1)}, bf16[256,256]{1,0:T(8,128)(2,1)S(1)}) custom-call(s32[1]{0:T(128)} %bitcast.at_ref, bf16[4096,256]{1,0:T(8,128)(2,1)S(1)} %bitcast.13, bf16[1040,128]{1,0:T(8,128)(2,1)S(1)} %collective-permute-done.from_below, bf16[1040,128]{1,0:T(8,128)(2,1)S(1)} %collective-permute-done.1.from_above, ...), custom_call_target="tpu_custom_call" | custom-call | flops 536870912 | bytes 3145728 | tf_op jit(solution)/shard_map/sum_far/pallas_call | solution.py:176
  44.8 0.0 collective-permute-done.3.from_below
  44.8 0.0 collective-permute-done.4.from_above
  44.8 1.6 %sum_near.1 = (bf16[256,256]{1,0:T(8,128)(2,1)S(1)}, bf16[256,256]{1,0:T(8,128)(2,1)S(1)}) custom-call(s32[1]{0:T(128)} %bitcast.at_ref, bf16[4096,256]{1,0:T(8,128)(2,1)S(1)} %bitcast.14, bf16[2064,128]{1,0:T(8,128)(2,1)S(1)} %collective-permute-done.3.from_below, bf16[2064,128]{1,0:T(8,128)(2,1)S(1)} %collective-permute-done.4.from_above), custom_call_target="tpu_custom_call" | custom-call | flops 536870912 | bytes 3145728 | tf_op jit(solution)/shard_map/sum_near/pallas_call | solution.py:176
  46.4 0.7 collective-permute-start.7
  47.1 4.7 %collective-permute-start.8 = (bf16[256,256]{1,0:T(8,128)(2,1)S(1)}, bf16[256,256]{1,0:T(8,128)(2,1)S(1)}, u32[]{:S(2)}, u32[]{:S(2)}) collective-permute-start(bf16[256,256]{1,0:T(8,128)(2,1)S(1)} %get-tuple-element.58), channel_id=1, source_target_pairs={{0,244},{1,245},{2,246},{3,247},{4,240},{5,241},{6,242},{7,243},{8... | collective-permute-start | bytes 393224 | tf_op jit(solution)/shard_map/ppermute | solution.py:28
  51.8 0.0 collective-permute-start.5
  51.8 3.2 %collective-permute-start.6 = (bf16[256,256]{1,0:T(8,128)(2,1)S(1)}, bf16[256,256]{1,0:T(8,128)(2,1)S(1)}, u32[]{:S(2)}, u32[]{:S(2)}) collective-permute-start(bf16[256,256]{1,0:T(8,128)(2,1)S(1)} %get-tuple-element.56), channel_id=1, source_target_pairs={{0,224},{1,225},{2,226},{3,227},{4,228},{5,229},{6,230},{7,231},{8... | collective-permute-start | bytes 393224 | tf_op jit(solution)/shard_map/ppermute | solution.py:28
  55.1 0.0 copy-done.1
  55.1 2.9 %pick_active.1.picked_ref = bf16[20,256,1024]{2,1,0:T(8,128)(2,1)S(1)} custom-call(bf16[20,1,1024]{2,1,0:T(2,128)(2,1)S(1)} %get-tuple-element.53.columns_ref, bf16[256,256]{1,0:T(8,128)(2,1)S(1)} %copy-done.1), custom_call_target="tpu_custom_call" | custom-call | flops 2684354560 | bytes 10485760 | tf_op jit(solution)/shard_map/pick_active/pallas_call | solution.py:278
  58.0 0.0 collective-permute-done.7.n2
  58.0 0.0 collective-permute-done.8.n3
  58.0 0.0 collective-permute-done.5.n0
  58.0 0.0 collective-permute-done.6.n1
  58.0 3.4 %join_sets.1 = bf16[8,256,128]{2,1,0:T(8,128)(2,1)S(1)} custom-call(bf16[20,1,1024]{2,1,0:T(2,128)(2,1)S(1)} %get-tuple-element.40.columns_ref, bf16[20,256,1024]{2,1,0:T(8,128)(2,1)S(1)} %pick_active.1.picked_ref, f32[256,256]{1,0:T(8,128)S(1)} %sum_own.1.own_ref, bf16[256,256]{1,0:T(8,128)(2,1)S(1)} %collective-permute-done.5.n0, ...), custom_call_target="tpu_custom_call" | custom-call | flops 2684354560 | bytes 524288 | tf_op jit(solution)/shard_map/join_sets/pallas_call | solution.py:317
  61.4 11.8 %all_to_all.16 = bf16[8,256,128]{2,1,0:T(8,128)(2,1)S(1)} all-to-all(bf16[8,256,128]{2,1,0:T(8,128)(2,1)S(1)} %join_sets.1), channel_id=1, replica_groups=mesh['blk'=32,'cset'=8] {'cset'}, dimensions={0} | all-to-all | bytes 1048576 | tf_op jit(solution)/shard_map/all_to_all | solution.py:379
  73.2 0.8 %copy.10 = bf16[2048,128]{1,0:T(8,128)(2,1)} copy(bf16[2048,128]{1,0:T(8,128)(2,1)S(1)} %bitcast.23) | data formatting | bytes 1048576
Async XLA Ops:
  0.0 16.5 %copy-start.7 = (bf16[256,256]{1,0:T(8,128)(2,1)S(1)}, bf16[256,256]{1,0:T(8,128)(2,1)}, u32[]{:S(2)}) copy-start(bf16[256,256]{1,0:T(8,128)(2,1)} %param.9) | copy-start | bytes 393220
  0.0 22.4 %copy-start.5 = (s32[20,924]{1,0:T(8,128)S(1)}, s32[20,924]{1,0:T(8,128)}, u32[]{:S(2)}) copy-start(s32[20,924]{1,0:T(8,128)} %left_ref.1) | copy-start | bytes 221764
  0.0 22.4 %copy-start.6 = (s32[20,924]{1,0:T(8,128)S(1)}, s32[20,924]{1,0:T(8,128)}, u32[]{:S(2)}) copy-start(s32[20,924]{1,0:T(8,128)} %right_ref.1) | copy-start | bytes 221764
  3.2 39.8 %collective-permute-start = (bf16[1040,128]{1,0:T(8,128)(2,1)}, bf16[1040,128]{1,0:T(8,128)(2,1)S(1)}, u32[]{:S(2)}, u32[]{:S(2)}) collective-permute-start(bf16[1040,128]{1,0:T(8,128)(2,1)} %get-tuple-element.42), channel_id=1, source_target_pairs={{0,32},{1,33},{2,34},{3,35},{4,36},{5,37},{6,38},{7,39},{8,40},{9,... | collective-permute-start | bytes 798728 | tf_op jit(solution)/shard_map/ppermute | solution.py:28
  5.2 37.9 %collective-permute-start.1 = (bf16[1040,128]{1,0:T(8,128)(2,1)}, bf16[1040,128]{1,0:T(8,128)(2,1)S(1)}, u32[]{:S(2)}, u32[]{:S(2)}) collective-permute-start(bf16[1040,128]{1,0:T(8,128)(2,1)} %get-tuple-element.43), channel_id=1, source_target_pairs={{0,224},{1,225},{2,226},{3,227},{4,228},{5,229},{6,230},{7,231},{8... | collective-permute-start | bytes 798728 | tf_op jit(solution)/shard_map/ppermute | solution.py:28
  9.2 33.8 %collective-permute-start.2 = (bf16[1040,128]{1,0:T(8,128)(2,1)S(1)}, bf16[1040,128]{1,0:T(8,128)(2,1)S(1)}, u32[]{:S(2)}, u32[]{:S(2)}) collective-permute-start(bf16[1040,128]{1,0:T(8,128)(2,1)S(1)} %get-tuple-element.44), channel_id=1, source_target_pairs={{0,224},{1,225},{2,226},{3,227},{4,228},{5,229},{6,230},{7,231},{8... | collective-permute-start | bytes 798728 | tf_op jit(solution)/shard_map/ppermute | solution.py:28
  11.2 33.6 %collective-permute-start.3 = (bf16[2064,128]{1,0:T(8,128)(2,1)S(1)}, bf16[2064,128]{1,0:T(8,128)(2,1)S(1)}, u32[]{:S(2)}, u32[]{:S(2)}) collective-permute-start(bf16[2064,128]{1,0:T(8,128)(2,1)S(1)} %get-tuple-element.48), channel_id=1, source_target_pairs={{0,20},{1,21},{2,22},{3,23},{4,16},{5,17},{6,18},{7,19},{8,28},{9,... | collective-permute-start | bytes 1585160 | tf_op jit(solution)/shard_map/ppermute | solution.py:28
  14.2 30.6 %collective-permute-start.4 = (bf16[2064,128]{1,0:T(8,128)(2,1)S(1)}, bf16[2064,128]{1,0:T(8,128)(2,1)S(1)}, u32[]{:S(2)}, u32[]{:S(2)}) collective-permute-start(bf16[2064,128]{1,0:T(8,128)(2,1)S(1)} %get-tuple-element.49), channel_id=1, source_target_pairs={{0,244},{1,245},{2,246},{3,247},{4,240},{5,241},{6,242},{7,243},{8... | collective-permute-start | bytes 1585160 | tf_op jit(solution)/shard_map/ppermute | solution.py:28
  17.6 17.3 %all-to-all-start = ((bf16[8,256,256]{2,1,0:T(8,128)(2,1)}), bf16[8,256,256]{2,1,0:T(8,128)(2,1)}, u32[]{:S(2)}, u32[]{:S(2)}) async-start(bf16[8,256,256]{2,1,0:T(8,128)(2,1)} %broadcast_in_dim.17), calls=%async_computation | async-start | bytes 2097152 | tf_op jit(solution)/shard_map/all_to_all | solution.py:351
  36.2 5.6 %copy-start = (bf16[1,1,9,8,128,128]{5,4,3,2,1,0:T(8,128)(2,1)S(1)}, bf16[1,1,9,8,128,128]{5,4,3,2,1,0:T(8,128)(2,1)}, u32[]{:S(2)}) copy-start(bf16[1,1,9,8,128,128]{5,4,3,2,1,0:T(8,128)(2,1)} %param.10) | copy-start | bytes 7077892
  36.2 5.6 %copy-start.2 = (s32[1,1,9,8]{2,3,1,0:T(8,128)S(1)}, s32[1,1,9,8]{2,3,1,0:T(8,128)}, u32[]{:S(2)}) copy-start(s32[1,1,9,8]{2,3,1,0:T(8,128)} %param.11) | copy-start | bytes 868
  36.3 5.6 %copy-start.3 = (s32[1,1,9,8]{2,3,1,0:T(8,128)S(1)}, s32[1,1,9,8]{2,3,1,0:T(8,128)}, u32[]{:S(2)}) copy-start(s32[1,1,9,8]{2,3,1,0:T(8,128)} %param.12) | copy-start | bytes 868
  36.3 5.6 %copy-start.4 = (s32[1,1,9]{2,1,0:T(1,128)S(1)}, s32[1,1,9]{2,1,0:T(1,128)}, u32[]{:S(2)}) copy-start(s32[1,1,9]{2,1,0:T(1,128)} %param.13) | copy-start | bytes 112
  43.0 12.0 %copy-start.1 = (bf16[256,256]{1,0:T(8,128)(2,1)S(1)}, bf16[256,256]{1,0:T(8,128)(2,1)}, u32[]{:S(2)}) copy-start(bf16[256,256]{1,0:T(8,128)(2,1)} %table_ref.1) | copy-start | bytes 393220
  46.4 11.6 %collective-permute-start.7 = (bf16[256,256]{1,0:T(8,128)(2,1)S(1)}, bf16[256,256]{1,0:T(8,128)(2,1)S(1)}, u32[]{:S(2)}, u32[]{:S(2)}) collective-permute-start(bf16[256,256]{1,0:T(8,128)(2,1)S(1)} %get-tuple-element.57), channel_id=1, source_target_pairs={{0,20},{1,21},{2,22},{3,23},{4,16},{5,17},{6,18},{7,19},{8,28},{9,... | collective-permute-start | bytes 393224 | tf_op jit(solution)/shard_map/ppermute | solution.py:28
  47.1 10.9 %collective-permute-start.8 = (bf16[256,256]{1,0:T(8,128)(2,1)S(1)}, bf16[256,256]{1,0:T(8,128)(2,1)S(1)}, u32[]{:S(2)}, u32[]{:S(2)}) collective-permute-start(bf16[256,256]{1,0:T(8,128)(2,1)S(1)} %get-tuple-element.58), channel_id=1, source_target_pairs={{0,244},{1,245},{2,246},{3,247},{4,240},{5,241},{6,242},{7,243},{8... | collective-permute-start | bytes 393224 | tf_op jit(solution)/shard_map/ppermute | solution.py:28
  51.8 6.2 %collective-permute-start.5 = (bf16[256,256]{1,0:T(8,128)(2,1)S(1)}, bf16[256,256]{1,0:T(8,128)(2,1)S(1)}, u32[]{:S(2)}, u32[]{:S(2)}) collective-permute-start(bf16[256,256]{1,0:T(8,128)(2,1)S(1)} %get-tuple-element.55), channel_id=1, source_target_pairs={{0,32},{1,33},{2,34},{3,35},{4,36},{5,37},{6,38},{7,39},{8,40},{9,... | collective-permute-start | bytes 393224 | tf_op jit(solution)/shard_map/ppermute | solution.py:28
  51.8 6.2 %collective-permute-start.6 = (bf16[256,256]{1,0:T(8,128)(2,1)S(1)}, bf16[256,256]{1,0:T(8,128)(2,1)S(1)}, u32[]{:S(2)}, u32[]{:S(2)}) collective-permute-start(bf16[256,256]{1,0:T(8,128)(2,1)S(1)} %get-tuple-element.56), channel_id=1, source_target_pairs={{0,224},{1,225},{2,226},{3,227},{4,228},{5,229},{6,230},{7,231},{8... | collective-permute-start | bytes 393224 | tf_op jit(solution)/shard_map/ppermute | solution.py:28

commit v9 on v8

--- a/solution.py
+++ b/solution.py
@@ -1,3 +1,5 @@
+import functools
+
 import jax
 import jax.numpy as jnp
 from jax import lax
@@ -62,13 +64,14 @@
 LENGTHS = [PAIR, PAIR, SLOTS, SLOTS, SLOTS]
 
 
-def pack_kernel(at_ref, dst_ref, src_ref, count_ref, tiles_ref, *rest):
-    outs, sems = rest[: len(HOPS)], rest[len(HOPS)]
+def pack_kernel(which, at_ref, dst_ref, src_ref, count_ref, tiles_ref, *rest):
+    outs, sems = rest[: len(which)], rest[len(which)]
+    lengths = [LENGTHS[n] for n in which]
     lane = lax.broadcasted_iota(jnp.int32, (TAIL, TILE), 1)
     line = lax.broadcasted_iota(jnp.int32, (TAIL, TILE), 0)
-    slots = message_slots(at_ref[0])
+    slots = [message_slots(at_ref[0])[n] for n in which]
     copies = []
-    for n, length in enumerate(LENGTHS):
+    for n, length in enumerate(lengths):
         begin = pl.multiple_of(slots[n][0][0] * (SLOTS * TILE), SLOTS * TILE)
         copies.append(
             pltpu.make_async_copy(
@@ -79,7 +82,7 @@
         )
     for copy in copies:
         copy.start()
-    for n, length in enumerate(LENGTHS):
+    for n, length in enumerate(lengths):
         held, rows = places(slots[n], dst_ref, src_ref, count_ref)
         tail = jnp.zeros((TAIL, TILE), jnp.int32)
         for t in range(length):
@@ -99,15 +102,19 @@
     return [pltpu.with_memory_space_constraint(array, space) for array in arrays]
 
 
-def pack_tiles(at, dst, src, count, tiles):
-    return pl.pallas_call(
-        pack_kernel,
+def pack_tiles(which, at, dst, src, count, tiles, name):
+    shapes = [(LENGTHS[n] * TILE + TAIL, TILE) for n in which]
+    return pl.pallas_call(
+        functools.partial(pack_kernel, which),
         in_specs=[SMEM, SMEM, SMEM, SMEM, HBM],
-        out_specs=[VMEM] * len(LENGTHS),
-        out_shape=[pltpu.VMEM((length * TILE + TAIL, TILE), jnp.bfloat16) for length in LENGTHS],
-        scratch_shapes=[pltpu.SemaphoreType.DMA((len(LENGTHS),))],
-        compiler_params=pltpu.CompilerParams(vmem_limit_bytes=VMEM_LIMIT),
-        name="pack_tiles",
+        out_specs=[VMEM] * len(which),
+        out_shape=[pltpu.VMEM(shape, jnp.bfloat16) for shape in shapes],
+        scratch_shapes=[pltpu.SemaphoreType.DMA((len(which),))],
+        compiler_params=pltpu.CompilerParams(vmem_limit_bytes=VMEM_LIMIT),
+        cost_estimate=pl.CostEstimate(
+            flops=0, bytes_accessed=sum(2 * rows * cols for rows, cols in shapes), transcendentals=0
+        ),
+        name=name,
     )(at, *in_space(pltpu.HBM, dst, src, count, tiles))
 
 
@@ -344,9 +351,12 @@
     nc = lax.axis_size("cset")
     at = (lax.axis_index("blk") % 2).astype(jnp.int32)[None]
 
-    messages = pack_tiles(at, dst, src, count, tiles_all)
-    *messages, passive_table = lax.optimization_barrier((*messages, passive_table))
-    messages = [routed(message, hops) for message, hops in zip(messages, HOPS)]
+    near = pack_tiles((0, 1), at, dst, src, count, tiles_all, "pack_near")
+    *near, passive_table = lax.optimization_barrier((*near, passive_table))
+    left, right = as_columns(split_active, split_passive)
+    left, later = lax.optimization_barrier((left, at))
+    far = pack_tiles((2, 3, 4), later, dst, src, count, tiles_all, "pack_far")
+    messages = [routed(message, hops) for message, hops in zip((*near, *far), HOPS)]
     copies = jnp.broadcast_to(passive_table[None], (nc,) + passive_table.shape)
     own_rows = lax.all_to_all(copies, "cset", split_axis=0, concat_axis=0, tiled=True)
     own_rows = own_rows.reshape(-1, passive_table.shape[1])
@@ -356,9 +366,7 @@
         twice, "blk", split_axis=0, concat_axis=0, tiled=True, axis_index_groups=groups
     ).reshape(-1, own_rows.shape[1])
 
-    left, right = as_columns(split_active, split_passive)
-    own = sum_own(at, dst, src, count, sources, tiles_all)
-    sources, own, left, right = lax.optimization_barrier((sources, own, left, right))
+    sources, left, right = lax.optimization_barrier((sources, left, right))
     near_up, near_down, far_up, far_down, odd = messages
     far_below, far_above = sum_away(
         sum_far_kernel, at, sources, (far_up, far_down, odd), "sum_far"
@@ -369,6 +377,7 @@
     )
     near_below, near_above, left = lax.optimization_barrier((near_below, near_above, left))
     picked = pick_columns(active_table, left)
+    own = sum_own(at, dst, src, count, sources, tiles_all)
     parts = [
         routed(far_above, lambda core: 2),
         routed(far_below, lambda core: -2),

time: 74.4 us -> 70.5 us (0.948)
  waiting for transfers between devices: 12.3 us -> 7.92 us
  Pallas kernels: 14.1 us -> 15.8 us
  starting transfers between devices: 26.8 us -> 25.6 us
    all_to_all x1, waiting for transfers between devices: 12.3 us -> 7.9 us  [local(): lax.all_to_all(copies, 'cset', split_axis=0, concat_axis=0, tiled=True)]
    pallas_call x1 -> x2, Pallas kernels: 3.2 us -> 4.88 us  [pack_tiles(): pl.pallas_call(functools.partial(pack_kernel, which), in_specs=[SMEM, SME...]
    ppermute x9, starting transfers between devices: 22 us -> 20.8 us  [routed(): return lax.ppermute(block, ('blk', 'cset'), route)]
  transfers between devices with their start and end apart: 10 -> 10, of which waited for: 1 -> 1; matrix products, arithmetic and copies ran while one was open for 3% -> 3% of each run, Pallas kernels for 8% -> 12%
where the time goes in v9:
time: 70.5 us; the launch traced here: 70.2 us
  starting transfers between devices  25.6 us (36%)
  blocking collectives  17.4 us (25%)
  Pallas kernels  15.8 us (22%)
  waiting for transfers between devices  7.92 us (11%)
  local copies, waits for them, and re-layouts  3.23 us (5%)
    ppermute x9, starting transfers between devices, routed(): return lax.ppermute(block, ('blk', 'cset'), route)  20.8 us
    all_to_all x1, blocking collectives, local(): lax.all_to_all(joined, 'cset', split_axis=0, concat_axis=0, tiled=True)  12 us
    all_to_all x1, waiting for transfers between devices, local(): lax.all_to_all(copies, 'cset', split_axis=0, concat_axis=0, tiled=True)  7.9 us
    all_to_all x1, blocking collectives, local(): lax.all_to_all(twice, 'blk', split_axis=0, concat_axis=0, tiled=True, axi...  5.42 us
    pallas_call x2, Pallas kernels, pack_tiles(): pl.pallas_call(functools.partial(pack_kernel, which), in_specs=[SMEM, SME...  4.88 us
    all_to_all x1, starting transfers between devices, local(): lax.all_to_all(copies, 'cset', split_axis=0, concat_axis=0, tiled=True)  4.83 us
    pallas_call x1, Pallas kernels, join(): pl.pallas_call(join_kernel, in_specs=[VMEM] * 7, out_specs=VMEM, out_shap...  3.38 us
    pallas_call x2, Pallas kernels, sum_away(): pl.pallas_call(kernel, in_specs=[SMEM] + [VMEM] * (1 + len(messages)), ou...  3.28 us
  transfers between devices with their start and end apart: 10, of which 1 were waited for; matrix products, arithmetic and copies ran while one was open for 3% of the time, Pallas kernels for 12%

profile of v9, /device:TPU:2, one launch (start us, length us, event | category | flops | bytes accessed | tf_op | source)
XLA Modules:
  0.0 70.2 jit_solution(12145346999069838505)
XLA Ops:
  0.0 0.0 copy-start.7
  0.0 0.0 copy-start.5
  0.0 0.0 copy-start.6
  0.0 2.2 %pack_near.1 = (bf16[2064,128]{1,0:T(8,128)(2,1)S(1)}, bf16[2064,128]{1,0:T(8,128)(2,1)S(1)}) custom-call(s32[1]{0:T(128)} %bitcast.at_ref, s32[8,9]{1,0:T(8,128)} %bitcast.18, s32[8,9]{1,0:T(8,128)} %bitcast.21, s32[9]{0:T(128)} %bitcast.24, bf16[9216,128]{1,0:T(8,128)(2,1)} %bitcast.15), custom_call_target="tpu_custom_call" | custom-call | bytes 1056768 | tf_op jit(solution)/shard_map/pack_near/pallas_call | solution.py:107
  2.2 3.1 %collective-permute-start.3 = (bf16[2064,128]{1,0:T(8,128)(2,1)S(1)}, bf16[2064,128]{1,0:T(8,128)(2,1)S(1)}, u32[]{:S(2)}, u32[]{:S(2)}) collective-permute-start(bf16[2064,128]{1,0:T(8,128)(2,1)S(1)} %get-tuple-element.45), channel_id=1, source_target_pairs={{0,20},{1,21},{2,22},{3,23},{4,16},{5,17},{6,18},{7,19},{8,28},{9,... | collective-permute-start | bytes 1585160 | tf_op jit(solution)/shard_map/ppermute | solution.py:30
  5.3 5.4 %collective-permute-start.4 = (bf16[2064,128]{1,0:T(8,128)(2,1)S(1)}, bf16[2064,128]{1,0:T(8,128)(2,1)S(1)}, u32[]{:S(2)}, u32[]{:S(2)}) collective-permute-start(bf16[2064,128]{1,0:T(8,128)(2,1)S(1)} %get-tuple-element.46), channel_id=1, source_target_pairs={{0,244},{1,245},{2,246},{3,247},{4,240},{5,241},{6,242},{7,243},{8... | collective-permute-start | bytes 1585160 | tf_op jit(solution)/shard_map/ppermute | solution.py:30
  10.6 0.0 copy-done.7
  10.6 1.0 %broadcast_in_dim.17 = bf16[8,256,256]{2,1,0:T(8,128)(2,1)} broadcast(bf16[256,256]{1,0:T(8,128)(2,1)S(1)} %copy-done.7), dimensions={1,2} | broadcast | bytes 1179648 | tf_op jit(solution)/shard_map/broadcast_in_dim | solution.py:360
  11.7 4.8 %all-to-all-start = ((bf16[8,256,256]{2,1,0:T(8,128)(2,1)}), bf16[8,256,256]{2,1,0:T(8,128)(2,1)}, u32[]{:S(2)}, u32[]{:S(2)}) async-start(bf16[8,256,256]{2,1,0:T(8,128)(2,1)} %broadcast_in_dim.17), calls=%async_computation | async-start | bytes 2097152 | tf_op jit(solution)/shard_map/all_to_all | solution.py:361
  16.5 0.0 copy-done.5
  16.5 0.0 copy-done.6
  16.5 0.1 as_columns.1
  16.7 2.7 %pack_far.1 = (bf16[1040,128]{1,0:T(8,128)(2,1)}, bf16[1040,128]{1,0:T(8,128)(2,1)}, bf16[1040,128]{1,0:T(8,128)(2,1)S(1)}) custom-call(s32[1]{0:T(128)} %bitcast.at_ref, s32[8,9]{1,0:T(8,128)} %bitcast.19, s32[8,9]{1,0:T(8,128)} %bitcast.22, s32[9]{0:T(128)} %bitcast.25, bf16[9216,128]{1,0:T(8,128)(2,1)} %bitcast.16), custom_call_target="tpu_custom_call" | custom-call | bytes 798720 | tf_op jit(solution)/shard_map/pack_far/pallas_call | solution.py:107
  19.4 0.1 collective-permute-start
  19.5 3.2 %collective-permute-start.1 = (bf16[1040,128]{1,0:T(8,128)(2,1)}, bf16[1040,128]{1,0:T(8,128)(2,1)S(1)}, u32[]{:S(2)}, u32[]{:S(2)}) collective-permute-start(bf16[1040,128]{1,0:T(8,128)(2,1)} %get-tuple-element.40), channel_id=1, source_target_pairs={{0,224},{1,225},{2,226},{3,227},{4,228},{5,229},{6,230},{7,231},{8... | collective-permute-start | bytes 798728 | tf_op jit(solution)/shard_map/ppermute | solution.py:30
  22.7 0.4 collective-permute-start.2
  23.1 7.9 %all-to-all-done = bf16[8,256,256]{2,1,0:T(8,128)(2,1)} async-done(((bf16[8,256,256]{2,1,0:T(8,128)(2,1)}), bf16[8,256,256]{2,1,0:T(8,128)(2,1)}, u32[]{:S(2)}, u32[]{:S(2)}) %all-to-all-start) | async-done | bytes 1048608 | tf_op jit(solution)/shard_map/all_to_all | solution.py:361
  31.0 1.4 %broadcast_in_dim.19 = bf16[2,2048,256]{2,1,0:T(8,128)(2,1)S(1)} broadcast(bf16[2048,256]{1,0:T(8,128)(2,1)} %bitcast.7), dimensions={1,2} | broadcast | bytes 3145728 | tf_op jit(solution)/shard_map/broadcast_in_dim | solution.py:364
  32.4 5.4 %all_to_all.15 = bf16[2,2048,256]{2,1,0:T(8,128)(2,1)S(1)} all-to-all(bf16[2,2048,256]{2,1,0:T(8,128)(2,1)S(1)} %broadcast_in_dim.19), channel_id=1, replica_groups={{0,8},{16,24},{32,40},{48,56},{64,72},{80,88},{96,104},{112,120},{128,1..., dimensions={0} | all-to-all | bytes 4194304 | tf_op jit(solution)/shard_map/all_to_all | solution.py:365
  37.8 0.0 copy-start.1
  37.8 0.0 collective-permute-done.from_below
  37.8 0.0 collective-permute-done.1.from_above
  37.8 0.0 collective-permute-done.2.odd
  37.8 1.7 %sum_far.1 = (bf16[256,256]{1,0:T(8,128)(2,1)S(1)}, bf16[256,256]{1,0:T(8,128)(2,1)S(1)}) custom-call(s32[1]{0:T(128)} %bitcast.at_ref, bf16[4096,256]{1,0:T(8,128)(2,1)S(1)} %bitcast.12, bf16[1040,128]{1,0:T(8,128)(2,1)S(1)} %collective-permute-done.from_below, bf16[1040,128]{1,0:T(8,128)(2,1)S(1)} %collective-permute-done.1.from_above, ...), custom_call_target="tpu_custom_call" | custom-call | flops 536870912 | bytes 3145728 | tf_op jit(solution)/shard_map/sum_far/pallas_call | solution.py:183
  39.5 0.0 collective-permute-done.3.from_below
  39.5 0.0 collective-permute-done.4.from_above
  39.5 1.6 %sum_near.1 = (bf16[256,256]{1,0:T(8,128)(2,1)S(1)}, bf16[256,256]{1,0:T(8,128)(2,1)S(1)}) custom-call(s32[1]{0:T(128)} %bitcast.at_ref, bf16[4096,256]{1,0:T(8,128)(2,1)S(1)} %bitcast.13, bf16[2064,128]{1,0:T(8,128)(2,1)S(1)} %collective-permute-done.3.from_below, bf16[2064,128]{1,0:T(8,128)(2,1)S(1)} %collective-permute-done.4.from_above), custom_call_target="tpu_custom_call" | custom-call | flops 536870912 | bytes 3145728 | tf_op jit(solution)/shard_map/sum_near/pallas_call | solution.py:183
  41.1 0.0 copy-start
  41.1 0.0 copy-start.2
  41.2 0.0 copy-start.3
  41.2 0.0 copy-start.4
  41.2 0.1 collective-permute-start.7
  41.3 5.3 %collective-permute-start.8 = (bf16[256,256]{1,0:T(8,128)(2,1)S(1)}, bf16[256,256]{1,0:T(8,128)(2,1)S(1)}, u32[]{:S(2)}, u32[]{:S(2)}) collective-permute-start(bf16[256,256]{1,0:T(8,128)(2,1)S(1)} %get-tuple-element.54), channel_id=1, source_target_pairs={{0,244},{1,245},{2,246},{3,247},{4,240},{5,241},{6,242},{7,243},{8... | collective-permute-start | bytes 393224 | tf_op jit(solution)/shard_map/ppermute | solution.py:30
  46.6 0.0 collective-permute-start.5
  46.6 3.2 %collective-permute-start.6 = (bf16[256,256]{1,0:T(8,128)(2,1)S(1)}, bf16[256,256]{1,0:T(8,128)(2,1)S(1)}, u32[]{:S(2)}, u32[]{:S(2)}) collective-permute-start(bf16[256,256]{1,0:T(8,128)(2,1)S(1)} %get-tuple-element.52), channel_id=1, source_target_pairs={{0,224},{1,225},{2,226},{3,227},{4,228},{5,229},{6,230},{7,231},{8... | collective-permute-start | bytes 393224 | tf_op jit(solution)/shard_map/ppermute | solution.py:30
  49.8 0.0 copy-done.1
  49.8 2.9 %pick_active.1.picked_ref = bf16[20,256,1024]{2,1,0:T(8,128)(2,1)S(1)} custom-call(bf16[20,1,1024]{2,1,0:T(2,128)(2,1)S(1)} %get-tuple-element.50.columns_ref, bf16[256,256]{1,0:T(8,128)(2,1)S(1)} %copy-done.1), custom_call_target="tpu_custom_call" | custom-call | flops 2684354560 | bytes 10485760 | tf_op jit(solution)/shard_map/pick_active/pallas_call | solution.py:285
  52.8 0.0 copy-done
  52.8 0.0 copy-done.2
  52.8 0.0 copy-done.3
  52.8 0.0 copy-done.4
  52.8 1.2 %sum_own.1.own_ref = f32[256,256]{1,0:T(8,128)S(1)} custom-call(s32[1]{0:T(128)} %bitcast.at_ref, s32[8,9]{1,0:T(8,128)S(1)} %bitcast.20, s32[8,9]{1,0:T(8,128)S(1)} %bitcast.23, s32[9]{0:T(128)S(1)} %bitcast.26, bf16[4096,256]{1,0:T(8,128)(2,1)S(1)} %bitcast.14, bf16[9216,128]{1,0:T(8,128)(2,1)S(1)} %bitcast.17), custom_call_target="tpu_custom_call" | custom-call | flops 268435456 | bytes 2621440 | tf_op jit(solution)/shard_map/sum_own/pallas_call | solution.py:216
  54.0 0.0 collective-permute-done.7.n2
  54.0 0.0 collective-permute-done.8.n3
  54.0 0.0 collective-permute-done.5.n0
  54.0 0.0 collective-permute-done.6.n1
  54.0 3.4 %join_sets.1 = bf16[8,256,128]{2,1,0:T(8,128)(2,1)S(1)} custom-call(bf16[20,1,1024]{2,1,0:T(2,128)(2,1)S(1)} %get-tuple-element.36.columns_ref, bf16[20,256,1024]{2,1,0:T(8,128)(2,1)S(1)} %pick_active.1.picked_ref, f32[256,256]{1,0:T(8,128)S(1)} %sum_own.1.own_ref, bf16[256,256]{1,0:T(8,128)(2,1)S(1)} %collective-permute-done.5.n0, ...), custom_call_target="tpu_custom_call" | custom-call | flops 2684354560 | bytes 524288 | tf_op jit(solution)/shard_map/join_sets/pallas_call | solution.py:324
  57.4 12.0 %all_to_all.16 = bf16[8,256,128]{2,1,0:T(8,128)(2,1)S(1)} all-to-all(bf16[8,256,128]{2,1,0:T(8,128)(2,1)S(1)} %join_sets.1), channel_id=1, replica_groups=mesh['blk'=32,'cset'=8] {'cset'}, dimensions={0} | all-to-all | bytes 1048576 | tf_op jit(solution)/shard_map/all_to_all | solution.py:388
  69.4 0.8 %copy.10 = bf16[2048,128]{1,0:T(8,128)(2,1)} copy(bf16[2048,128]{1,0:T(8,128)(2,1)S(1)} %bitcast.27) | data formatting | bytes 1048576
Async XLA Ops:
  0.0 10.6 %copy-start.7 = (bf16[256,256]{1,0:T(8,128)(2,1)S(1)}, bf16[256,256]{1,0:T(8,128)(2,1)}, u32[]{:S(2)}) copy-start(bf16[256,256]{1,0:T(8,128)(2,1)} %param.9) | copy-start | bytes 393220
  0.0 16.5 %copy-start.5 = (s32[20,924]{1,0:T(8,128)S(1)}, s32[20,924]{1,0:T(8,128)}, u32[]{:S(2)}) copy-start(s32[20,924]{1,0:T(8,128)} %left_ref.1) | copy-start | bytes 221764
  0.0 16.5 %copy-start.6 = (s32[20,924]{1,0:T(8,128)S(1)}, s32[20,924]{1,0:T(8,128)}, u32[]{:S(2)}) copy-start(s32[20,924]{1,0:T(8,128)} %right_ref.1) | copy-start | bytes 221764
  2.2 37.4 %collective-permute-start.3 = (bf16[2064,128]{1,0:T(8,128)(2,1)S(1)}, bf16[2064,128]{1,0:T(8,128)(2,1)S(1)}, u32[]{:S(2)}, u32[]{:S(2)}) collective-permute-start(bf16[2064,128]{1,0:T(8,128)(2,1)S(1)} %get-tuple-element.45), channel_id=1, source_target_pairs={{0,20},{1,21},{2,22},{3,23},{4,16},{5,17},{6,18},{7,19},{8,28},{9,... | collective-permute-start | bytes 1585160 | tf_op jit(solution)/shard_map/ppermute | solution.py:30
  5.3 34.3 %collective-permute-start.4 = (bf16[2064,128]{1,0:T(8,128)(2,1)S(1)}, bf16[2064,128]{1,0:T(8,128)(2,1)S(1)}, u32[]{:S(2)}, u32[]{:S(2)}) collective-permute-start(bf16[2064,128]{1,0:T(8,128)(2,1)S(1)} %get-tuple-element.46), channel_id=1, source_target_pairs={{0,244},{1,245},{2,246},{3,247},{4,240},{5,241},{6,242},{7,243},{8... | collective-permute-start | bytes 1585160 | tf_op jit(solution)/shard_map/ppermute | solution.py:30
  11.7 19.3 %all-to-all-start = ((bf16[8,256,256]{2,1,0:T(8,128)(2,1)}), bf16[8,256,256]{2,1,0:T(8,128)(2,1)}, u32[]{:S(2)}, u32[]{:S(2)}) async-start(bf16[8,256,256]{2,1,0:T(8,128)(2,1)} %broadcast_in_dim.17), calls=%async_computation | async-start | bytes 2097152 | tf_op jit(solution)/shard_map/all_to_all | solution.py:361
  19.4 18.4 %collective-permute-start = (bf16[1040,128]{1,0:T(8,128)(2,1)}, bf16[1040,128]{1,0:T(8,128)(2,1)S(1)}, u32[]{:S(2)}, u32[]{:S(2)}) collective-permute-start(bf16[1040,128]{1,0:T(8,128)(2,1)} %get-tuple-element.39), channel_id=1, source_target_pairs={{0,32},{1,33},{2,34},{3,35},{4,36},{5,37},{6,38},{7,39},{8,40},{9,... | collective-permute-start | bytes 798728 | tf_op jit(solution)/shard_map/ppermute | solution.py:30
  19.5 18.3 %collective-permute-start.1 = (bf16[1040,128]{1,0:T(8,128)(2,1)}, bf16[1040,128]{1,0:T(8,128)(2,1)S(1)}, u32[]{:S(2)}, u32[]{:S(2)}) collective-permute-start(bf16[1040,128]{1,0:T(8,128)(2,1)} %get-tuple-element.40), channel_id=1, source_target_pairs={{0,224},{1,225},{2,226},{3,227},{4,228},{5,229},{6,230},{7,231},{8... | collective-permute-start | bytes 798728 | tf_op jit(solution)/shard_map/ppermute | solution.py:30
  22.7 15.1 %collective-permute-start.2 = (bf16[1040,128]{1,0:T(8,128)(2,1)S(1)}, bf16[1040,128]{1,0:T(8,128)(2,1)S(1)}, u32[]{:S(2)}, u32[]{:S(2)}) collective-permute-start(bf16[1040,128]{1,0:T(8,128)(2,1)S(1)} %get-tuple-element.41), channel_id=1, source_target_pairs={{0,224},{1,225},{2,226},{3,227},{4,228},{5,229},{6,230},{7,231},{8... | collective-permute-start | bytes 798728 | tf_op jit(solution)/shard_map/ppermute | solution.py:30
  37.8 12.1 %copy-start.1 = (bf16[256,256]{1,0:T(8,128)(2,1)S(1)}, bf16[256,256]{1,0:T(8,128)(2,1)}, u32[]{:S(2)}) copy-start(bf16[256,256]{1,0:T(8,128)(2,1)} %table_ref.1) | copy-start | bytes 393220
  41.1 11.6 %copy-start = (bf16[1,1,9,8,128,128]{5,4,3,2,1,0:T(8,128)(2,1)S(1)}, bf16[1,1,9,8,128,128]{5,4,3,2,1,0:T(8,128)(2,1)}, u32[]{:S(2)}) copy-start(bf16[1,1,9,8,128,128]{5,4,3,2,1,0:T(8,128)(2,1)} %param.10) | copy-start | bytes 7077892
  41.1 11.6 %copy-start.2 = (s32[1,1,9,8]{2,3,1,0:T(8,128)S(1)}, s32[1,1,9,8]{2,3,1,0:T(8,128)}, u32[]{:S(2)}) copy-start(s32[1,1,9,8]{2,3,1,0:T(8,128)} %param.11) | copy-start | bytes 868
  41.2 11.6 %copy-start.3 = (s32[1,1,9,8]{2,3,1,0:T(8,128)S(1)}, s32[1,1,9,8]{2,3,1,0:T(8,128)}, u32[]{:S(2)}) copy-start(s32[1,1,9,8]{2,3,1,0:T(8,128)} %param.12) | copy-start | bytes 868
  41.2 11.6 %copy-start.4 = (s32[1,1,9]{2,1,0:T(1,128)S(1)}, s32[1,1,9]{2,1,0:T(1,128)}, u32[]{:S(2)}) copy-start(s32[1,1,9]{2,1,0:T(1,128)} %param.13) | copy-start | bytes 112
  41.2 12.8 %collective-permute-start.7 = (bf16[256,256]{1,0:T(8,128)(2,1)S(1)}, bf16[256,256]{1,0:T(8,128)(2,1)S(1)}, u32[]{:S(2)}, u32[]{:S(2)}) collective-permute-start(bf16[256,256]{1,0:T(8,128)(2,1)S(1)} %get-tuple-element.53), channel_id=1, source_target_pairs={{0,20},{1,21},{2,22},{3,23},{4,16},{5,17},{6,18},{7,19},{8,28},{9,... | collective-permute-start | bytes 393224 | tf_op jit(solution)/shard_map/ppermute | solution.py:30
  41.3 12.7 %collective-permute-start.8 = (bf16[256,256]{1,0:T(8,128)(2,1)S(1)}, bf16[256,256]{1,0:T(8,128)(2,1)S(1)}, u32[]{:S(2)}, u32[]{:S(2)}) collective-permute-start(bf16[256,256]{1,0:T(8,128)(2,1)S(1)} %get-tuple-element.54), channel_id=1, source_target_pairs={{0,244},{1,245},{2,246},{3,247},{4,240},{5,241},{6,242},{7,243},{8... | collective-permute-start | bytes 393224 | tf_op jit(solution)/shard_map/ppermute | solution.py:30
  46.6 7.4 %collective-permute-start.5 = (bf16[256,256]{1,0:T(8,128)(2,1)S(1)}, bf16[256,256]{1,0:T(8,128)(2,1)S(1)}, u32[]{:S(2)}, u32[]{:S(2)}) collective-permute-start(bf16[256,256]{1,0:T(8,128)(2,1)S(1)} %get-tuple-element.51), channel_id=1, source_target_pairs={{0,32},{1,33},{2,34},{3,35},{4,36},{5,37},{6,38},{7,39},{8,40},{9,... | collective-permute-start | bytes 393224 | tf_op jit(solution)/shard_map/ppermute | solution.py:30
  46.6 7.4 %collective-permute-start.6 = (bf16[256,256]{1,0:T(8,128)(2,1)S(1)}, bf16[256,256]{1,0:T(8,128)(2,1)S(1)}, u32[]{:S(2)}, u32[]{:S(2)}) collective-permute-start(bf16[256,256]{1,0:T(8,128)(2,1)S(1)} %get-tuple-element.52), channel_id=1, source_target_pairs={{0,224},{1,225},{2,226},{3,227},{4,228},{5,229},{6,230},{7,231},{8... | collective-permute-start | bytes 393224 | tf_op jit(solution)/shard_map/ppermute | solution.py:30

commit v10 on v9

--- a/solution.py
+++ b/solution.py
@@ -162,20 +162,11 @@
     out[...] = products(held, rows, lambda n: refs[n][...], sources).astype(jnp.bfloat16)
 
 
-def sum_near_kernel(at_ref, sources, from_below, from_above, to_below, to_above, *scratch):
-    below, above = read_places((from_below, from_above), *scratch)
-    write_products(to_below, below, sources)
-    write_products(to_above, above, sources)
-
-
-def sum_far_kernel(at_ref, sources, from_below, from_above, odd, to_below, to_above, *scratch):
-    below, above, extra = read_places((from_below, from_above, odd), *scratch)
-
-    def kept(core):
-        return [(held, jnp.where(at_ref[0] == core, row, 2), tile) for held, row, tile in extra]
-
-    write_products(to_below, below + kept(1), sources)
-    write_products(to_above, above + kept(0), sources)
+def sum_side_kernel(core, at_ref, sources, near, far, odd, to_near, to_far, *scratch):
+    near, far, odd = read_places((near, far, odd), *scratch)
+    odd = [(held, jnp.where(at_ref[0] == core, row, 2), tile) for held, row, tile in odd]
+    write_products(to_near, near, sources)
+    write_products(to_far, far + odd, sources)
 
 
 def sum_away(kernel, at, sources, messages, name):
@@ -351,12 +342,12 @@
     nc = lax.axis_size("cset")
     at = (lax.axis_index("blk") % 2).astype(jnp.int32)[None]
 
-    near = pack_tiles((0, 1), at, dst, src, count, tiles_all, "pack_near")
-    *near, passive_table = lax.optimization_barrier((*near, passive_table))
+    first = pack_tiles((0,), at, dst, src, count, tiles_all, "pack_first")
+    *first, passive_table = lax.optimization_barrier((*first, passive_table))
     left, right = as_columns(split_active, split_passive)
     left, later = lax.optimization_barrier((left, at))
-    far = pack_tiles((2, 3, 4), later, dst, src, count, tiles_all, "pack_far")
-    messages = [routed(message, hops) for message, hops in zip((*near, *far), HOPS)]
+    rest = pack_tiles((1, 2, 3, 4), later, dst, src, count, tiles_all, "pack_rest")
+    messages = [routed(message, hops) for message, hops in zip((*first, *rest), HOPS)]
     copies = jnp.broadcast_to(passive_table[None], (nc,) + passive_table.shape)
     own_rows = lax.all_to_all(copies, "cset", split_axis=0, concat_axis=0, tiled=True)
     own_rows = own_rows.reshape(-1, passive_table.shape[1])
@@ -368,21 +359,21 @@
 
     sources, left, right = lax.optimization_barrier((sources, left, right))
     near_up, near_down, far_up, far_down, odd = messages
-    far_below, far_above = sum_away(
-        sum_far_kernel, at, sources, (far_up, far_down, odd), "sum_far"
+    near_above, far_above = sum_away(
+        functools.partial(sum_side_kernel, 0), at, sources, (near_down, far_down, odd), "sum_above"
     )
-    far_below, far_above, sources = lax.optimization_barrier((far_below, far_above, sources))
-    near_below, near_above = sum_away(
-        sum_near_kernel, at, sources, (near_up, near_down), "sum_near"
+    near_above, far_above, sources = lax.optimization_barrier((near_above, far_above, sources))
+    near_below, far_below = sum_away(
+        functools.partial(sum_side_kernel, 1), at, sources, (near_up, far_up, odd), "sum_below"
     )
-    near_below, near_above, left = lax.optimization_barrier((near_below, near_above, left))
+    near_below, far_below, left = lax.optimization_barrier((near_below, far_below, left))
     picked = pick_columns(active_table, left)
     own = sum_own(at, dst, src, count, sources, tiles_all)
     parts = [
+        routed(near_above, lambda core: 1),
         routed(far_above, lambda core: 2),
+        routed(near_below, lambda core: -1),
         routed(far_below, lambda core: -2),
-        routed(near_above, lambda core: 1),
-        routed(near_below, lambda core: -1),
     ]
     joined = join(picked, own, parts, right)
     spread = lax.all_to_all(joined, "cset", split_axis=0, concat_axis=0, tiled=True)

time: 70.5 us -> 75.3 us (1.068)
  waiting for transfers between devices: 7.92 us -> 13.3 us
  starting transfers between devices: 25.6 us -> 24.4 us
    ppermute x9, waiting for transfers between devices: 0.02 us -> 13.1 us  [routed(): return lax.ppermute(block, ('blk', 'cset'), route)]
    all_to_all x1, waiting for transfers between devices: 7.9 us -> 0.26 us  [local(): lax.all_to_all(copies, 'cset', split_axis=0, concat_axis=0, tiled=True)]
    ppermute x9, starting transfers between devices: 20.8 us -> 18 us  [routed(): return lax.ppermute(block, ('blk', 'cset'), route)]
    all_to_all x1, starting transfers between devices: 4.83 us -> 6.39 us  [local(): lax.all_to_all(copies, 'cset', split_axis=0, concat_axis=0, tiled=True)]
  transfers between devices with their start and end apart: 10 -> 10, of which waited for: 1 -> 5; matrix products, arithmetic and copies ran while one was open for 3% -> 2% of each run, Pallas kernels for 12% -> 12%
where the time goes in v10:
time: 75.3 us; the launch traced here: 74.7 us
  starting transfers between devices  24.4 us (32%)
  blocking collectives  17.5 us (23%)
  Pallas kernels  15.9 us (21%)
  waiting for transfers between devices  13.3 us (18%)
  local copies, waits for them, and re-layouts  3.24 us (4%)
    ppermute x9, starting transfers between devices, routed(): return lax.ppermute(block, ('blk', 'cset'), route)  18 us
    ppermute x9, waiting for transfers between devices, routed(): return lax.ppermute(block, ('blk', 'cset'), route)  13.1 us
    all_to_all x1, blocking collectives, local(): lax.all_to_all(joined, 'cset', split_axis=0, concat_axis=0, tiled=True)  12.1 us
    all_to_all x1, starting transfers between devices, local(): lax.all_to_all(copies, 'cset', split_axis=0, concat_axis=0, tiled=True)  6.39 us
    all_to_all x1, blocking collectives, local(): lax.all_to_all(twice, 'blk', split_axis=0, concat_axis=0, tiled=True, axi...  5.42 us
    pallas_call x2, Pallas kernels, pack_tiles(): pl.pallas_call(functools.partial(pack_kernel, which), in_specs=[SMEM, SME...  4.88 us
    pallas_call x2, Pallas kernels, sum_away(): pl.pallas_call(kernel, in_specs=[SMEM] + [VMEM] * (1 + len(messages)), ou...  3.4 us
    pallas_call x1, Pallas kernels, join(): pl.pallas_call(join_kernel, in_specs=[VMEM] * 7, out_specs=VMEM, out_shap...  3.39 us
  transfers between devices with their start and end apart: 10, of which 5 were waited for; matrix products, arithmetic and copies ran while one was open for 2% of the time, Pallas kernels for 12%

profile of v10, /device:TPU:2, one launch (start us, length us, event | category | flops | bytes accessed | tf_op | source)
XLA Modules:
  0.0 74.7 jit_solution(13400357325844433414)
XLA Ops:
  0.0 0.0 copy-start.7
  0.0 2.0 %pack_first.1 = bf16[2064,128]{1,0:T(8,128)(2,1)S(1)} custom-call(s32[1]{0:T(128)} %bitcast.at_ref, s32[8,9]{1,0:T(8,128)} %bitcast.18, s32[8,9]{1,0:T(8,128)} %bitcast.21, s32[9]{0:T(128)} %bitcast.24, bf16[9216,128]{1,0:T(8,128)(2,1)} %bitcast.15), custom_call_target="tpu_custom_call" | custom-call | bytes 528384 | tf_op jit(solution)/shard_map/pack_first/pallas_call | solution.py:107
  2.0 0.0 copy-done.7
  2.0 0.0 copy-start.5
  2.0 0.0 copy-start.6
  2.0 1.0 %broadcast_in_dim.17 = bf16[8,256,256]{2,1,0:T(8,128)(2,1)} broadcast(bf16[256,256]{1,0:T(8,128)(2,1)S(1)} %copy-done.7), dimensions={1,2} | broadcast | bytes 1179648 | tf_op jit(solution)/shard_map/broadcast_in_dim | solution.py:351
  3.1 6.4 %all-to-all-start = ((bf16[8,256,256]{2,1,0:T(8,128)(2,1)}), bf16[8,256,256]{2,1,0:T(8,128)(2,1)}, u32[]{:S(2)}, u32[]{:S(2)}) async-start(bf16[8,256,256]{2,1,0:T(8,128)(2,1)} %broadcast_in_dim.17), calls=%async_computation | async-start | bytes 2097152 | tf_op jit(solution)/shard_map/all_to_all | solution.py:352
  9.5 0.0 copy-done.5
  9.5 0.0 copy-done.6
  9.5 0.1 as_columns.1
  9.6 2.9 %pack_rest.1 = (bf16[2064,128]{1,0:T(8,128)(2,1)S(1)}, bf16[1040,128]{1,0:T(8,128)(2,1)S(1)}, bf16[1040,128]{1,0:T(8,128)(2,1)}, bf16[1040,128]{1,0:T(8,128)(2,1)}) custom-call(s32[1]{0:T(128)} %bitcast.at_ref, s32[8,9]{1,0:T(8,128)} %bitcast.19, s32[8,9]{1,0:T(8,128)} %bitcast.22, s32[9]{0:T(128)} %bitcast.25, bf16[9216,128]{1,0:T(8,128)(2,1)} %bitcast.16), custom_call_target="tpu_custom_call" | custom-call | bytes 1327104 | tf_op jit(solution)/shard_map/pack_rest/pallas_call | solution.py:107
  12.5 7.7 %collective-permute-start = (bf16[2064,128]{1,0:T(8,128)(2,1)S(1)}, bf16[2064,128]{1,0:T(8,128)(2,1)S(1)}, u32[]{:S(2)}, u32[]{:S(2)}) collective-permute-start(bf16[2064,128]{1,0:T(8,128)(2,1)S(1)} %get-tuple-element.35), channel_id=1, source_target_pairs={{0,244},{1,245},{2,246},{3,247},{4,240},{5,241},{6,242},{7,243},{8... | collective-permute-start | bytes 1585160 | tf_op jit(solution)/shard_map/ppermute | solution.py:30
  20.3 0.0 collective-permute-start.3
  20.3 1.0 %collective-permute-start.1 = (bf16[1040,128]{1,0:T(8,128)(2,1)}, bf16[1040,128]{1,0:T(8,128)(2,1)S(1)}, u32[]{:S(2)}, u32[]{:S(2)}) collective-permute-start(bf16[1040,128]{1,0:T(8,128)(2,1)} %get-tuple-element.36), channel_id=1, source_target_pairs={{0,224},{1,225},{2,226},{3,227},{4,228},{5,229},{6,230},{7,231},{8... | collective-permute-start | bytes 798728 | tf_op jit(solution)/shard_map/ppermute | solution.py:30
  21.3 1.0 %collective-permute-start.2 = (bf16[1040,128]{1,0:T(8,128)(2,1)}, bf16[1040,128]{1,0:T(8,128)(2,1)S(1)}, u32[]{:S(2)}, u32[]{:S(2)}) collective-permute-start(bf16[1040,128]{1,0:T(8,128)(2,1)} %get-tuple-element.37), channel_id=1, source_target_pairs={{0,224},{1,225},{2,226},{3,227},{4,228},{5,229},{6,230},{7,231},{8... | collective-permute-start | bytes 798728 | tf_op jit(solution)/shard_map/ppermute | solution.py:30
  22.3 1.0 %collective-permute-start.4 = (bf16[1040,128]{1,0:T(8,128)(2,1)S(1)}, bf16[1040,128]{1,0:T(8,128)(2,1)S(1)}, u32[]{:S(2)}, u32[]{:S(2)}) collective-permute-start(bf16[1040,128]{1,0:T(8,128)(2,1)S(1)} %get-tuple-element.42), channel_id=1, source_target_pairs={{0,32},{1,33},{2,34},{3,35},{4,36},{5,37},{6,38},{7,39},{8,40},{9,... | collective-permute-start | bytes 798728 | tf_op jit(solution)/shard_map/ppermute | solution.py:30
  23.3 0.3 all-to-all-done
  23.5 1.4 %broadcast_in_dim.19 = bf16[2,2048,256]{2,1,0:T(8,128)(2,1)S(1)} broadcast(bf16[2048,256]{1,0:T(8,128)(2,1)} %bitcast.7), dimensions={1,2} | broadcast | bytes 3145728 | tf_op jit(solution)/shard_map/broadcast_in_dim | solution.py:355
  24.9 5.4 %all_to_all.15 = bf16[2,2048,256]{2,1,0:T(8,128)(2,1)S(1)} all-to-all(bf16[2,2048,256]{2,1,0:T(8,128)(2,1)S(1)} %broadcast_in_dim.19), channel_id=1, replica_groups={{0,8},{16,24},{32,40},{48,56},{64,72},{80,88},{96,104},{112,120},{128,1..., dimensions={0} | all-to-all | bytes 4194304 | tf_op jit(solution)/shard_map/all_to_all | solution.py:356
  30.3 6.5 %collective-permute-done.1.far = bf16[1040,128]{1,0:T(8,128)(2,1)S(1)} collective-permute-done((bf16[1040,128]{1,0:T(8,128)(2,1)}, bf16[1040,128]{1,0:T(8,128)(2,1)S(1)}, u32[]{:S(2)}, u32[]{:S(2)}) %collective-permute-start.1) | collective-permute-done | bytes 266272 | tf_op jit(solution)/shard_map/ppermute | solution.py:30
  36.8 2.9 %collective-permute-done.2.odd = bf16[1040,128]{1,0:T(8,128)(2,1)S(1)} collective-permute-done((bf16[1040,128]{1,0:T(8,128)(2,1)}, bf16[1040,128]{1,0:T(8,128)(2,1)S(1)}, u32[]{:S(2)}, u32[]{:S(2)}) %collective-permute-start.2) | collective-permute-done | bytes 266272 | tf_op jit(solution)/shard_map/ppermute | solution.py:30
  39.7 0.0 collective-permute-done.near
  39.7 1.7 %sum_above.1 = (bf16[256,256]{1,0:T(8,128)(2,1)S(1)}, bf16[256,256]{1,0:T(8,128)(2,1)S(1)}) custom-call(s32[1]{0:T(128)} %bitcast.at_ref, bf16[4096,256]{1,0:T(8,128)(2,1)S(1)} %bitcast.12, bf16[2064,128]{1,0:T(8,128)(2,1)S(1)} %collective-permute-done.near, bf16[1040,128]{1,0:T(8,128)(2,1)S(1)} %collective-permute-done.1.far, ...), custom_call_target="tpu_custom_call" | custom-call | flops 536870912 | bytes 3145728 | tf_op jit(solution)/shard_map/sum_above/pallas_call | solution.py:174
  41.4 0.0 copy-start.1
  41.4 0.0 collective-permute-done.4.far
  41.4 0.0 collective-permute-done.3.near
  41.4 1.7 %sum_below.1 = (bf16[256,256]{1,0:T(8,128)(2,1)S(1)}, bf16[256,256]{1,0:T(8,128)(2,1)S(1)}) custom-call(s32[1]{0:T(128)} %bitcast.at_ref, bf16[4096,256]{1,0:T(8,128)(2,1)S(1)} %bitcast.13, bf16[2064,128]{1,0:T(8,128)(2,1)S(1)} %collective-permute-done.3.near, bf16[1040,128]{1,0:T(8,128)(2,1)S(1)} %collective-permute-done.4.far, ...), custom_call_target="tpu_custom_call" | custom-call | flops 536870912 | bytes 3145728 | tf_op jit(solution)/shard_map/sum_below/pallas_call | solution.py:174
  43.1 0.0 copy-start
  43.1 0.0 copy-start.2
  43.1 0.0 copy-start.3
  43.2 0.0 copy-start.4
  43.2 5.1 %collective-permute-start.7 = (bf16[256,256]{1,0:T(8,128)(2,1)S(1)}, bf16[256,256]{1,0:T(8,128)(2,1)S(1)}, u32[]{:S(2)}, u32[]{:S(2)}) collective-permute-start(bf16[256,256]{1,0:T(8,128)(2,1)S(1)} %get-tuple-element.49), channel_id=1, source_target_pairs={{0,244},{1,245},{2,246},{3,247},{4,240},{5,241},{6,242},{7,243},{8... | collective-permute-start | bytes 393224 | tf_op jit(solution)/shard_map/ppermute | solution.py:30
  48.3 1.0 %collective-permute-start.8 = (bf16[256,256]{1,0:T(8,128)(2,1)S(1)}, bf16[256,256]{1,0:T(8,128)(2,1)S(1)}, u32[]{:S(2)}, u32[]{:S(2)}) collective-permute-start(bf16[256,256]{1,0:T(8,128)(2,1)S(1)} %get-tuple-element.50), channel_id=1, source_target_pairs={{0,224},{1,225},{2,226},{3,227},{4,228},{5,229},{6,230},{7,231},{8... | collective-permute-start | bytes 393224 | tf_op jit(solution)/shard_map/ppermute | solution.py:30
  49.3 1.2 %collective-permute-start.5 = (bf16[256,256]{1,0:T(8,128)(2,1)S(1)}, bf16[256,256]{1,0:T(8,128)(2,1)S(1)}, u32[]{:S(2)}, u32[]{:S(2)}) collective-permute-start(bf16[256,256]{1,0:T(8,128)(2,1)S(1)} %get-tuple-element.47), channel_id=1, source_target_pairs={{0,20},{1,21},{2,22},{3,23},{4,16},{5,17},{6,18},{7,19},{8,28},{9,... | collective-permute-start | bytes 393224 | tf_op jit(solution)/shard_map/ppermute | solution.py:30
  50.5 0.0 collective-permute-start.6
  50.5 0.0 copy-done.1
  50.5 2.9 %pick_active.1.picked_ref = bf16[20,256,1024]{2,1,0:T(8,128)(2,1)S(1)} custom-call(bf16[20,1,1024]{2,1,0:T(2,128)(2,1)S(1)} %get-tuple-element.46.columns_ref, bf16[256,256]{1,0:T(8,128)(2,1)S(1)} %copy-done.1), custom_call_target="tpu_custom_call" | custom-call | flops 2684354560 | bytes 10485760 | tf_op jit(solution)/shard_map/pick_active/pallas_call | solution.py:276
  53.4 0.0 copy-done
  53.4 0.0 copy-done.2
  53.4 0.0 copy-done.3
  53.4 0.0 copy-done.4
  53.4 1.2 %sum_own.1.own_ref = f32[256,256]{1,0:T(8,128)S(1)} custom-call(s32[1]{0:T(128)} %bitcast.at_ref, s32[8,9]{1,0:T(8,128)S(1)} %bitcast.20, s32[8,9]{1,0:T(8,128)S(1)} %bitcast.23, s32[9]{0:T(128)S(1)} %bitcast.26, bf16[4096,256]{1,0:T(8,128)(2,1)S(1)} %bitcast.14, bf16[9216,128]{1,0:T(8,128)(2,1)S(1)} %bitcast.17), custom_call_target="tpu_custom_call" | custom-call | flops 268435456 | bytes 2621440 | tf_op jit(solution)/shard_map/sum_own/pallas_call | solution.py:207
  54.6 0.0 collective-permute-done.7.n2
  54.6 0.4 collective-permute-done.8.n3
  55.0 3.3 %collective-permute-done.5.n0 = bf16[256,256]{1,0:T(8,128)(2,1)S(1)} collective-permute-done((bf16[256,256]{1,0:T(8,128)(2,1)S(1)}, bf16[256,256]{1,0:T(8,128)(2,1)S(1)}, u32[]{:S(2)}, u32[]{:S(2)}) %collective-permute-start.5) | collective-permute-done | bytes 131104 | tf_op jit(solution)/shard_map/ppermute | solution.py:30
  58.3 0.0 collective-permute-done.6.n1
  58.3 3.4 %join_sets.1 = bf16[8,256,128]{2,1,0:T(8,128)(2,1)S(1)} custom-call(bf16[20,1,1024]{2,1,0:T(2,128)(2,1)S(1)} %get-tuple-element.32.columns_ref, bf16[20,256,1024]{2,1,0:T(8,128)(2,1)S(1)} %pick_active.1.picked_ref, f32[256,256]{1,0:T(8,128)S(1)} %sum_own.1.own_ref, bf16[256,256]{1,0:T(8,128)(2,1)S(1)} %collective-permute-done.5.n0, ...), custom_call_target="tpu_custom_call" | custom-call | flops 2684354560 | bytes 524288 | tf_op jit(solution)/shard_map/join_sets/pallas_call | solution.py:315
  61.7 12.1 %all_to_all.16 = bf16[8,256,128]{2,1,0:T(8,128)(2,1)S(1)} all-to-all(bf16[8,256,128]{2,1,0:T(8,128)(2,1)S(1)} %join_sets.1), channel_id=1, replica_groups=mesh['blk'=32,'cset'=8] {'cset'}, dimensions={0} | all-to-all | bytes 1048576 | tf_op jit(solution)/shard_map/all_to_all | solution.py:379
  73.9 0.8 %copy.10 = bf16[2048,128]{1,0:T(8,128)(2,1)} copy(bf16[2048,128]{1,0:T(8,128)(2,1)S(1)} %bitcast.27) | data formatting | bytes 1048576
Async XLA Ops:
  0.0 2.0 %copy-start.7 = (bf16[256,256]{1,0:T(8,128)(2,1)S(1)}, bf16[256,256]{1,0:T(8,128)(2,1)}, u32[]{:S(2)}) copy-start(bf16[256,256]{1,0:T(8,128)(2,1)} %param.9) | copy-start | bytes 393220
  2.0 7.5 %copy-start.5 = (s32[20,924]{1,0:T(8,128)S(1)}, s32[20,924]{1,0:T(8,128)}, u32[]{:S(2)}) copy-start(s32[20,924]{1,0:T(8,128)} %left_ref.1) | copy-start | bytes 221764
  2.0 7.4 %copy-start.6 = (s32[20,924]{1,0:T(8,128)S(1)}, s32[20,924]{1,0:T(8,128)}, u32[]{:S(2)}) copy-start(s32[20,924]{1,0:T(8,128)} %right_ref.1) | copy-start | bytes 221764
  3.1 20.5 %all-to-all-start = ((bf16[8,256,256]{2,1,0:T(8,128)(2,1)}), bf16[8,256,256]{2,1,0:T(8,128)(2,1)}, u32[]{:S(2)}, u32[]{:S(2)}) async-start(bf16[8,256,256]{2,1,0:T(8,128)(2,1)} %broadcast_in_dim.17), calls=%async_computation | async-start | bytes 2097152 | tf_op jit(solution)/shard_map/all_to_all | solution.py:352
  12.5 27.1 %collective-permute-start = (bf16[2064,128]{1,0:T(8,128)(2,1)S(1)}, bf16[2064,128]{1,0:T(8,128)(2,1)S(1)}, u32[]{:S(2)}, u32[]{:S(2)}) collective-permute-start(bf16[2064,128]{1,0:T(8,128)(2,1)S(1)} %get-tuple-element.35), channel_id=1, source_target_pairs={{0,244},{1,245},{2,246},{3,247},{4,240},{5,241},{6,242},{7,243},{8... | collective-permute-start | bytes 1585160 | tf_op jit(solution)/shard_map/ppermute | solution.py:30
  20.3 21.1 %collective-permute-start.3 = (bf16[2064,128]{1,0:T(8,128)(2,1)S(1)}, bf16[2064,128]{1,0:T(8,128)(2,1)S(1)}, u32[]{:S(2)}, u32[]{:S(2)}) collective-permute-start(bf16[2064,128]{1,0:T(8,128)(2,1)S(1)} %pack_first.1), channel_id=1, source_target_pairs={{0,20},{1,21},{2,22},{3,23},{4,16},{5,17},{6,18},{7,19},{8,28},{9,... | collective-permute-start | bytes 1585160 | tf_op jit(solution)/shard_map/ppermute | solution.py:30
  20.3 16.6 %collective-permute-start.1 = (bf16[1040,128]{1,0:T(8,128)(2,1)}, bf16[1040,128]{1,0:T(8,128)(2,1)S(1)}, u32[]{:S(2)}, u32[]{:S(2)}) collective-permute-start(bf16[1040,128]{1,0:T(8,128)(2,1)} %get-tuple-element.36), channel_id=1, source_target_pairs={{0,224},{1,225},{2,226},{3,227},{4,228},{5,229},{6,230},{7,231},{8... | collective-permute-start | bytes 798728 | tf_op jit(solution)/shard_map/ppermute | solution.py:30
  21.3 18.4 %collective-permute-start.2 = (bf16[1040,128]{1,0:T(8,128)(2,1)}, bf16[1040,128]{1,0:T(8,128)(2,1)S(1)}, u32[]{:S(2)}, u32[]{:S(2)}) collective-permute-start(bf16[1040,128]{1,0:T(8,128)(2,1)} %get-tuple-element.37), channel_id=1, source_target_pairs={{0,224},{1,225},{2,226},{3,227},{4,228},{5,229},{6,230},{7,231},{8... | collective-permute-start | bytes 798728 | tf_op jit(solution)/shard_map/ppermute | solution.py:30
  22.3 19.1 %collective-permute-start.4 = (bf16[1040,128]{1,0:T(8,128)(2,1)S(1)}, bf16[1040,128]{1,0:T(8,128)(2,1)S(1)}, u32[]{:S(2)}, u32[]{:S(2)}) collective-permute-start(bf16[1040,128]{1,0:T(8,128)(2,1)S(1)} %get-tuple-element.42), channel_id=1, source_target_pairs={{0,32},{1,33},{2,34},{3,35},{4,36},{5,37},{6,38},{7,39},{8,40},{9,... | collective-permute-start | bytes 798728 | tf_op jit(solution)/shard_map/ppermute | solution.py:30
  41.4 9.1 %copy-start.1 = (bf16[256,256]{1,0:T(8,128)(2,1)S(1)}, bf16[256,256]{1,0:T(8,128)(2,1)}, u32[]{:S(2)}) copy-start(bf16[256,256]{1,0:T(8,128)(2,1)} %table_ref.1) | copy-start | bytes 393220
  43.1 10.3 %copy-start = (bf16[1,1,9,8,128,128]{5,4,3,2,1,0:T(8,128)(2,1)S(1)}, bf16[1,1,9,8,128,128]{5,4,3,2,1,0:T(8,128)(2,1)}, u32[]{:S(2)}) copy-start(bf16[1,1,9,8,128,128]{5,4,3,2,1,0:T(8,128)(2,1)} %param.10) | copy-start | bytes 7077892
  43.1 10.3 %copy-start.2 = (s32[1,1,9,8]{2,3,1,0:T(8,128)S(1)}, s32[1,1,9,8]{2,3,1,0:T(8,128)}, u32[]{:S(2)}) copy-start(s32[1,1,9,8]{2,3,1,0:T(8,128)} %param.11) | copy-start | bytes 868
  43.1 10.2 %copy-start.3 = (s32[1,1,9,8]{2,3,1,0:T(8,128)S(1)}, s32[1,1,9,8]{2,3,1,0:T(8,128)}, u32[]{:S(2)}) copy-start(s32[1,1,9,8]{2,3,1,0:T(8,128)} %param.12) | copy-start | bytes 868
  43.2 10.2 %copy-start.4 = (s32[1,1,9]{2,1,0:T(1,128)S(1)}, s32[1,1,9]{2,1,0:T(1,128)}, u32[]{:S(2)}) copy-start(s32[1,1,9]{2,1,0:T(1,128)} %param.13) | copy-start | bytes 112
  43.2 11.4 %collective-permute-start.7 = (bf16[256,256]{1,0:T(8,128)(2,1)S(1)}, bf16[256,256]{1,0:T(8,128)(2,1)S(1)}, u32[]{:S(2)}, u32[]{:S(2)}) collective-permute-start(bf16[256,256]{1,0:T(8,128)(2,1)S(1)} %get-tuple-element.49), channel_id=1, source_target_pairs={{0,244},{1,245},{2,246},{3,247},{4,240},{5,241},{6,242},{7,243},{8... | collective-permute-start | bytes 393224 | tf_op jit(solution)/shard_map/ppermute | solution.py:30
  48.3 6.7 %collective-permute-start.8 = (bf16[256,256]{1,0:T(8,128)(2,1)S(1)}, bf16[256,256]{1,0:T(8,128)(2,1)S(1)}, u32[]{:S(2)}, u32[]{:S(2)}) collective-permute-start(bf16[256,256]{1,0:T(8,128)(2,1)S(1)} %get-tuple-element.50), channel_id=1, source_target_pairs={{0,224},{1,225},{2,226},{3,227},{4,228},{5,229},{6,230},{7,231},{8... | collective-permute-start | bytes 393224 | tf_op jit(solution)/shard_map/ppermute | solution.py:30
  49.3 9.1 %collective-permute-start.5 = (bf16[256,256]{1,0:T(8,128)(2,1)S(1)}, bf16[256,256]{1,0:T(8,128)(2,1)S(1)}, u32[]{:S(2)}, u32[]{:S(2)}) collective-permute-start(bf16[256,256]{1,0:T(8,128)(2,1)S(1)} %get-tuple-element.47), channel_id=1, source_target_pairs={{0,20},{1,21},{2,22},{3,23},{4,16},{5,17},{6,18},{7,19},{8,28},{9,... | collective-permute-start | bytes 393224 | tf_op jit(solution)/shard_map/ppermute | solution.py:30
  50.5 7.9 %collective-permute-start.6 = (bf16[256,256]{1,0:T(8,128)(2,1)S(1)}, bf16[256,256]{1,0:T(8,128)(2,1)S(1)}, u32[]{:S(2)}, u32[]{:S(2)}) collective-permute-start(bf16[256,256]{1,0:T(8,128)(2,1)S(1)} %get-tuple-element.48), channel_id=1, source_target_pairs={{0,32},{1,33},{2,34},{3,35},{4,36},{5,37},{6,38},{7,39},{8,40},{9,... | collective-permute-start | bytes 393224 | tf_op jit(solution)/shard_map/ppermute | solution.py:30

commit v11 on v9

--- a/solution.py
+++ b/solution.py
@@ -351,12 +351,12 @@
     nc = lax.axis_size("cset")
     at = (lax.axis_index("blk") % 2).astype(jnp.int32)[None]
 
-    near = pack_tiles((0, 1), at, dst, src, count, tiles_all, "pack_near")
-    *near, passive_table = lax.optimization_barrier((*near, passive_table))
+    first = pack_tiles((0,), at, dst, src, count, tiles_all, "pack_first")
+    *first, passive_table = lax.optimization_barrier((*first, passive_table))
     left, right = as_columns(split_active, split_passive)
     left, later = lax.optimization_barrier((left, at))
-    far = pack_tiles((2, 3, 4), later, dst, src, count, tiles_all, "pack_far")
-    messages = [routed(message, hops) for message, hops in zip((*near, *far), HOPS)]
+    rest = pack_tiles((1, 2, 3, 4), later, dst, src, count, tiles_all, "pack_rest")
+    messages = [routed(message, hops) for message, hops in zip((*first, *rest), HOPS)]
     copies = jnp.broadcast_to(passive_table[None], (nc,) + passive_table.shape)
     own_rows = lax.all_to_all(copies, "cset", split_axis=0, concat_axis=0, tiled=True)
     own_rows = own_rows.reshape(-1, passive_table.shape[1])
@@ -375,14 +375,16 @@
     near_below, near_above = sum_away(
         sum_near_kernel, at, sources, (near_up, near_down), "sum_near"
     )
-    near_below, near_above, left = lax.optimization_barrier((near_below, near_above, left))
+    near_below, near_above, far_below, left = lax.optimization_barrier(
+        (near_below, near_above, far_below, left)
+    )
     picked = pick_columns(active_table, left)
     own = sum_own(at, dst, src, count, sources, tiles_all)
     parts = [
+        routed(near_above, lambda core: 1),
         routed(far_above, lambda core: 2),
+        routed(near_below, lambda core: -1),
         routed(far_below, lambda core: -2),
-        routed(near_above, lambda core: 1),
-        routed(near_below, lambda core: -1),
     ]
     joined = join(picked, own, parts, right)
     spread = lax.all_to_all(joined, "cset", split_axis=0, concat_axis=0, tiled=True)

time: 70.5 us -> 73 us (1.035)
  the two profiles are of different devices: /device:TPU:2 before, /device:TPU:32 now
where the time goes in v11:
time: 73 us; the launch traced here: 72.7 us
  starting transfers between devices  25.3 us (35%)
  blocking collectives  18.1 us (25%)
  Pallas kernels  15.8 us (22%)
  waiting for transfers between devices  10 us (14%)
  local copies, waits for them, and re-layouts  3.24 us (4%)
    ppermute x9, starting transfers between devices, routed(): return lax.ppermute(block, ('blk', 'cset'), route)  21 us
    all_to_all x1, blocking collectives, local(): lax.all_to_all(joined, 'cset', split_axis=0, concat_axis=0, tiled=True)  12.7 us
    ppermute x9, waiting for transfers between devices, routed(): return lax.ppermute(block, ('blk', 'cset'), route)  7.63 us
    all_to_all x1, blocking collectives, local(): lax.all_to_all(twice, 'blk', split_axis=0, concat_axis=0, tiled=True, axi...  5.42 us
    pallas_call x2, Pallas kernels, pack_tiles(): pl.pallas_call(functools.partial(pack_kernel, which), in_specs=[SMEM, SME...  4.88 us
    all_to_all x1, starting transfers between devices, local(): lax.all_to_all(copies, 'cset', split_axis=0, concat_axis=0, tiled=True)  4.3 us
    pallas_call x1, Pallas kernels, join(): pl.pallas_call(join_kernel, in_specs=[VMEM] * 7, out_specs=VMEM, out_shap...  3.39 us
    pallas_call x2, Pallas kernels, sum_away(): pl.pallas_call(kernel, in_specs=[SMEM] + [VMEM] * (1 + len(messages)), ou...  3.24 us
  transfers between devices with their start and end apart: 10, of which 5 were waited for; matrix products, arithmetic and copies ran while one was open for 3% of the time, Pallas kernels for 14%

profile of v11, /device:TPU:32, one launch (start us, length us, event | category | flops | bytes accessed | tf_op | source)
XLA Modules:
  0.0 72.7 jit_solution(11450944292581091631)
XLA Ops:
  0.0 0.0 copy-start.7
  0.0 2.0 %pack_first.1 = bf16[2064,128]{1,0:T(8,128)(2,1)S(1)} custom-call(s32[1]{0:T(128)} %bitcast.at_ref, s32[8,9]{1,0:T(8,128)} %bitcast.18, s32[8,9]{1,0:T(8,128)} %bitcast.21, s32[9]{0:T(128)} %bitcast.24, bf16[9216,128]{1,0:T(8,128)(2,1)} %bitcast.15), custom_call_target="tpu_custom_call" | custom-call | bytes 528384 | tf_op jit(solution)/shard_map/pack_first/pallas_call | solution.py:107
  2.0 0.0 copy-start.5
  2.0 0.0 copy-start.6
  2.0 3.1 %collective-permute-start.3 = (bf16[2064,128]{1,0:T(8,128)(2,1)S(1)}, bf16[2064,128]{1,0:T(8,128)(2,1)S(1)}, u32[]{:S(2)}, u32[]{:S(2)}) collective-permute-start(bf16[2064,128]{1,0:T(8,128)(2,1)S(1)} %pack_first.1), channel_id=1, source_target_pairs={{0,20},{1,21},{2,22},{3,23},{4,16},{5,17},{6,18},{7,19},{8,28},{9,... | collective-permute-start | bytes 1585160 | tf_op jit(solution)/shard_map/ppermute | solution.py:30
  5.1 0.0 copy-done.7
  5.1 1.0 %broadcast_in_dim.17 = bf16[8,256,256]{2,1,0:T(8,128)(2,1)} broadcast(bf16[256,256]{1,0:T(8,128)(2,1)S(1)} %copy-done.7), dimensions={1,2} | broadcast | bytes 1179648 | tf_op jit(solution)/shard_map/broadcast_in_dim | solution.py:360
  6.1 4.3 %all-to-all-start = ((bf16[8,256,256]{2,1,0:T(8,128)(2,1)}), bf16[8,256,256]{2,1,0:T(8,128)(2,1)}, u32[]{:S(2)}, u32[]{:S(2)}) async-start(bf16[8,256,256]{2,1,0:T(8,128)(2,1)} %broadcast_in_dim.17), calls=%async_computation | async-start | bytes 2097152 | tf_op jit(solution)/shard_map/all_to_all | solution.py:361
  10.4 0.0 copy-done.5
  10.5 0.0 copy-done.6
  10.5 0.1 as_columns.1
  10.6 2.9 %pack_rest.1 = (bf16[2064,128]{1,0:T(8,128)(2,1)S(1)}, bf16[1040,128]{1,0:T(8,128)(2,1)}, bf16[1040,128]{1,0:T(8,128)(2,1)}, bf16[1040,128]{1,0:T(8,128)(2,1)S(1)}) custom-call(s32[1]{0:T(128)} %bitcast.at_ref, s32[8,9]{1,0:T(8,128)} %bitcast.19, s32[8,9]{1,0:T(8,128)} %bitcast.22, s32[9]{0:T(128)} %bitcast.25, bf16[9216,128]{1,0:T(8,128)(2,1)} %bitcast.16), custom_call_target="tpu_custom_call" | custom-call | bytes 1327104 | tf_op jit(solution)/shard_map/pack_rest/pallas_call | solution.py:107
  13.5 2.7 %collective-permute-start.4 = (bf16[2064,128]{1,0:T(8,128)(2,1)S(1)}, bf16[2064,128]{1,0:T(8,128)(2,1)S(1)}, u32[]{:S(2)}, u32[]{:S(2)}) collective-permute-start(bf16[2064,128]{1,0:T(8,128)(2,1)S(1)} %get-tuple-element.43), channel_id=1, source_target_pairs={{0,244},{1,245},{2,246},{3,247},{4,240},{5,241},{6,242},{7,243},{8... | collective-permute-start | bytes 1585160 | tf_op jit(solution)/shard_map/ppermute | solution.py:30
  16.2 1.9 %collective-permute-start = (bf16[1040,128]{1,0:T(8,128)(2,1)}, bf16[1040,128]{1,0:T(8,128)(2,1)S(1)}, u32[]{:S(2)}, u32[]{:S(2)}) collective-permute-start(bf16[1040,128]{1,0:T(8,128)(2,1)} %get-tuple-element.36), channel_id=1, source_target_pairs={{0,32},{1,33},{2,34},{3,35},{4,36},{5,37},{6,38},{7,39},{8,40},{9,... | collective-permute-start | bytes 798728 | tf_op jit(solution)/shard_map/ppermute | solution.py:30
  18.1 2.4 %collective-permute-start.1 = (bf16[1040,128]{1,0:T(8,128)(2,1)}, bf16[1040,128]{1,0:T(8,128)(2,1)S(1)}, u32[]{:S(2)}, u32[]{:S(2)}) collective-permute-start(bf16[1040,128]{1,0:T(8,128)(2,1)} %get-tuple-element.37), channel_id=1, source_target_pairs={{0,224},{1,225},{2,226},{3,227},{4,228},{5,229},{6,230},{7,231},{8... | collective-permute-start | bytes 798728 | tf_op jit(solution)/shard_map/ppermute | solution.py:30
  20.5 3.2 %collective-permute-start.2 = (bf16[1040,128]{1,0:T(8,128)(2,1)S(1)}, bf16[1040,128]{1,0:T(8,128)(2,1)S(1)}, u32[]{:S(2)}, u32[]{:S(2)}) collective-permute-start(bf16[1040,128]{1,0:T(8,128)(2,1)S(1)} %get-tuple-element.38), channel_id=1, source_target_pairs={{0,224},{1,225},{2,226},{3,227},{4,228},{5,229},{6,230},{7,231},{8... | collective-permute-start | bytes 798728 | tf_op jit(solution)/shard_map/ppermute | solution.py:30
  23.7 2.4 %all-to-all-done = bf16[8,256,256]{2,1,0:T(8,128)(2,1)} async-done(((bf16[8,256,256]{2,1,0:T(8,128)(2,1)}), bf16[8,256,256]{2,1,0:T(8,128)(2,1)}, u32[]{:S(2)}, u32[]{:S(2)}) %all-to-all-start) | async-done | bytes 1048608 | tf_op jit(solution)/shard_map/all_to_all | solution.py:361
  26.1 1.4 %broadcast_in_dim.19 = bf16[2,2048,256]{2,1,0:T(8,128)(2,1)S(1)} broadcast(bf16[2048,256]{1,0:T(8,128)(2,1)} %bitcast.7), dimensions={1,2} | broadcast | bytes 3145728 | tf_op jit(solution)/shard_map/broadcast_in_dim | solution.py:364
  27.5 5.4 %all_to_all.15 = bf16[2,2048,256]{2,1,0:T(8,128)(2,1)S(1)} all-to-all(bf16[2,2048,256]{2,1,0:T(8,128)(2,1)S(1)} %broadcast_in_dim.19), channel_id=1, replica_groups={{0,8},{16,24},{32,40},{48,56},{64,72},{80,88},{96,104},{112,120},{128,1..., dimensions={0} | all-to-all | bytes 4194304 | tf_op jit(solution)/shard_map/all_to_all | solution.py:365
  32.9 0.0 copy-start.1
  32.9 0.0 collective-permute-done.from_below
  32.9 1.8 %collective-permute-done.1.from_above = bf16[1040,128]{1,0:T(8,128)(2,1)S(1)} collective-permute-done((bf16[1040,128]{1,0:T(8,128)(2,1)}, bf16[1040,128]{1,0:T(8,128)(2,1)S(1)}, u32[]{:S(2)}, u32[]{:S(2)}) %collective-permute-start.1) | collective-permute-done | bytes 266272 | tf_op jit(solution)/shard_map/ppermute | solution.py:30
  34.7 2.9 %collective-permute-done.2.odd = bf16[1040,128]{1,0:T(8,128)(2,1)S(1)} collective-permute-done((bf16[1040,128]{1,0:T(8,128)(2,1)S(1)}, bf16[1040,128]{1,0:T(8,128)(2,1)S(1)}, u32[]{:S(2)}, u32[]{:S(2)}) %collective-permute-start.2) | collective-permute-done | bytes 266272 | tf_op jit(solution)/shard_map/ppermute | solution.py:30
  37.5 1.7 %sum_far.1 = (bf16[256,256]{1,0:T(8,128)(2,1)S(1)}, bf16[256,256]{1,0:T(8,128)(2,1)S(1)}) custom-call(s32[1]{0:T(128)} %bitcast.at_ref, bf16[4096,256]{1,0:T(8,128)(2,1)S(1)} %bitcast.12, bf16[1040,128]{1,0:T(8,128)(2,1)S(1)} %collective-permute-done.from_below, bf16[1040,128]{1,0:T(8,128)(2,1)S(1)} %collective-permute-done.1.from_above, ...), custom_call_target="tpu_custom_call" | custom-call | flops 536870912 | bytes 3145728 | tf_op jit(solution)/shard_map/sum_far/pallas_call | solution.py:183
  39.2 2.0 %collective-permute-start.6 = (bf16[256,256]{1,0:T(8,128)(2,1)S(1)}, bf16[256,256]{1,0:T(8,128)(2,1)S(1)}, u32[]{:S(2)}, u32[]{:S(2)}) collective-permute-start(bf16[256,256]{1,0:T(8,128)(2,1)S(1)} %get-tuple-element.50), channel_id=1, source_target_pairs={{0,32},{1,33},{2,34},{3,35},{4,36},{5,37},{6,38},{7,39},{8,40},{9,... | collective-permute-start | bytes 393224 | tf_op jit(solution)/shard_map/ppermute | solution.py:30
  41.2 0.0 collective-permute-done.3.from_below
  41.2 0.0 collective-permute-done.4.from_above
  41.2 1.6 %sum_near.1 = (bf16[256,256]{1,0:T(8,128)(2,1)S(1)}, bf16[256,256]{1,0:T(8,128)(2,1)S(1)}) custom-call(s32[1]{0:T(128)} %bitcast.at_ref, bf16[4096,256]{1,0:T(8,128)(2,1)S(1)} %bitcast.13, bf16[2064,128]{1,0:T(8,128)(2,1)S(1)} %collective-permute-done.3.from_below, bf16[2064,128]{1,0:T(8,128)(2,1)S(1)} %collective-permute-done.4.from_above), custom_call_target="tpu_custom_call" | custom-call | flops 536870912 | bytes 3145728 | tf_op jit(solution)/shard_map/sum_near/pallas_call | solution.py:183
  42.8 0.0 copy-start
  42.8 0.0 copy-start.2
  42.8 0.0 copy-start.3
  42.8 0.0 copy-start.4
  42.8 0.1 collective-permute-start.5
  42.9 4.1 %collective-permute-start.7 = (bf16[256,256]{1,0:T(8,128)(2,1)S(1)}, bf16[256,256]{1,0:T(8,128)(2,1)S(1)}, u32[]{:S(2)}, u32[]{:S(2)}) collective-permute-start(bf16[256,256]{1,0:T(8,128)(2,1)S(1)} %get-tuple-element.51), channel_id=1, source_target_pairs={{0,244},{1,245},{2,246},{3,247},{4,240},{5,241},{6,242},{7,243},{8... | collective-permute-start | bytes 393224 | tf_op jit(solution)/shard_map/ppermute | solution.py:30
  47.1 1.5 %collective-permute-start.8 = (bf16[256,256]{1,0:T(8,128)(2,1)S(1)}, bf16[256,256]{1,0:T(8,128)(2,1)S(1)}, u32[]{:S(2)}, u32[]{:S(2)}) collective-permute-start(bf16[256,256]{1,0:T(8,128)(2,1)S(1)} %get-tuple-element.52), channel_id=1, source_target_pairs={{0,224},{1,225},{2,226},{3,227},{4,228},{5,229},{6,230},{7,231},{8... | collective-permute-start | bytes 393224 | tf_op jit(solution)/shard_map/ppermute | solution.py:30
  48.6 0.0 copy-done.1
  48.6 2.9 %pick_active.1.picked_ref = bf16[20,256,1024]{2,1,0:T(8,128)(2,1)S(1)} custom-call(bf16[20,1,1024]{2,1,0:T(2,128)(2,1)S(1)} %get-tuple-element.48.columns_ref, bf16[256,256]{1,0:T(8,128)(2,1)S(1)} %copy-done.1), custom_call_target="tpu_custom_call" | custom-call | flops 2684354560 | bytes 10485760 | tf_op jit(solution)/shard_map/pick_active/pallas_call | solution.py:285
  51.5 0.0 copy-done
  51.5 0.0 copy-done.2
  51.5 0.0 copy-done.3
  51.5 0.0 copy-done.4
  51.5 1.2 %sum_own.1.own_ref = f32[256,256]{1,0:T(8,128)S(1)} custom-call(s32[1]{0:T(128)} %bitcast.at_ref, s32[8,9]{1,0:T(8,128)S(1)} %bitcast.20, s32[8,9]{1,0:T(8,128)S(1)} %bitcast.23, s32[9]{0:T(128)S(1)} %bitcast.26, bf16[4096,256]{1,0:T(8,128)(2,1)S(1)} %bitcast.14, bf16[9216,128]{1,0:T(8,128)(2,1)S(1)} %bitcast.17), custom_call_target="tpu_custom_call" | custom-call | flops 268435456 | bytes 2621440 | tf_op jit(solution)/shard_map/sum_own/pallas_call | solution.py:216
  52.7 0.0 collective-permute-done.6.n1
  52.8 0.0 collective-permute-done.5.n0
  52.8 0.1 collective-permute-done.7.n2
  52.9 2.9 %collective-permute-done.8.n3 = bf16[256,256]{1,0:T(8,128)(2,1)S(1)} collective-permute-done((bf16[256,256]{1,0:T(8,128)(2,1)S(1)}, bf16[256,256]{1,0:T(8,128)(2,1)S(1)}, u32[]{:S(2)}, u32[]{:S(2)}) %collective-permute-start.8) | collective-permute-done | bytes 131104 | tf_op jit(solution)/shard_map/ppermute | solution.py:30
  55.7 3.4 %join_sets.1 = bf16[8,256,128]{2,1,0:T(8,128)(2,1)S(1)} custom-call(bf16[20,1,1024]{2,1,0:T(2,128)(2,1)S(1)} %get-tuple-element.33.columns_ref, bf16[20,256,1024]{2,1,0:T(8,128)(2,1)S(1)} %pick_active.1.picked_ref, f32[256,256]{1,0:T(8,128)S(1)} %sum_own.1.own_ref, bf16[256,256]{1,0:T(8,128)(2,1)S(1)} %collective-permute-done.5.n0, ...), custom_call_target="tpu_custom_call" | custom-call | flops 2684354560 | bytes 524288 | tf_op jit(solution)/shard_map/join_sets/pallas_call | solution.py:324
  59.1 12.7 %all_to_all.16 = bf16[8,256,128]{2,1,0:T(8,128)(2,1)S(1)} all-to-all(bf16[8,256,128]{2,1,0:T(8,128)(2,1)S(1)} %join_sets.1), channel_id=1, replica_groups=mesh['blk'=32,'cset'=8] {'cset'}, dimensions={0} | all-to-all | bytes 1048576 | tf_op jit(solution)/shard_map/all_to_all | solution.py:390
  71.9 0.8 %copy.10 = bf16[2048,128]{1,0:T(8,128)(2,1)} copy(bf16[2048,128]{1,0:T(8,128)(2,1)S(1)} %bitcast.27) | data formatting | bytes 1048576
Async XLA Ops:
  0.0 5.1 %copy-start.7 = (bf16[256,256]{1,0:T(8,128)(2,1)S(1)}, bf16[256,256]{1,0:T(8,128)(2,1)}, u32[]{:S(2)}) copy-start(bf16[256,256]{1,0:T(8,128)(2,1)} %param.9) | copy-start | bytes 393220
  2.0 8.5 %copy-start.5 = (s32[20,924]{1,0:T(8,128)S(1)}, s32[20,924]{1,0:T(8,128)}, u32[]{:S(2)}) copy-start(s32[20,924]{1,0:T(8,128)} %left_ref.1) | copy-start | bytes 221764
  2.0 8.5 %copy-start.6 = (s32[20,924]{1,0:T(8,128)S(1)}, s32[20,924]{1,0:T(8,128)}, u32[]{:S(2)}) copy-start(s32[20,924]{1,0:T(8,128)} %right_ref.1) | copy-start | bytes 221764
  2.0 39.2 %collective-permute-start.3 = (bf16[2064,128]{1,0:T(8,128)(2,1)S(1)}, bf16[2064,128]{1,0:T(8,128)(2,1)S(1)}, u32[]{:S(2)}, u32[]{:S(2)}) collective-permute-start(bf16[2064,128]{1,0:T(8,128)(2,1)S(1)} %pack_first.1), channel_id=1, source_target_pairs={{0,20},{1,21},{2,22},{3,23},{4,16},{5,17},{6,18},{7,19},{8,28},{9,... | collective-permute-start | bytes 1585160 | tf_op jit(solution)/shard_map/ppermute | solution.py:30
  6.1 20.0 %all-to-all-start = ((bf16[8,256,256]{2,1,0:T(8,128)(2,1)}), bf16[8,256,256]{2,1,0:T(8,128)(2,1)}, u32[]{:S(2)}, u32[]{:S(2)}) async-start(bf16[8,256,256]{2,1,0:T(8,128)(2,1)} %broadcast_in_dim.17), calls=%async_computation | async-start | bytes 2097152 | tf_op jit(solution)/shard_map/all_to_all | solution.py:361
  13.5 27.7 %collective-permute-start.4 = (bf16[2064,128]{1,0:T(8,128)(2,1)S(1)}, bf16[2064,128]{1,0:T(8,128)(2,1)S(1)}, u32[]{:S(2)}, u32[]{:S(2)}) collective-permute-start(bf16[2064,128]{1,0:T(8,128)(2,1)S(1)} %get-tuple-element.43), channel_id=1, source_target_pairs={{0,244},{1,245},{2,246},{3,247},{4,240},{5,241},{6,242},{7,243},{8... | collective-permute-start | bytes 1585160 | tf_op jit(solution)/shard_map/ppermute | solution.py:30
  16.2 16.7 %collective-permute-start = (bf16[1040,128]{1,0:T(8,128)(2,1)}, bf16[1040,128]{1,0:T(8,128)(2,1)S(1)}, u32[]{:S(2)}, u32[]{:S(2)}) collective-permute-start(bf16[1040,128]{1,0:T(8,128)(2,1)} %get-tuple-element.36), channel_id=1, source_target_pairs={{0,32},{1,33},{2,34},{3,35},{4,36},{5,37},{6,38},{7,39},{8,40},{9,... | collective-permute-start | bytes 798728 | tf_op jit(solution)/shard_map/ppermute | solution.py:30
  18.1 16.6 %collective-permute-start.1 = (bf16[1040,128]{1,0:T(8,128)(2,1)}, bf16[1040,128]{1,0:T(8,128)(2,1)S(1)}, u32[]{:S(2)}, u32[]{:S(2)}) collective-permute-start(bf16[1040,128]{1,0:T(8,128)(2,1)} %get-tuple-element.37), channel_id=1, source_target_pairs={{0,224},{1,225},{2,226},{3,227},{4,228},{5,229},{6,230},{7,231},{8... | collective-permute-start | bytes 798728 | tf_op jit(solution)/shard_map/ppermute | solution.py:30
  20.5 17.1 %collective-permute-start.2 = (bf16[1040,128]{1,0:T(8,128)(2,1)S(1)}, bf16[1040,128]{1,0:T(8,128)(2,1)S(1)}, u32[]{:S(2)}, u32[]{:S(2)}) collective-permute-start(bf16[1040,128]{1,0:T(8,128)(2,1)S(1)} %get-tuple-element.38), channel_id=1, source_target_pairs={{0,224},{1,225},{2,226},{3,227},{4,228},{5,229},{6,230},{7,231},{8... | collective-permute-start | bytes 798728 | tf_op jit(solution)/shard_map/ppermute | solution.py:30
  32.9 15.7 %copy-start.1 = (bf16[256,256]{1,0:T(8,128)(2,1)S(1)}, bf16[256,256]{1,0:T(8,128)(2,1)}, u32[]{:S(2)}) copy-start(bf16[256,256]{1,0:T(8,128)(2,1)} %table_ref.1) | copy-start | bytes 393220
  39.2 13.5 %collective-permute-start.6 = (bf16[256,256]{1,0:T(8,128)(2,1)S(1)}, bf16[256,256]{1,0:T(8,128)(2,1)S(1)}, u32[]{:S(2)}, u32[]{:S(2)}) collective-permute-start(bf16[256,256]{1,0:T(8,128)(2,1)S(1)} %get-tuple-element.50), channel_id=1, source_target_pairs={{0,32},{1,33},{2,34},{3,35},{4,36},{5,37},{6,38},{7,39},{8,40},{9,... | collective-permute-start | bytes 393224 | tf_op jit(solution)/shard_map/ppermute | solution.py:30
  42.8 8.7 %copy-start = (bf16[1,1,9,8,128,128]{5,4,3,2,1,0:T(8,128)(2,1)S(1)}, bf16[1,1,9,8,128,128]{5,4,3,2,1,0:T(8,128)(2,1)}, u32[]{:S(2)}) copy-start(bf16[1,1,9,8,128,128]{5,4,3,2,1,0:T(8,128)(2,1)} %param.10) | copy-start | bytes 7077892
  42.8 8.7 %copy-start.2 = (s32[1,1,9,8]{2,3,1,0:T(8,128)S(1)}, s32[1,1,9,8]{2,3,1,0:T(8,128)}, u32[]{:S(2)}) copy-start(s32[1,1,9,8]{2,3,1,0:T(8,128)} %param.11) | copy-start | bytes 868
  42.8 8.7 %copy-start.3 = (s32[1,1,9,8]{2,3,1,0:T(8,128)S(1)}, s32[1,1,9,8]{2,3,1,0:T(8,128)}, u32[]{:S(2)}) copy-start(s32[1,1,9,8]{2,3,1,0:T(8,128)} %param.12) | copy-start | bytes 868
  42.8 8.7 %copy-start.4 = (s32[1,1,9]{2,1,0:T(1,128)S(1)}, s32[1,1,9]{2,1,0:T(1,128)}, u32[]{:S(2)}) copy-start(s32[1,1,9]{2,1,0:T(1,128)} %param.13) | copy-start | bytes 112
  42.8 9.9 %collective-permute-start.5 = (bf16[256,256]{1,0:T(8,128)(2,1)S(1)}, bf16[256,256]{1,0:T(8,128)(2,1)S(1)}, u32[]{:S(2)}, u32[]{:S(2)}) collective-permute-start(bf16[256,256]{1,0:T(8,128)(2,1)S(1)} %get-tuple-element.49), channel_id=1, source_target_pairs={{0,20},{1,21},{2,22},{3,23},{4,16},{5,17},{6,18},{7,19},{8,28},{9,... | collective-permute-start | bytes 393224 | tf_op jit(solution)/shard_map/ppermute | solution.py:30
  42.9 9.9 %collective-permute-start.7 = (bf16[256,256]{1,0:T(8,128)(2,1)S(1)}, bf16[256,256]{1,0:T(8,128)(2,1)S(1)}, u32[]{:S(2)}, u32[]{:S(2)}) collective-permute-start(bf16[256,256]{1,0:T(8,128)(2,1)S(1)} %get-tuple-element.51), channel_id=1, source_target_pairs={{0,244},{1,245},{2,246},{3,247},{4,240},{5,241},{6,242},{7,243},{8... | collective-permute-start | bytes 393224 | tf_op jit(solution)/shard_map/ppermute | solution.py:30
  47.1 8.7 %collective-permute-start.8 = (bf16[256,256]{1,0:T(8,128)(2,1)S(1)}, bf16[256,256]{1,0:T(8,128)(2,1)S(1)}, u32[]{:S(2)}, u32[]{:S(2)}) collective-permute-start(bf16[256,256]{1,0:T(8,128)(2,1)S(1)} %get-tuple-element.52), channel_id=1, source_target_pairs={{0,224},{1,225},{2,226},{3,227},{4,228},{5,229},{6,230},{7,231},{8... | collective-permute-start | bytes 393224 | tf_op jit(solution)/shard_map/ppermute | solution.py:30

commit v12 on v9

--- a/solution.py
+++ b/solution.py
@@ -46,8 +46,8 @@
 
 def message_slots(core):
     return [
+        pair_slots(1, core),
         pair_slots(3, core),
-        pair_slots(1, core),
         [(REACH - 1, core)],
         [(0, core)],
         [(1 + (REACH - 3) * core, 1 - core)],
@@ -55,8 +55,8 @@
 
 
 HOPS = [
+    lambda core: -1,
     lambda core: 1,
-    lambda core: -1,
     lambda core: 2,
     lambda core: -2,
     lambda core: 4 * core - 2,
@@ -162,10 +162,10 @@
     out[...] = products(held, rows, lambda n: refs[n][...], sources).astype(jnp.bfloat16)
 
 
-def sum_near_kernel(at_ref, sources, from_below, from_above, to_below, to_above, *scratch):
-    below, above = read_places((from_below, from_above), *scratch)
+def sum_near_kernel(at_ref, sources, from_above, from_below, to_above, to_below, *scratch):
+    above, below = read_places((from_above, from_below), *scratch)
+    write_products(to_above, above, sources)
     write_products(to_below, below, sources)
-    write_products(to_above, above, sources)
 
 
 def sum_far_kernel(at_ref, sources, from_below, from_above, odd, to_below, to_above, *scratch):
@@ -367,13 +367,13 @@
     ).reshape(-1, own_rows.shape[1])
 
     sources, left, right = lax.optimization_barrier((sources, left, right))
-    near_up, near_down, far_up, far_down, odd = messages
+    near_down, near_up, far_up, far_down, odd = messages
     far_below, far_above = sum_away(
         sum_far_kernel, at, sources, (far_up, far_down, odd), "sum_far"
     )
     far_below, far_above, sources = lax.optimization_barrier((far_below, far_above, sources))
-    near_below, near_above = sum_away(
-        sum_near_kernel, at, sources, (near_up, near_down), "sum_near"
+    near_above, near_below = sum_away(
+        sum_near_kernel, at, sources, (near_down, near_up), "sum_near"
     )
     near_below, near_above, left = lax.optimization_barrier((near_below, near_above, left))
     picked = pick_columns(active_table, left)

time: 70.5 us -> 70.4 us (level)
  no operation moved by 1% of the time
where the time goes in v12:
time: 70.4 us; the launch traced here: 70.1 us
  starting transfers between devices  25.2 us (36%)
  blocking collectives  17.4 us (25%)
  Pallas kernels  15.8 us (22%)
  waiting for transfers between devices  8.27 us (12%)
  local copies, waits for them, and re-layouts  3.23 us (5%)
    ppermute x9, starting transfers between devices, routed(): return lax.ppermute(block, ('blk', 'cset'), route)  20.4 us
    all_to_all x1, blocking collectives, local(): lax.all_to_all(joined, 'cset', split_axis=0, concat_axis=0, tiled=True)  11.9 us
    all_to_all x1, waiting for transfers between devices, local(): lax.all_to_all(copies, 'cset', split_axis=0, concat_axis=0, tiled=True)  8.25 us
    all_to_all x1, blocking collectives, local(): lax.all_to_all(twice, 'blk', split_axis=0, concat_axis=0, tiled=True, axi...  5.42 us
    pallas_call x2, Pallas kernels, pack_tiles(): pl.pallas_call(functools.partial(pack_kernel, which), in_specs=[SMEM, SME...  4.88 us
    all_to_all x1, starting transfers between devices, local(): lax.all_to_all(copies, 'cset', split_axis=0, concat_axis=0, tiled=True)  4.83 us
    pallas_call x1, Pallas kernels, join(): pl.pallas_call(join_kernel, in_specs=[VMEM] * 7, out_specs=VMEM, out_shap...  3.39 us
    pallas_call x2, Pallas kernels, sum_away(): pl.pallas_call(kernel, in_specs=[SMEM] + [VMEM] * (1 + len(messages)), ou...  3.28 us
  transfers between devices with their start and end apart: 10, of which 1 were waited for; matrix products, arithmetic and copies ran while one was open for 3% of the time, Pallas kernels for 12%

profile of v12, /device:TPU:2, one launch (start us, length us, event | category | flops | bytes accessed | tf_op | source)
XLA Modules:
  0.0 70.1 jit_solution(17535242757718935529)
XLA Ops:
  0.0 0.0 copy-start.7
  0.0 0.0 copy-start.5
  0.0 0.0 copy-start.6
  0.0 2.2 %pack_near.1 = (bf16[2064,128]{1,0:T(8,128)(2,1)S(1)}, bf16[2064,128]{1,0:T(8,128)(2,1)S(1)}) custom-call(s32[1]{0:T(128)} %bitcast.at_ref, s32[8,9]{1,0:T(8,128)} %bitcast.18, s32[8,9]{1,0:T(8,128)} %bitcast.21, s32[9]{0:T(128)} %bitcast.24, bf16[9216,128]{1,0:T(8,128)(2,1)} %bitcast.15), custom_call_target="tpu_custom_call" | custom-call | bytes 1056768 | tf_op jit(solution)/shard_map/pack_near/pallas_call | solution.py:107
  2.2 8.4 %collective-permute-start.3 = (bf16[2064,128]{1,0:T(8,128)(2,1)S(1)}, bf16[2064,128]{1,0:T(8,128)(2,1)S(1)}, u32[]{:S(2)}, u32[]{:S(2)}) collective-permute-start(bf16[2064,128]{1,0:T(8,128)(2,1)S(1)} %get-tuple-element.45), channel_id=1, source_target_pairs={{0,244},{1,245},{2,246},{3,247},{4,240},{5,241},{6,242},{7,243},{8... | collective-permute-start | bytes 1585160 | tf_op jit(solution)/shard_map/ppermute | solution.py:30
  10.6 0.0 collective-permute-start.4
  10.6 0.0 copy-done.7
  10.6 1.0 %broadcast_in_dim.17 = bf16[8,256,256]{2,1,0:T(8,128)(2,1)} broadcast(bf16[256,256]{1,0:T(8,128)(2,1)S(1)} %copy-done.7), dimensions={1,2} | broadcast | bytes 1179648 | tf_op jit(solution)/shard_map/broadcast_in_dim | solution.py:360
  11.6 4.8 %all-to-all-start = ((bf16[8,256,256]{2,1,0:T(8,128)(2,1)}), bf16[8,256,256]{2,1,0:T(8,128)(2,1)}, u32[]{:S(2)}, u32[]{:S(2)}) async-start(bf16[8,256,256]{2,1,0:T(8,128)(2,1)} %broadcast_in_dim.17), calls=%async_computation | async-start | bytes 2097152 | tf_op jit(solution)/shard_map/all_to_all | solution.py:361
  16.4 0.0 copy-done.5
  16.4 0.0 copy-done.6
  16.4 0.1 as_columns.1
  16.6 2.7 %pack_far.1 = (bf16[1040,128]{1,0:T(8,128)(2,1)}, bf16[1040,128]{1,0:T(8,128)(2,1)}, bf16[1040,128]{1,0:T(8,128)(2,1)S(1)}) custom-call(s32[1]{0:T(128)} %bitcast.at_ref, s32[8,9]{1,0:T(8,128)} %bitcast.19, s32[8,9]{1,0:T(8,128)} %bitcast.22, s32[9]{0:T(128)} %bitcast.25, bf16[9216,128]{1,0:T(8,128)(2,1)} %bitcast.16), custom_call_target="tpu_custom_call" | custom-call | bytes 798720 | tf_op jit(solution)/shard_map/pack_far/pallas_call | solution.py:107
  19.3 0.1 collective-permute-start
  19.4 3.2 %collective-permute-start.1 = (bf16[1040,128]{1,0:T(8,128)(2,1)}, bf16[1040,128]{1,0:T(8,128)(2,1)S(1)}, u32[]{:S(2)}, u32[]{:S(2)}) collective-permute-start(bf16[1040,128]{1,0:T(8,128)(2,1)} %get-tuple-element.40), channel_id=1, source_target_pairs={{0,224},{1,225},{2,226},{3,227},{4,228},{5,229},{6,230},{7,231},{8... | collective-permute-start | bytes 798728 | tf_op jit(solution)/shard_map/ppermute | solution.py:30
  22.6 0.0 collective-permute-start.2
  22.7 8.3 %all-to-all-done = bf16[8,256,256]{2,1,0:T(8,128)(2,1)} async-done(((bf16[8,256,256]{2,1,0:T(8,128)(2,1)}), bf16[8,256,256]{2,1,0:T(8,128)(2,1)}, u32[]{:S(2)}, u32[]{:S(2)}) %all-to-all-start) | async-done | bytes 1048608 | tf_op jit(solution)/shard_map/all_to_all | solution.py:361
  30.9 1.4 %broadcast_in_dim.19 = bf16[2,2048,256]{2,1,0:T(8,128)(2,1)S(1)} broadcast(bf16[2048,256]{1,0:T(8,128)(2,1)} %bitcast.7), dimensions={1,2} | broadcast | bytes 3145728 | tf_op jit(solution)/shard_map/broadcast_in_dim | solution.py:364
  32.3 5.4 %all_to_all.15 = bf16[2,2048,256]{2,1,0:T(8,128)(2,1)S(1)} all-to-all(bf16[2,2048,256]{2,1,0:T(8,128)(2,1)S(1)} %broadcast_in_dim.19), channel_id=1, replica_groups={{0,8},{16,24},{32,40},{48,56},{64,72},{80,88},{96,104},{112,120},{128,1..., dimensions={0} | all-to-all | bytes 4194304 | tf_op jit(solution)/shard_map/all_to_all | solution.py:365
  37.7 0.0 copy-start.1
  37.7 0.0 collective-permute-done.from_below
  37.7 0.0 collective-permute-done.1.from_above
  37.7 0.0 collective-permute-done.2.odd
  37.7 1.7 %sum_far.1 = (bf16[256,256]{1,0:T(8,128)(2,1)S(1)}, bf16[256,256]{1,0:T(8,128)(2,1)S(1)}) custom-call(s32[1]{0:T(128)} %bitcast.at_ref, bf16[4096,256]{1,0:T(8,128)(2,1)S(1)} %bitcast.12, bf16[1040,128]{1,0:T(8,128)(2,1)S(1)} %collective-permute-done.from_below, bf16[1040,128]{1,0:T(8,128)(2,1)S(1)} %collective-permute-done.1.from_above, ...), custom_call_target="tpu_custom_call" | custom-call | flops 536870912 | bytes 3145728 | tf_op jit(solution)/shard_map/sum_far/pallas_call | solution.py:183
  39.4 0.0 collective-permute-done.3.from_above
  39.4 0.0 collective-permute-done.4.from_below
  39.5 1.6 %sum_near.1 = (bf16[256,256]{1,0:T(8,128)(2,1)S(1)}, bf16[256,256]{1,0:T(8,128)(2,1)S(1)}) custom-call(s32[1]{0:T(128)} %bitcast.at_ref, bf16[4096,256]{1,0:T(8,128)(2,1)S(1)} %bitcast.13, bf16[2064,128]{1,0:T(8,128)(2,1)S(1)} %collective-permute-done.3.from_above, bf16[2064,128]{1,0:T(8,128)(2,1)S(1)} %collective-permute-done.4.from_below), custom_call_target="tpu_custom_call" | custom-call | flops 536870912 | bytes 3145728 | tf_op jit(solution)/shard_map/sum_near/pallas_call | solution.py:183
  41.0 0.0 copy-start
  41.1 0.0 copy-start.2
  41.1 0.0 copy-start.3
  41.1 0.0 copy-start.4
  41.1 0.1 collective-permute-start.7
  41.2 5.3 %collective-permute-start.8 = (bf16[256,256]{1,0:T(8,128)(2,1)S(1)}, bf16[256,256]{1,0:T(8,128)(2,1)S(1)}, u32[]{:S(2)}, u32[]{:S(2)}) collective-permute-start(bf16[256,256]{1,0:T(8,128)(2,1)S(1)} %get-tuple-element.54), channel_id=1, source_target_pairs={{0,244},{1,245},{2,246},{3,247},{4,240},{5,241},{6,242},{7,243},{8... | collective-permute-start | bytes 393224 | tf_op jit(solution)/shard_map/ppermute | solution.py:30
  46.5 0.0 collective-permute-start.5
  46.5 3.2 %collective-permute-start.6 = (bf16[256,256]{1,0:T(8,128)(2,1)S(1)}, bf16[256,256]{1,0:T(8,128)(2,1)S(1)}, u32[]{:S(2)}, u32[]{:S(2)}) collective-permute-start(bf16[256,256]{1,0:T(8,128)(2,1)S(1)} %get-tuple-element.52), channel_id=1, source_target_pairs={{0,224},{1,225},{2,226},{3,227},{4,228},{5,229},{6,230},{7,231},{8... | collective-permute-start | bytes 393224 | tf_op jit(solution)/shard_map/ppermute | solution.py:30
  49.8 0.0 copy-done.1
  49.8 2.9 %pick_active.1.picked_ref = bf16[20,256,1024]{2,1,0:T(8,128)(2,1)S(1)} custom-call(bf16[20,1,1024]{2,1,0:T(2,128)(2,1)S(1)} %get-tuple-element.50.columns_ref, bf16[256,256]{1,0:T(8,128)(2,1)S(1)} %copy-done.1), custom_call_target="tpu_custom_call" | custom-call | flops 2684354560 | bytes 10485760 | tf_op jit(solution)/shard_map/pick_active/pallas_call | solution.py:285
  52.7 0.0 copy-done
  52.7 0.0 copy-done.2
  52.7 0.0 copy-done.3
  52.7 0.0 copy-done.4
  52.7 1.2 %sum_own.1.own_ref = f32[256,256]{1,0:T(8,128)S(1)} custom-call(s32[1]{0:T(128)} %bitcast.at_ref, s32[8,9]{1,0:T(8,128)S(1)} %bitcast.20, s32[8,9]{1,0:T(8,128)S(1)} %bitcast.23, s32[9]{0:T(128)S(1)} %bitcast.26, bf16[4096,256]{1,0:T(8,128)(2,1)S(1)} %bitcast.14, bf16[9216,128]{1,0:T(8,128)(2,1)S(1)} %bitcast.17), custom_call_target="tpu_custom_call" | custom-call | flops 268435456 | bytes 2621440 | tf_op jit(solution)/shard_map/sum_own/pallas_call | solution.py:216
  53.9 0.0 collective-permute-done.7.n2
  53.9 0.0 collective-permute-done.8.n3
  53.9 0.0 collective-permute-done.5.n0
  53.9 0.0 collective-permute-done.6.n1
  54.0 3.4 %join_sets.1 = bf16[8,256,128]{2,1,0:T(8,128)(2,1)S(1)} custom-call(bf16[20,1,1024]{2,1,0:T(2,128)(2,1)S(1)} %get-tuple-element.36.columns_ref, bf16[20,256,1024]{2,1,0:T(8,128)(2,1)S(1)} %pick_active.1.picked_ref, f32[256,256]{1,0:T(8,128)S(1)} %sum_own.1.own_ref, bf16[256,256]{1,0:T(8,128)(2,1)S(1)} %collective-permute-done.5.n0, ...), custom_call_target="tpu_custom_call" | custom-call | flops 2684354560 | bytes 524288 | tf_op jit(solution)/shard_map/join_sets/pallas_call | solution.py:324
  57.3 11.9 %all_to_all.16 = bf16[8,256,128]{2,1,0:T(8,128)(2,1)S(1)} all-to-all(bf16[8,256,128]{2,1,0:T(8,128)(2,1)S(1)} %join_sets.1), channel_id=1, replica_groups=mesh['blk'=32,'cset'=8] {'cset'}, dimensions={0} | all-to-all | bytes 1048576 | tf_op jit(solution)/shard_map/all_to_all | solution.py:388
  69.3 0.8 %copy.10 = bf16[2048,128]{1,0:T(8,128)(2,1)} copy(bf16[2048,128]{1,0:T(8,128)(2,1)S(1)} %bitcast.27) | data formatting | bytes 1048576
Async XLA Ops:
  0.0 10.6 %copy-start.7 = (bf16[256,256]{1,0:T(8,128)(2,1)S(1)}, bf16[256,256]{1,0:T(8,128)(2,1)}, u32[]{:S(2)}) copy-start(bf16[256,256]{1,0:T(8,128)(2,1)} %param.9) | copy-start | bytes 393220
  0.0 16.4 %copy-start.5 = (s32[20,924]{1,0:T(8,128)S(1)}, s32[20,924]{1,0:T(8,128)}, u32[]{:S(2)}) copy-start(s32[20,924]{1,0:T(8,128)} %left_ref.1) | copy-start | bytes 221764
  0.0 16.4 %copy-start.6 = (s32[20,924]{1,0:T(8,128)S(1)}, s32[20,924]{1,0:T(8,128)}, u32[]{:S(2)}) copy-start(s32[20,924]{1,0:T(8,128)} %right_ref.1) | copy-start | bytes 221764
  2.2 37.3 %collective-permute-start.3 = (bf16[2064,128]{1,0:T(8,128)(2,1)S(1)}, bf16[2064,128]{1,0:T(8,128)(2,1)S(1)}, u32[]{:S(2)}, u32[]{:S(2)}) collective-permute-start(bf16[2064,128]{1,0:T(8,128)(2,1)S(1)} %get-tuple-element.45), channel_id=1, source_target_pairs={{0,244},{1,245},{2,246},{3,247},{4,240},{5,241},{6,242},{7,243},{8... | collective-permute-start | bytes 1585160 | tf_op jit(solution)/shard_map/ppermute | solution.py:30
  10.6 28.9 %collective-permute-start.4 = (bf16[2064,128]{1,0:T(8,128)(2,1)S(1)}, bf16[2064,128]{1,0:T(8,128)(2,1)S(1)}, u32[]{:S(2)}, u32[]{:S(2)}) collective-permute-start(bf16[2064,128]{1,0:T(8,128)(2,1)S(1)} %get-tuple-element.46), channel_id=1, source_target_pairs={{0,20},{1,21},{2,22},{3,23},{4,16},{5,17},{6,18},{7,19},{8,28},{9,... | collective-permute-start | bytes 1585160 | tf_op jit(solution)/shard_map/ppermute | solution.py:30
  11.6 19.3 %all-to-all-start = ((bf16[8,256,256]{2,1,0:T(8,128)(2,1)}), bf16[8,256,256]{2,1,0:T(8,128)(2,1)}, u32[]{:S(2)}, u32[]{:S(2)}) async-start(bf16[8,256,256]{2,1,0:T(8,128)(2,1)} %broadcast_in_dim.17), calls=%async_computation | async-start | bytes 2097152 | tf_op jit(solution)/shard_map/all_to_all | solution.py:361
  19.3 18.4 %collective-permute-start = (bf16[1040,128]{1,0:T(8,128)(2,1)}, bf16[1040,128]{1,0:T(8,128)(2,1)S(1)}, u32[]{:S(2)}, u32[]{:S(2)}) collective-permute-start(bf16[1040,128]{1,0:T(8,128)(2,1)} %get-tuple-element.39), channel_id=1, source_target_pairs={{0,32},{1,33},{2,34},{3,35},{4,36},{5,37},{6,38},{7,39},{8,40},{9,... | collective-permute-start | bytes 798728 | tf_op jit(solution)/shard_map/ppermute | solution.py:30
  19.4 18.3 %collective-permute-start.1 = (bf16[1040,128]{1,0:T(8,128)(2,1)}, bf16[1040,128]{1,0:T(8,128)(2,1)S(1)}, u32[]{:S(2)}, u32[]{:S(2)}) collective-permute-start(bf16[1040,128]{1,0:T(8,128)(2,1)} %get-tuple-element.40), channel_id=1, source_target_pairs={{0,224},{1,225},{2,226},{3,227},{4,228},{5,229},{6,230},{7,231},{8... | collective-permute-start | bytes 798728 | tf_op jit(solution)/shard_map/ppermute | solution.py:30
  22.6 15.1 %collective-permute-start.2 = (bf16[1040,128]{1,0:T(8,128)(2,1)S(1)}, bf16[1040,128]{1,0:T(8,128)(2,1)S(1)}, u32[]{:S(2)}, u32[]{:S(2)}) collective-permute-start(bf16[1040,128]{1,0:T(8,128)(2,1)S(1)} %get-tuple-element.41), channel_id=1, source_target_pairs={{0,224},{1,225},{2,226},{3,227},{4,228},{5,229},{6,230},{7,231},{8... | collective-permute-start | bytes 798728 | tf_op jit(solution)/shard_map/ppermute | solution.py:30
  37.7 12.1 %copy-start.1 = (bf16[256,256]{1,0:T(8,128)(2,1)S(1)}, bf16[256,256]{1,0:T(8,128)(2,1)}, u32[]{:S(2)}) copy-start(bf16[256,256]{1,0:T(8,128)(2,1)} %table_ref.1) | copy-start | bytes 393220
  41.0 11.6 %copy-start = (bf16[1,1,9,8,128,128]{5,4,3,2,1,0:T(8,128)(2,1)S(1)}, bf16[1,1,9,8,128,128]{5,4,3,2,1,0:T(8,128)(2,1)}, u32[]{:S(2)}) copy-start(bf16[1,1,9,8,128,128]{5,4,3,2,1,0:T(8,128)(2,1)} %param.10) | copy-start | bytes 7077892
  41.1 11.6 %copy-start.2 = (s32[1,1,9,8]{2,3,1,0:T(8,128)S(1)}, s32[1,1,9,8]{2,3,1,0:T(8,128)}, u32[]{:S(2)}) copy-start(s32[1,1,9,8]{2,3,1,0:T(8,128)} %param.11) | copy-start | bytes 868
  41.1 11.6 %copy-start.3 = (s32[1,1,9,8]{2,3,1,0:T(8,128)S(1)}, s32[1,1,9,8]{2,3,1,0:T(8,128)}, u32[]{:S(2)}) copy-start(s32[1,1,9,8]{2,3,1,0:T(8,128)} %param.12) | copy-start | bytes 868
  41.1 11.6 %copy-start.4 = (s32[1,1,9]{2,1,0:T(1,128)S(1)}, s32[1,1,9]{2,1,0:T(1,128)}, u32[]{:S(2)}) copy-start(s32[1,1,9]{2,1,0:T(1,128)} %param.13) | copy-start | bytes 112
  41.1 12.8 %collective-permute-start.7 = (bf16[256,256]{1,0:T(8,128)(2,1)S(1)}, bf16[256,256]{1,0:T(8,128)(2,1)S(1)}, u32[]{:S(2)}, u32[]{:S(2)}) collective-permute-start(bf16[256,256]{1,0:T(8,128)(2,1)S(1)} %get-tuple-element.53), channel_id=1, source_target_pairs={{0,20},{1,21},{2,22},{3,23},{4,16},{5,17},{6,18},{7,19},{8,28},{9,... | collective-permute-start | bytes 393224 | tf_op jit(solution)/shard_map/ppermute | solution.py:30
  41.2 12.7 %collective-permute-start.8 = (bf16[256,256]{1,0:T(8,128)(2,1)S(1)}, bf16[256,256]{1,0:T(8,128)(2,1)S(1)}, u32[]{:S(2)}, u32[]{:S(2)}) collective-permute-start(bf16[256,256]{1,0:T(8,128)(2,1)S(1)} %get-tuple-element.54), channel_id=1, source_target_pairs={{0,244},{1,245},{2,246},{3,247},{4,240},{5,241},{6,242},{7,243},{8... | collective-permute-start | bytes 393224 | tf_op jit(solution)/shard_map/ppermute | solution.py:30
  46.5 7.4 %collective-permute-start.5 = (bf16[256,256]{1,0:T(8,128)(2,1)S(1)}, bf16[256,256]{1,0:T(8,128)(2,1)S(1)}, u32[]{:S(2)}, u32[]{:S(2)}) collective-permute-start(bf16[256,256]{1,0:T(8,128)(2,1)S(1)} %get-tuple-element.51), channel_id=1, source_target_pairs={{0,32},{1,33},{2,34},{3,35},{4,36},{5,37},{6,38},{7,39},{8,40},{9,... | collective-permute-start | bytes 393224 | tf_op jit(solution)/shard_map/ppermute | solution.py:30
  46.5 7.4 %collective-permute-start.6 = (bf16[256,256]{1,0:T(8,128)(2,1)S(1)}, bf16[256,256]{1,0:T(8,128)(2,1)S(1)}, u32[]{:S(2)}, u32[]{:S(2)}) collective-permute-start(bf16[256,256]{1,0:T(8,128)(2,1)S(1)} %get-tuple-element.52), channel_id=1, source_target_pairs={{0,224},{1,225},{2,226},{3,227},{4,228},{5,229},{6,230},{7,231},{8... | collective-permute-start | bytes 393224 | tf_op jit(solution)/shard_map/ppermute | solution.py:30

commit v13 on v10

--- a/solution.py
+++ b/solution.py
@@ -342,12 +342,12 @@
     nc = lax.axis_size("cset")
     at = (lax.axis_index("blk") % 2).astype(jnp.int32)[None]
 
-    first = pack_tiles((0,), at, dst, src, count, tiles_all, "pack_first")
-    *first, passive_table = lax.optimization_barrier((*first, passive_table))
+    up, down = pack_tiles((0, 1), at, dst, src, count, tiles_all, "pack_near")
+    up, down, passive_table = lax.optimization_barrier((up, down, passive_table))
     left, right = as_columns(split_active, split_passive)
-    left, later = lax.optimization_barrier((left, at))
-    rest = pack_tiles((1, 2, 3, 4), later, dst, src, count, tiles_all, "pack_rest")
-    messages = [routed(message, hops) for message, hops in zip((*first, *rest), HOPS)]
+    left, later, down = lax.optimization_barrier((left, at, down))
+    far = pack_tiles((2, 3, 4), later, dst, src, count, tiles_all, "pack_far")
+    messages = [routed(message, hops) for message, hops in zip((up, down, *far), HOPS)]
     copies = jnp.broadcast_to(passive_table[None], (nc,) + passive_table.shape)
     own_rows = lax.all_to_all(copies, "cset", split_axis=0, concat_axis=0, tiled=True)
     own_rows = own_rows.reshape(-1, passive_table.shape[1])
@@ -359,14 +359,14 @@
 
     sources, left, right = lax.optimization_barrier((sources, left, right))
     near_up, near_down, far_up, far_down, odd = messages
+    near_below, far_below = sum_away(
+        functools.partial(sum_side_kernel, 1), at, sources, (near_up, far_up, odd), "sum_below"
+    )
+    near_below, far_below, sources = lax.optimization_barrier((near_below, far_below, sources))
     near_above, far_above = sum_away(
         functools.partial(sum_side_kernel, 0), at, sources, (near_down, far_down, odd), "sum_above"
     )
-    near_above, far_above, sources = lax.optimization_barrier((near_above, far_above, sources))
-    near_below, far_below = sum_away(
-        functools.partial(sum_side_kernel, 1), at, sources, (near_up, far_up, odd), "sum_below"
-    )
-    near_below, far_below, left = lax.optimization_barrier((near_below, far_below, left))
+    near_above, far_above, left = lax.optimization_barrier((near_above, far_above, left))
     picked = pick_columns(active_table, left)
     own = sum_own(at, dst, src, count, sources, tiles_all)
     parts = [

time: 75.3 us -> 68.7 us (0.912)
  the two profiles are of different devices: /device:TPU:2 before, /device:TPU:32 now
where the time goes in v13:
time: 68.7 us; the launch traced here: 68.3 us
  starting transfers between devices  25.3 us (37%)
  blocking collectives  18.1 us (26%)
  Pallas kernels  15.9 us (23%)
  waiting for transfers between devices  5.54 us (8%)
  local copies, waits for them, and re-layouts  3.23 us (5%)
    ppermute x9, starting transfers between devices, routed(): return lax.ppermute(block, ('blk', 'cset'), route)  21 us
    all_to_all x1, blocking collectives, local(): lax.all_to_all(joined, 'cset', split_axis=0, concat_axis=0, tiled=True)  12.7 us
    all_to_all x1, blocking collectives, local(): lax.all_to_all(twice, 'blk', split_axis=0, concat_axis=0, tiled=True, axi...  5.42 us
    pallas_call x2, Pallas kernels, pack_tiles(): pl.pallas_call(functools.partial(pack_kernel, which), in_specs=[SMEM, SME...  4.88 us
    all_to_all x1, starting transfers between devices, local(): lax.all_to_all(copies, 'cset', split_axis=0, concat_axis=0, tiled=True)  4.3 us
    pallas_call x2, Pallas kernels, sum_away(): pl.pallas_call(kernel, in_specs=[SMEM] + [VMEM] * (1 + len(messages)), ou...  3.43 us
    pallas_call x1, Pallas kernels, join(): pl.pallas_call(join_kernel, in_specs=[VMEM] * 7, out_specs=VMEM, out_shap...  3.38 us
    ppermute x9, waiting for transfers between devices, routed(): return lax.ppermute(block, ('blk', 'cset'), route)  3.04 us
  transfers between devices with their start and end apart: 10, of which 3 were waited for; matrix products, arithmetic and copies ran while one was open for 4% of the time, Pallas kernels for 13%

profile of v13, /device:TPU:32, one launch (start us, length us, event | category | flops | bytes accessed | tf_op | source)
XLA Modules:
  0.0 68.3 jit_solution(434639464520603993)
XLA Ops:
  0.0 0.0 copy-start.7
  0.0 0.0 copy-start.5
  0.0 0.0 copy-start.6
  0.0 2.2 %pack_near.1 = (bf16[2064,128]{1,0:T(8,128)(2,1)S(1)}, bf16[2064,128]{1,0:T(8,128)(2,1)S(1)}) custom-call(s32[1]{0:T(128)} %bitcast.at_ref, s32[8,9]{1,0:T(8,128)} %bitcast.18, s32[8,9]{1,0:T(8,128)} %bitcast.21, s32[9]{0:T(128)} %bitcast.24, bf16[9216,128]{1,0:T(8,128)(2,1)} %bitcast.15), custom_call_target="tpu_custom_call" | custom-call | bytes 1056768 | tf_op jit(solution)/shard_map/pack_near/pallas_call | solution.py:107
  2.2 3.1 %collective-permute-start = (bf16[2064,128]{1,0:T(8,128)(2,1)S(1)}, bf16[2064,128]{1,0:T(8,128)(2,1)S(1)}, u32[]{:S(2)}, u32[]{:S(2)}) collective-permute-start(bf16[2064,128]{1,0:T(8,128)(2,1)S(1)} %get-tuple-element.40), channel_id=1, source_target_pairs={{0,20},{1,21},{2,22},{3,23},{4,16},{5,17},{6,18},{7,19},{8,28},{9,... | collective-permute-start | bytes 1585160 | tf_op jit(solution)/shard_map/ppermute | solution.py:30
  5.3 0.0 copy-done.7
  5.3 1.0 %broadcast_in_dim.17 = bf16[8,256,256]{2,1,0:T(8,128)(2,1)} broadcast(bf16[256,256]{1,0:T(8,128)(2,1)S(1)} %copy-done.7), dimensions={1,2} | broadcast | bytes 1179648 | tf_op jit(solution)/shard_map/broadcast_in_dim | solution.py:351
  6.3 4.3 %all-to-all-start = ((bf16[8,256,256]{2,1,0:T(8,128)(2,1)}), bf16[8,256,256]{2,1,0:T(8,128)(2,1)}, u32[]{:S(2)}, u32[]{:S(2)}) async-start(bf16[8,256,256]{2,1,0:T(8,128)(2,1)} %broadcast_in_dim.17), calls=%async_computation | async-start | bytes 2097152 | tf_op jit(solution)/shard_map/all_to_all | solution.py:352
  10.6 0.0 copy-done.5
  10.6 0.0 copy-done.6
  10.6 0.1 as_columns.1
  10.8 2.7 %collective-permute-start.3 = (bf16[2064,128]{1,0:T(8,128)(2,1)S(1)}, bf16[2064,128]{1,0:T(8,128)(2,1)S(1)}, u32[]{:S(2)}, u32[]{:S(2)}) collective-permute-start(bf16[2064,128]{1,0:T(8,128)(2,1)S(1)} %get-tuple-element.47), channel_id=1, source_target_pairs={{0,244},{1,245},{2,246},{3,247},{4,240},{5,241},{6,242},{7,243},{8... | collective-permute-start | bytes 1585160 | tf_op jit(solution)/shard_map/ppermute | solution.py:30
  13.4 2.7 %pack_far.1 = (bf16[1040,128]{1,0:T(8,128)(2,1)}, bf16[1040,128]{1,0:T(8,128)(2,1)S(1)}, bf16[1040,128]{1,0:T(8,128)(2,1)}) custom-call(s32[1]{0:T(128)} %bitcast.at_ref, s32[8,9]{1,0:T(8,128)} %bitcast.19, s32[8,9]{1,0:T(8,128)} %bitcast.22, s32[9]{0:T(128)} %bitcast.25, bf16[9216,128]{1,0:T(8,128)(2,1)} %bitcast.16), custom_call_target="tpu_custom_call" | custom-call | bytes 798720 | tf_op jit(solution)/shard_map/pack_far/pallas_call | solution.py:107
  16.2 2.0 %collective-permute-start.1 = (bf16[1040,128]{1,0:T(8,128)(2,1)}, bf16[1040,128]{1,0:T(8,128)(2,1)S(1)}, u32[]{:S(2)}, u32[]{:S(2)}) collective-permute-start(bf16[1040,128]{1,0:T(8,128)(2,1)} %get-tuple-element.42), channel_id=1, source_target_pairs={{0,32},{1,33},{2,34},{3,35},{4,36},{5,37},{6,38},{7,39},{8,40},{9,... | collective-permute-start | bytes 798728 | tf_op jit(solution)/shard_map/ppermute | solution.py:30
  18.1 2.5 %collective-permute-start.2 = (bf16[1040,128]{1,0:T(8,128)(2,1)}, bf16[1040,128]{1,0:T(8,128)(2,1)S(1)}, u32[]{:S(2)}, u32[]{:S(2)}) collective-permute-start(bf16[1040,128]{1,0:T(8,128)(2,1)} %get-tuple-element.43), channel_id=1, source_target_pairs={{0,224},{1,225},{2,226},{3,227},{4,228},{5,229},{6,230},{7,231},{8... | collective-permute-start | bytes 798728 | tf_op jit(solution)/shard_map/ppermute | solution.py:30
  20.6 3.1 %collective-permute-start.4 = (bf16[1040,128]{1,0:T(8,128)(2,1)S(1)}, bf16[1040,128]{1,0:T(8,128)(2,1)S(1)}, u32[]{:S(2)}, u32[]{:S(2)}) collective-permute-start(bf16[1040,128]{1,0:T(8,128)(2,1)S(1)} %get-tuple-element.48), channel_id=1, source_target_pairs={{0,224},{1,225},{2,226},{3,227},{4,228},{5,229},{6,230},{7,231},{8... | collective-permute-start | bytes 798728 | tf_op jit(solution)/shard_map/ppermute | solution.py:30
  23.8 2.5 %all-to-all-done = bf16[8,256,256]{2,1,0:T(8,128)(2,1)} async-done(((bf16[8,256,256]{2,1,0:T(8,128)(2,1)}), bf16[8,256,256]{2,1,0:T(8,128)(2,1)}, u32[]{:S(2)}, u32[]{:S(2)}) %all-to-all-start) | async-done | bytes 1048608 | tf_op jit(solution)/shard_map/all_to_all | solution.py:352
  26.3 1.4 %broadcast_in_dim.19 = bf16[2,2048,256]{2,1,0:T(8,128)(2,1)S(1)} broadcast(bf16[2048,256]{1,0:T(8,128)(2,1)} %bitcast.7), dimensions={1,2} | broadcast | bytes 3145728 | tf_op jit(solution)/shard_map/broadcast_in_dim | solution.py:355
  27.6 5.4 %all_to_all.15 = bf16[2,2048,256]{2,1,0:T(8,128)(2,1)S(1)} all-to-all(bf16[2,2048,256]{2,1,0:T(8,128)(2,1)S(1)} %broadcast_in_dim.19), channel_id=1, replica_groups={{0,8},{16,24},{32,40},{48,56},{64,72},{80,88},{96,104},{112,120},{128,1..., dimensions={0} | all-to-all | bytes 4194304 | tf_op jit(solution)/shard_map/all_to_all | solution.py:356
  33.0 0.0 collective-permute-done.1.far
  33.1 0.0 collective-permute-done.2.odd
  33.1 0.0 collective-permute-done.near
  33.1 1.7 %sum_below.1 = (bf16[256,256]{1,0:T(8,128)(2,1)S(1)}, bf16[256,256]{1,0:T(8,128)(2,1)S(1)}) custom-call(s32[1]{0:T(128)} %bitcast.at_ref, bf16[4096,256]{1,0:T(8,128)(2,1)S(1)} %bitcast.12, bf16[2064,128]{1,0:T(8,128)(2,1)S(1)} %collective-permute-done.near, bf16[1040,128]{1,0:T(8,128)(2,1)S(1)} %collective-permute-done.1.far, ...), custom_call_target="tpu_custom_call" | custom-call | flops 536870912 | bytes 3145728 | tf_op jit(solution)/shard_map/sum_below/pallas_call | solution.py:174
  34.8 0.0 copy-start.1
  34.8 0.0 collective-permute-done.4.far
  34.8 0.0 collective-permute-done.3.near
  34.8 1.7 %sum_above.1 = (bf16[256,256]{1,0:T(8,128)(2,1)S(1)}, bf16[256,256]{1,0:T(8,128)(2,1)S(1)}) custom-call(s32[1]{0:T(128)} %bitcast.at_ref, bf16[4096,256]{1,0:T(8,128)(2,1)S(1)} %bitcast.13, bf16[2064,128]{1,0:T(8,128)(2,1)S(1)} %collective-permute-done.3.near, bf16[1040,128]{1,0:T(8,128)(2,1)S(1)} %collective-permute-done.4.far, ...), custom_call_target="tpu_custom_call" | custom-call | flops 536870912 | bytes 3145728 | tf_op jit(solution)/shard_map/sum_above/pallas_call | solution.py:174
  36.5 0.0 copy-start
  36.6 0.0 copy-start.2
  36.6 0.0 copy-start.3
  36.6 0.0 copy-start.4
  36.6 1.5 %collective-permute-start.5 = (bf16[256,256]{1,0:T(8,128)(2,1)S(1)}, bf16[256,256]{1,0:T(8,128)(2,1)S(1)}, u32[]{:S(2)}, u32[]{:S(2)}) collective-permute-start(bf16[256,256]{1,0:T(8,128)(2,1)S(1)} %get-tuple-element.53), channel_id=1, source_target_pairs={{0,20},{1,21},{2,22},{3,23},{4,16},{5,17},{6,18},{7,19},{8,28},{9,... | collective-permute-start | bytes 393224 | tf_op jit(solution)/shard_map/ppermute | solution.py:30
  38.1 1.9 %collective-permute-start.6 = (bf16[256,256]{1,0:T(8,128)(2,1)S(1)}, bf16[256,256]{1,0:T(8,128)(2,1)S(1)}, u32[]{:S(2)}, u32[]{:S(2)}) collective-permute-start(bf16[256,256]{1,0:T(8,128)(2,1)S(1)} %get-tuple-element.54), channel_id=1, source_target_pairs={{0,32},{1,33},{2,34},{3,35},{4,36},{5,37},{6,38},{7,39},{8,40},{9,... | collective-permute-start | bytes 393224 | tf_op jit(solution)/shard_map/ppermute | solution.py:30
  40.0 2.7 %collective-permute-start.7 = (bf16[256,256]{1,0:T(8,128)(2,1)S(1)}, bf16[256,256]{1,0:T(8,128)(2,1)S(1)}, u32[]{:S(2)}, u32[]{:S(2)}) collective-permute-start(bf16[256,256]{1,0:T(8,128)(2,1)S(1)} %get-tuple-element.55), channel_id=1, source_target_pairs={{0,244},{1,245},{2,246},{3,247},{4,240},{5,241},{6,242},{7,243},{8... | collective-permute-start | bytes 393224 | tf_op jit(solution)/shard_map/ppermute | solution.py:30
  42.7 1.5 %collective-permute-start.8 = (bf16[256,256]{1,0:T(8,128)(2,1)S(1)}, bf16[256,256]{1,0:T(8,128)(2,1)S(1)}, u32[]{:S(2)}, u32[]{:S(2)}) collective-permute-start(bf16[256,256]{1,0:T(8,128)(2,1)S(1)} %get-tuple-element.56), channel_id=1, source_target_pairs={{0,224},{1,225},{2,226},{3,227},{4,228},{5,229},{6,230},{7,231},{8... | collective-permute-start | bytes 393224 | tf_op jit(solution)/shard_map/ppermute | solution.py:30
  44.2 0.0 copy-done.1
  44.2 2.9 %pick_active.1.picked_ref = bf16[20,256,1024]{2,1,0:T(8,128)(2,1)S(1)} custom-call(bf16[20,1,1024]{2,1,0:T(2,128)(2,1)S(1)} %get-tuple-element.52.columns_ref, bf16[256,256]{1,0:T(8,128)(2,1)S(1)} %copy-done.1), custom_call_target="tpu_custom_call" | custom-call | flops 2684354560 | bytes 10485760 | tf_op jit(solution)/shard_map/pick_active/pallas_call | solution.py:276
  47.1 0.0 copy-done
  47.2 0.0 copy-done.2
  47.2 0.0 copy-done.3
  47.2 0.0 copy-done.4
  47.2 1.2 %sum_own.1.own_ref = f32[256,256]{1,0:T(8,128)S(1)} custom-call(s32[1]{0:T(128)} %bitcast.at_ref, s32[8,9]{1,0:T(8,128)S(1)} %bitcast.20, s32[8,9]{1,0:T(8,128)S(1)} %bitcast.23, s32[9]{0:T(128)S(1)} %bitcast.26, bf16[4096,256]{1,0:T(8,128)(2,1)S(1)} %bitcast.14, bf16[9216,128]{1,0:T(8,128)(2,1)S(1)} %bitcast.17), custom_call_target="tpu_custom_call" | custom-call | flops 268435456 | bytes 2621440 | tf_op jit(solution)/shard_map/sum_own/pallas_call | solution.py:207
  48.4 0.0 collective-permute-done.5.n0
  48.4 0.0 collective-permute-done.6.n1
  48.4 0.1 collective-permute-done.7.n2
  48.5 2.9 %collective-permute-done.8.n3 = bf16[256,256]{1,0:T(8,128)(2,1)S(1)} collective-permute-done((bf16[256,256]{1,0:T(8,128)(2,1)S(1)}, bf16[256,256]{1,0:T(8,128)(2,1)S(1)}, u32[]{:S(2)}, u32[]{:S(2)}) %collective-permute-start.8) | collective-permute-done | bytes 131104 | tf_op jit(solution)/shard_map/ppermute | solution.py:30
  51.4 3.4 %join_sets.1 = bf16[8,256,128]{2,1,0:T(8,128)(2,1)S(1)} custom-call(bf16[20,1,1024]{2,1,0:T(2,128)(2,1)S(1)} %get-tuple-element.38.columns_ref, bf16[20,256,1024]{2,1,0:T(8,128)(2,1)S(1)} %pick_active.1.picked_ref, f32[256,256]{1,0:T(8,128)S(1)} %sum_own.1.own_ref, bf16[256,256]{1,0:T(8,128)(2,1)S(1)} %collective-permute-done.5.n0, ...), custom_call_target="tpu_custom_call" | custom-call | flops 2684354560 | bytes 524288 | tf_op jit(solution)/shard_map/join_sets/pallas_call | solution.py:315
  54.8 12.7 %all_to_all.16 = bf16[8,256,128]{2,1,0:T(8,128)(2,1)S(1)} all-to-all(bf16[8,256,128]{2,1,0:T(8,128)(2,1)S(1)} %join_sets.1), channel_id=1, replica_groups=mesh['blk'=32,'cset'=8] {'cset'}, dimensions={0} | all-to-all | bytes 1048576 | tf_op jit(solution)/shard_map/all_to_all | solution.py:379
  67.5 0.8 %copy.10 = bf16[2048,128]{1,0:T(8,128)(2,1)} copy(bf16[2048,128]{1,0:T(8,128)(2,1)S(1)} %bitcast.27) | data formatting | bytes 1048576
Async XLA Ops:
  0.0 5.3 %copy-start.7 = (bf16[256,256]{1,0:T(8,128)(2,1)S(1)}, bf16[256,256]{1,0:T(8,128)(2,1)}, u32[]{:S(2)}) copy-start(bf16[256,256]{1,0:T(8,128)(2,1)} %param.9) | copy-start | bytes 393220
  0.0 10.6 %copy-start.5 = (s32[20,924]{1,0:T(8,128)S(1)}, s32[20,924]{1,0:T(8,128)}, u32[]{:S(2)}) copy-start(s32[20,924]{1,0:T(8,128)} %left_ref.1) | copy-start | bytes 221764
  0.0 10.6 %copy-start.6 = (s32[20,924]{1,0:T(8,128)S(1)}, s32[20,924]{1,0:T(8,128)}, u32[]{:S(2)}) copy-start(s32[20,924]{1,0:T(8,128)} %right_ref.1) | copy-start | bytes 221764
  2.2 30.9 %collective-permute-start = (bf16[2064,128]{1,0:T(8,128)(2,1)S(1)}, bf16[2064,128]{1,0:T(8,128)(2,1)S(1)}, u32[]{:S(2)}, u32[]{:S(2)}) collective-permute-start(bf16[2064,128]{1,0:T(8,128)(2,1)S(1)} %get-tuple-element.40), channel_id=1, source_target_pairs={{0,20},{1,21},{2,22},{3,23},{4,16},{5,17},{6,18},{7,19},{8,28},{9,... | collective-permute-start | bytes 1585160 | tf_op jit(solution)/shard_map/ppermute | solution.py:30
  6.3 20.0 %all-to-all-start = ((bf16[8,256,256]{2,1,0:T(8,128)(2,1)}), bf16[8,256,256]{2,1,0:T(8,128)(2,1)}, u32[]{:S(2)}, u32[]{:S(2)}) async-start(bf16[8,256,256]{2,1,0:T(8,128)(2,1)} %broadcast_in_dim.17), calls=%async_computation | async-start | bytes 2097152 | tf_op jit(solution)/shard_map/all_to_all | solution.py:352
  10.8 24.1 %collective-permute-start.3 = (bf16[2064,128]{1,0:T(8,128)(2,1)S(1)}, bf16[2064,128]{1,0:T(8,128)(2,1)S(1)}, u32[]{:S(2)}, u32[]{:S(2)}) collective-permute-start(bf16[2064,128]{1,0:T(8,128)(2,1)S(1)} %get-tuple-element.47), channel_id=1, source_target_pairs={{0,244},{1,245},{2,246},{3,247},{4,240},{5,241},{6,242},{7,243},{8... | collective-permute-start | bytes 1585160 | tf_op jit(solution)/shard_map/ppermute | solution.py:30
  16.2 16.9 %collective-permute-start.1 = (bf16[1040,128]{1,0:T(8,128)(2,1)}, bf16[1040,128]{1,0:T(8,128)(2,1)S(1)}, u32[]{:S(2)}, u32[]{:S(2)}) collective-permute-start(bf16[1040,128]{1,0:T(8,128)(2,1)} %get-tuple-element.42), channel_id=1, source_target_pairs={{0,32},{1,33},{2,34},{3,35},{4,36},{5,37},{6,38},{7,39},{8,40},{9,... | collective-permute-start | bytes 798728 | tf_op jit(solution)/shard_map/ppermute | solution.py:30
  18.1 14.9 %collective-permute-start.2 = (bf16[1040,128]{1,0:T(8,128)(2,1)}, bf16[1040,128]{1,0:T(8,128)(2,1)S(1)}, u32[]{:S(2)}, u32[]{:S(2)}) collective-permute-start(bf16[1040,128]{1,0:T(8,128)(2,1)} %get-tuple-element.43), channel_id=1, source_target_pairs={{0,224},{1,225},{2,226},{3,227},{4,228},{5,229},{6,230},{7,231},{8... | collective-permute-start | bytes 798728 | tf_op jit(solution)/shard_map/ppermute | solution.py:30
  20.6 14.2 %collective-permute-start.4 = (bf16[1040,128]{1,0:T(8,128)(2,1)S(1)}, bf16[1040,128]{1,0:T(8,128)(2,1)S(1)}, u32[]{:S(2)}, u32[]{:S(2)}) collective-permute-start(bf16[1040,128]{1,0:T(8,128)(2,1)S(1)} %get-tuple-element.48), channel_id=1, source_target_pairs={{0,224},{1,225},{2,226},{3,227},{4,228},{5,229},{6,230},{7,231},{8... | collective-permute-start | bytes 798728 | tf_op jit(solution)/shard_map/ppermute | solution.py:30
  34.8 9.4 %copy-start.1 = (bf16[256,256]{1,0:T(8,128)(2,1)S(1)}, bf16[256,256]{1,0:T(8,128)(2,1)}, u32[]{:S(2)}) copy-start(bf16[256,256]{1,0:T(8,128)(2,1)} %table_ref.1) | copy-start | bytes 393220
  36.5 10.6 %copy-start = (bf16[1,1,9,8,128,128]{5,4,3,2,1,0:T(8,128)(2,1)S(1)}, bf16[1,1,9,8,128,128]{5,4,3,2,1,0:T(8,128)(2,1)}, u32[]{:S(2)}) copy-start(bf16[1,1,9,8,128,128]{5,4,3,2,1,0:T(8,128)(2,1)} %param.10) | copy-start | bytes 7077892
  36.6 10.6 %copy-start.2 = (s32[1,1,9,8]{2,3,1,0:T(8,128)S(1)}, s32[1,1,9,8]{2,3,1,0:T(8,128)}, u32[]{:S(2)}) copy-start(s32[1,1,9,8]{2,3,1,0:T(8,128)} %param.11) | copy-start | bytes 868
  36.6 10.6 %copy-start.3 = (s32[1,1,9,8]{2,3,1,0:T(8,128)S(1)}, s32[1,1,9,8]{2,3,1,0:T(8,128)}, u32[]{:S(2)}) copy-start(s32[1,1,9,8]{2,3,1,0:T(8,128)} %param.12) | copy-start | bytes 868
  36.6 10.6 %copy-start.4 = (s32[1,1,9]{2,1,0:T(1,128)S(1)}, s32[1,1,9]{2,1,0:T(1,128)}, u32[]{:S(2)}) copy-start(s32[1,1,9]{2,1,0:T(1,128)} %param.13) | copy-start | bytes 112
  36.6 11.8 %collective-permute-start.5 = (bf16[256,256]{1,0:T(8,128)(2,1)S(1)}, bf16[256,256]{1,0:T(8,128)(2,1)S(1)}, u32[]{:S(2)}, u32[]{:S(2)}) collective-permute-start(bf16[256,256]{1,0:T(8,128)(2,1)S(1)} %get-tuple-element.53), channel_id=1, source_target_pairs={{0,20},{1,21},{2,22},{3,23},{4,16},{5,17},{6,18},{7,19},{8,28},{9,... | collective-permute-start | bytes 393224 | tf_op jit(solution)/shard_map/ppermute | solution.py:30
  38.1 10.3 %collective-permute-start.6 = (bf16[256,256]{1,0:T(8,128)(2,1)S(1)}, bf16[256,256]{1,0:T(8,128)(2,1)S(1)}, u32[]{:S(2)}, u32[]{:S(2)}) collective-permute-start(bf16[256,256]{1,0:T(8,128)(2,1)S(1)} %get-tuple-element.54), channel_id=1, source_target_pairs={{0,32},{1,33},{2,34},{3,35},{4,36},{5,37},{6,38},{7,39},{8,40},{9,... | collective-permute-start | bytes 393224 | tf_op jit(solution)/shard_map/ppermute | solution.py:30
  40.0 8.5 %collective-permute-start.7 = (bf16[256,256]{1,0:T(8,128)(2,1)S(1)}, bf16[256,256]{1,0:T(8,128)(2,1)S(1)}, u32[]{:S(2)}, u32[]{:S(2)}) collective-permute-start(bf16[256,256]{1,0:T(8,128)(2,1)S(1)} %get-tuple-element.55), channel_id=1, source_target_pairs={{0,244},{1,245},{2,246},{3,247},{4,240},{5,241},{6,242},{7,243},{8... | collective-permute-start | bytes 393224 | tf_op jit(solution)/shard_map/ppermute | solution.py:30
  42.7 8.7 %collective-permute-start.8 = (bf16[256,256]{1,0:T(8,128)(2,1)S(1)}, bf16[256,256]{1,0:T(8,128)(2,1)S(1)}, u32[]{:S(2)}, u32[]{:S(2)}) collective-permute-start(bf16[256,256]{1,0:T(8,128)(2,1)S(1)} %get-tuple-element.56), channel_id=1, source_target_pairs={{0,224},{1,225},{2,226},{3,227},{4,228},{5,229},{6,230},{7,231},{8... | collective-permute-start | bytes 393224 | tf_op jit(solution)/shard_map/ppermute | solution.py:30

commit v14 on v13

--- a/solution.py
+++ b/solution.py
@@ -10,7 +10,7 @@
 SPLITS = 20
 OUTPAD = 1024
 TILE = 128
-CHUNK = 512
+CHUNK = 1024
 SLOTS = 8
 PAIR = 2 * SLOTS
 TAIL = 16

time: 68.7 us -> 68.6 us (level)
  no operation moved by 1% of the time
where the time goes in v14:
time: 68.6 us; the launch traced here: 68.3 us
  starting transfers between devices  25.3 us (37%)
  blocking collectives  18.1 us (26%)
  Pallas kernels  15.9 us (23%)
  waiting for transfers between devices  5.54 us (8%)
  local copies, waits for them, and re-layouts  3.23 us (5%)
    ppermute x9, starting transfers between devices, routed(): return lax.ppermute(block, ('blk', 'cset'), route)  21 us
    all_to_all x1, blocking collectives, local(): lax.all_to_all(joined, 'cset', split_axis=0, concat_axis=0, tiled=True)  12.7 us
    all_to_all x1, blocking collectives, local(): lax.all_to_all(twice, 'blk', split_axis=0, concat_axis=0, tiled=True, axi...  5.42 us
    pallas_call x2, Pallas kernels, pack_tiles(): pl.pallas_call(functools.partial(pack_kernel, which), in_specs=[SMEM, SME...  4.88 us
    all_to_all x1, starting transfers between devices, local(): lax.all_to_all(copies, 'cset', split_axis=0, concat_axis=0, tiled=True)  4.3 us
    pallas_call x2, Pallas kernels, sum_away(): pl.pallas_call(kernel, in_specs=[SMEM] + [VMEM] * (1 + len(messages)), ou...  3.43 us
    pallas_call x1, Pallas kernels, join(): pl.pallas_call(join_kernel, in_specs=[VMEM] * 7, out_specs=VMEM, out_shap...  3.36 us
    ppermute x9, waiting for transfers between devices, routed(): return lax.ppermute(block, ('blk', 'cset'), route)  3.04 us
  transfers between devices with their start and end apart: 10, of which 3 were waited for; matrix products, arithmetic and copies ran while one was open for 4% of the time, Pallas kernels for 13%

profile of v14, /device:TPU:32, one launch (start us, length us, event | category | flops | bytes accessed | tf_op | source)
XLA Modules:
  0.0 68.3 jit_solution(4685300729905447089)
XLA Ops:
  0.0 0.0 copy-start.7
  0.0 0.0 copy-start.5
  0.0 0.0 copy-start.6
  0.0 2.2 %pack_near.1 = (bf16[2064,128]{1,0:T(8,128)(2,1)S(1)}, bf16[2064,128]{1,0:T(8,128)(2,1)S(1)}) custom-call(s32[1]{0:T(128)} %bitcast.at_ref, s32[8,9]{1,0:T(8,128)} %bitcast.18, s32[8,9]{1,0:T(8,128)} %bitcast.21, s32[9]{0:T(128)} %bitcast.24, bf16[9216,128]{1,0:T(8,128)(2,1)} %bitcast.15), custom_call_target="tpu_custom_call" | custom-call | bytes 1056768 | tf_op jit(solution)/shard_map/pack_near/pallas_call | solution.py:107
  2.2 3.1 %collective-permute-start = (bf16[2064,128]{1,0:T(8,128)(2,1)S(1)}, bf16[2064,128]{1,0:T(8,128)(2,1)S(1)}, u32[]{:S(2)}, u32[]{:S(2)}) collective-permute-start(bf16[2064,128]{1,0:T(8,128)(2,1)S(1)} %get-tuple-element.40), channel_id=1, source_target_pairs={{0,20},{1,21},{2,22},{3,23},{4,16},{5,17},{6,18},{7,19},{8,28},{9,... | collective-permute-start | bytes 1585160 | tf_op jit(solution)/shard_map/ppermute | solution.py:30
  5.3 0.0 copy-done.7
  5.3 1.0 %broadcast_in_dim.17 = bf16[8,256,256]{2,1,0:T(8,128)(2,1)} broadcast(bf16[256,256]{1,0:T(8,128)(2,1)S(1)} %copy-done.7), dimensions={1,2} | broadcast | bytes 1179648 | tf_op jit(solution)/shard_map/broadcast_in_dim | solution.py:351
  6.3 4.3 %all-to-all-start = ((bf16[8,256,256]{2,1,0:T(8,128)(2,1)}), bf16[8,256,256]{2,1,0:T(8,128)(2,1)}, u32[]{:S(2)}, u32[]{:S(2)}) async-start(bf16[8,256,256]{2,1,0:T(8,128)(2,1)} %broadcast_in_dim.17), calls=%async_computation | async-start | bytes 2097152 | tf_op jit(solution)/shard_map/all_to_all | solution.py:352
  10.6 0.0 copy-done.5
  10.6 0.0 copy-done.6
  10.6 0.1 as_columns.1
  10.8 2.7 %collective-permute-start.3 = (bf16[2064,128]{1,0:T(8,128)(2,1)S(1)}, bf16[2064,128]{1,0:T(8,128)(2,1)S(1)}, u32[]{:S(2)}, u32[]{:S(2)}) collective-permute-start(bf16[2064,128]{1,0:T(8,128)(2,1)S(1)} %get-tuple-element.47), channel_id=1, source_target_pairs={{0,244},{1,245},{2,246},{3,247},{4,240},{5,241},{6,242},{7,243},{8... | collective-permute-start | bytes 1585160 | tf_op jit(solution)/shard_map/ppermute | solution.py:30
  13.4 2.7 %pack_far.1 = (bf16[1040,128]{1,0:T(8,128)(2,1)}, bf16[1040,128]{1,0:T(8,128)(2,1)S(1)}, bf16[1040,128]{1,0:T(8,128)(2,1)}) custom-call(s32[1]{0:T(128)} %bitcast.at_ref, s32[8,9]{1,0:T(8,128)} %bitcast.19, s32[8,9]{1,0:T(8,128)} %bitcast.22, s32[9]{0:T(128)} %bitcast.25, bf16[9216,128]{1,0:T(8,128)(2,1)} %bitcast.16), custom_call_target="tpu_custom_call" | custom-call | bytes 798720 | tf_op jit(solution)/shard_map/pack_far/pallas_call | solution.py:107
  16.2 2.0 %collective-permute-start.1 = (bf16[1040,128]{1,0:T(8,128)(2,1)}, bf16[1040,128]{1,0:T(8,128)(2,1)S(1)}, u32[]{:S(2)}, u32[]{:S(2)}) collective-permute-start(bf16[1040,128]{1,0:T(8,128)(2,1)} %get-tuple-element.42), channel_id=1, source_target_pairs={{0,32},{1,33},{2,34},{3,35},{4,36},{5,37},{6,38},{7,39},{8,40},{9,... | collective-permute-start | bytes 798728 | tf_op jit(solution)/shard_map/ppermute | solution.py:30
  18.1 2.5 %collective-permute-start.2 = (bf16[1040,128]{1,0:T(8,128)(2,1)}, bf16[1040,128]{1,0:T(8,128)(2,1)S(1)}, u32[]{:S(2)}, u32[]{:S(2)}) collective-permute-start(bf16[1040,128]{1,0:T(8,128)(2,1)} %get-tuple-element.43), channel_id=1, source_target_pairs={{0,224},{1,225},{2,226},{3,227},{4,228},{5,229},{6,230},{7,231},{8... | collective-permute-start | bytes 798728 | tf_op jit(solution)/shard_map/ppermute | solution.py:30
  20.6 3.1 %collective-permute-start.4 = (bf16[1040,128]{1,0:T(8,128)(2,1)S(1)}, bf16[1040,128]{1,0:T(8,128)(2,1)S(1)}, u32[]{:S(2)}, u32[]{:S(2)}) collective-permute-start(bf16[1040,128]{1,0:T(8,128)(2,1)S(1)} %get-tuple-element.48), channel_id=1, source_target_pairs={{0,224},{1,225},{2,226},{3,227},{4,228},{5,229},{6,230},{7,231},{8... | collective-permute-start | bytes 798728 | tf_op jit(solution)/shard_map/ppermute | solution.py:30
  23.8 2.5 %all-to-all-done = bf16[8,256,256]{2,1,0:T(8,128)(2,1)} async-done(((bf16[8,256,256]{2,1,0:T(8,128)(2,1)}), bf16[8,256,256]{2,1,0:T(8,128)(2,1)}, u32[]{:S(2)}, u32[]{:S(2)}) %all-to-all-start) | async-done | bytes 1048608 | tf_op jit(solution)/shard_map/all_to_all | solution.py:352
  26.3 1.4 %broadcast_in_dim.19 = bf16[2,2048,256]{2,1,0:T(8,128)(2,1)S(1)} broadcast(bf16[2048,256]{1,0:T(8,128)(2,1)} %bitcast.7), dimensions={1,2} | broadcast | bytes 3145728 | tf_op jit(solution)/shard_map/broadcast_in_dim | solution.py:355
  27.6 5.4 %all_to_all.15 = bf16[2,2048,256]{2,1,0:T(8,128)(2,1)S(1)} all-to-all(bf16[2,2048,256]{2,1,0:T(8,128)(2,1)S(1)} %broadcast_in_dim.19), channel_id=1, replica_groups={{0,8},{16,24},{32,40},{48,56},{64,72},{80,88},{96,104},{112,120},{128,1..., dimensions={0} | all-to-all | bytes 4194304 | tf_op jit(solution)/shard_map/all_to_all | solution.py:356
  33.0 0.0 collective-permute-done.1.far
  33.1 0.0 collective-permute-done.2.odd
  33.1 0.0 collective-permute-done.near
  33.1 1.7 %sum_below.1 = (bf16[256,256]{1,0:T(8,128)(2,1)S(1)}, bf16[256,256]{1,0:T(8,128)(2,1)S(1)}) custom-call(s32[1]{0:T(128)} %bitcast.at_ref, bf16[4096,256]{1,0:T(8,128)(2,1)S(1)} %bitcast.12, bf16[2064,128]{1,0:T(8,128)(2,1)S(1)} %collective-permute-done.near, bf16[1040,128]{1,0:T(8,128)(2,1)S(1)} %collective-permute-done.1.far, ...), custom_call_target="tpu_custom_call" | custom-call | flops 536870912 | bytes 3145728 | tf_op jit(solution)/shard_map/sum_below/pallas_call | solution.py:174
  34.8 0.0 copy-start.1
  34.8 0.0 collective-permute-done.4.far
  34.8 0.0 collective-permute-done.3.near
  34.8 1.7 %sum_above.1 = (bf16[256,256]{1,0:T(8,128)(2,1)S(1)}, bf16[256,256]{1,0:T(8,128)(2,1)S(1)}) custom-call(s32[1]{0:T(128)} %bitcast.at_ref, bf16[4096,256]{1,0:T(8,128)(2,1)S(1)} %bitcast.13, bf16[2064,128]{1,0:T(8,128)(2,1)S(1)} %collective-permute-done.3.near, bf16[1040,128]{1,0:T(8,128)(2,1)S(1)} %collective-permute-done.4.far, ...), custom_call_target="tpu_custom_call" | custom-call | flops 536870912 | bytes 3145728 | tf_op jit(solution)/shard_map/sum_above/pallas_call | solution.py:174
  36.5 0.0 copy-start
  36.6 0.0 copy-start.2
  36.6 0.0 copy-start.3
  36.6 0.0 copy-start.4
  36.6 1.5 %collective-permute-start.5 = (bf16[256,256]{1,0:T(8,128)(2,1)S(1)}, bf16[256,256]{1,0:T(8,128)(2,1)S(1)}, u32[]{:S(2)}, u32[]{:S(2)}) collective-permute-start(bf16[256,256]{1,0:T(8,128)(2,1)S(1)} %get-tuple-element.53), channel_id=1, source_target_pairs={{0,20},{1,21},{2,22},{3,23},{4,16},{5,17},{6,18},{7,19},{8,28},{9,... | collective-permute-start | bytes 393224 | tf_op jit(solution)/shard_map/ppermute | solution.py:30
  38.1 1.9 %collective-permute-start.6 = (bf16[256,256]{1,0:T(8,128)(2,1)S(1)}, bf16[256,256]{1,0:T(8,128)(2,1)S(1)}, u32[]{:S(2)}, u32[]{:S(2)}) collective-permute-start(bf16[256,256]{1,0:T(8,128)(2,1)S(1)} %get-tuple-element.54), channel_id=1, source_target_pairs={{0,32},{1,33},{2,34},{3,35},{4,36},{5,37},{6,38},{7,39},{8,40},{9,... | collective-permute-start | bytes 393224 | tf_op jit(solution)/shard_map/ppermute | solution.py:30
  40.0 2.7 %collective-permute-start.7 = (bf16[256,256]{1,0:T(8,128)(2,1)S(1)}, bf16[256,256]{1,0:T(8,128)(2,1)S(1)}, u32[]{:S(2)}, u32[]{:S(2)}) collective-permute-start(bf16[256,256]{1,0:T(8,128)(2,1)S(1)} %get-tuple-element.55), channel_id=1, source_target_pairs={{0,244},{1,245},{2,246},{3,247},{4,240},{5,241},{6,242},{7,243},{8... | collective-permute-start | bytes 393224 | tf_op jit(solution)/shard_map/ppermute | solution.py:30
  42.7 1.5 %collective-permute-start.8 = (bf16[256,256]{1,0:T(8,128)(2,1)S(1)}, bf16[256,256]{1,0:T(8,128)(2,1)S(1)}, u32[]{:S(2)}, u32[]{:S(2)}) collective-permute-start(bf16[256,256]{1,0:T(8,128)(2,1)S(1)} %get-tuple-element.56), channel_id=1, source_target_pairs={{0,224},{1,225},{2,226},{3,227},{4,228},{5,229},{6,230},{7,231},{8... | collective-permute-start | bytes 393224 | tf_op jit(solution)/shard_map/ppermute | solution.py:30
  44.2 0.0 copy-done.1
  44.2 2.9 %pick_active.1.picked_ref = bf16[20,256,1024]{2,1,0:T(8,128)(2,1)S(1)} custom-call(bf16[20,1,1024]{2,1,0:T(2,128)(2,1)S(1)} %get-tuple-element.52.columns_ref, bf16[256,256]{1,0:T(8,128)(2,1)S(1)} %copy-done.1), custom_call_target="tpu_custom_call" | custom-call | flops 2684354560 | bytes 10485760 | tf_op jit(solution)/shard_map/pick_active/pallas_call | solution.py:276
  47.1 0.0 copy-done
  47.2 0.0 copy-done.2
  47.2 0.0 copy-done.3
  47.2 0.0 copy-done.4
  47.2 1.2 %sum_own.1.own_ref = f32[256,256]{1,0:T(8,128)S(1)} custom-call(s32[1]{0:T(128)} %bitcast.at_ref, s32[8,9]{1,0:T(8,128)S(1)} %bitcast.20, s32[8,9]{1,0:T(8,128)S(1)} %bitcast.23, s32[9]{0:T(128)S(1)} %bitcast.26, bf16[4096,256]{1,0:T(8,128)(2,1)S(1)} %bitcast.14, bf16[9216,128]{1,0:T(8,128)(2,1)S(1)} %bitcast.17), custom_call_target="tpu_custom_call" | custom-call | flops 268435456 | bytes 2621440 | tf_op jit(solution)/shard_map/sum_own/pallas_call | solution.py:207
  48.4 0.0 collective-permute-done.5.n0
  48.4 0.0 collective-permute-done.6.n1
  48.4 0.1 collective-permute-done.7.n2
  48.5 2.9 %collective-permute-done.8.n3 = bf16[256,256]{1,0:T(8,128)(2,1)S(1)} collective-permute-done((bf16[256,256]{1,0:T(8,128)(2,1)S(1)}, bf16[256,256]{1,0:T(8,128)(2,1)S(1)}, u32[]{:S(2)}, u32[]{:S(2)}) %collective-permute-start.8) | collective-permute-done | bytes 131104 | tf_op jit(solution)/shard_map/ppermute | solution.py:30
  51.4 3.4 %join_sets.1 = bf16[8,256,128]{2,1,0:T(8,128)(2,1)S(1)} custom-call(bf16[20,1,1024]{2,1,0:T(2,128)(2,1)S(1)} %get-tuple-element.38.columns_ref, bf16[20,256,1024]{2,1,0:T(8,128)(2,1)S(1)} %pick_active.1.picked_ref, f32[256,256]{1,0:T(8,128)S(1)} %sum_own.1.own_ref, bf16[256,256]{1,0:T(8,128)(2,1)S(1)} %collective-permute-done.5.n0, ...), custom_call_target="tpu_custom_call" | custom-call | flops 2684354560 | bytes 524288 | tf_op jit(solution)/shard_map/join_sets/pallas_call | solution.py:315
  54.8 12.7 %all_to_all.16 = bf16[8,256,128]{2,1,0:T(8,128)(2,1)S(1)} all-to-all(bf16[8,256,128]{2,1,0:T(8,128)(2,1)S(1)} %join_sets.1), channel_id=1, replica_groups=mesh['blk'=32,'cset'=8] {'cset'}, dimensions={0} | all-to-all | bytes 1048576 | tf_op jit(solution)/shard_map/all_to_all | solution.py:379
  67.5 0.8 %copy.10 = bf16[2048,128]{1,0:T(8,128)(2,1)} copy(bf16[2048,128]{1,0:T(8,128)(2,1)S(1)} %bitcast.27) | data formatting | bytes 1048576
Async XLA Ops:
  0.0 5.3 %copy-start.7 = (bf16[256,256]{1,0:T(8,128)(2,1)S(1)}, bf16[256,256]{1,0:T(8,128)(2,1)}, u32[]{:S(2)}) copy-start(bf16[256,256]{1,0:T(8,128)(2,1)} %param.9) | copy-start | bytes 393220
  0.0 10.6 %copy-start.5 = (s32[20,924]{1,0:T(8,128)S(1)}, s32[20,924]{1,0:T(8,128)}, u32[]{:S(2)}) copy-start(s32[20,924]{1,0:T(8,128)} %left_ref.1) | copy-start | bytes 221764
  0.0 10.6 %copy-start.6 = (s32[20,924]{1,0:T(8,128)S(1)}, s32[20,924]{1,0:T(8,128)}, u32[]{:S(2)}) copy-start(s32[20,924]{1,0:T(8,128)} %right_ref.1) | copy-start | bytes 221764
  2.2 30.9 %collective-permute-start = (bf16[2064,128]{1,0:T(8,128)(2,1)S(1)}, bf16[2064,128]{1,0:T(8,128)(2,1)S(1)}, u32[]{:S(2)}, u32[]{:S(2)}) collective-permute-start(bf16[2064,128]{1,0:T(8,128)(2,1)S(1)} %get-tuple-element.40), channel_id=1, source_target_pairs={{0,20},{1,21},{2,22},{3,23},{4,16},{5,17},{6,18},{7,19},{8,28},{9,... | collective-permute-start | bytes 1585160 | tf_op jit(solution)/shard_map/ppermute | solution.py:30
  6.3 20.0 %all-to-all-start = ((bf16[8,256,256]{2,1,0:T(8,128)(2,1)}), bf16[8,256,256]{2,1,0:T(8,128)(2,1)}, u32[]{:S(2)}, u32[]{:S(2)}) async-start(bf16[8,256,256]{2,1,0:T(8,128)(2,1)} %broadcast_in_dim.17), calls=%async_computation | async-start | bytes 2097152 | tf_op jit(solution)/shard_map/all_to_all | solution.py:352
  10.8 24.1 %collective-permute-start.3 = (bf16[2064,128]{1,0:T(8,128)(2,1)S(1)}, bf16[2064,128]{1,0:T(8,128)(2,1)S(1)}, u32[]{:S(2)}, u32[]{:S(2)}) collective-permute-start(bf16[2064,128]{1,0:T(8,128)(2,1)S(1)} %get-tuple-element.47), channel_id=1, source_target_pairs={{0,244},{1,245},{2,246},{3,247},{4,240},{5,241},{6,242},{7,243},{8... | collective-permute-start | bytes 1585160 | tf_op jit(solution)/shard_map/ppermute | solution.py:30
  16.2 16.9 %collective-permute-start.1 = (bf16[1040,128]{1,0:T(8,128)(2,1)}, bf16[1040,128]{1,0:T(8,128)(2,1)S(1)}, u32[]{:S(2)}, u32[]{:S(2)}) collective-permute-start(bf16[1040,128]{1,0:T(8,128)(2,1)} %get-tuple-element.42), channel_id=1, source_target_pairs={{0,32},{1,33},{2,34},{3,35},{4,36},{5,37},{6,38},{7,39},{8,40},{9,... | collective-permute-start | bytes 798728 | tf_op jit(solution)/shard_map/ppermute | solution.py:30
  18.1 14.9 %collective-permute-start.2 = (bf16[1040,128]{1,0:T(8,128)(2,1)}, bf16[1040,128]{1,0:T(8,128)(2,1)S(1)}, u32[]{:S(2)}, u32[]{:S(2)}) collective-permute-start(bf16[1040,128]{1,0:T(8,128)(2,1)} %get-tuple-element.43), channel_id=1, source_target_pairs={{0,224},{1,225},{2,226},{3,227},{4,228},{5,229},{6,230},{7,231},{8... | collective-permute-start | bytes 798728 | tf_op jit(solution)/shard_map/ppermute | solution.py:30
  20.6 14.2 %collective-permute-start.4 = (bf16[1040,128]{1,0:T(8,128)(2,1)S(1)}, bf16[1040,128]{1,0:T(8,128)(2,1)S(1)}, u32[]{:S(2)}, u32[]{:S(2)}) collective-permute-start(bf16[1040,128]{1,0:T(8,128)(2,1)S(1)} %get-tuple-element.48), channel_id=1, source_target_pairs={{0,224},{1,225},{2,226},{3,227},{4,228},{5,229},{6,230},{7,231},{8... | collective-permute-start | bytes 798728 | tf_op jit(solution)/shard_map/ppermute | solution.py:30
  34.8 9.4 %copy-start.1 = (bf16[256,256]{1,0:T(8,128)(2,1)S(1)}, bf16[256,256]{1,0:T(8,128)(2,1)}, u32[]{:S(2)}) copy-start(bf16[256,256]{1,0:T(8,128)(2,1)} %table_ref.1) | copy-start | bytes 393220
  36.5 10.6 %copy-start = (bf16[1,1,9,8,128,128]{5,4,3,2,1,0:T(8,128)(2,1)S(1)}, bf16[1,1,9,8,128,128]{5,4,3,2,1,0:T(8,128)(2,1)}, u32[]{:S(2)}) copy-start(bf16[1,1,9,8,128,128]{5,4,3,2,1,0:T(8,128)(2,1)} %param.10) | copy-start | bytes 7077892
  36.6 10.6 %copy-start.2 = (s32[1,1,9,8]{2,3,1,0:T(8,128)S(1)}, s32[1,1,9,8]{2,3,1,0:T(8,128)}, u32[]{:S(2)}) copy-start(s32[1,1,9,8]{2,3,1,0:T(8,128)} %param.11) | copy-start | bytes 868
  36.6 10.6 %copy-start.3 = (s32[1,1,9,8]{2,3,1,0:T(8,128)S(1)}, s32[1,1,9,8]{2,3,1,0:T(8,128)}, u32[]{:S(2)}) copy-start(s32[1,1,9,8]{2,3,1,0:T(8,128)} %param.12) | copy-start | bytes 868
  36.6 10.6 %copy-start.4 = (s32[1,1,9]{2,1,0:T(1,128)S(1)}, s32[1,1,9]{2,1,0:T(1,128)}, u32[]{:S(2)}) copy-start(s32[1,1,9]{2,1,0:T(1,128)} %param.13) | copy-start | bytes 112
  36.6 11.8 %collective-permute-start.5 = (bf16[256,256]{1,0:T(8,128)(2,1)S(1)}, bf16[256,256]{1,0:T(8,128)(2,1)S(1)}, u32[]{:S(2)}, u32[]{:S(2)}) collective-permute-start(bf16[256,256]{1,0:T(8,128)(2,1)S(1)} %get-tuple-element.53), channel_id=1, source_target_pairs={{0,20},{1,21},{2,22},{3,23},{4,16},{5,17},{6,18},{7,19},{8,28},{9,... | collective-permute-start | bytes 393224 | tf_op jit(solution)/shard_map/ppermute | solution.py:30
  38.1 10.3 %collective-permute-start.6 = (bf16[256,256]{1,0:T(8,128)(2,1)S(1)}, bf16[256,256]{1,0:T(8,128)(2,1)S(1)}, u32[]{:S(2)}, u32[]{:S(2)}) collective-permute-start(bf16[256,256]{1,0:T(8,128)(2,1)S(1)} %get-tuple-element.54), channel_id=1, source_target_pairs={{0,32},{1,33},{2,34},{3,35},{4,36},{5,37},{6,38},{7,39},{8,40},{9,... | collective-permute-start | bytes 393224 | tf_op jit(solution)/shard_map/ppermute | solution.py:30
  40.0 8.5 %collective-permute-start.7 = (bf16[256,256]{1,0:T(8,128)(2,1)S(1)}, bf16[256,256]{1,0:T(8,128)(2,1)S(1)}, u32[]{:S(2)}, u32[]{:S(2)}) collective-permute-start(bf16[256,256]{1,0:T(8,128)(2,1)S(1)} %get-tuple-element.55), channel_id=1, source_target_pairs={{0,244},{1,245},{2,246},{3,247},{4,240},{5,241},{6,242},{7,243},{8... | collective-permute-start | bytes 393224 | tf_op jit(solution)/shard_map/ppermute | solution.py:30
  42.7 8.7 %collective-permute-start.8 = (bf16[256,256]{1,0:T(8,128)(2,1)S(1)}, bf16[256,256]{1,0:T(8,128)(2,1)S(1)}, u32[]{:S(2)}, u32[]{:S(2)}) collective-permute-start(bf16[256,256]{1,0:T(8,128)(2,1)S(1)} %get-tuple-element.56), channel_id=1, source_target_pairs={{0,224},{1,225},{2,226},{3,227},{4,228},{5,229},{6,230},{7,231},{8... | collective-permute-start | bytes 393224 | tf_op jit(solution)/shard_map/ppermute | solution.py:30
